TPU v7x, 32 devices: a whole 2x2x4 slice. The times are simulated.
32 devices in a mesh: fsdp: 2 (over y), ctx: 8 (over z, x), tp: 2 (over core).
Axes of the slice: x: 2, y: 2, z: 4, core: 2. Of those that a mesh axis runs over, the one named last changes fastest.
Arguments:
- hidden_in: bfloat16 [8192, 2048], P(('fsdp', 'ctx')), may hold values from -6 to 6
- block_order: int32 [2, 16], P('fsdp'), may hold values from 0 to 15, as said below
- attn_norm_gain: bfloat16 [2048], replicated, may hold values from 0.25 to 1.75
- attn_norm_bias: bfloat16 [2048], replicated, may hold values from -1.75 to 1.75
- query_weight: bfloat16 [2048, 2048], P(('fsdp', 'ctx'), 'tp'), may hold values from -0.125 to 0.125
- query_bias: bfloat16 [2048], P('tp'), may hold values from -1.75 to 1.75
- keyval_weight: bfloat16 [2048, 256], P(('fsdp', 'ctx')), may hold values from -0.125 to 0.125
- value_bias: bfloat16 [128], replicated, may hold values from -0.3125 to 0.3125
- proj_weight: bfloat16 [2048, 2048], P(('fsdp', 'ctx'), 'tp'), may hold values from -4 to 4
- proj_bias: bfloat16 [2048], replicated, may hold values from -1.75 to 1.75
- mlp_norm_gain: bfloat16 [2048], replicated, may hold values from 0.25 to 1.75
- mlp_norm_bias: bfloat16 [2048], replicated, may hold values from -1.75 to 1.75
- up_weight: bfloat16 [2048, 8192], P(('fsdp', 'ctx'), 'tp'), may hold values from -0.125 to 0.125
- up_bias: bfloat16 [8192], P('tp'), may hold values from -1.75 to 1.75
- down_weight: bfloat16 [2048, 8192], P(('fsdp', 'ctx'), 'tp'), may hold values from -0.0625 to 0.0625
- down_bias: bfloat16 [2048], replicated, may hold values from -1.75 to 1.75
- out_cotangent: bfloat16 [8192, 2048], P(('fsdp', 'ctx')), may hold values from -8 to 8
Outputs:
- layer_out: bfloat16 [8192, 2048], P(('fsdp', 'ctx'))
- input_grad: bfloat16 [8192, 2048], P(('fsdp', 'ctx'))
- grad_attn_norm_gain: float32 [2048], replicated
- grad_attn_norm_bias: float32 [2048], replicated
- grad_query_weight: float32 [2048, 2048], P(('fsdp', 'ctx'), 'tp')
- grad_query_bias: float32 [2048], P('tp')
- grad_keyval_weight: float32 [2048, 256], P(('fsdp', 'ctx'))
- grad_value_bias: float32 [128], replicated
- grad_proj_weight: float32 [2048, 2048], P(('fsdp', 'ctx'), 'tp')
- grad_proj_bias: float32 [2048], replicated
- grad_mlp_norm_gain: float32 [2048], replicated
- grad_mlp_norm_bias: float32 [2048], replicated
- grad_up_weight: float32 [2048, 8192], P(('fsdp', 'ctx'), 'tp')
- grad_up_bias: float32 [8192], P('tp')
- grad_down_weight: float32 [2048, 8192], P(('fsdp', 'ctx'), 'tp')
- grad_down_bias: float32 [2048], replicated
Inputs may be any that keep to these rules, and one draw needn't show every extreme that they name: `block_order`: each row is a permutation of the 16 block numbers. In each row the first, the middle (8) and the last slot hold prompt blocks of one group.
All inputs are finite; a program needn't handle non-finite values.
Results may differ from a plain program's by a relative error of at most 0.012.
Values may be sent and summed in bfloat16 or wider, within the bound.
A program may use at most 256 MiB of HBM per device.

v0:
```python
import jax
import jax.numpy as jnp
from jax import lax
from jax.sharding import PartitionSpec as P

HD = 128
BLK = 256
PBLK = 8
CONTS = 8


EPSILON = 1e-05
MASKED = -1e30


def layer_norm(values, norm_gain, norm_shift):
    average = jnp.mean(values, axis=-1, keepdims=True)
    centered = values - average
    spread = jnp.mean(centered * centered, axis=-1, keepdims=True)
    return centered * lax.rsqrt(spread + EPSILON) * norm_gain + norm_shift


def gelu_tanh(values):
    return jax.nn.gelu(values, approximate=True)


def visible_mask(position, query_rows, key_count):
    prompt_len = PBLK * BLK
    key_index = lax.broadcasted_iota(jnp.int32, (query_rows, key_count), 1)
    query_index = lax.broadcasted_iota(jnp.int32, (query_rows, key_count), 0)
    key_block = key_index // BLK
    key_pos = jnp.where(key_block < PBLK, key_index, prompt_len + key_index % BLK)
    is_prompt = position < PBLK
    query_pos = jnp.where(is_prompt, position * BLK + query_index, prompt_len + query_index)
    own_slot = key_block == PBLK
    return (key_pos <= query_pos) & jnp.logical_not(is_prompt & own_slot)


def attend_block(inputs):
    queries, keyset, position = inputs
    head_size = queries.shape[-1]
    key_part = keyset[:, :head_size]
    value_part = keyset[:, head_size:]
    scores = jnp.einsum(
        "hqd,kd->hqk", queries, key_part, preferred_element_type=jnp.float32
    ) * head_size ** (-0.5)
    allowed = visible_mask(position, queries.shape[1], key_part.shape[0])
    masked = jnp.where(allowed[None], scores, MASKED)
    largest = jnp.max(masked, axis=-1, keepdims=True)
    exponent = jnp.exp(masked - largest)
    row_total = jnp.sum(exponent, axis=-1, keepdims=True)
    attention = (exponent / row_total).astype(jnp.bfloat16)
    mixed = jnp.einsum("hqk,kd->hqd", attention, value_part, preferred_element_type=jnp.float32)
    return (mixed, (largest + jnp.log(row_total))[..., 0])


def attend_back(inputs):
    queries, keyset, position, logsum, grad_mixed = inputs
    head_size = queries.shape[-1]
    scale = head_size ** (-0.5)
    key_part = keyset[:, :head_size]
    value_part = keyset[:, head_size:]
    scores = (
        jnp.einsum("hqd,kd->hqk", queries, key_part, preferred_element_type=jnp.float32) * scale
    )
    allowed = visible_mask(position, queries.shape[1], key_part.shape[0])
    attention = jnp.where(allowed[None], jnp.exp(scores - logsum[..., None]), 0.0)
    grad_probs = jnp.einsum(
        "hqd,kd->hqk", grad_mixed, value_part, preferred_element_type=jnp.float32
    )
    inner = jnp.sum(grad_probs * attention, axis=-1, keepdims=True)
    grad_scores = (attention * (grad_probs - inner)).astype(jnp.bfloat16)
    grad_queries = (
        jnp.einsum("hqk,kd->hqd", grad_scores, key_part, preferred_element_type=jnp.float32) * scale
    )
    grad_keys = (
        jnp.einsum("hqk,hqd->kd", grad_scores, queries, preferred_element_type=jnp.float32) * scale
    )
    grad_values = jnp.einsum(
        "hqk,hqd->kd",
        attention.astype(jnp.bfloat16),
        grad_mixed,
        preferred_element_type=jnp.float32,
    )
    return (grad_queries, jnp.concatenate([grad_keys, grad_values], axis=1))


def body(
    hidden_in,
    block_order,
    attn_norm_gain,
    attn_norm_bias,
    query_weight,
    query_bias,
    keyval_weight,
    value_bias,
    proj_weight,
    proj_bias,
    mlp_norm_gain,
    mlp_norm_bias,
    up_weight,
    up_bias,
    down_weight,
    down_bias,
    out_cotangent,
):
    floats = jnp.float32
    halves = jnp.bfloat16
    rows_dev = hidden_in.shape[0]
    blocks_dev = rows_dev // BLK
    slot_count = block_order.shape[1]
    group_blocks = PBLK + CONTS
    heads_dev = query_bias.shape[0] // HD
    gain_one = attn_norm_gain.astype(floats)
    shift_one = attn_norm_bias.astype(floats)
    gain_two = mlp_norm_gain.astype(floats)
    shift_two = mlp_norm_bias.astype(floats)
    slot_ids = jnp.arange(slot_count, dtype=jnp.int32)
    ordering = block_order[0]
    inverse = jnp.sum(
        jnp.where(ordering[None, :] == slot_ids[:, None], slot_ids[None, :], 0), axis=1
    )
    first_slot = lax.axis_index("ctx") * blocks_dev
    my_slots = first_slot + jnp.arange(blocks_dev, dtype=jnp.int32)
    my_blocks = lax.dynamic_slice_in_dim(ordering, first_slot, blocks_dev)
    positions = my_blocks % group_blocks
    group_base = my_blocks // group_blocks * group_blocks
    prompt_slots = jnp.take(
        inverse, group_base[:, None] + jnp.arange(PBLK, dtype=jnp.int32)[None, :]
    )
    key_slots = jnp.concatenate([prompt_slots, my_slots[:, None]], axis=1)
    query_all, keyval_all, proj_all = (
        lax.all_gather(query_weight, ("fsdp", "ctx"), axis=0, tiled=True),
        lax.all_gather(keyval_weight, ("fsdp", "ctx"), axis=0, tiled=True),
        lax.all_gather(proj_weight, ("fsdp", "ctx"), axis=0, tiled=True),
    )
    stream = hidden_in.astype(floats)
    normed_one = layer_norm(stream, gain_one, shift_one).astype(halves)
    query_low = (jnp.dot(normed_one, query_all, preferred_element_type=floats) + query_bias).astype(
        halves
    )
    value_shift = jnp.concatenate([jnp.zeros((HD,), floats), value_bias.astype(floats)])
    keyval_low = (
        jnp.dot(normed_one, keyval_all, preferred_element_type=floats) + value_shift
    ).astype(halves)
    keyval_every = lax.all_gather(keyval_low, "ctx", axis=0, tiled=True)
    keyval_table = keyval_every.reshape(slot_count, BLK, 2 * HD)
    own_table = keyval_low.reshape(blocks_dev, 1, BLK, 2 * HD)
    keysets = jnp.concatenate([keyval_table[prompt_slots], own_table], axis=1)
    keysets = keysets.reshape(blocks_dev, (PBLK + 1) * BLK, 2 * HD)
    queries = query_low.reshape(blocks_dev, BLK, heads_dev, HD).transpose(0, 2, 1, 3)
    mixed, logsums = lax.map(attend_block, (queries, keysets, positions))
    mixed_low = mixed.transpose(0, 2, 1, 3).reshape(rows_dev, heads_dev * HD).astype(halves)
    proj_part = jnp.einsum("rk,ok->ro", mixed_low, proj_all, preferred_element_type=floats)
    attn_out = lax.psum(proj_part, "tp") + proj_bias.astype(floats)
    middle = stream + attn_out
    up_all, down_all = (
        lax.all_gather(up_weight, ("fsdp", "ctx"), axis=0, tiled=True),
        lax.all_gather(down_weight, ("fsdp", "ctx"), axis=0, tiled=True),
    )
    normed_two = layer_norm(middle, gain_two, shift_two).astype(halves)
    pre_act = jnp.dot(normed_two, up_all, preferred_element_type=floats) + up_bias.astype(floats)
    act_low = gelu_tanh(pre_act).astype(halves)
    down_part = jnp.einsum("rf,of->ro", act_low, down_all, preferred_element_type=floats)
    mlp_out = lax.psum(down_part.astype(jnp.bfloat16), "tp").astype(jnp.float32) + down_bias.astype(
        floats
    )
    layer_out = (middle + mlp_out).astype(halves)
    up_back, down_back = (up_all, down_all)
    grad_out = out_cotangent.astype(floats)
    grad_down_bias = jnp.sum(out_cotangent, axis=0, dtype=floats)
    grad_act = jnp.einsum("ro,of->rf", out_cotangent, down_back, preferred_element_type=floats)
    gelu_pull = jax.vjp(gelu_tanh, pre_act)[1]
    grad_pre = gelu_pull(grad_act)[0].astype(halves)
    grad_up_bias = jnp.sum(grad_pre, axis=0, dtype=floats)
    up_weight_grad = jnp.einsum("rd,rf->df", normed_two, grad_pre, preferred_element_type=floats)
    down_weight_grad = jnp.einsum(
        "ro,rf->of", out_cotangent, act_low, preferred_element_type=floats
    )
    grad_up_weight, grad_down_weight = (
        lax.psum_scatter(up_weight_grad, ("fsdp", "ctx"), scatter_dimension=0, tiled=True),
        lax.psum_scatter(down_weight_grad, ("fsdp", "ctx"), scatter_dimension=0, tiled=True),
    )
    normed_two_part = jnp.einsum("rf,df->rd", grad_pre, up_back, preferred_element_type=floats)
    grad_normed_two = lax.psum(normed_two_part, "tp")
    norm_two_pull = jax.vjp(layer_norm, middle, gain_two, shift_two)[1]
    grad_mid_norm, grad_mlp_norm_gain, grad_mlp_norm_bias = norm_two_pull(grad_normed_two)
    grad_middle = grad_out + grad_mid_norm
    query_back, keyval_back, proj_back = (query_all, keyval_all, proj_all)
    grad_attn = grad_middle.astype(halves)
    grad_proj_bias = jnp.sum(grad_attn, axis=0, dtype=floats)
    proj_weight_grad = jnp.einsum("ro,rk->ok", grad_attn, mixed_low, preferred_element_type=floats)
    grad_mixed = jnp.einsum(
        "ro,ok->rk", grad_attn, proj_back, preferred_element_type=floats
    ).astype(halves)
    grad_mixed_heads = grad_mixed.reshape(blocks_dev, BLK, heads_dev, HD).transpose(0, 2, 1, 3)
    grad_queries, grad_keysets = lax.map(
        attend_back, (queries, keysets, positions, logsums, grad_mixed_heads)
    )
    grad_query = grad_queries.transpose(0, 2, 1, 3).reshape(rows_dev, heads_dev * HD).astype(halves)
    grad_query_bias = jnp.sum(grad_query, axis=0, dtype=floats)
    query_weight_grad = jnp.einsum(
        "rd,rk->dk", normed_one, grad_query, preferred_element_type=floats
    )
    normed_one_part = jnp.einsum("rk,dk->rd", grad_query, query_back, preferred_element_type=floats)
    keyset_terms = grad_keysets.reshape(blocks_dev, PBLK + 1, BLK * 2 * HD)
    target_hits = (key_slots[:, :, None] == slot_ids[None, None, :]).astype(floats)
    spread_back = jnp.einsum(
        "bts,btc->sc",
        target_hits,
        keyset_terms,
        precision=lax.Precision.HIGHEST,
        preferred_element_type=floats,
    )
    incoming = lax.psum_scatter(spread_back, "ctx", scatter_dimension=0, tiled=True)
    incoming = incoming.reshape(rows_dev, 2 * HD)
    normed_one_sum, keyval_sum = lax.psum((normed_one_part, incoming), "tp")
    grad_keyval = keyval_sum.astype(halves)
    grad_value_bias = jnp.sum(grad_keyval[:, HD:], axis=0, dtype=floats)
    keyval_weight_grad = jnp.einsum(
        "rd,rc->dc", normed_one, grad_keyval, preferred_element_type=floats
    )
    grad_normed_one = normed_one_sum + jnp.einsum(
        "rc,dc->rd", grad_keyval, keyval_back, preferred_element_type=floats
    )
    norm_one_pull = jax.vjp(layer_norm, stream, gain_one, shift_one)[1]
    grad_in_norm, grad_attn_norm_gain, grad_attn_norm_bias = norm_one_pull(grad_normed_one)
    input_grad = (grad_middle + grad_in_norm).astype(halves)
    grad_query_weight, grad_keyval_weight, grad_proj_weight = (
        lax.psum_scatter(query_weight_grad, ("fsdp", "ctx"), scatter_dimension=0, tiled=True),
        lax.psum_scatter(keyval_weight_grad, ("fsdp", "ctx"), scatter_dimension=0, tiled=True),
        lax.psum_scatter(proj_weight_grad, ("fsdp", "ctx"), scatter_dimension=0, tiled=True),
    )
    summed = lax.psum(
        (
            grad_attn_norm_gain,
            grad_attn_norm_bias,
            grad_query_bias,
            grad_value_bias,
            grad_proj_bias,
            grad_mlp_norm_gain,
            grad_mlp_norm_bias,
            grad_up_bias,
            grad_down_bias,
        ),
        ("fsdp", "ctx"),
    )
    return (
        layer_out,
        input_grad,
        summed[0],
        summed[1],
        grad_query_weight,
        summed[2],
        grad_keyval_weight,
        summed[3],
        grad_proj_weight,
        summed[4],
        summed[5],
        summed[6],
        grad_up_weight,
        summed[7],
        grad_down_weight,
        summed[8],
    )


def solution(mesh):
    return jax.shard_map(
        body,
        mesh=mesh,
        in_specs=(
            P(("fsdp", "ctx"), None),
            P("fsdp", None),
            P(),
            P(),
            P(("fsdp", "ctx"), "tp"),
            P("tp"),
            P(("fsdp", "ctx"), None),
            P(),
            P(("fsdp", "ctx"), "tp"),
            P(),
            P(),
            P(),
            P(("fsdp", "ctx"), "tp"),
            P("tp"),
            P(("fsdp", "ctx"), "tp"),
            P(),
            P(("fsdp", "ctx"), None),
        ),
        out_specs=(
            P(("fsdp", "ctx"), None),
            P(("fsdp", "ctx"), None),
            P(),
            P(),
            P(("fsdp", "ctx"), "tp"),
            P("tp"),
            P(("fsdp", "ctx"), None),
            P(),
            P(("fsdp", "ctx"), "tp"),
            P(),
            P(),
            P(),
            P(("fsdp", "ctx"), "tp"),
            P("tp"),
            P(("fsdp", "ctx"), "tp"),
            P(),
        ),
        check_vma=False,
    )
```

profile of v0, /device:TPU:0, one launch (start us, length us, event | category | flops | bytes accessed | tf_op | source)
XLA Modules:
  0.0 3074.2 jit_solution(586213685154178732)
XLA Ops:
  17.6 51.3 %all-gather.9.cloned.1.call-done = bf16[2048,256]{1,0:T(8,128)(2,1)} async-done(((bf16[128,256]{1,0:T(8,128)(2,1)}), bf16[2048,256]{1,0:T(8,128)(2,1)}) %all-gather.9.cloned.1.call-update) | async-done | bytes 1048592 | tf_op jit(solution)/shard_map/all_gather | solution.py:134
  74.9 45.5 %all-gather.11.cloned.1.call-done = bf16[4096,256]{1,0:T(8,128)(2,1)} async-done(((bf16[512,256]{1,0:T(8,128)(2,1)}), bf16[4096,256]{1,0:T(8,128)(2,1)}) %all-gather.11.cloned.1.call-update) | async-done | bytes 2097168 | tf_op jit(solution)/shard_map/all_gather | solution.py:146
  127.4 70.2 %all-gather.7.cloned.1.call-done = bf16[2048,1024]{1,0:T(8,128)(2,1)} async-done(((bf16[128,1024]{1,0:T(8,128)(2,1)}), bf16[2048,1024]{1,0:T(8,128)(2,1)}) %all-gather.7.cloned.1.call-update) | async-done | bytes 4194320 | tf_op jit(solution)/shard_map/all_gather | solution.py:133
  203.8 68.8 %while.28 = (s32[]{:T(128)}, bf16[2,8,256,128]{3,2,1,0:T(8,128)(2,1)S(1)}, f32[2,8,256]{2,1,0:T(8,128)S(1)}, s32[2]{0:T(128)S(1)}, bf16[2,8,256,128]{3,2,1,0:T(8...) while((s32[]{:T(128)}, bf16[2,8,256,128]{3,2,1,0:T(8,128)(2,1)S(1)}, ...), condition=%wide.region_6.7_spmd, body=%wide.region_3.6_spmd.sunk | while | flops 2478469120 | bytes 64244892 | solution.py:152
  217.4 11.5 fusion.145
  241.8 9.6 fusion.144
  251.4 11.6 fusion.145
  282.9 25.7 all-reduce.11.cloned.1.call-done
  314.0 190.4 %all-gather.15.cloned.1.call-done = bf16[2048,4096]{1,0:T(8,128)(2,1)} async-done(((bf16[128,4096]{1,0:T(8,128)(2,1)}), bf16[2048,4096]{1,0:T(8,128)(2,1)}) %all-gather.15.cloned.1.call-update) | async-done | bytes 16777232 | tf_op jit(solution)/shard_map/all_gather | solution.py:158
  504.4 15.8 fusion.90
  520.2 177.2 %all-gather.17.cloned.1.call-done = bf16[2048,4096]{1,0:T(8,128)(2,1)} async-done(((bf16[128,4096]{1,0:T(8,128)(2,1)}), bf16[2048,4096]{1,0:T(8,128)(2,1)}) %all-gather.17.cloned.1.call-update) | async-done | bytes 16777232 | tf_op jit(solution)/shard_map/all_gather | solution.py:159
  697.4 19.0 convert_reduce_fusion
  718.5 14.1 fusion.96
  732.7 18.4 convolution_convert_fusion
  764.2 20.5 all-reduce.13.cloned.1.call-done
  799.0 124.8 %while.29 = (s32[]{:T(128)}, bf16[2,8,256,128]{3,2,1,0:T(8,128)(2,1)}, f32[2,2304,256]{2,1,0:T(8,128)}, s32[2]{0:T(128)S(1)}, bf16[2,8,256,128]{3,2,1,0:T(8,128)...) while((s32[]{:T(128)}, ...), condition=%wide.region_16.17_spmd, body=%wide.region_14.16_spmd.sunk | while | flops 6089338880 | bytes 223276368 | solution.py:197
  803.1 9.9 exponential_select_fusion.2
  813.0 12.0 multiply_reduce_fusion.5
  825.0 16.7 multiply_convert_fusion.5
  865.3 9.9 exponential_select_fusion.2
  875.2 12.0 multiply_reduce_fusion.5
  887.2 16.7 multiply_convert_fusion.5
  949.1 21.8 convolution_bitcast_fusion.2
  974.8 120.8 %all-reduce.19.cloned.1.call-done = f32[16,65536]{1,0:T(8,128)} async-done(((f32[16,65536]{1,0:T(8,128)}), f32[16,65536]{1,0:T(8,128)}) %all-reduce.19.cloned.1.call-update) | async-done | bytes 4194320
  1103.2 22.5 all-reduce.17.cloned.1.call-done
  1154.7 18.5 fusion.89
  1173.2 639.4 %reduce-scatter.14.cloned.1.call-done = f32[128,4096]{0,1:T(8,128)} async-done(((f32[2048,4096]{0,1:T(8,128)}), f32[128,4096]{0,1:T(8,128)}) %reduce-scatter.14.cloned.1.call-update) | async-done | bytes 2097168 | tf_op jit(solution)/shard_map/reduce_scatter | solution.py:182
  1815.4 112.6 %all-reduce.21.cloned.1.call-done = (f32[2048]{0:T(1024)}, f32[2048]{0:T(1024)}, f32[1024]{0:T(1024)}, f32[128]{0:T(128)}, f32[2048]{0:T(1024)}, /*index=5*/f32[...) async-done(((f32[2048]{0:T(1024)}, f32[2048]{0:T(1024)}, f32[1024]{0:T(1024)}, f32[128]{0:T(128)}, f32[2048]{0:T(1024)}, /*index=5*/f32[2048]{0:T(1024)}, ...) | async-done | bytes 70160 | tf_op jit(solution)/shard_map/psum | solution.py:234
  1928.0 83.5 %reduce-scatter.8.cloned.1.call-done = f32[128,256]{1,0:T(8,128)} async-done(((f32[2048,256]{1,0:T(8,128)}), f32[128,256]{1,0:T(8,128)}) %reduce-scatter.8.cloned.1.call-update) | async-done | bytes 131088 | tf_op jit(solution)/shard_map/reduce_scatter | solution.py:231
  2011.5 178.8 %reduce-scatter.6.cloned.1.call-done = f32[128,1024]{1,0:T(8,128)} async-done(((f32[2048,1024]{1,0:T(8,128)}), f32[128,1024]{1,0:T(8,128)}) %reduce-scatter.6.cloned.1.call-update) | async-done | bytes 524304 | tf_op jit(solution)/shard_map/reduce_scatter | solution.py:230
  2190.2 180.4 %reduce-scatter.10.cloned.1.call-done = f32[128,1024]{1,0:T(8,128)} async-done(((f32[2048,1024]{1,0:T(8,128)}), f32[128,1024]{1,0:T(8,128)}) %reduce-scatter.10.cloned.1.call-update) | async-done | bytes 524304 | tf_op jit(solution)/shard_map/reduce_scatter | solution.py:232
  2370.7 685.2 %reduce-scatter.12.cloned.1.call-done = f32[128,4096]{1,0:T(8,128)} async-done(((f32[2048,4096]{1,0:T(8,128)}), f32[128,4096]{1,0:T(8,128)}) %reduce-scatter.12.cloned.1.call-update) | async-done | bytes 2097168 | tf_op jit(solution)/shard_map/reduce_scatter | solution.py:181
  (292 shorter events, 231.0 us)
Async XLA Ops:
  7.2 61.7 %all-gather.9.cloned.1.call-start = ((), (), s32[]{:S(2)}) async-start(), calls=%async_computation.6 | async-start | bytes 1114112 | tf_op jit(solution)/shard_map/all_gather | solution.py:134
  7.9 112.5 %all-gather.11.cloned.1.call-start = ((), (), s32[]{:S(2)}) async-start(), calls=%async_computation.7 | async-start | bytes 2359296 | tf_op jit(solution)/shard_map/all_gather | solution.py:146
  15.4 58.1 %copy-start.49 = (s32[1,16]{1,0:T(1,128)S(1)}, s32[1,16]{1,0:T(1,128)}, u32[]{:S(2)}) copy-start(s32[1,16]{1,0:T(1,128)} %param.22) | copy-start | bytes 196
  15.4 58.2 %copy-start.46 = (bf16[1024]{0:T(1024)(128)(2,1)S(1)}, bf16[1024]{0:T(1024)(128)(2,1)}, u32[]{:S(2)}) copy-start(bf16[1024]{0:T(1024)(128)(2,1)} %param.26) | copy-start | bytes 6148
  72.2 52.0 %copy-start.13 = (bf16[512,256]{1,0:T(8,128)(2,1)S(1)}, bf16[512,256]{1,0:T(8,128)(2,1)}, u32[]{:S(2)}) copy-start(bf16[512,256]{1,0:T(8,128)(2,1)} %fusion.71) | copy-start | bytes 786436
  72.2 125.5 %all-gather.7.cloned.1.call-start = ((), (), s32[]{:S(2)}) async-start(), calls=%async_computation.5 | async-start | bytes 4456448 | tf_op jit(solution)/shard_map/all_gather | solution.py:133
  72.9 201.9 %all-gather.13.cloned.1.call-start = ((), (), s32[]{:S(2)}) async-start(), calls=%async_computation.8 | async-start | bytes 4456448 | tf_op jit(solution)/shard_map/all_gather | solution.py:135
  73.5 235.1 %all-reduce.11.cloned.1.call-start = ((), (), s32[]{:S(2)}) async-start(), calls=%async_computation.9 | async-start | bytes 8388608 | tf_op jit(solution)/shard_map/psum | solution.py:155
  73.7 53.8 %copy-start.39 = (s32[2]{0:T(128)}, s32[2]{0:T(128)S(1)}, u32[]{:S(2)}) copy-start(s32[2]{0:T(128)S(1)} %get-tuple-element.322) | copy-start | bytes 28
  74.6 52.8 %copy-start.47 = (s32[16]{0:T(128)}, s32[16]{0:T(128)S(1)}, u32[]{:S(2)}) copy-start(s32[16]{0:T(128)S(1)} %gather_fusion) | copy-start | bytes 196
  120.4 77.2 %copy-start.6 = (bf16[512,2048]{1,0:T(8,128)(2,1)S(1)}, bf16[512,2048]{1,0:T(8,128)(2,1)}, u32[]{:S(2)}) copy-start(bf16[512,2048]{1,0:T(8,128)(2,1)} %fusion.64) | copy-start | bytes 6291460
  281.4 223.0 %all-gather.15.cloned.1.call-start = ((), (), s32[]{:S(2)}) async-start(), calls=%async_computation.10 | async-start | bytes 17825792 | tf_op jit(solution)/shard_map/all_gather | solution.py:158
  282.0 415.5 %all-gather.17.cloned.1.call-start = ((), (), s32[]{:S(2)}) async-start(), calls=%async_computation.11 | async-start | bytes 17825792 | tf_op jit(solution)/shard_map/all_gather | solution.py:159
  282.7 476.6 %all-reduce.15.cloned.1.call-start = ((), (), s32[]{:S(2)}) async-start(), calls=%async_computation.13 | async-start | bytes 8388608 | tf_op jit(solution)/shard_map/psum | solution.py:185
  282.8 221.6 %copy-start.37 = (f32[2048]{0:T(1024)}, f32[2048]{0:T(1024)S(1)}, u32[]{:S(2)}) copy-start(f32[2048]{0:T(1024)S(1)} %convert_element_type.136) | copy-start | bytes 24580
  282.9 501.8 %copy-start.20 = (f32[2048]{0:T(1024)}, f32[2048]{0:T(1024)S(1)}, u32[]{:S(2)}) copy-start(f32[2048]{0:T(1024)S(1)} %convert_element_type.135) | copy-start | bytes 24580
  282.9 449.8 %copy-start.34 = (f32[4096]{0:T(1024)}, f32[4096]{0:T(1024)S(1)}, u32[]{:S(2)}) copy-start(f32[4096]{0:T(1024)S(1)} %convert_element_type.138) | copy-start | bytes 49156
  311.4 473.3 %copy-start.26 = (f32[512]{0:T(512)}, f32[512]{0:T(512)S(1)}, u32[]{:S(2)}) copy-start(f32[512]{0:T(512)S(1)} %broadcast_multiply_fusion) | copy-start | bytes 6148
  314.0 470.7 %copy-start.28 = (f32[512]{0:T(512)}, f32[512]{0:T(512)S(1)}, u32[]{:S(2)}) copy-start(f32[512]{0:T(512)S(1)} %fusion.86) | copy-start | bytes 6148
  314.0 383.5 %copy-start.8 = (bf16[512,2048]{1,0:T(8,128)(2,1)S(1)}, bf16[512,2048]{1,0:T(8,128)(2,1)}, u32[]{:S(2)}) copy-start(bf16[512,2048]{1,0:T(8,128)(2,1)} %param.37) | copy-start | bytes 6291460
  732.6 52.1 %all-reduce.13.cloned.1.call-start = ((), (), s32[]{:S(2)}) async-start(), calls=%async_computation.12 | async-start | bytes 4194304 | tf_op jit(solution)/shard_map/psum | solution.py:165
  751.0 344.5 %all-reduce.19.cloned.1.call-start = ((), (), s32[]{:S(2)}) async-start(), calls=%async_computation.20 | async-start | bytes 8388608
  937.9 187.8 %all-reduce.17.cloned.1.call-start = ((), (), s32[]{:S(2)}) async-start(), calls=%async_computation.14 | async-start | bytes 8388608 | tf_op jit(solution)/shard_map/psum | solution.py:217
  947.5 865.0 %reduce-scatter.14.cloned.1.call-start = ((), (), s32[]{:S(2)}) async-start(), calls=%async_computation.19 | async-start | bytes 35651584 | tf_op jit(solution)/shard_map/reduce_scatter | solution.py:182
  970.9 154.8 %copy-start.19 = (f32[2048]{0:T(1024)S(1)}, f32[2048]{0:T(1024)}, u32[]{:S(2)}) copy-start(f32[2048]{0:T(1024)} %copy-done.18) | copy-start | bytes 24580
  970.9 154.8 %copy-start.23 = (f32[512]{0:T(512)S(1)}, f32[512]{0:T(512)}, u32[]{:S(2)}) copy-start(f32[512]{0:T(512)} %copy-done.22) | copy-start | bytes 6148
  970.9 154.8 %copy-start.2 = (bf16[512,2048]{1,0:T(8,128)(2,1)S(1)}, bf16[512,2048]{1,0:T(8,128)(2,1)}, u32[]{:S(2)}) copy-start(bf16[512,2048]{1,0:T(8,128)(2,1)} %param.21) | copy-start | bytes 6291460
  970.9 957.1 %all-reduce.21.cloned.1.call-start = ((), (), s32[]{:S(2)}) async-start(), calls=%async_computation.21 | async-start | bytes 140288 | tf_op jit(solution)/shard_map/psum | solution.py:234
  1136.7 874.7 %reduce-scatter.8.cloned.1.call-start = ((), (), s32[]{:S(2)}) async-start(), calls=%async_computation.16 | async-start | bytes 2228224 | tf_op jit(solution)/shard_map/reduce_scatter | solution.py:231
  1140.7 1049.5 %reduce-scatter.6.cloned.1.call-start = ((), (), s32[]{:S(2)}) async-start(), calls=%async_computation.15 | async-start | bytes 8912896 | tf_op jit(solution)/shard_map/reduce_scatter | solution.py:230
  1146.4 1224.2 %reduce-scatter.10.cloned.1.call-start = ((), (), s32[]{:S(2)}) async-start(), calls=%async_computation.17 | async-start | bytes 8912896 | tf_op jit(solution)/shard_map/reduce_scatter | solution.py:232
  1154.0 1901.8 %reduce-scatter.12.cloned.1.call-start = ((), (), s32[]{:S(2)}) async-start(), calls=%async_computation.18 | async-start | bytes 35651584 | tf_op jit(solution)/shard_map/reduce_scatter | solution.py:181
  (48 other events, 426.6 us)
Sparse Core Ops, SparseCore 0:
  10.8 58.0 all-gather.8
  72.3 48.0 all-gather.10
  123.2 74.3 all-gather.6
  200.3 74.4 all-gather.12
  281.5 27.0 all-reduce.10
  311.6 192.7 all-gather.14
  507.6 189.7 all-gather.16
  732.7 26.6 all-reduce.14
  762.3 22.3 all-reduce.12
  938.0 157.4 all-reduce.18
  1098.2 27.4 all-reduce.16
  1127.9 684.5 reduce-scatter.13
  1820.1 107.8 all-reduce.20
  1930.8 80.6 reduce-scatter.7
  2014.3 175.9 reduce-scatter.5
  2193.1 177.5 reduce-scatter.9
  2373.6 682.2 reduce-scatter.11
where the time goes:
time: 3080 us; the launch traced here: 3070 us
  waiting for transfers between devices  2620 us (85%)
  matrix products  270 us (9%)
  other arithmetic  98.6 us (3%)
  local copies, waits for them, and re-layouts  62.1 us (2%)
    reduce_scatter x1, waiting for transfers between devices, body(): lax.psum_scatter(up_weight_grad, ('fsdp', 'ctx'), scatter_dimension=0, ti...  685 us
    reduce_scatter x1, waiting for transfers between devices, body(): lax.psum_scatter(down_weight_grad, ('fsdp', 'ctx'), scatter_dimension=0,...  639 us
    all_gather x1, waiting for transfers between devices, body(): lax.all_gather(up_weight, ('fsdp', 'ctx'), axis=0, tiled=True)  190 us
    reduce_scatter x1, waiting for transfers between devices, body(): lax.psum_scatter(proj_weight_grad, ('fsdp', 'ctx'), scatter_dimension=0,...  180 us
    reduce_scatter x1, waiting for transfers between devices, body(): lax.psum_scatter(query_weight_grad, ('fsdp', 'ctx'), scatter_dimension=0,...  179 us
    all_gather x1, waiting for transfers between devices, body(): lax.all_gather(down_weight, ('fsdp', 'ctx'), axis=0, tiled=True)  177 us
    unnamed x18, waiting for transfers between devices  124 us
    psum x1, waiting for transfers between devices, body(): lax.psum((grad_attn_norm_gain, grad_attn_norm_bias, grad_query_bias, grad...  113 us
  transfers between devices with their start and end apart: 17, of which 17 were waited for; matrix products, arithmetic and copies ran while one was open for 7% of the time, Pallas kernels for 0%

commit v1 on v0

v1 whole, which is shorter than its diff:
```python
import jax
import jax.numpy as jnp
from jax import lax
from jax.sharding import Mesh, PartitionSpec as P

HD = 128
BLK = 256
PBLK = 8
CONTS = 8
EPSILON = 1e-05
MASKED = -1e30
F32 = jnp.float32
BF16 = jnp.bfloat16
ROWS = ("fsdp", "line", "pair")
PLANE = ("fsdp", "pair")
CTX = ("line", "pair")
EVERY = ("fsdp", "line", "pair", "tp")


def layer_norm(values, norm_gain, norm_shift):
    average = jnp.mean(values, axis=-1, keepdims=True)
    centered = values - average
    spread = jnp.mean(centered * centered, axis=-1, keepdims=True)
    return centered * lax.rsqrt(spread + EPSILON) * norm_gain + norm_shift


def gelu_tanh(values):
    return jax.nn.gelu(values, approximate=True)


def visible_mask(position, query_rows, key_count):
    prompt_len = PBLK * BLK
    key_index = lax.broadcasted_iota(jnp.int32, (query_rows, key_count), 1)
    query_index = lax.broadcasted_iota(jnp.int32, (query_rows, key_count), 0)
    key_block = key_index // BLK
    key_pos = jnp.where(key_block < PBLK, key_index, prompt_len + key_index % BLK)
    is_prompt = position < PBLK
    query_pos = jnp.where(is_prompt, position * BLK + query_index, prompt_len + query_index)
    own_slot = key_block == PBLK
    return (key_pos <= query_pos) & jnp.logical_not(is_prompt & own_slot)


def attend_block(inputs):
    queries, keyset, position = inputs
    head_size = queries.shape[-1]
    key_part = keyset[:, :head_size]
    value_part = keyset[:, head_size:]
    scores = jnp.einsum(
        "hqd,kd->hqk", queries, key_part, preferred_element_type=jnp.float32
    ) * head_size ** (-0.5)
    allowed = visible_mask(position, queries.shape[1], key_part.shape[0])
    masked = jnp.where(allowed[None], scores, MASKED)
    largest = jnp.max(masked, axis=-1, keepdims=True)
    exponent = jnp.exp(masked - largest)
    row_total = jnp.sum(exponent, axis=-1, keepdims=True)
    attention = (exponent / row_total).astype(jnp.bfloat16)
    mixed = jnp.einsum("hqk,kd->hqd", attention, value_part, preferred_element_type=jnp.float32)
    return (mixed, (largest + jnp.log(row_total))[..., 0])


def attend_back(inputs):
    queries, keyset, position, logsum, grad_mixed = inputs
    head_size = queries.shape[-1]
    scale = head_size ** (-0.5)
    key_part = keyset[:, :head_size]
    value_part = keyset[:, head_size:]
    scores = (
        jnp.einsum("hqd,kd->hqk", queries, key_part, preferred_element_type=jnp.float32) * scale
    )
    allowed = visible_mask(position, queries.shape[1], key_part.shape[0])
    attention = jnp.where(allowed[None], jnp.exp(scores - logsum[..., None]), 0.0)
    grad_probs = jnp.einsum(
        "hqd,kd->hqk", grad_mixed, value_part, preferred_element_type=jnp.float32
    )
    inner = jnp.sum(grad_probs * attention, axis=-1, keepdims=True)
    grad_scores = (attention * (grad_probs - inner)).astype(jnp.bfloat16)
    grad_queries = (
        jnp.einsum("hqk,kd->hqd", grad_scores, key_part, preferred_element_type=jnp.float32) * scale
    )
    grad_keys = (
        jnp.einsum("hqk,hqd->kd", grad_scores, queries, preferred_element_type=jnp.float32) * scale
    )
    grad_values = jnp.einsum(
        "hqk,hqd->kd",
        attention.astype(jnp.bfloat16),
        grad_mixed,
        preferred_element_type=jnp.float32,
    )
    return (grad_queries, jnp.concatenate([grad_keys, grad_values], axis=1))


def swap_tp(values):
    return lax.ppermute(values, "tp", [(0, 1), (1, 0)])


def gather_rows(values):
    return lax.all_gather(values, ROWS, axis=0, tiled=True)


def sum_rows(values):
    return lax.psum_scatter(values.astype(BF16), ROWS, scatter_dimension=0, tiled=True).astype(F32)


def gather_plane(values):
    return lax.all_gather(values, PLANE + ("tp",), axis=0, tiled=True)


def sum_plane(values):
    return lax.psum_scatter(values, PLANE + ("tp",), scatter_dimension=0, tiled=True).astype(F32)


def spread_columns(values):
    quarters = lax.axis_size("fsdp") * lax.axis_size("pair")
    rows, columns = values.shape
    cut = values.reshape(rows, quarters, columns // quarters).transpose(1, 0, 2)
    return lax.all_to_all(cut, PLANE, split_axis=0, concat_axis=0, tiled=True)


def collect_columns(values):
    quarters, rows, columns = values.shape
    back = lax.all_to_all(values, PLANE, split_axis=0, concat_axis=0, tiled=True)
    return back.transpose(1, 0, 2).reshape(rows, quarters * columns)


def gather_line(values):
    lines = lax.axis_size("line")
    quarters, rows, columns = values.shape
    fsdp = lax.axis_size("fsdp")
    every = lax.all_gather(values, "line", axis=0, tiled=False)
    every = every.reshape(lines, fsdp, quarters // fsdp, rows, columns).transpose(1, 0, 2, 3, 4)
    return every.reshape(lines * quarters * rows, columns)


def sum_line(values):
    lines, fsdp, pair = lax.axis_size("line"), lax.axis_size("fsdp"), lax.axis_size("pair")
    total, columns = values.shape
    rows = total // (lines * fsdp * pair)
    ordered = values.reshape(fsdp, lines, pair, rows, columns).transpose(1, 0, 2, 3, 4)
    ordered = ordered.reshape(total, columns).astype(BF16)
    summed = lax.psum_scatter(ordered, "line", scatter_dimension=0, tiled=True)
    return summed.reshape(fsdp * pair, rows, columns)


def gather_ctx(values):
    return lax.all_gather(values, CTX, axis=0, tiled=True)


def sum_ctx(values):
    return lax.psum_scatter(values, CTX, scatter_dimension=0, tiled=True).astype(F32)


def body(
    hidden_in,
    block_order,
    attn_norm_gain,
    attn_norm_bias,
    query_weight,
    query_bias,
    keyval_weight,
    value_bias,
    proj_weight,
    proj_bias,
    mlp_norm_gain,
    mlp_norm_bias,
    up_weight,
    up_bias,
    down_weight,
    down_bias,
    out_cotangent,
):
    rows_dev = hidden_in.shape[0]
    half_rows = rows_dev // 2
    width = hidden_in.shape[1]
    blocks_dev = rows_dev // BLK
    slot_count = block_order.shape[1]
    group_blocks = PBLK + CONTS
    heads_dev = query_bias.shape[0] // HD
    head_width = heads_dev * HD
    core = lax.axis_index("tp")
    quarter = lax.axis_index("fsdp") * lax.axis_size("pair") + lax.axis_index("pair")
    quarters = lax.axis_size("fsdp") * lax.axis_size("pair")
    hidden_dev = up_weight.shape[1] // quarters

    def own_half(values):
        return lax.dynamic_slice_in_dim(values, core * half_rows, half_rows, axis=0)

    def other_half(values):
        return lax.dynamic_slice_in_dim(values, (1 - core) * half_rows, half_rows, axis=0)

    def in_order(mine, other, axis=0):
        first = jnp.where(core == 0, mine, other)
        second = jnp.where(core == 0, other, mine)
        return jnp.concatenate([first, second], axis=axis)

    def sum_halves(values):
        return own_half(values) + swap_tp(other_half(values))

    def join_halves(values):
        return in_order(values, swap_tp(values))

    gain_one = attn_norm_gain.astype(F32)
    shift_one = attn_norm_bias.astype(F32)
    gain_two = mlp_norm_gain.astype(F32)
    shift_two = mlp_norm_bias.astype(F32)

    slot_ids = jnp.arange(slot_count, dtype=jnp.int32)
    ordering = block_order[0]
    inverse = jnp.sum(
        jnp.where(ordering[None, :] == slot_ids[:, None], slot_ids[None, :], 0), axis=1
    )
    ctx_index = lax.axis_index("line") * lax.axis_size("pair") + lax.axis_index("pair")
    first_slot = ctx_index * blocks_dev
    my_slots = first_slot + jnp.arange(blocks_dev, dtype=jnp.int32)
    my_blocks = lax.dynamic_slice_in_dim(ordering, first_slot, blocks_dev)
    positions = my_blocks % group_blocks
    group_base = my_blocks // group_blocks * group_blocks
    prompt_slots = jnp.take(
        inverse, group_base[:, None] + jnp.arange(PBLK, dtype=jnp.int32)[None, :]
    )
    key_slots = jnp.concatenate([prompt_slots, my_slots[:, None]], axis=1)

    keyval_cut = lax.dynamic_slice_in_dim(keyval_weight, core * HD, HD, axis=1)
    first_all = gather_rows(jnp.concatenate([query_weight, keyval_cut], axis=1))
    proj_all = gather_rows(proj_weight)
    down_all = gather_line(spread_columns(down_weight))
    up_all = gather_line(spread_columns(up_weight))

    stream = hidden_in.astype(F32)
    normed_one = layer_norm(stream, gain_one, shift_one).astype(BF16)
    value_shift = jnp.where(core == 1, value_bias.astype(F32), 0.0)
    first_shift = jnp.concatenate([query_bias.astype(F32), value_shift])
    first_low = (jnp.dot(normed_one, first_all, preferred_element_type=F32) + first_shift).astype(
        BF16
    )
    query_low = first_low[:, :head_width]
    part_low = first_low[:, head_width:]
    part_every = gather_ctx(part_low)
    keyval_every = in_order(part_every, swap_tp(part_every), axis=1)
    keyval_low = in_order(part_low, swap_tp(part_low), axis=1)
    keyval_table = keyval_every.reshape(slot_count, BLK, 2 * HD)
    own_table = keyval_low.reshape(blocks_dev, 1, BLK, 2 * HD)
    keysets = jnp.concatenate([keyval_table[prompt_slots], own_table], axis=1)
    keysets = keysets.reshape(blocks_dev, (PBLK + 1) * BLK, 2 * HD)
    queries = query_low.reshape(blocks_dev, BLK, heads_dev, HD).transpose(0, 2, 1, 3)
    mixed, logsums = lax.map(attend_block, (queries, keysets, positions))
    mixed_low = mixed.transpose(0, 2, 1, 3).reshape(rows_dev, head_width).astype(BF16)
    proj_part = jnp.einsum("rk,ok->ro", mixed_low, proj_all, preferred_element_type=F32)
    middle = own_half(stream) + sum_halves(proj_part) + proj_bias.astype(F32)

    normed_two = layer_norm(middle, gain_two, shift_two).astype(BF16)
    cotangent = own_half(out_cotangent)
    cotangent_all = gather_plane(cotangent)
    normed_two_all = gather_plane(normed_two)
    up_shift = lax.dynamic_slice_in_dim(up_bias, quarter * hidden_dev, hidden_dev).astype(F32)
    grad_act = jnp.dot(cotangent_all, down_all, preferred_element_type=F32)
    pre_act = jnp.dot(normed_two_all, up_all, preferred_element_type=F32) + up_shift
    act, gelu_pull = jax.vjp(gelu_tanh, pre_act)
    act_low = act.astype(BF16)
    grad_pre_wide = gelu_pull(grad_act)[0]
    grad_pre = grad_pre_wide.astype(BF16)
    normed_two_part = jnp.einsum("rf,df->rd", grad_pre, up_all, preferred_element_type=F32)
    grad_normed_two = sum_plane(normed_two_part.astype(BF16))
    down_part = jnp.einsum("rf,of->ro", act_low, down_all, preferred_element_type=F32)
    mlp_out = sum_plane(down_part.astype(BF16)) + down_bias.astype(F32)
    layer_out = join_halves((middle + mlp_out).astype(BF16))
    grad_up_bias = jnp.sum(grad_pre, axis=0, dtype=F32)
    down_weight_grad = jnp.einsum("ro,rf->of", cotangent_all, act_low, preferred_element_type=F32)
    up_weight_grad = jnp.einsum("rd,rf->df", normed_two_all, grad_pre, preferred_element_type=F32)
    grad_down_weight = collect_columns(sum_line(down_weight_grad)).astype(F32)
    grad_up_weight = collect_columns(sum_line(up_weight_grad)).astype(F32)

    norm_two_pull = jax.vjp(layer_norm, middle, gain_two, shift_two)[1]
    grad_mid_norm, grad_mlp_norm_gain, grad_mlp_norm_bias = norm_two_pull(grad_normed_two)
    grad_middle = cotangent.astype(F32) + grad_mid_norm
    grad_down_bias = jnp.sum(cotangent, axis=0, dtype=F32)

    grad_attn_half = grad_middle.astype(BF16)
    grad_proj_bias = jnp.sum(grad_attn_half, axis=0, dtype=F32)
    grad_attn = join_halves(grad_attn_half)
    proj_weight_grad = jnp.einsum("ro,rk->ok", grad_attn, mixed_low, preferred_element_type=F32)
    grad_proj_weight = sum_rows(proj_weight_grad)
    grad_mixed = jnp.einsum("ro,ok->rk", grad_attn, proj_all, preferred_element_type=F32).astype(
        BF16
    )
    grad_mixed_heads = grad_mixed.reshape(blocks_dev, BLK, heads_dev, HD).transpose(0, 2, 1, 3)
    grad_queries, grad_keysets = lax.map(
        attend_back, (queries, keysets, positions, logsums, grad_mixed_heads)
    )
    grad_query = grad_queries.transpose(0, 2, 1, 3).reshape(rows_dev, head_width).astype(BF16)
    grad_query_bias = jnp.sum(grad_query, axis=0, dtype=F32)
    keyset_terms = grad_keysets.reshape(blocks_dev, PBLK + 1, BLK * 2 * HD)
    target_hits = (key_slots[:, :, None] == slot_ids[None, None, :]).astype(F32)
    spread_back = jnp.einsum(
        "bts,btc->sc",
        target_hits,
        keyset_terms,
        precision=lax.Precision.HIGHEST,
        preferred_element_type=F32,
    ).reshape(slot_count * BLK, 2 * HD)
    own_part = lax.dynamic_slice_in_dim(spread_back, core * HD, HD, axis=1)
    other_part = lax.dynamic_slice_in_dim(spread_back, (1 - core) * HD, HD, axis=1)
    part_sum = (own_part + swap_tp(other_part)).astype(BF16)
    grad_part = sum_ctx(part_sum).astype(BF16)
    grad_value_bias = jnp.where(core == 1, jnp.sum(grad_part, axis=0, dtype=F32), 0.0)
    grad_first = jnp.concatenate([grad_query, grad_part], axis=1)
    normed_one_part = jnp.einsum("rk,dk->rd", grad_first, first_all, preferred_element_type=F32)
    grad_normed_one = sum_halves(normed_one_part)
    first_weight_grad = jnp.einsum("rd,rk->dk", normed_one, grad_first, preferred_element_type=F32)
    grad_first_weight = sum_rows(first_weight_grad)
    grad_query_weight = grad_first_weight[:, :head_width]
    grad_cut = grad_first_weight[:, head_width:]
    grad_keyval_weight = in_order(grad_cut, swap_tp(grad_cut), axis=1)
    norm_one_pull = jax.vjp(layer_norm, own_half(stream), gain_one, shift_one)[1]
    grad_in_norm, grad_attn_norm_gain, grad_attn_norm_bias = norm_one_pull(grad_normed_one)
    input_grad = join_halves((grad_middle + grad_in_norm).astype(BF16))

    query_slots = jnp.zeros((2 * head_width,), F32)
    query_slots = lax.dynamic_update_slice_in_dim(
        query_slots, grad_query_bias, core * head_width, axis=0
    )
    hidden_slots = jnp.zeros((2 * quarters * hidden_dev,), F32)
    hidden_slots = lax.dynamic_update_slice_in_dim(
        hidden_slots, grad_up_bias, (core * quarters + quarter) * hidden_dev, axis=0
    )
    pieces = [
        grad_attn_norm_gain,
        grad_attn_norm_bias,
        grad_proj_bias,
        grad_mlp_norm_gain,
        grad_mlp_norm_bias,
        grad_down_bias,
        grad_value_bias,
        query_slots,
        hidden_slots,
    ]
    summed = lax.psum(jnp.concatenate(pieces), EVERY)
    cuts, start = [], 0
    for piece in pieces:
        cuts.append(summed[start : start + piece.shape[0]])
        start += piece.shape[0]
    sum_query = lax.dynamic_slice_in_dim(cuts[7], core * head_width, head_width)
    sum_up = lax.dynamic_slice_in_dim(cuts[8], core * quarters * hidden_dev, quarters * hidden_dev)
    return (
        layer_out,
        input_grad,
        cuts[0],
        cuts[1],
        grad_query_weight,
        sum_query,
        grad_keyval_weight,
        cuts[6],
        grad_proj_weight,
        cuts[2],
        cuts[3],
        cuts[4],
        grad_up_weight,
        sum_up,
        grad_down_weight,
        cuts[5],
    )


def solution(mesh):
    fsdp, ctx, tp = mesh.devices.shape
    grid = Mesh(mesh.devices.reshape(fsdp, ctx // 2, 2, tp), EVERY)
    by_rows = P(ROWS, None)
    by_both = P(ROWS, "tp")
    return jax.shard_map(
        body,
        mesh=grid,
        in_specs=(
            by_rows,
            P("fsdp", None),
            P(),
            P(),
            by_both,
            P("tp"),
            by_rows,
            P(),
            by_both,
            P(),
            P(),
            P(),
            by_both,
            P("tp"),
            by_both,
            P(),
            by_rows,
        ),
        out_specs=(
            by_rows,
            by_rows,
            P(),
            P(),
            by_both,
            P("tp"),
            by_rows,
            P(),
            by_both,
            P(),
            P(),
            P(),
            by_both,
            P("tp"),
            by_both,
            P(),
        ),
        check_vma=False,
    )
```

time: 3080 us -> 1430 us (0.46)
  waiting for transfers between devices: 2620 us -> 934 us
  matrix products: 270 us -> 212 us
  local copies, waits for them, and re-layouts: 62.1 us -> 103 us
    reduce_scatter x5 -> x7, waiting for transfers between devices: 1770 us -> 511 us  [the longest x2 234 us: sum_rows(): lax.psum_scatter(values.astype(BF16), ROWS, scatter_dimension=0, tiled=True)]
    all_gather x6 -> x7, waiting for transfers between devices: 536 us -> 307 us  [the longest x2 120 us: gather_line(): every = lax.all_gather(values, 'line', axis=0, tiled=False)]
    unnamed x18 -> x15, waiting for transfers between devices: 124 us -> 0.91 us
    psum x5 -> x1, waiting for transfers between devices: 189 us -> 98.6 us  [body(): summed = lax.psum(jnp.concatenate(pieces), EVERY)]
    dot_general x15 -> x12, matrix products: 150 us -> 117 us  [the longest x1 19.2 us: body(): grad_act = jnp.dot(cotangent_all, down_all, preferred_element_type=F32)]
  transfers between devices with their start and end apart: 17 -> 27, of which waited for: 17 -> 19; matrix products, arithmetic and copies ran while one was open for 7% -> 17% of each run, Pallas kernels for 0% -> 0%
where the time goes in v1:
time: 1430 us; the launch traced here: 1420 us
  waiting for transfers between devices  934 us (65%)
  matrix products  212 us (15%)
  other arithmetic  106 us (7%)
  local copies, waits for them, and re-layouts  103 us (7%)
  loops' own time  18.5 us (1%)
  blocking collectives  17.4 us (1%)
  between operations  15.1 us (1%)
    reduce_scatter x2, waiting for transfers between devices, sum_rows(): lax.psum_scatter(values.astype(BF16), ROWS, scatter_dimension=0, tiled=True)  234 us
    reduce_scatter x2, waiting for transfers between devices, sum_plane(): lax.psum_scatter(values, PLANE + ('tp',), scatter_dimension=0, tiled=True)  125 us
    reduce_scatter x2, waiting for transfers between devices, sum_line(): summed = lax.psum_scatter(ordered, 'line', scatter_dimension=0, tiled=True)  123 us
    all_gather x2, waiting for transfers between devices, gather_line(): every = lax.all_gather(values, 'line', axis=0, tiled=False)  120 us
    psum x1, waiting for transfers between devices, body(): summed = lax.psum(jnp.concatenate(pieces), EVERY)  98.6 us
    all_gather x2, waiting for transfers between devices, gather_plane(): return lax.all_gather(values, PLANE + ('tp',), axis=0, tiled=True)  92.3 us
    all_gather x2, waiting for transfers between devices, gather_rows(): return lax.all_gather(values, ROWS, axis=0, tiled=True)  79.4 us
  transfers between devices with their start and end apart: 27, of which 19 were waited for; matrix products, arithmetic and copies ran while one was open for 17% of the time, Pallas kernels for 0%

profile of v1, /device:TPU:0, one launch (start us, length us, event | category | flops | bytes accessed | tf_op | source)
XLA Modules:
  0.0 1420.1 jit_solution(2712811752359950843)
XLA Ops:
  15.2 79.3 %all-gather.10.cloned.1.call-done = bf16[2048,1152]{1,0:T(8,128)(2,1)} async-done(((bf16[128,1152]{1,0:T(8,128)(2,1)}), bf16[2048,1152]{1,0:T(8,128)(2,1)}) %all-gather.10.cloned.1.call-update) | async-done | bytes 4718608 | tf_op jit(solution)/shard_map/all_gather | solution.py:97
  103.0 17.4 %all_to_all.20 = bf16[4,128,1024]{1,2,0:T(8,128)(2,1)S(1)} all-to-all(bf16[4,128,1024]{1,2,0:T(8,128)(2,1)S(1)} %bitcast.232), channel_id=1, replica_groups=mesh['fsdp'=2,'line'=4,'pair'=2,'tp'=2] {'fsdp','pair'}, dimensions={0} | all-to-all | bytes 2097152 | tf_op jit(solution)/shard_map/all_to_all | solution.py:116
  128.7 15.1 %all-gather.12.cloned.1.call-done = bf16[4096,128]{1,0:T(8,128)(2,1)} async-done(((bf16[512,128]{1,0:T(8,128)(2,1)}), bf16[4096,128]{1,0:T(8,128)(2,1)}) %all-gather.12.cloned.1.call-update) | async-done | bytes 1048592 | tf_op jit(solution)/shard_map/all_gather | solution.py:145
  153.5 80.9 %while.28 = (s32[]{:T(128)}, bf16[2,8,256,128]{3,2,1,0:T(8,128)(2,1)S(1)}, f32[2,8,256]{2,1,0:T(8,128)S(1)}, s32[2]{0:T(128)S(1)}, bf16[2,8,256,128]{3,2,1,0:T(8...) while((s32[]{:T(128)}, bf16[2,8,256,128]{3,2,1,0:T(8,128)(2,1)S(1)}, ...), condition=%wide.region_6.7_spmd, body=%wide.region_3.6_spmd.sunk | while | flops 2478469120 | bytes 64244892 | solution.py:245
  157.6 9.6 fusion.124
  167.2 11.8 fusion.125
  191.8 9.6 fusion.124
  201.5 11.6 fusion.125
  259.2 43.4 %all-gather.20.cloned.1.call-done = bf16[16,128,1024]{2,1,0:T(8,128)(2,1)} async-done(((bf16[4,128,1024]{2,1,0:T(8,128)(2,1)}), bf16[16,128,1024]{2,1,0:T(8,128)(2,1)}) %all-gather.20.cloned.1.call-update) | async-done | bytes 4194320 | tf_op jit(solution)/shard_map/all_gather | solution.py:129
  307.4 76.5 %all-gather.22.cloned.1.call-done = bf16[16,128,1024]{2,1,0:T(8,128)(2,1)} async-done(((bf16[4,128,1024]{2,1,0:T(8,128)(2,1)}), bf16[16,128,1024]{2,1,0:T(8,128)(2,1)}) %all-gather.22.cloned.1.call-update) | async-done | bytes 4194320 | tf_op jit(solution)/shard_map/all_gather | solution.py:129
  388.7 50.4 %all-gather.16.cloned.1.call-done = bf16[2048,2048]{1,0:T(8,128)(2,1)} async-done(((bf16[256,2048]{1,0:T(8,128)(2,1)}), bf16[2048,2048]{1,0:T(8,128)(2,1)}) %all-gather.16.cloned.1.call-update) | async-done | bytes 8388624 | tf_op jit(solution)/shard_map/all_gather | solution.py:105
  439.1 14.4 %fusion.82 = f32[2048,1024]{1,0:T(8,128)} fusion(bf16[2048,2048]{1,0:T(8,128)(2,1)} %all-gather.16.cloned.1.call-done, bf16[2048,1024]{1,0:T(8,128)(2,1)} %bitcast.225), kind=kOutput, calls=%fused_computation.228 | convolution fusion | flops 8589934592 | bytes 20971520 | tf_op jit(solution)/shard_map/dot_general | solution.py:256
  453.6 41.9 %all-gather.18.cloned.1.call-done = bf16[2048,2048]{1,0:T(8,128)(2,1)} async-done(((bf16[256,2048]{1,0:T(8,128)(2,1)}), bf16[2048,2048]{1,0:T(8,128)(2,1)}) %all-gather.18.cloned.1.call-update) | async-done | bytes 8388624 | tf_op jit(solution)/shard_map/all_gather | solution.py:105
  495.4 19.2 %convert_reduce_fusion = (f32[1024]{0:T(1024)}, bf16[2048,1024]{1,0:T(8,128)(2,1)S(1)}) fusion(f32[2048,1024]{1,0:T(8,128)} %fusion.82, f32[1024]{0:T(1024)S(1)} %dynamic-slice_convert_fusion, bf16[2048,2048]{1,0:T(8,128)(2,1)} %all-gather.18.cloned.1.call-done, bf16[2048,1024]{1,0:T(8,128)(2,1)} %bitcast.223), kind=kOutput, calls=%fused_computation.94 | convolution fusion | flops 8638168064 | bytes 25174016 | tf_op jit(solution)/shard_map/dot_general | solution.py:255
  516.8 10.9 convolution_convert_fusion.1
  527.8 18.1 %convolution_convert_fusion.2 = bf16[2048,2048]{1,0:T(8,128)(2,1)} fusion(bf16[2048,1024]{1,0:T(8,128)(2,1)} %bitcast.224, f32[2048,1024]{1,0:T(8,128)} %fusion.82, f32[1024]{0:T(1024)S(1)} %dynamic-slice_convert_fusion), kind=kOutput, calls=%fused_computation.98 | convolution fusion | flops 8615100416 | bytes 20975616 | tf_op jit(solution)/shard_map/rf,of->ro/dot_general | solution.py:263
  546.6 52.6 %reduce-scatter.10.cloned.1.call-done = bf16[256,2048]{1,0:T(8,128)(2,1)} async-done(((bf16[2048,2048]{1,0:T(8,128)(2,1)}), bf16[256,2048]{1,0:T(8,128)(2,1)}) %reduce-scatter.10.cloned.1.call-update) | async-done | bytes 1048592 | tf_op jit(solution)/shard_map/reduce_scatter | solution.py:109
  601.8 72.5 %reduce-scatter.8.cloned.1.call-done = bf16[256,2048]{1,0:T(8,128)(2,1)} async-done(((bf16[2048,2048]{1,0:T(8,128)(2,1)}), bf16[256,2048]{1,0:T(8,128)(2,1)}) %reduce-scatter.8.cloned.1.call-update) | async-done | bytes 1048592 | tf_op jit(solution)/shard_map/reduce_scatter | solution.py:109
  686.9 106.1 %while.29 = (s32[]{:T(128)}, bf16[2,8,256,128]{3,2,1,0:T(8,128)(2,1)}, f32[2,2304,256]{2,1,0:T(8,128)}, s32[2]{0:T(128)S(1)}, bf16[2,8,256,128]{3,2,1,0:T(8,128)...) while((s32[]{:T(128)}, ...), condition=%wide.region_15.16_spmd, body=%wide.region_13.15_spmd.sunk | while | flops 6089338880 | bytes 242150608 | solution.py:286
  704.2 12.0 multiply_reduce_fusion.7
  716.2 12.6 multiply_convert_fusion.5
  757.1 12.0 multiply_reduce_fusion.7
  769.1 12.6 multiply_convert_fusion.5
  818.2 14.5 %convolution_convert_fusion.4 = bf16[2048,1024]{1,0:T(8,128)(2,1)S(1)} fusion(bf16[2048,2048]{1,0:T(8,128)(2,1)} %all-gather.18.cloned.1.call-done, f32[2048,1024]{1,0:T(8,128)} %fusion.82, f32[1024]{0:T(1024)S(1)} %copy-done.51), kind=kOutput, calls=%fused_computation.102 | convolution fusion | flops 8613003264 | bytes 20975616 | tf_op jit(solution)/shard_map/ro,rf->of/dot_general | solution.py:267
  835.4 13.2 convolution_convert_fusion.5
  853.4 28.5 %reduce-scatter.12.cloned.1.call-done = bf16[512,128]{1,0:T(8,128)(2,1)} async-done(((bf16[4096,128]{1,0:T(8,128)(2,1)}), bf16[512,128]{1,0:T(8,128)(2,1)}) %reduce-scatter.12.cloned.1.call-update) | async-done | bytes 131088 | tf_op jit(solution)/shard_map/reduce_scatter | solution.py:149
  912.7 47.3 %reduce-scatter.20.cloned.1.call-done = bf16[512,1024]{1,0:T(8,128)(2,1)} async-done(((bf16[2048,1024]{1,0:T(8,128)(2,1)}), bf16[512,1024]{1,0:T(8,128)(2,1)}) %reduce-scatter.20.cloned.1.call-update) | async-done | bytes 1048592 | tf_op jit(solution)/shard_map/reduce_scatter | solution.py:140
  963.7 75.8 %reduce-scatter.18.cloned.1.call-done = bf16[512,1024]{1,0:T(8,128)(2,1)} async-done(((bf16[2048,1024]{1,0:T(8,128)(2,1)}), bf16[512,1024]{1,0:T(8,128)(2,1)}) %reduce-scatter.18.cloned.1.call-update) | async-done | bytes 1048592 | tf_op jit(solution)/shard_map/reduce_scatter | solution.py:140
  1048.7 9.2 all-to-all-done.2
  1069.4 98.6 %all-reduce.2.cloned.1.call-done = f32[22656]{0:T(1024)} async-done(((f32[22656]{0:T(1024)}), f32[22656]{0:T(1024)}) %all-reduce.2.cloned.1.call-update) | async-done | bytes 90640 | tf_op jit(solution)/shard_map/psum | solution.py:336
  1174.0 138.0 %reduce-scatter.14.cloned.1.call-done = bf16[128,1152]{1,0:T(8,128)(2,1)} async-done(((bf16[2048,1152]{1,0:T(8,128)(2,1)}), bf16[128,1152]{1,0:T(8,128)(2,1)}) %reduce-scatter.14.cloned.1.call-update) | async-done | bytes 294928 | tf_op jit(solution)/shard_map/reduce_scatter | solution.py:101
  1314.3 95.7 %reduce-scatter.16.cloned.1.call-done = bf16[128,1024]{1,0:T(8,128)(2,1)} async-done(((bf16[2048,1024]{1,0:T(8,128)(2,1)}), bf16[128,1024]{1,0:T(8,128)(2,1)}) %reduce-scatter.16.cloned.1.call-update) | async-done | bytes 262160 | tf_op jit(solution)/shard_map/reduce_scatter | solution.py:101
  (351 shorter events, 262.3 us)
Async XLA Ops:
  7.2 87.4 %all-gather.10.cloned.1.call-start = ((), (), s32[]{:S(2)}) async-start(), calls=%async_computation.11 | async-start | bytes 5013504 | tf_op jit(solution)/shard_map/all_gather | solution.py:97
  9.7 134.1 %all-gather.12.cloned.1.call-start = ((), (), s32[]{:S(2)}) async-start(), calls=%async_computation.12 | async-start | bytes 1179648 | tf_op jit(solution)/shard_map/all_gather | solution.py:145
  11.2 88.7 %copy-start.27 = (f32[2048]{0:T(1024)}, f32[2048]{0:T(1024)S(1)}, u32[]{:S(2)}) copy-start(f32[2048]{0:T(1024)S(1)} %convert_element_type.186) | copy-start | bytes 24580
  11.9 88.0 %copy-start.38 = (f32[2048]{0:T(1024)}, f32[2048]{0:T(1024)S(1)}, u32[]{:S(2)}) copy-start(f32[2048]{0:T(1024)S(1)} %convert_element_type.187) | copy-start | bytes 24580
  100.6 134.6 %all-gather.14.cloned.1.call-start = ((), (), s32[]{:S(2)}) async-start(), calls=%async_computation.13 | async-start | bytes 4456448 | tf_op jit(solution)/shard_map/all_gather | solution.py:97
  101.3 201.2 %all-gather.20.cloned.1.call-start = ((), (), s32[]{:S(2)}) async-start(), calls=%async_computation.24 | async-start | bytes 5242880 | tf_op jit(solution)/shard_map/all_gather | solution.py:129
  124.0 20.3 %all-to-all-start.1 = ((bf16[4,128,1024]{1,2,0:T(8,128)(2,1)}), bf16[4,128,1024]{1,2,0:T(8,128)(2,1)S(1)}, u32[]{:S(2)}, u32[]{:S(2)}) async-start(bf16[4,128,1024]{1,2,0:T(8,128)(2,1)} %bitcast.35), calls=%async_computation.1 | async-start | bytes 2097152 | tf_op jit(solution)/shard_map/all_to_all | solution.py:116
  127.6 256.3 %all-gather.22.cloned.1.call-start = ((), (), s32[]{:S(2)}) async-start(), calls=%async_computation.25 | async-start | bytes 5242880 | tf_op jit(solution)/shard_map/all_gather | solution.py:129
  143.9 3.8 collective-permute-start
  145.7 293.5 %all-gather.16.cloned.1.call-start = ((), (), s32[]{:S(2)}) async-start(), calls=%async_computation.14 | async-start | bytes 9437184 | tf_op jit(solution)/shard_map/all_gather | solution.py:105
  145.7 1.9 collective-permute-start.1
  244.3 5.2 collective-permute-start.2
  255.3 240.1 %all-gather.18.cloned.1.call-start = ((), (), s32[]{:S(2)}) async-start(), calls=%async_computation.16 | async-start | bytes 9437184 | tf_op jit(solution)/shard_map/all_gather | solution.py:105
  258.4 340.8 %reduce-scatter.10.cloned.1.call-start = ((), (), s32[]{:S(2)}) async-start(), calls=%async_computation.17 | async-start | bytes 9437184 | tf_op jit(solution)/shard_map/reduce_scatter | solution.py:109
  259.2 268.6 %copy-start.50 = (f32[1024]{0:T(1024)}, f32[1024]{0:T(1024)S(1)}, u32[]{:S(2)}) copy-start(f32[1024]{0:T(1024)S(1)} %dynamic-slice_convert_fusion) | copy-start | bytes 12292
  527.7 146.6 %reduce-scatter.8.cloned.1.call-start = ((), (), s32[]{:S(2)}) async-start(), calls=%async_computation.15 | async-start | bytes 9437184 | tf_op jit(solution)/shard_map/reduce_scatter | solution.py:109
  545.9 335.9 %reduce-scatter.12.cloned.1.call-start = ((), (), s32[]{:S(2)}) async-start(), calls=%async_computation.18 | async-start | bytes 1179648 | tf_op jit(solution)/shard_map/reduce_scatter | solution.py:149
  680.0 2.7 collective-permute-start.4
  812.7 4.2 collective-permute-start.5
  818.2 141.9 %reduce-scatter.20.cloned.1.call-start = ((), (), s32[]{:S(2)}) async-start(), calls=%async_computation.23 | async-start | bytes 5242880 | tf_op jit(solution)/shard_map/reduce_scatter | solution.py:140
  835.4 204.1 %reduce-scatter.18.cloned.1.call-start = ((), (), s32[]{:S(2)}) async-start(), calls=%async_computation.22 | async-start | bytes 5242880 | tf_op jit(solution)/shard_map/reduce_scatter | solution.py:140
  851.2 316.8 %all-reduce.2.cloned.1.call-start = ((), (), s32[]{:S(2)}) async-start(), calls=%async_computation.19 | async-start | bytes 188416 | tf_op jit(solution)/shard_map/psum | solution.py:336
  891.2 4.5 collective-permute-start.6
  901.4 410.5 %reduce-scatter.14.cloned.1.call-start = ((), (), s32[]{:S(2)}) async-start(), calls=%async_computation.20 | async-start | bytes 5013504 | tf_op jit(solution)/shard_map/reduce_scatter | solution.py:101
  906.5 503.6 %reduce-scatter.16.cloned.1.call-start = ((), (), s32[]{:S(2)}) async-start(), calls=%async_computation.21 | async-start | bytes 4456448 | tf_op jit(solution)/shard_map/reduce_scatter | solution.py:101
  960.1 79.5 %all-to-all-start.3 = ((bf16[4,128,1024]{2,1,0:T(8,128)(2,1)}), bf16[4,128,1024]{2,1,0:T(8,128)(2,1)S(1)}, u32[]{:S(2)}, u32[]{:S(2)}) async-start(bf16[4,128,1024]{2,1,0:T(8,128)(2,1)} %bitcast.238), calls=%async_computation.10 | async-start | bytes 2097152 | tf_op jit(solution)/shard_map/all_to_all | solution.py:121
  1039.5 18.3 %all-to-all-start.2 = ((bf16[4,128,1024]{2,1,0:T(8,128)(2,1)}), bf16[4,128,1024]{2,1,0:T(8,128)(2,1)}, u32[]{:S(2)}, u32[]{:S(2)}) async-start(bf16[4,128,1024]{2,1,0:T(8,128)(2,1)} %bitcast.237), calls=%async_computation.8 | async-start | bytes 2097152 | tf_op jit(solution)/shard_map/all_to_all | solution.py:121
  1064.2 3.4 collective-permute-start.3
  1067.2 105.4 %collective-permute-start.7 = (bf16[256,2048]{1,0:T(8,128)(2,1)S(1)}, bf16[256,2048]{1,0:T(8,128)(2,1)}, u32[]{:S(2)}, u32[]{:S(2)}) collective-permute-start(bf16[256,2048]{1,0:T(8,128)(2,1)S(1)} %add_convert_fusion.1), channel_id=1, source_target_pairs={{0,1},{1,0},{2,3},{3,2},{4,5},{5,4},{6,7},{7,6},{8,9},{9,8},{10,11... | collective-permute-start | bytes 3145736 | tf_op jit(solution)/shard_map/ppermute | solution.py:93
  1172.6 240.8 %copy-start.1 = (bf16[128,256]{1,0:T(8,128)(2,1)S(1)}, bf16[128,256]{1,0:T(8,128)(2,1)}, u32[]{:S(2)}) copy-start(bf16[128,256]{1,0:T(8,128)(2,1)} %param.27) | copy-start | bytes 196612
  1312.0 99.8 %copy-start.16 = (bf16[128,1152]{1,0:T(8,128)(2,1)S(1)}, bf16[128,1152]{1,0:T(8,128)(2,1)}, u32[]{:S(2)}) copy-start(bf16[128,1152]{1,0:T(8,128)(2,1)} %reduce-scatter.14.cloned.1.call-done) | copy-start | bytes 884740
  1312.8 99.9 %collective-permute-start.8 = (f32[128,128]{1,0:T(8,128)S(1)}, f32[128,128]{1,0:T(8,128)S(1)}, u32[]{:S(2)}, u32[]{:S(2)}) collective-permute-start(f32[128,128]{1,0:T(8,128)S(1)} %slice.90), channel_id=1, source_target_pairs={{0,1},{1,0},{2,3},{3,2},{4,5},{5,4},{6,7},{7,6},{8,9},{9,8},{10,11... | collective-permute-start | bytes 196616 | tf_op jit(solution)/shard_map/ppermute | solution.py:93
  (55 other events, 675.9 us)
Sparse Core Ops, SparseCore 0:
  11.4 83.1 all-gather.9
  100.7 43.1 all-gather.11
  146.7 74.4 all-gather.13
  223.1 79.3 all-gather.19
  304.5 79.2 all-gather.21
  386.2 52.9 all-gather.15
  441.0 54.3 all-gather.17
  527.9 71.2 reduce-scatter.9
  603.0 71.2 reduce-scatter.7
  818.3 63.5 reduce-scatter.11
  884.3 75.7 reduce-scatter.19
  962.2 77.2 reduce-scatter.17
  1046.6 121.3 all-reduce.1
  1173.8 138.1 reduce-scatter.13
  1314.1 95.8 reduce-scatter.15

commit v2 on v1

v2 whole, which is shorter than its diff:
```python
import functools

import jax
import jax.numpy as jnp
from jax import lax
from jax.experimental import pallas as pl
from jax.experimental.pallas import tpu as pltpu
from jax.sharding import Mesh, PartitionSpec as P

HD = 128
BLK = 256
PBLK = 8
CONTS = 8
EPSILON = 1e-05
MASKED = -1e30
F32 = jnp.float32
BF16 = jnp.bfloat16
ROWS = ("fsdp", "line", "pair")
EVERY = ("fsdp", "line", "pair", "tp")


def layer_norm(values, norm_gain, norm_shift):
    average = jnp.mean(values, axis=-1, keepdims=True)
    centered = values - average
    spread = jnp.mean(centered * centered, axis=-1, keepdims=True)
    return centered * lax.rsqrt(spread + EPSILON) * norm_gain + norm_shift


def gelu_tanh(values):
    return jax.nn.gelu(values, approximate=True)


MESH_ID = pl.DeviceIdType.MESH
VMEM_BYTES = 56 * 1024 * 1024
SIDE = ("pair", "fsdp")
FRONT = ("fsdp", "pair")


def here():
    return {name: lax.axis_index(name) for name in EVERY}


def flip(place, step):
    place = dict(place)
    if isinstance(step, str):
        place[step] = 1 - place[step]
    else:
        core = place["tp"]
        for name, used in ((step[0], 1 - core), (step[1], core)):
            place[name] = place[name] + (1 - 2 * place[name]) * used
    return place


def along(place, amount):
    return dict(place, line=place["line"] + amount)


def greet(me, steps, lines):
    barrier = pltpu.get_barrier_semaphore()
    for step in steps:
        pl.semaphore_signal(barrier, inc=1, device_id=flip(me, step), device_id_type=MESH_ID)
    count = len(steps)
    if lines > 1:
        for amount in (-1, 1):
            there = me["line"] + amount
            inside = (there >= 0) & (there < lines)

            @pl.when(inside)
            def _():
                pl.semaphore_signal(
                    barrier, inc=1, device_id=along(me, amount), device_id_type=MESH_ID
                )

            count = count + inside.astype(jnp.int32)
    pl.semaphore_wait(barrier, count)


def remote(source, target, send_sem, recv_sem, place):
    return pltpu.make_async_remote_copy(
        src_ref=source,
        dst_ref=target,
        send_sem=send_sem,
        recv_sem=recv_sem,
        device_id=place,
        device_id_type=MESH_ID,
    )


def top_bit(bits):
    return bits.bit_length() - 1


def gather_kernel(steps, lines, slot, x_ref, out_ref, own_sem, line_send, line_recv, send, recv):
    me = here()
    count = len(steps)
    my_line = me["line"] if lines > 1 else 0

    def origin(bits, shard):
        place = me
        for k in reversed(range(count)):
            if bits >> k & 1:
                place = flip(place, steps[k])
        return dict(place, line=shard)

    def block(bits, shard):
        return slot(out_ref, origin(bits, shard))

    def to_step(k, bits, shard, source):
        return remote(
            source,
            block(bits, shard),
            send.at[shard, k * (1 << count) + bits],
            recv.at[shard, bits | 1 << k],
            flip(me, steps[k]),
        )

    def to_line(amount, shard, source):
        return remote(
            source,
            block(0, shard),
            line_send.at[(amount + 1) // 2, shard],
            line_recv.at[shard],
            along(me, amount),
        )

    def arrived(bits, shard):
        remote(
            block(bits, shard),
            block(bits, shard),
            send.at[shard, 0],
            recv.at[shard, bits],
            me,
        ).wait_recv()

    def send_on(bits, shard, source):
        for k in range(top_bit(bits) + 1, count):
            to_step(k, bits, shard, source).start()

    def at_distance(distance, work):
        if distance == 0:
            work(my_line, 0)
            return
        for amount in (1, -1):
            shard = my_line - amount * distance
            pl.when((shard >= 0) & (shard < lines))(functools.partial(work, shard, amount))

    def line_inside(amount):
        there = my_line + amount
        return (there >= 0) & (there < lines)

    greet(me, steps, lines)
    own = pltpu.make_async_copy(x_ref, block(0, my_line), own_sem)
    own.start()
    if lines > 1:
        for amount in (1, -1):
            pl.when(line_inside(amount))(
                lambda amount=amount: to_line(amount, my_line, x_ref).start()
            )
    send_on(0, my_line, x_ref)

    def line_arrival(shard, amount):
        remote(
            block(0, shard), block(0, shard), line_send.at[0, shard], line_recv.at[shard], me
        ).wait_recv()
        pl.when(line_inside(amount))(lambda: to_line(amount, shard, block(0, shard)).start())
        send_on(0, shard, block(0, shard))

    def level_arrival(level, shard, amount):
        del amount
        for bits in range(1 << level, 2 << level):
            arrived(bits, shard)
            send_on(bits, shard, block(bits, shard))

    for tick in range(1, lines + count):
        if tick < lines:
            at_distance(tick, line_arrival)
        for level in range(count):
            distance = tick - 1 - level
            if 0 <= distance < lines:
                at_distance(distance, functools.partial(level_arrival, level))

    own.wait()
    if lines > 1:
        for amount in (1, -1):
            for distance in range(lines):
                shard = my_line - amount * distance
                pl.when((shard >= 0) & (shard < lines) & line_inside(amount))(
                    lambda amount=amount, shard=shard: to_line(
                        amount, shard, block(0, shard)
                    ).wait_send()
                )
    for shard in range(lines):
        for bits in range(1 << count):
            for k in range(top_bit(bits) + 1, count):
                to_step(k, bits, shard, block(bits, shard)).wait_send()


def gather(values, steps, lines, shape, slot, number):
    parts = 1 << len(steps)
    return pl.pallas_call(
        functools.partial(gather_kernel, steps, lines, slot),
        out_shape=jax.ShapeDtypeStruct(shape, values.dtype),
        in_specs=[pl.BlockSpec(memory_space=pl.ANY)],
        out_specs=pl.BlockSpec(memory_space=pl.ANY),
        scratch_shapes=[
            pltpu.SemaphoreType.DMA(()),
            pltpu.SemaphoreType.DMA((2, lines)),
            pltpu.SemaphoreType.DMA((lines,)),
            pltpu.SemaphoreType.DMA((lines, len(steps) * parts)),
            pltpu.SemaphoreType.DMA((lines, parts)),
        ],
        compiler_params=pltpu.CompilerParams(collective_id=number, has_side_effects=True),
    )(values)


def add_blocks(target, first, second, rows):
    tile = min(rows, 64)

    def one(index, carry):
        cut = pl.ds(pl.multiple_of(index * tile, tile), tile)
        total = first(cut).astype(F32) + second(cut).astype(F32)
        target[cut, :] = total.astype(target.dtype)
        return carry

    lax.fori_loop(0, rows // tile, one, 0)


def sum_kernel(steps, lines, rows, read, x_ref, slot, out_ref, held, on_line, sems):
    send, recv, line_send, line_recv = sems
    me = here()
    count = len(steps)
    my_line = me["line"] if lines > 1 else 0

    def target_of(bits, shard):
        place = me
        for k in range(count):
            if bits >> k & 1:
                place = flip(place, steps[k])
        return dict(place, line=shard)

    def store(k, shard, bits):
        return held[k].at[shard, bits >> (k + 1)]

    def copy(k, shard, bits):
        source = slot(x_ref, target_of(bits, shard)) if k == 0 else store(k - 1, shard, bits)
        return remote(
            source,
            store(k, shard, bits ^ (1 << k)),
            send[k].at[shard, bits >> (k + 1)],
            recv[k].at[shard, bits >> (k + 1)],
            flip(me, steps[k]),
        )

    def parts_of(k):
        return [high << (k + 1) for high in reversed(range(1 << (count - 1 - k)))]

    def send_step(k, shard):
        for bits in parts_of(k):
            copy(k, shard, bits | 1 << k).start()

    def take_step(k, shard):
        for bits in parts_of(k):
            copy(k, shard, bits | 1 << k).wait_recv()
            here_ref = store(k, shard, bits)
            if k == 0:
                place = target_of(bits, shard)
                mine = lambda cut, place=place: read(x_ref, place, cut)
            else:
                before = store(k - 1, shard, bits)
                mine = lambda cut, before=before: before[cut, :]
            add_blocks(here_ref, mine, lambda cut, here_ref=here_ref: here_ref[cut, :], rows)
            if k + 1 < count and bits >> (k + 1) & 1:
                copy(k + 1, shard, bits).start()

    def line_inside(amount):
        there = my_line + amount
        return (there >= 0) & (there < lines)

    def line_copy(amount, shard):
        way = (amount + 1) // 2
        return remote(
            on_line.at[way, shard],
            on_line.at[way, shard],
            line_send.at[way, shard],
            line_recv.at[way, shard],
            along(me, amount),
        )

    last = count - 1

    def each(distance, work):
        if distance == 0:
            work(my_line, 0)
            return
        for amount in (1, -1):
            shard = my_line + amount * distance
            pl.when((shard >= 0) & (shard < lines))(functools.partial(work, shard, amount))

    def line_step(shard, amount):
        done = held[last].at[shard, 0]
        moving = on_line.at[(amount + 1) // 2, shard]

        @pl.when(line_inside(-amount))
        def _():
            line_copy(amount, shard).wait_recv()
            add_blocks(moving, lambda cut: moving[cut, :], lambda cut: done[cut, :], rows)

        @pl.when(jnp.logical_not(line_inside(-amount)))
        def _():
            add_blocks(moving, lambda cut: done[cut, :], lambda cut: jnp.zeros_like(done[cut, :]), rows)

        line_copy(amount, shard).start()

    greet(me, steps, lines)
    order = list(reversed(range(lines)))
    for distance in order:
        each(distance, lambda shard, amount: send_step(0, shard))
    for tick in range(lines + count):
        for k in reversed(range(count)):
            index = tick - k
            if 0 <= index < lines:
                each(order[index], lambda shard, amount, k=k: take_step(k, shard))
        index = tick - count
        if 0 <= index < lines and order[index] > 0:
            each(order[index], line_step)
    final = held[last].at[my_line, 0]
    if lines == 1:
        add_blocks(out_ref, lambda cut: final[cut, :], lambda cut: jnp.zeros_like(final[cut, :]), rows)
    else:
        add_blocks(out_ref, lambda cut: final[cut, :], lambda cut: jnp.zeros_like(final[cut, :]), rows)
        for amount in (1, -1):

            @pl.when(line_inside(-amount))
            def _():
                line_copy(amount, my_line).wait_recv()
                moving = on_line.at[(amount + 1) // 2, my_line]
                add_blocks(
                    out_ref, lambda cut: out_ref[cut, :], lambda cut: moving[cut, :], rows
                )

        for amount in (1, -1):
            for distance in range(1, lines):
                shard = my_line + amount * distance
                pl.when((shard >= 0) & (shard < lines))(
                    lambda amount=amount, shard=shard: line_copy(amount, shard).wait_send()
                )
    for k in range(count):
        for shard in range(lines):
            for bits in parts_of(k):
                copy(k, shard, bits | 1 << k).wait_send()


def sum_parts(values, steps, lines, rows, columns, slot, read, number, kind=F32):
    count = len(steps)

    def kernel(x_ref, out_ref, *rest):
        held, rest = rest[:count], rest[count:]
        on_line, rest = rest[0], rest[1:]
        send, rest = rest[:count], rest[count:]
        recv, rest = rest[:count], rest[count:]
        sum_kernel(
            steps, lines, rows, read, x_ref, slot, out_ref, held, on_line, (send, recv) + rest
        )

    sizes = [1 << (count - 1 - k) for k in range(count)]
    return pl.pallas_call(
        kernel,
        out_shape=jax.ShapeDtypeStruct((rows, columns), kind),
        in_specs=[pl.BlockSpec(memory_space=pltpu.VMEM)],
        out_specs=pl.BlockSpec(memory_space=pltpu.VMEM),
        scratch_shapes=[pltpu.VMEM((lines, size, rows, columns), BF16) for size in sizes]
        + [pltpu.VMEM((2, lines, rows, columns), BF16) if lines > 1 else pltpu.VMEM((2, 1, 16, 128), BF16)]
        + [pltpu.SemaphoreType.DMA((lines, size)) for size in sizes] * 2
        + [pltpu.SemaphoreType.DMA((2, lines))] * 2,
        compiler_params=pltpu.CompilerParams(
            collective_id=number, has_side_effects=True, vmem_limit_bytes=VMEM_BYTES
        ),
    )(values)


def gather_rows(values, number):
    lines, (rows, columns) = lax.axis_size("line"), values.shape
    out = gather(
        values,
        (SIDE, FRONT),
        lines,
        (2, lines, 2, rows, columns),
        lambda ref, at: ref.at[at["fsdp"], at["line"], at["pair"]],
        number,
    )
    return out.reshape(4 * lines * rows, columns)


def sum_rows(values, number):
    lines, (total, columns) = lax.axis_size("line"), values.shape
    rows = total // (4 * lines)
    return sum_parts(
        values.astype(BF16).reshape(2, lines, 2, rows, columns),
        (FRONT, SIDE),
        lines,
        rows,
        columns,
        lambda ref, at: ref.at[at["fsdp"], at["line"], at["pair"]],
        lambda ref, at, cut: ref[at["fsdp"], at["line"], at["pair"], cut, :],
        number,
    )


def gather_plane(values, number):
    rows, columns = values.shape
    out = gather(
        values,
        (SIDE, FRONT, "tp"),
        1,
        (2, 2, 2, rows, columns),
        lambda ref, at: ref.at[at["fsdp"], at["pair"], at["tp"]],
        number,
    )
    return out.reshape(8 * rows, columns)


def sum_plane(values, number):
    total, columns = values.shape
    rows = total // 8
    return sum_parts(
        values.reshape(2, 2, 2, rows, columns),
        ("tp", FRONT, SIDE),
        1,
        rows,
        columns,
        lambda ref, at: ref.at[at["fsdp"], at["pair"], at["tp"]],
        lambda ref, at, cut: ref[at["fsdp"], at["pair"], at["tp"], cut, :],
        number,
    )


def gather_ctx(values, number):
    lines, (rows, columns) = lax.axis_size("line"), values.shape
    out = gather(
        values,
        ("pair", "tp"),
        lines,
        (lines, 2, 2, rows, columns),
        lambda ref, at: ref.at[at["line"], at["pair"], at["tp"]],
        number,
    )
    return out


def sum_ctx(values, number):
    lines, _, _, rows, columns = values.shape
    return sum_parts(
        values,
        ("tp", "pair"),
        lines,
        rows,
        columns,
        lambda ref, at: ref.at[at["line"], at["pair"], at["tp"]],
        lambda ref, at, cut: ref[at["line"], at["pair"], at["tp"], cut, :],
        number,
    )


DIRECT = (("pair",), ("fsdp",), ("pair", "fsdp"))


def move(me, names):
    place = me
    for name in names:
        place = flip(place, name)
    return place


def quarter_of(place):
    return place["fsdp"] * 2 + place["pair"]


def exchange_kernel(count, spread, *refs):
    sources, targets = refs[:count], refs[count : 2 * count]
    own_sem, send, recv = refs[2 * count :]
    me = here()

    def wide(ref, quarter):
        columns = ref.shape[1] // 4
        return ref.at[:, pl.ds(pl.multiple_of(quarter * columns, columns), columns)]

    def narrow(ref, quarter):
        return ref.at[quarter]

    cut, put = (wide, narrow) if spread else (narrow, wide)
    barrier = pltpu.get_barrier_semaphore()
    for names in DIRECT:
        pl.semaphore_signal(barrier, inc=1, device_id=move(me, names), device_id_type=MESH_ID)
    pl.semaphore_wait(barrier, len(DIRECT))
    copies = []
    for n in range(count):
        for k, names in reversed(list(enumerate(DIRECT))):
            there = move(me, names)
            copies.append(
                remote(
                    cut(sources[n], quarter_of(there)),
                    put(targets[n], quarter_of(me)),
                    send.at[n, k],
                    recv.at[n, k],
                    there,
                )
            )
        copies.append(
            pltpu.make_async_copy(
                cut(sources[n], quarter_of(me)), put(targets[n], quarter_of(me)), own_sem.at[n]
            )
        )
    for one in copies:
        one.start()
    for one in copies:
        one.wait()


def exchange_columns(arrays, spread, number):
    count = len(arrays)
    if spread:
        shapes = [(4, a.shape[0], a.shape[1] // 4) for a in arrays]
    else:
        shapes = [(a.shape[1], a.shape[2] * 4) for a in arrays]
    return pl.pallas_call(
        functools.partial(exchange_kernel, count, spread),
        out_shape=[jax.ShapeDtypeStruct(s, a.dtype) for s, a in zip(shapes, arrays)],
        in_specs=[pl.BlockSpec(memory_space=pl.ANY)] * count,
        out_specs=[pl.BlockSpec(memory_space=pl.ANY)] * count,
        scratch_shapes=[
            pltpu.SemaphoreType.DMA((count,)),
            pltpu.SemaphoreType.DMA((count, 3)),
            pltpu.SemaphoreType.DMA((count, 3)),
        ],
        compiler_params=pltpu.CompilerParams(collective_id=number, has_side_effects=True),
    )(*arrays)


def total_kernel(lines, x_ref, out_ref, moved, on_line, send, recv, line_send, line_recv):
    me = here()
    steps = ("tp", "pair", "fsdp")
    greet(me, steps, lines)
    out_ref[...] = x_ref[...]
    for k, step in enumerate(steps):
        swap = remote(moved.at[k, 0], moved.at[k, 1], send.at[k], recv.at[k], flip(me, step))
        moved[k, 0] = out_ref[...]
        swap.start()
        swap.wait()
        out_ref[...] = out_ref[...] + moved[k, 1]
    on_line[me["line"]] = out_ref[...]

    def copy(amount, shard):
        return remote(
            on_line.at[shard],
            on_line.at[shard],
            line_send.at[(amount + 1) // 2, shard],
            line_recv.at[shard],
            along(me, amount),
        )

    def inside(amount):
        there = me["line"] + amount
        return (there >= 0) & (there < lines)

    for amount in (1, -1):
        pl.when(inside(amount))(lambda amount=amount: copy(amount, me["line"]).start())
    for distance in range(1, lines):
        for amount in (1, -1):
            shard = me["line"] - amount * distance

            @pl.when((shard >= 0) & (shard < lines))
            def _():
                copy(amount, shard).wait_recv()
                pl.when(inside(amount))(lambda: copy(amount, shard).start())

    total = on_line[0]
    for shard in range(1, lines):
        total = total + on_line[shard]
    out_ref[...] = total
    for amount in (1, -1):
        for distance in range(lines):
            shard = me["line"] - amount * distance
            pl.when((shard >= 0) & (shard < lines) & inside(amount))(
                lambda amount=amount, shard=shard: copy(amount, shard).wait_send()
            )


def total_sum(values, number):
    lines = lax.axis_size("line")
    size = values.shape[0]
    shape = (-(-size // 1024) * 8, 128)
    padded = jnp.pad(values, (0, shape[0] * 128 - size)).reshape(shape)
    out = pl.pallas_call(
        functools.partial(total_kernel, lines),
        out_shape=jax.ShapeDtypeStruct(shape, F32),
        in_specs=[pl.BlockSpec(memory_space=pltpu.VMEM)],
        out_specs=pl.BlockSpec(memory_space=pltpu.VMEM),
        scratch_shapes=[
            pltpu.VMEM((3, 2) + shape, F32),
            pltpu.VMEM((lines,) + shape, F32),
            pltpu.SemaphoreType.DMA((3,)),
            pltpu.SemaphoreType.DMA((3,)),
            pltpu.SemaphoreType.DMA((2, lines)),
            pltpu.SemaphoreType.DMA((lines,)),
        ],
        compiler_params=pltpu.CompilerParams(
            collective_id=number, has_side_effects=True, vmem_limit_bytes=VMEM_BYTES
        ),
    )(padded)
    return out.reshape(-1)[:size]


def swap_tp(values):
    return lax.ppermute(values, "tp", [(0, 1), (1, 0)])


def gather_line(values):
    lines = lax.axis_size("line")
    quarters, rows, columns = values.shape
    fsdp = lax.axis_size("fsdp")
    every = lax.all_gather(values, "line", axis=0, tiled=False)
    every = every.reshape(lines, fsdp, quarters // fsdp, rows, columns).transpose(1, 0, 2, 3, 4)
    return every.reshape(lines * quarters * rows, columns)


def sum_line(values):
    lines, fsdp, pair = lax.axis_size("line"), lax.axis_size("fsdp"), lax.axis_size("pair")
    total, columns = values.shape
    rows = total // (lines * fsdp * pair)
    ordered = values.reshape(fsdp, lines, pair, rows, columns).transpose(1, 0, 2, 3, 4)
    ordered = ordered.reshape(total, columns).astype(BF16)
    summed = lax.psum_scatter(ordered, "line", scatter_dimension=0, tiled=True)
    return summed.reshape(fsdp * pair, rows, columns)


LOG2E = 1.4426950408889634


def visible_bias(bias_ref, position, chunks):
    prompt = position < PBLK
    row = lax.broadcasted_iota(jnp.int32, (BLK, BLK), 0)
    column = lax.broadcasted_iota(jnp.int32, (BLK, BLK), 1)
    limit = jnp.where(prompt, position * BLK + column, PBLK * BLK)
    for chunk in range(chunks - 1):
        bias_ref[chunk] = jnp.where(row + chunk * BLK <= limit, 0.0, MASKED)
    own_limit = jnp.where(prompt, -1, column)
    bias_ref[chunks - 1] = jnp.where(row <= own_limit, 0.0, MASKED)


def rows_by_rows(left, right):
    return lax.dot_general(left, right, (((1,), (1,)), ((), ())), preferred_element_type=F32)


def attend_kernel(position_ref, query_ref, key_ref, value_t_ref, mixed_ref, logsum_ref, bias_ref, score_ref):
    chunks = PBLK + 1
    factor = HD**-0.5 * LOG2E

    @pl.when(pl.program_id(1) == 0)
    def _():
        visible_bias(bias_ref, position_ref[pl.program_id(0)], chunks)

    query = query_ref[...]
    largest = None
    for chunk in range(chunks):
        keys = key_ref[0, chunk * BLK : (chunk + 1) * BLK, :]
        score = rows_by_rows(keys, query) + bias_ref[chunk]
        score_ref[chunk] = score
        top = jnp.max(score.reshape(BLK // 8, 8, BLK), axis=0)
        largest = top if largest is None else jnp.maximum(largest, top)
    largest = jnp.max(largest, axis=0, keepdims=True)
    total = jnp.zeros((8, BLK), F32)
    mixed = jnp.zeros((HD, BLK), F32)
    for chunk in range(chunks):
        weight = jnp.exp2((score_ref[chunk] - largest) * factor)
        total = total + jnp.sum(weight.reshape(BLK // 8, 8, BLK), axis=0)
        values = value_t_ref[0, :, chunk * BLK : (chunk + 1) * BLK]
        mixed = mixed + jnp.dot(values, weight.astype(BF16), preferred_element_type=F32)
    total = jnp.sum(total, axis=0, keepdims=True)
    mixed_ref[...] = (mixed / total).T.astype(BF16)
    logsum_ref[0, 0] = largest * factor + jnp.log2(total)


def attend(queries, keysets, positions):
    rows, width = queries.shape
    blocks, heads = rows // BLK, width // HD
    keys = keysets[:, :, :HD]
    values_t = keysets[:, :, HD:].transpose(0, 2, 1)
    count = keysets.shape[1]
    return pl.pallas_call(
        attend_kernel,
        grid=(blocks, heads),
        out_shape=[
            jax.ShapeDtypeStruct((rows, width), BF16),
            jax.ShapeDtypeStruct((blocks, heads, 1, BLK), F32),
        ],
        in_specs=[
            pl.BlockSpec(memory_space=pltpu.SMEM),
            pl.BlockSpec((BLK, HD), lambda b, h: (b, h)),
            pl.BlockSpec((1, count, HD), lambda b, h: (b, 0, 0)),
            pl.BlockSpec((1, HD, count), lambda b, h: (b, 0, 0)),
        ],
        out_specs=[
            pl.BlockSpec((BLK, HD), lambda b, h: (b, h)),
            pl.BlockSpec((1, 1, 1, BLK), lambda b, h: (b, h, 0, 0)),
        ],
        scratch_shapes=[
            pltpu.VMEM((PBLK + 1, BLK, BLK), F32),
            pltpu.VMEM((PBLK + 1, BLK, BLK), F32),
        ],
        compiler_params=pltpu.CompilerParams(vmem_limit_bytes=VMEM_BYTES),
        cost_estimate=pl.CostEstimate(
            flops=4 * rows * width * count, bytes_accessed=8 * rows * width, transcendentals=rows * heads * count
        ),
    )(positions, queries, keys, values_t)


def attend_back_kernel(
    position_ref, slot_ref, query_ref, grad_ref, mixed_ref, logsum_ref, key_ref, key_t_ref, value_ref,
    grad_query_ref, table_out_ref, bias_ref, set_ref, table_ref,
):
    chunks = PBLK + 1
    scale = HD**-0.5
    block, head = pl.program_id(0), pl.program_id(1)

    @pl.when(head == 0)
    def _():
        visible_bias(bias_ref, position_ref[block], chunks)
        set_ref[...] = jnp.zeros_like(set_ref)

    @pl.when((head == 0) & (block == 0))
    def _():
        def clear(index, carry):
            table_ref[index] = jnp.zeros(table_ref.shape[1:], F32)
            return carry

        lax.fori_loop(0, table_ref.shape[0], clear, 0)

    query, grad = query_ref[...], grad_ref[...]
    inner = jnp.sum(grad.astype(F32) * mixed_ref[...].astype(F32), axis=1, keepdims=True)
    inner = jnp.broadcast_to(inner, (BLK, HD)).T[:1, :]
    logsum = logsum_ref[0, 0]
    grad_query = jnp.zeros((HD, BLK), F32)
    for chunk in range(chunks):
        cut = slice(chunk * BLK, (chunk + 1) * BLK)
        score = rows_by_rows(key_ref[0, cut, :], query)
        weight = jnp.exp2(score * (scale * LOG2E) + bias_ref[chunk] - logsum)
        grad_weight = rows_by_rows(value_ref[0, cut, :], grad)
        grad_score = (weight * (grad_weight - inner)).astype(BF16)
        set_ref[cut, :HD] += jnp.dot(grad_score, query, preferred_element_type=F32)
        set_ref[cut, HD:] += jnp.dot(weight.astype(BF16), grad, preferred_element_type=F32)
        grad_query = grad_query + jnp.dot(key_t_ref[0, :, cut], grad_score, preferred_element_type=F32)
    grad_query_ref[...] = (grad_query * scale).T.astype(BF16)

    @pl.when(head == pl.num_programs(1) - 1)
    def _():
        for chunk in range(chunks):
            slot = slot_ref[block, chunk]
            cut = slice(chunk * BLK, (chunk + 1) * BLK)
            table_ref[slot, :, :HD] += set_ref[cut, :HD] * scale
            table_ref[slot, :, HD:] += set_ref[cut, HD:]

    @pl.when((head == pl.num_programs(1) - 1) & (block == pl.num_programs(0) - 1))
    def _():
        per_device = table_out_ref.shape[2] // BLK

        def give(index, carry):
            holder, place = index // per_device, index % per_device
            rows = pl.ds(pl.multiple_of(place * BLK, BLK), BLK)
            table_out_ref[holder, 0, rows, :] = table_ref[index, :, :HD].astype(BF16)
            table_out_ref[holder, 1, rows, :] = table_ref[index, :, HD:].astype(BF16)
            return carry

        lax.fori_loop(0, table_ref.shape[0], give, 0)


def attend_back(queries, grads, mixed, logsums, keysets, positions, key_slots, slot_count):
    rows, width = queries.shape
    blocks, heads = rows // BLK, width // HD
    keys, values = keysets[:, :, :HD], keysets[:, :, HD:]
    count = keysets.shape[1]
    by_head = pl.BlockSpec((BLK, HD), lambda b, h: (b, h))
    by_block = pl.BlockSpec((1, count, HD), lambda b, h: (b, 0, 0))
    table = (slot_count // blocks, 2, blocks * BLK, HD)
    return pl.pallas_call(
        attend_back_kernel,
        grid=(blocks, heads),
        out_shape=[
            jax.ShapeDtypeStruct((rows, width), BF16),
            jax.ShapeDtypeStruct(table, BF16),
        ],
        in_specs=[
            pl.BlockSpec(memory_space=pltpu.SMEM),
            pl.BlockSpec(memory_space=pltpu.SMEM),
            by_head,
            by_head,
            by_head,
            pl.BlockSpec((1, 1, 1, BLK), lambda b, h: (b, h, 0, 0)),
            by_block,
            pl.BlockSpec((1, HD, count), lambda b, h: (b, 0, 0)),
            by_block,
        ],
        out_specs=[by_head, pl.BlockSpec(table, lambda b, h: (0, 0, 0, 0))],
        scratch_shapes=[
            pltpu.VMEM((PBLK + 1, BLK, BLK), F32),
            pltpu.VMEM((count, 2 * HD), F32),
            pltpu.VMEM((slot_count, BLK, 2 * HD), F32),
        ],
        compiler_params=pltpu.CompilerParams(vmem_limit_bytes=VMEM_BYTES),
        cost_estimate=pl.CostEstimate(
            flops=10 * rows * width * count, bytes_accessed=16 * rows * width, transcendentals=rows * heads * count
        ),
    )(positions, key_slots, queries, grads, mixed, logsums, keys, keys.transpose(0, 2, 1), values)


def body(
    hidden_in,
    block_order,
    attn_norm_gain,
    attn_norm_bias,
    query_weight,
    query_bias,
    keyval_weight,
    value_bias,
    proj_weight,
    proj_bias,
    mlp_norm_gain,
    mlp_norm_bias,
    up_weight,
    up_bias,
    down_weight,
    down_bias,
    out_cotangent,
):
    rows_dev = hidden_in.shape[0]
    half_rows = rows_dev // 2
    width = hidden_in.shape[1]
    blocks_dev = rows_dev // BLK
    slot_count = block_order.shape[1]
    group_blocks = PBLK + CONTS
    heads_dev = query_bias.shape[0] // HD
    head_width = heads_dev * HD
    core = lax.axis_index("tp")
    quarter = lax.axis_index("fsdp") * lax.axis_size("pair") + lax.axis_index("pair")
    quarters = lax.axis_size("fsdp") * lax.axis_size("pair")
    hidden_dev = up_weight.shape[1] // quarters

    def own_half(values):
        return lax.dynamic_slice_in_dim(values, core * half_rows, half_rows, axis=0)

    def other_half(values):
        return lax.dynamic_slice_in_dim(values, (1 - core) * half_rows, half_rows, axis=0)

    def in_order(mine, other, axis=0):
        first = jnp.where(core == 0, mine, other)
        second = jnp.where(core == 0, other, mine)
        return jnp.concatenate([first, second], axis=axis)

    def sum_halves(values):
        return own_half(values) + swap_tp(other_half(values))

    def join_halves(values):
        return in_order(values, swap_tp(values))

    gain_one = attn_norm_gain.astype(F32)
    shift_one = attn_norm_bias.astype(F32)
    gain_two = mlp_norm_gain.astype(F32)
    shift_two = mlp_norm_bias.astype(F32)

    slot_ids = jnp.arange(slot_count, dtype=jnp.int32)
    ordering = block_order[0]
    inverse = jnp.sum(
        jnp.where(ordering[None, :] == slot_ids[:, None], slot_ids[None, :], 0), axis=1
    )
    ctx_index = lax.axis_index("line") * lax.axis_size("pair") + lax.axis_index("pair")
    first_slot = ctx_index * blocks_dev
    my_slots = first_slot + jnp.arange(blocks_dev, dtype=jnp.int32)
    my_blocks = lax.dynamic_slice_in_dim(ordering, first_slot, blocks_dev)
    positions = my_blocks % group_blocks
    group_base = my_blocks // group_blocks * group_blocks
    prompt_slots = jnp.take(
        inverse, group_base[:, None] + jnp.arange(PBLK, dtype=jnp.int32)[None, :]
    )
    key_slots = jnp.concatenate([prompt_slots, my_slots[:, None]], axis=1)

    keyval_cut = lax.dynamic_slice_in_dim(keyval_weight, core * HD, HD, axis=1)
    first_all = gather_rows(jnp.concatenate([query_weight, keyval_cut], axis=1), 1)
    proj_all = gather_rows(proj_weight, 2)
    down_cut, up_cut = exchange_columns([down_weight, up_weight], True, 3)
    down_all = gather_line(down_cut)
    up_all = gather_line(up_cut)

    stream = hidden_in.astype(F32)
    normed_one = layer_norm(stream, gain_one, shift_one).astype(BF16)
    value_shift = jnp.where(core == 1, value_bias.astype(F32), 0.0)
    first_shift = jnp.concatenate([query_bias.astype(F32), value_shift])
    first_low = (jnp.dot(normed_one, first_all, preferred_element_type=F32) + first_shift).astype(
        BF16
    )
    query_low = first_low[:, :head_width]
    part_low = first_low[:, head_width:]
    keyval_every = gather_ctx(part_low, 4)
    keyval_low = in_order(part_low, swap_tp(part_low), axis=1)
    keyval_table = keyval_every.transpose(0, 1, 3, 2, 4).reshape(slot_count, BLK, 2 * HD)
    own_table = keyval_low.reshape(blocks_dev, 1, BLK, 2 * HD)
    keysets = jnp.concatenate([keyval_table[prompt_slots], own_table], axis=1)
    keysets = keysets.reshape(blocks_dev, (PBLK + 1) * BLK, 2 * HD)
    mixed_low, logsums = attend(query_low, keysets, positions)
    proj_part = jnp.einsum("rk,ok->ro", mixed_low, proj_all, preferred_element_type=F32)
    middle = own_half(stream) + sum_halves(proj_part) + proj_bias.astype(F32)

    normed_two = layer_norm(middle, gain_two, shift_two).astype(BF16)
    cotangent = own_half(out_cotangent)
    cotangent_all = gather_plane(cotangent, 5)
    normed_two_all = gather_plane(normed_two, 6)
    up_shift = lax.dynamic_slice_in_dim(up_bias, quarter * hidden_dev, hidden_dev).astype(F32)
    grad_act = jnp.dot(cotangent_all, down_all, preferred_element_type=F32)
    pre_act = jnp.dot(normed_two_all, up_all, preferred_element_type=F32) + up_shift
    act, gelu_pull = jax.vjp(gelu_tanh, pre_act)
    act_low = act.astype(BF16)
    grad_pre_wide = gelu_pull(grad_act)[0]
    grad_pre = grad_pre_wide.astype(BF16)
    normed_two_part = jnp.einsum("rf,df->rd", grad_pre, up_all, preferred_element_type=F32)
    grad_normed_two = sum_plane(normed_two_part.astype(BF16), 7)
    down_part = jnp.einsum("rf,of->ro", act_low, down_all, preferred_element_type=F32)
    mlp_out = sum_plane(down_part.astype(BF16), 8) + down_bias.astype(F32)
    layer_out = join_halves((middle + mlp_out).astype(BF16))
    grad_up_bias = jnp.sum(grad_pre, axis=0, dtype=F32)
    down_weight_grad = jnp.einsum("ro,rf->of", cotangent_all, act_low, preferred_element_type=F32)
    up_weight_grad = jnp.einsum("rd,rf->df", normed_two_all, grad_pre, preferred_element_type=F32)
    down_cut_grad = sum_line(down_weight_grad)
    up_cut_grad = sum_line(up_weight_grad)
    wide_grads = exchange_columns([down_cut_grad, up_cut_grad], False, 9)
    grad_down_weight, grad_up_weight = [one.astype(F32) for one in wide_grads]

    norm_two_pull = jax.vjp(layer_norm, middle, gain_two, shift_two)[1]
    grad_mid_norm, grad_mlp_norm_gain, grad_mlp_norm_bias = norm_two_pull(grad_normed_two)
    grad_middle = cotangent.astype(F32) + grad_mid_norm
    grad_down_bias = jnp.sum(cotangent, axis=0, dtype=F32)

    grad_attn_half = grad_middle.astype(BF16)
    grad_proj_bias = jnp.sum(grad_attn_half, axis=0, dtype=F32)
    grad_attn = join_halves(grad_attn_half)
    proj_weight_grad = jnp.einsum("ro,rk->ok", grad_attn, mixed_low, preferred_element_type=F32)
    grad_proj_weight = sum_rows(proj_weight_grad, 10)
    grad_mixed = jnp.einsum("ro,ok->rk", grad_attn, proj_all, preferred_element_type=F32).astype(
        BF16
    )
    grad_query, grad_table = attend_back(
        query_low, grad_mixed, mixed_low, logsums, keysets, positions, key_slots, slot_count
    )
    grad_query_bias = jnp.sum(grad_query, axis=0, dtype=F32)
    grad_parts = grad_table.reshape(
        lax.axis_size("line"), lax.axis_size("pair"), 2, rows_dev, HD
    )
    grad_part = sum_ctx(grad_parts, 12).astype(BF16)
    grad_value_bias = jnp.where(core == 1, jnp.sum(grad_part, axis=0, dtype=F32), 0.0)
    grad_first = jnp.concatenate([grad_query, grad_part], axis=1)
    normed_one_part = jnp.einsum("rk,dk->rd", grad_first, first_all, preferred_element_type=F32)
    grad_normed_one = sum_halves(normed_one_part)
    first_weight_grad = jnp.einsum("rd,rk->dk", normed_one, grad_first, preferred_element_type=F32)
    grad_first_weight = sum_rows(first_weight_grad, 11)
    grad_query_weight = grad_first_weight[:, :head_width]
    grad_cut = grad_first_weight[:, head_width:]
    grad_keyval_weight = in_order(grad_cut, swap_tp(grad_cut), axis=1)
    norm_one_pull = jax.vjp(layer_norm, own_half(stream), gain_one, shift_one)[1]
    grad_in_norm, grad_attn_norm_gain, grad_attn_norm_bias = norm_one_pull(grad_normed_one)
    input_grad = join_halves((grad_middle + grad_in_norm).astype(BF16))

    query_slots = jnp.zeros((2 * head_width,), F32)
    query_slots = lax.dynamic_update_slice_in_dim(
        query_slots, grad_query_bias, core * head_width, axis=0
    )
    hidden_slots = jnp.zeros((2 * quarters * hidden_dev,), F32)
    hidden_slots = lax.dynamic_update_slice_in_dim(
        hidden_slots, grad_up_bias, (core * quarters + quarter) * hidden_dev, axis=0
    )
    pieces = [
        grad_attn_norm_gain,
        grad_attn_norm_bias,
        grad_proj_bias,
        grad_mlp_norm_gain,
        grad_mlp_norm_bias,
        grad_down_bias,
        grad_value_bias,
        query_slots,
        hidden_slots,
    ]
    summed = total_sum(jnp.concatenate(pieces), 13)
    cuts, start = [], 0
    for piece in pieces:
        cuts.append(summed[start : start + piece.shape[0]])
        start += piece.shape[0]
    sum_query = lax.dynamic_slice_in_dim(cuts[7], core * head_width, head_width)
    sum_up = lax.dynamic_slice_in_dim(cuts[8], core * quarters * hidden_dev, quarters * hidden_dev)
    return (
        layer_out,
        input_grad,
        cuts[0],
        cuts[1],
        grad_query_weight,
        sum_query,
        grad_keyval_weight,
        cuts[6],
        grad_proj_weight,
        cuts[2],
        cuts[3],
        cuts[4],
        grad_up_weight,
        sum_up,
        grad_down_weight,
        cuts[5],
    )


def solution(mesh):
    fsdp, ctx, tp = mesh.devices.shape
    grid = Mesh(mesh.devices.reshape(fsdp, ctx // 2, 2, tp), EVERY)
    by_rows = P(ROWS, None)
    by_both = P(ROWS, "tp")
    return jax.shard_map(
        body,
        mesh=grid,
        in_specs=(
            by_rows,
            P("fsdp", None),
            P(),
            P(),
            by_both,
            P("tp"),
            by_rows,
            P(),
            by_both,
            P(),
            P(),
            P(),
            by_both,
            P("tp"),
            by_both,
            P(),
            by_rows,
        ),
        out_specs=(
            by_rows,
            by_rows,
            P(),
            P(),
            by_both,
            P("tp"),
            by_rows,
            P(),
            by_both,
            P(),
            P(),
            P(),
            by_both,
            P("tp"),
            by_both,
            P(),
        ),
        check_vma=False,
    )
```

time: 1430 us -> 916 us (0.64)
  waiting for transfers between devices: 934 us -> 0.09 us
  Pallas kernels: 0 us -> 657 us
  matrix products: 212 us -> 114 us
  other arithmetic: 106 us -> 40.9 us
  local copies, waits for them, and re-layouts: 103 us -> 78.4 us
  loops' own time: 18.5 us -> 0 us
  blocking collectives: 17.4 us -> 0 us
    pallas_call x0 -> x15, Pallas kernels: none -> 657 us  [the longest x5 271 us: gather(): pl.pallas_call(functools.partial(gather_kernel, steps, lines, slot), out_...]
    reduce_scatter x5 -> x0, waiting for transfers between devices: 387 us -> none  [the longest x2 234 us: sum_rows(): lax.psum_scatter(values.astype(BF16), ROWS, scatter_dimension=0, tiled=True)]
    all_gather x5 -> x0, waiting for transfers between devices: 187 us -> none  [the longest x2 92.3 us: gather_plane(): return lax.all_gather(values, PLANE + ('tp',), axis=0, tiled=True)]
    reduce_scatter x2, waiting for transfers between devices: 123 us -> 0.01 us  [sum_line(): summed = lax.psum_scatter(ordered, 'line', scatter_dimension=0, tiled=True)]
    all_gather x2, waiting for transfers between devices: 120 us -> 0.01 us  [gather_line(): every = lax.all_gather(values, 'line', axis=0, tiled=False)]
    psum x1 -> x0, waiting for transfers between devices: 98.6 us -> none  [body(): summed = lax.psum(jnp.concatenate(pieces), EVERY)]
    dot_general x15 -> x0, matrix products: 95.6 us -> none  [the longest x2 24 us: attend_back(): jnp.einsum('hqd,kd->hqk', grad_mixed, value_part, preferred_element_type=...]
    dot_general x0 -> x2, local copies, waits for them, and re-layouts: none -> 24.7 us  [the longest x1 12.4 us: body(): jnp.einsum('rd,rf->df', normed_two_all, grad_pre, preferred_element_type=...]
  transfers between devices with their start and end apart: 27 -> 11, of which waited for: 19 -> 0; matrix products, arithmetic and copies ran while one was open for 17% -> 19% of each run, Pallas kernels for 0% -> 67%
where the time goes in v2:
time: 916 us; the launch traced here: 907 us
  Pallas kernels  657 us (72%)
  matrix products  114 us (12%)
  local copies, waits for them, and re-layouts  78.4 us (9%)
  other arithmetic  40.9 us (4%)
  between operations  15.2 us (2%)
    pallas_call x5, Pallas kernels, gather(): pl.pallas_call(functools.partial(gather_kernel, steps, lines, slot), out_...  271 us
    pallas_call x5, Pallas kernels, sum_parts(): pl.pallas_call(kernel, out_shape=jax.ShapeDtypeStruct((rows, columns), ki...  238 us
    pallas_call x2, Pallas kernels, exchange_columns(): pl.pallas_call(functools.partial(exchange_kernel, count, spread), out_sha...  50.8 us
    pallas_call x1, Pallas kernels, attend_back(): pl.pallas_call(attend_back_kernel, grid=(blocks, heads), out_shape=[jax.S...  46.1 us
    pallas_call x1, Pallas kernels, attend(): pl.pallas_call(attend_kernel, grid=(blocks, heads), out_shape=[jax.ShapeD...  27.6 us
    pallas_call x1, Pallas kernels, total_sum(): pl.pallas_call(functools.partial(total_kernel, lines), out_shape=jax.Shap...  23.3 us
  transfers between devices with their start and end apart: 11, of which 0 were waited for; matrix products, arithmetic and copies ran while one was open for 19% of the time, Pallas kernels for 67%

profile of v2, /device:TPU:0, one launch (start us, length us, event | category | flops | bytes accessed | tf_op | source)
XLA Modules:
  0.0 906.9 jit_solution(2985224050094188292)
XLA Ops:
  7.3 27.9 %shard_map.293 = (bf16[4,128,1024]{2,1,0:T(8,128)(2,1)}, bf16[4,128,1024]{2,1,0:T(8,128)(2,1)}) custom-call(bf16[128,4096]{1,0:T(8,128)(2,1)} %refs_0_.1, bf16[128,4096]{1,0:T(8,128)(2,1)} %refs_1_.1), custom_call_target="tpu_custom_call" | custom-call | tf_op jit(solution)/shard_map/pallas_call | solution.py:525
  37.0 81.0 %shard_map.288 = bf16[2,4,2,128,1152]{4,3,2,1,0:T(8,128)(2,1)} custom-call(bf16[128,1152]{1,0:T(8,128)(2,1)} %pad_maximum_fusion.9.x_ref), custom_call_target="tpu_custom_call" | custom-call | tf_op jit(solution)/shard_map/pallas_call | solution.py:200
  119.2 5.3 fusion.11
  125.2 21.3 %shard_map.289 = bf16[4,2,2,512,128]{4,3,2,1,0:T(8,128)(2,1)} custom-call(bf16[512,128]{1,0:T(8,128)(2,1)} %copy-done.25), custom_call_target="tpu_custom_call" | custom-call | tf_op jit(solution)/shard_map/pallas_call | solution.py:200
  148.9 5.1 copy.66
  154.0 4.4 reshape.331
  158.4 83.1 %shard_map.291 = bf16[2,4,2,128,1024]{4,3,2,1,0:T(8,128)(2,1)} custom-call(bf16[128,1024]{1,0:T(8,128)(2,1)} %x_ref.1), custom_call_target="tpu_custom_call" | custom-call | tf_op jit(solution)/shard_map/pallas_call | solution.py:200
  241.5 3.6 gather_fusion.1
  253.0 27.6 %shard_map.290 = (bf16[512,1024]{1,0:T(8,128)(2,1)}, f32[2,8,1,256]{3,2,1,0:T(1,128)}) custom-call(s32[2]{0:T(128)} %and_select_fusion.3.position_ref, bf16[512,1024]{1,0:T(8,128)(2,1)} %slice.113.query_ref, bf16[2,2304,128]{2,1,0:T(8,128)(2,1)} %get-tuple-element.59.key_ref, bf16[2,128,2304]{2,1,0:T(8,128)(2,1)} %copy.68.value_t_ref), custom_call_target="tpu_custom_call" | custom-call | flops 4831838208 | bytes 4194304 | tf_op jit(solution)/shard_map/pallas_call | solution.py:689
  295.0 5.5 convert_reduce_fusion.2
  302.3 42.6 %shard_map.292 = bf16[2,2,2,256,2048]{4,3,2,1,0:T(8,128)(2,1)} custom-call(bf16[256,2048]{1,0:T(8,128)(2,1)} %add_convert_fusion.3.x_ref), custom_call_target="tpu_custom_call" | custom-call | tf_op jit(solution)/shard_map/pallas_call | solution.py:200
  345.0 43.3 %shard_map.295 = bf16[2,2,2,256,2048]{4,3,2,1,0:T(8,128)(2,1)} custom-call(bf16[256,2048]{1,0:T(8,128)(2,1)} %get-tuple-element.43.x_ref), custom_call_target="tpu_custom_call" | custom-call | tf_op jit(solution)/shard_map/pallas_call | solution.py:200
  388.2 12.4 %copy.74 = bf16[2048,2048]{1,0:T(8,128)(2,1)} copy(bf16[2048,2048]{0,1:T(8,128)(2,1)} %bitcast.106) | data formatting | bytes 16777216 | tf_op jit(solution)/shard_map/rd,rf->df/dot_general | solution.py:929
  400.6 12.3 %copy.72 = bf16[2048,2048]{1,0:T(8,128)(2,1)} copy(bf16[2048,2048]{0,1:T(8,128)(2,1)} %bitcast.102) | data formatting | bytes 16777216 | tf_op jit(solution)/shard_map/ro,rf->of/dot_general | solution.py:928
  413.5 4.8 copy.69
  421.7 14.9 %fusion.33 = f32[2048,1024]{1,0:T(8,128)} fusion(bf16[2048,2048]{1,0:T(8,128)(2,1)} %bitcast.107, bf16[2048,1024]{1,0:T(8,128)(2,1)S(1)} %bitcast.130), kind=kOutput, calls=%fused_computation.138 | convolution fusion | flops 8589934592 | bytes 20971520 | tf_op jit(solution)/shard_map/dot_general | solution.py:917
  436.7 17.4 %convert_reduce_fusion = (f32[1024]{0:T(1024)S(1)}, bf16[2048,1024]{1,0:T(8,128)(2,1)}) fusion(f32[2048,1024]{1,0:T(8,128)} %fusion.33, f32[1024]{0:T(1024)S(1)} %dynamic-slice_convert_fusion, bf16[2048,2048]{1,0:T(8,128)(2,1)S(1)} %bitcast.105, bf16[2048,1024]{1,0:T(8,128)(2,1)S(1)} %bitcast.131), kind=kOutput, calls=%fused_computation.11 | convolution fusion | flops 8638168064 | bytes 25174016 | tf_op jit(solution)/shard_map/dot_general | solution.py:916
  454.1 10.7 %convert_bitcast_fusion = bf16[4,2,2,128,1024]{4,3,2,0,1:T(8,128)(2,1)S(1)} fusion(bf16[2,4,2,128,2048]{4,3,2,1,0:T(8,128)(2,1)S(1)} %bitcast.117, bf16[2048,1024]{1,0:T(8,128)(2,1)} %get-tuple-element.39), kind=kOutput, calls=%fused_computation.20 | convolution fusion | flops 8592031744 | bytes 16777216 | tf_op jit(solution)/shard_map/rd,rf->df/dot_general | solution.py:929
  467.6 14.5 %convolution_convert_fusion.1 = bf16[2048,2048]{1,0:T(8,128)(2,1)} fusion(bf16[2048,1024]{1,0:T(8,128)(2,1)} %get-tuple-element.39, bf16[2048,1024]{1,0:T(8,128)(2,1)} %bitcast.129), kind=kOutput, calls=%fused_computation.14 | convolution fusion | flops 8594128896 | bytes 16777216 | tf_op jit(solution)/shard_map/rf,df->rd/dot_general | solution.py:922
  482.1 44.9 %shard_map.296 = f32[256,2048]{1,0:T(8,128)} custom-call(bf16[2,2,2,256,2048]{4,3,2,1,0:T(8,128)(2,1)} %bitcast.111), custom_call_target="tpu_custom_call" | custom-call | tf_op jit(solution)/shard_map/pallas_call | solution.py:366
  527.0 17.1 %convolution_convert_fusion.2 = bf16[2048,2048]{1,0:T(8,128)(2,1)} fusion(bf16[2048,1024]{1,0:T(8,128)(2,1)S(1)} %bitcast.132, f32[2048,1024]{1,0:T(8,128)} %fusion.33, f32[1024]{0:T(1024)S(1)} %dynamic-slice_convert_fusion), kind=kOutput, calls=%fused_computation.15 | convolution fusion | flops 8615100416 | bytes 20975616 | tf_op jit(solution)/shard_map/rf,of->ro/dot_general | solution.py:924
  544.2 45.1 %shard_map.294 = f32[256,2048]{1,0:T(8,128)} custom-call(bf16[2,2,2,256,2048]{4,3,2,1,0:T(8,128)(2,1)} %bitcast.112), custom_call_target="tpu_custom_call" | custom-call | tf_op jit(solution)/shard_map/pallas_call | solution.py:366
  593.2 14.1 %convert_bitcast_fusion.1 = bf16[4,2,2,128,1024]{4,3,2,0,1:T(8,128)(2,1)S(1)} fusion(bf16[2,4,2,128,2048]{4,3,2,1,0:T(8,128)(2,1)} %bitcast.114, f32[2048,1024]{1,0:T(8,128)} %fusion.33, f32[1024]{0:T(1024)S(1)} %dynamic-slice_convert_fusion), kind=kOutput, calls=%fused_computation.21 | convolution fusion | flops 8613003264 | bytes 20975616 | tf_op jit(solution)/shard_map/ro,rf->of/dot_general | solution.py:928
  616.1 46.1 %shard_map.297 = (bf16[512,1024]{1,0:T(8,128)(2,1)}, bf16[8,2,512,128]{3,2,1,0:T(8,128)(2,1)}) custom-call(s32[2]{0:T(128)} %and_select_fusion.3.position_ref, s32[2,9]{1,0:T(2,128)} %pad_add_fusion.slot_ref, bf16[512,1024]{1,0:T(8,128)(2,1)} %slice.113.query_ref, bf16[512,1024]{1,0:T(8,128)(2,1)} %convolution_convert_fusion.4.grad_ref, ...), custom_call_target="tpu_custom_call" | custom-call | flops 12079595520 | bytes 8388608 | tf_op jit(solution)/shard_map/pallas_call | solution.py:784
  662.2 32.9 %shard_map.298 = f32[512,128]{1,0:T(8,128)} custom-call(bf16[4,2,2,512,128]{4,3,2,1,0:T(8,128)(2,1)} %bitcast.133), custom_call_target="tpu_custom_call" | custom-call | tf_op jit(solution)/shard_map/pallas_call | solution.py:366
  696.1 4.1 fusion.17
  704.3 4.9 convolution_convert_fusion
  709.3 61.0 %shard_map.300 = f32[128,1152]{1,0:T(8,128)} custom-call(bf16[2,4,2,128,1152]{4,3,2,1,0:T(8,128)(2,1)} %bitcast.123), custom_call_target="tpu_custom_call" | custom-call | tf_op jit(solution)/shard_map/pallas_call | solution.py:366
  774.4 4.4 convolution_convert_fusion.3
  779.8 54.1 %shard_map.301 = f32[128,1024]{1,0:T(8,128)} custom-call(bf16[2,4,2,128,1024]{4,3,2,1,0:T(8,128)(2,1)} %bitcast.124), custom_call_target="tpu_custom_call" | custom-call | tf_op jit(solution)/shard_map/pallas_call | solution.py:366
  841.1 23.3 %shard_map.299 = f32[184,128]{1,0:T(8,128)} custom-call(f32[184,128]{1,0:T(8,128)} %pad_bitcast_fusion.x_ref), custom_call_target="tpu_custom_call" | custom-call | tf_op jit(solution)/shard_map/pallas_call | solution.py:593
  870.7 22.9 %shard_map.302 = (bf16[128,4096]{1,0:T(8,128)(2,1)}, bf16[128,4096]{1,0:T(8,128)(2,1)}) custom-call(bf16[4,128,1024]{2,1,0:T(8,128)(2,1)} %bitcast.136, bf16[4,128,1024]{2,1,0:T(8,128)(2,1)} %bitcast.135), custom_call_target="tpu_custom_call" | custom-call | tf_op jit(solution)/shard_map/pallas_call | solution.py:525
  (238 shorter events, 79.2 us)
Async XLA Ops:
  7.2 28.1 %copy-start = (bf16[128,256]{1,0:T(8,128)(2,1)S(1)}, bf16[128,256]{1,0:T(8,128)(2,1)}, u32[]{:S(2)}) copy-start(bf16[128,256]{1,0:T(8,128)(2,1)} %param.23) | copy-start | bytes 196612
  7.2 110.8 %copy-start.44 = (bf16[1024]{0:T(1024)(128)(2,1)S(1)}, bf16[1024]{0:T(1024)(128)(2,1)}, u32[]{:S(2)}) copy-start(bf16[1024]{0:T(1024)(128)(2,1)} %param.22) | copy-start | bytes 6148
  7.2 110.8 %copy-start.38 = (bf16[2048]{0:T(1024)(128)(2,1)S(1)}, bf16[2048]{0:T(1024)(128)(2,1)}, u32[]{:S(2)}) copy-start(bf16[2048]{0:T(1024)(128)(2,1)} %param.19) | copy-start | bytes 12292
  7.2 110.8 %copy-start.39 = (bf16[2048]{0:T(1024)(128)(2,1)S(1)}, bf16[2048]{0:T(1024)(128)(2,1)}, u32[]{:S(2)}) copy-start(bf16[2048]{0:T(1024)(128)(2,1)} %param.20) | copy-start | bytes 12292
  7.2 110.8 %copy-start.48 = (bf16[128]{0:T(256)(128)(2,1)S(1)}, bf16[128]{0:T(256)(128)(2,1)}, u32[]{:S(2)}) copy-start(bf16[128]{0:T(256)(128)(2,1)} %param.24) | copy-start | bytes 772
  7.2 110.9 %copy-start.3 = (bf16[512,2048]{1,0:T(8,128)(2,1)S(1)}, bf16[512,2048]{1,0:T(8,128)(2,1)}, u32[]{:S(2)}) copy-start(bf16[512,2048]{1,0:T(8,128)(2,1)} %param.17) | copy-start | bytes 6291460
  7.3 406.2 %all-gather.5.cloned.1.call-start = ((), (), s32[]{:S(2)}) async-start(), calls=%async_computation.4 | async-start | bytes 5242880 | tf_op jit(solution)/shard_map/all_gather | solution.py:621
  35.2 383.0 %all-gather.7.cloned.1.call-start = ((), (), s32[]{:S(2)}) async-start(), calls=%async_computation.5 | async-start | bytes 5242880 | tf_op jit(solution)/shard_map/all_gather | solution.py:621
  124.5 23.1 %copy-start.47 = (s32[1,16]{1,0:T(1,128)S(1)}, s32[1,16]{1,0:T(1,128)}, u32[]{:S(2)}) copy-start(s32[1,16]{1,0:T(1,128)} %param.18) | copy-start | bytes 196
  124.6 121.0 %collective-permute-start = (bf16[512,128]{1,0:T(8,128)(2,1)S(1)}, bf16[512,128]{1,0:T(8,128)(2,1)}, u32[]{:S(2)}, u32[]{:S(2)}) collective-permute-start(bf16[512,128]{1,0:T(8,128)(2,1)S(1)} %slice.114.x_ref), channel_id=1, source_target_pairs={{0,1},{1,0},{2,3},{3,2},{4,5},{5,4},{6,7},{7,6},{8,9},{9,8},{10,11... | collective-permute-start | bytes 393224 | tf_op jit(solution)/shard_map/ppermute | solution.py:614
  124.7 746.0 %reduce-scatter.5.cloned.1.call-start = ((), (), s32[]{:S(2)}) async-start(), calls=%async_computation.3 | async-start | bytes 5242880 | tf_op jit(solution)/shard_map/reduce_scatter | solution.py:632
  253.0 27.6 %copy-start.10 = (bf16[2,4,2,128,1024]{4,3,2,1,0:T(8,128)(2,1)S(1)}, bf16[2,4,2,128,1024]{4,3,2,1,0:T(8,128)(2,1)}, u32[]{:S(2)}) copy-start(bf16[2,4,2,128,1024]{4,3,2,1,0:T(8,128)(2,1)} %shard_map.291) | copy-start | bytes 12582916
  287.7 7.3 collective-permute-start.1
  300.6 112.4 %copy-start.31 = (f32[256]{0:T(256)}, f32[256]{0:T(256)S(1)}, u32[]{:S(2)}) copy-start(f32[256]{0:T(256)S(1)} %get-tuple-element.78) | copy-start | bytes 3076
  418.3 18.4 %slice-start = ((s8[8388608]{0:T(1024)(128)(4,1)}), s8[4194304]{0:T(1024)(128)(4,1)S(1)}, s32[]{:S(2)}) async-start(s8[8388608]{0:T(1024)(128)(4,1)} %bitcast.103), calls=%async_computation.6 | async-start | bytes 8388608
  421.7 32.4 %slice-start.2 = ((s8[8388608]{0:T(1024)(128)(4,1)}), s8[4194304]{0:T(1024)(128)(4,1)S(1)}, s32[]{:S(2)}) async-start(s8[8388608]{0:T(1024)(128)(4,1)} %bitcast.115), calls=%async_computation.8 | async-start | bytes 8388608
  436.7 17.4 %slice-start.3 = ((s8[8388608]{0:T(1024)(128)(4,1)}), s8[4194304]{0:T(1024)(128)(4,1)S(1)}, s32[]{:S(2)}) async-start(s8[8388608]{0:T(1024)(128)(4,1)} %bitcast.115), calls=%async_computation.9 | async-start | bytes 8388608
  467.5 403.2 %reduce-scatter.3.cloned.1.call-start = ((), (), s32[]{:S(2)}) async-start(), calls=%async_computation.2 | async-start | bytes 5242880 | tf_op jit(solution)/shard_map/reduce_scatter | solution.py:632
  482.1 45.0 %copy-start.14 = (bf16[2,4,2,128,1024]{4,3,2,1,0:T(8,128)(2,1)S(1)}, bf16[2,4,2,128,1024]{4,3,2,1,0:T(8,128)(2,1)}, u32[]{:S(2)}) copy-start(bf16[2,4,2,128,1024]{4,3,2,1,0:T(8,128)(2,1)} %copy-done.13) | copy-start | bytes 12582916
  544.2 45.1 %copy-start.5 = (f32[256,2048]{1,0:T(8,128)S(1)}, f32[256,2048]{1,0:T(8,128)}, u32[]{:S(2)}) copy-start(f32[256,2048]{1,0:T(8,128)} %shard_map.296) | copy-start | bytes 6291460
  593.0 17.6 %collective-permute-start.3 = (bf16[256,2048]{1,0:T(8,128)(2,1)S(1)}, bf16[256,2048]{1,0:T(8,128)(2,1)}, u32[]{:S(2)}, u32[]{:S(2)}) collective-permute-start(bf16[256,2048]{1,0:T(8,128)(2,1)S(1)} %get-tuple-element.45), channel_id=1, source_target_pairs={{0,1},{1,0},{2,3},{3,2},{4,5},{5,4},{6,7},{7,6},{8,9},{9,8},{10,11... | collective-permute-start | bytes 3145736 | tf_op jit(solution)/shard_map/ppermute | solution.py:614
  609.9 161.4 %collective-permute-start.2 = (bf16[256,2048]{1,0:T(8,128)(2,1)}, bf16[256,2048]{1,0:T(8,128)(2,1)S(1)}, u32[]{:S(2)}, u32[]{:S(2)}) collective-permute-start(bf16[256,2048]{1,0:T(8,128)(2,1)} %get-tuple-element.64), channel_id=1, source_target_pairs={{0,1},{1,0},{2,3},{3,2},{4,5},{5,4},{6,7},{7,6},{8,9},{9,8},{10,11... | collective-permute-start | bytes 3145736 | tf_op jit(solution)/shard_map/ppermute | solution.py:614
  612.7 83.4 %slice-start.4 = ((s8[4718592]{0:T(1024)(128)(4,1)}), s8[4194304]{0:T(1024)(128)(4,1)S(1)}, s32[]{:S(2)}) async-start(s8[4718592]{0:T(1024)(128)(4,1)} %bitcast.120), calls=%async_computation.10 | async-start | bytes 8388608
  616.1 80.0 %slice-start.5 = ((s8[4718592]{0:T(1024)(128)(4,1)}), s8[524288]{0:T(1024)(128)(4,1)S(1)}, s32[]{:S(2)}) async-start(s8[4718592]{0:T(1024)(128)(4,1)} %bitcast.120), calls=%async_computation.11 | async-start | bytes 1048576
  701.9 133.1 %collective-permute-start.4 = (f32[256,2048]{1,0:T(8,128)}, f32[256,2048]{1,0:T(8,128)}, u32[]{:S(2)}, u32[]{:S(2)}) collective-permute-start(f32[256,2048]{1,0:T(8,128)} %constant_dynamic-slice_fusion), channel_id=1, source_target_pairs={{0,1},{1,0},{2,3},{3,2},{4,5},{5,4},{6,7},{7,6},{8,9},{9,8},{10,11... | collective-permute-start | bytes 6291464 | tf_op jit(solution)/shard_map/ppermute | solution.py:614
  771.2 63.1 %collective-permute-start.6 = (f32[128,128]{1,0:T(8,128)S(1)}, f32[128,128]{1,0:T(8,128)S(1)}, u32[]{:S(2)}, u32[]{:S(2)}) collective-permute-start(f32[128,128]{1,0:T(8,128)S(1)} %slice.96), channel_id=1, source_target_pairs={{0,1},{1,0},{2,3},{3,2},{4,5},{5,4},{6,7},{7,6},{8,9},{9,8},{10,11... | collective-permute-start | bytes 196616 | tf_op jit(solution)/shard_map/ppermute | solution.py:614
  778.8 56.2 %copy-start.2 = (f32[512,2048]{1,0:T(8,128)S(1)}, f32[512,2048]{1,0:T(8,128)}, u32[]{:S(2)}) copy-start(f32[512,2048]{1,0:T(8,128)} %convert_element_type.114) | copy-start | bytes 12582916
  778.8 56.2 %copy-start.30 = (f32[256]{0:T(256)S(1)}, f32[256]{0:T(256)}, u32[]{:S(2)}) copy-start(f32[256]{0:T(256)} %copy-done.29) | copy-start | bytes 3076
  778.8 56.2 %copy-start.33 = (f32[256]{0:T(256)S(1)}, f32[256]{0:T(256)}, u32[]{:S(2)}) copy-start(f32[256]{0:T(256)} %fusion.19) | copy-start | bytes 3076
  840.3 28.7 %collective-permute-start.5 = (bf16[256,2048]{1,0:T(8,128)(2,1)S(1)}, bf16[256,2048]{1,0:T(8,128)(2,1)S(1)}, u32[]{:S(2)}, u32[]{:S(2)}) collective-permute-start(bf16[256,2048]{1,0:T(8,128)(2,1)S(1)} %add_convert_fusion.1), channel_id=1, source_target_pairs={{0,1},{1,0},{2,3},{3,2},{4,5},{5,4},{6,7},{7,6},{8,9},{9,8},{10,11... | collective-permute-start | bytes 3145736 | tf_op jit(solution)/shard_map/ppermute | solution.py:614
  870.7 28.4 %copy-start.18 = (f32[128,1024]{1,0:T(8,128)S(1)}, f32[128,1024]{1,0:T(8,128)}, u32[]{:S(2)}) copy-start(f32[128,1024]{1,0:T(8,128)} %shard_map.301) | copy-start | bytes 1572868
  870.7 29.2 %copy-start.1 = (bf16[128,256]{1,0:T(8,128)(2,1)S(1)}, bf16[128,256]{1,0:T(8,128)(2,1)}, u32[]{:S(2)}) copy-start(bf16[128,256]{1,0:T(8,128)(2,1)} %param.23) | copy-start | bytes 196612
  (35 other events, 164.2 us)
Sparse Core Ops, SparseCore 0:
  35.4 92.1 all-gather.4
  129.2 95.0 all-gather.6
  467.7 75.1 reduce-scatter.4
  610.3 79.7 reduce-scatter.2

commit v3 on v1

v3 whole, which is shorter than its diff:
```python
import functools

import jax
import jax.numpy as jnp
from jax import lax
from jax.experimental import pallas as pl
from jax.experimental.pallas import tpu as pltpu
from jax.sharding import Mesh, PartitionSpec as P

HD = 128
BLK = 256
PBLK = 8
CONTS = 8
EPSILON = 1e-05
MASKED = -1e30
F32 = jnp.float32
BF16 = jnp.bfloat16
ROWS = ("fsdp", "line", "pair")
EVERY = ("fsdp", "line", "pair", "tp")


def layer_norm(values, norm_gain, norm_shift):
    average = jnp.mean(values, axis=-1, keepdims=True)
    centered = values - average
    spread = jnp.mean(centered * centered, axis=-1, keepdims=True)
    return centered * lax.rsqrt(spread + EPSILON) * norm_gain + norm_shift


def gelu_tanh(values):
    return jax.nn.gelu(values, approximate=True)


MESH_ID = pl.DeviceIdType.MESH
VMEM_BYTES = 60 * 1024 * 1024
SIDE = ("pair", "fsdp")
FRONT = ("fsdp", "pair")


def here():
    return {name: lax.axis_index(name) for name in EVERY}


def flip(place, step):
    place = dict(place)
    if isinstance(step, str):
        place[step] = 1 - place[step]
    else:
        core = place["tp"]
        for name, used in ((step[0], 1 - core), (step[1], core)):
            place[name] = place[name] + (1 - 2 * place[name]) * used
    return place


def along(place, amount):
    return dict(place, line=place["line"] + amount)


def remote(source, target, send_sem, recv_sem, place):
    return pltpu.make_async_remote_copy(
        src_ref=source,
        dst_ref=target,
        send_sem=send_sem,
        recv_sem=recv_sem,
        device_id=place,
        device_id_type=MESH_ID,
    )


def top_bit(bits):
    return bits.bit_length() - 1


def add_blocks(target, first, second, rows):
    tile = min(rows, 64)

    def one(index, carry):
        cut = pl.ds(pl.multiple_of(index * tile, tile), tile)
        total = first(cut).astype(F32)
        if second is not None:
            total = total + second(cut).astype(F32)
        target[cut, :] = total.astype(target.dtype)
        return carry

    lax.fori_loop(0, rows // tile, one, 0)


def rows_of(ref):
    return lambda cut: ref[cut, :]


class Gather:
    def __init__(self, values, steps, lines, shape, slot):
        self.steps, self.lines, self.slot = steps, lines, slot
        self.out = jax.ShapeDtypeStruct(shape, values.dtype)
        self.in_spec = self.out_spec = pl.BlockSpec(memory_space=pl.ANY)

    def scratch(self):
        parts = 1 << len(self.steps)
        return [
            pltpu.SemaphoreType.DMA(()),
            pltpu.SemaphoreType.DMA((2, self.lines)),
            pltpu.SemaphoreType.DMA((self.lines,)),
            pltpu.SemaphoreType.DMA((self.lines, len(self.steps) * parts)),
            pltpu.SemaphoreType.DMA((self.lines, parts)),
        ]

    def stages(self, me, x_ref, out_ref, own_sem, line_send, line_recv, send, recv):
        steps, lines, slot = self.steps, self.lines, self.slot
        count = len(steps)
        my_line = me["line"] if lines > 1 else 0

        def block(bits, shard):
            place = me
            for k in reversed(range(count)):
                if bits >> k & 1:
                    place = flip(place, steps[k])
            return slot(out_ref, dict(place, line=shard))

        def to_step(k, bits, shard, source):
            return remote(
                source,
                block(bits, shard),
                send.at[shard, k * (1 << count) + bits],
                recv.at[shard, bits | 1 << k],
                flip(me, steps[k]),
            )

        def to_line(amount, shard, source):
            return remote(
                source,
                block(0, shard),
                line_send.at[(amount + 1) // 2, shard],
                line_recv.at[shard],
                along(me, amount),
            )

        def send_on(bits, shard, source):
            for k in range(top_bit(bits) + 1, count):
                to_step(k, bits, shard, source).start()

        def at_distance(distance, work):
            if distance == 0:
                work(my_line, 0)
                return
            for amount in (1, -1):
                shard = my_line - amount * distance
                pl.when((shard >= 0) & (shard < lines))(functools.partial(work, shard, amount))

        def line_inside(amount):
            there = my_line + amount
            return (there >= 0) & (there < lines)

        own = pltpu.make_async_copy(x_ref, block(0, my_line), own_sem)

        def begin():
            if lines > 1:
                for amount in (1, -1):
                    pl.when(line_inside(amount))(
                        lambda amount=amount: to_line(amount, my_line, x_ref).start()
                    )
            send_on(0, my_line, x_ref)
            own.start()

        def line_arrival(shard, amount):
            remote(
                block(0, shard), block(0, shard), line_send.at[0, shard], line_recv.at[shard], me
            ).wait_recv()
            pl.when(line_inside(amount))(lambda: to_line(amount, shard, block(0, shard)).start())
            send_on(0, shard, block(0, shard))

        def level_arrival(level, shard, amount):
            for bits in range(1 << level, 2 << level):
                remote(
                    block(bits, shard),
                    block(bits, shard),
                    send.at[shard, 0],
                    recv.at[shard, bits],
                    me,
                ).wait_recv()
                send_on(bits, shard, block(bits, shard))

        def tick(number):
            if number < lines:
                at_distance(number, line_arrival)
            for level in range(count):
                distance = number - 1 - level
                if 0 <= distance < lines:
                    at_distance(distance, functools.partial(level_arrival, level))

        def end():
            own.wait()
            if lines > 1:
                for amount in (1, -1):
                    for distance in range(lines):
                        shard = my_line - amount * distance
                        pl.when((shard >= 0) & (shard < lines) & line_inside(amount))(
                            lambda amount=amount, shard=shard: to_line(
                                amount, shard, block(0, shard)
                            ).wait_send()
                        )
            for shard in range(lines):
                for bits in range(1 << count):
                    for k in range(top_bit(bits) + 1, count):
                        to_step(k, bits, shard, block(bits, shard)).wait_send()

        ticks = [functools.partial(tick, number) for number in range(1, lines + count)]
        return [begin] + ticks + [end]


class Sum:
    def __init__(self, steps, lines, rows, columns, slot):
        self.steps, self.lines, self.rows, self.columns = steps, lines, rows, columns
        self.slot = slot
        self.out = jax.ShapeDtypeStruct((rows, columns), F32)
        self.in_spec = pl.BlockSpec(memory_space=pl.ANY)
        self.out_spec = pl.BlockSpec(memory_space=pltpu.VMEM)

    def scratch(self):
        count, lines = len(self.steps), self.lines
        sizes = [1 << (count - 1 - k) for k in range(count)]
        block = (self.rows, self.columns)
        return (
            [pltpu.VMEM((lines, sizes[0]) + block, BF16)]
            + [pltpu.VMEM((lines, size) + block, BF16) for size in sizes]
            + [pltpu.VMEM((2, lines) + (block if lines > 1 else (16, 128)), BF16)]
            + [pltpu.SemaphoreType.DMA((lines, sizes[0]))]
            + [pltpu.SemaphoreType.DMA((lines, size)) for size in sizes] * 2
            + [pltpu.SemaphoreType.DMA((2, lines))] * 2
        )

    def stages(self, me, x_ref, out_ref, own, *rest):
        steps, lines, rows, slot = self.steps, self.lines, self.rows, self.slot
        count = len(steps)
        held, rest = rest[:count], rest[count:]
        on_line, own_sem, rest = rest[0], rest[1], rest[2:]
        send, recv, (line_send, line_recv) = rest[:count], rest[count : 2 * count], rest[2 * count :]
        my_line = me["line"] if lines > 1 else 0
        last = count - 1

        def target_of(bits, shard):
            place = me
            for k in range(count):
                if bits >> k & 1:
                    place = flip(place, steps[k])
            return dict(place, line=shard)

        def store(k, shard, bits):
            return held[k].at[shard, bits >> (k + 1)]

        def own_copy(shard, bits):
            return pltpu.make_async_copy(
                slot(x_ref, target_of(bits, shard)),
                own.at[shard, bits >> 1],
                own_sem.at[shard, bits >> 1],
            )

        def copy(k, shard, bits):
            source = slot(x_ref, target_of(bits, shard)) if k == 0 else store(k - 1, shard, bits)
            return remote(
                source,
                store(k, shard, bits ^ (1 << k)),
                send[k].at[shard, bits >> (k + 1)],
                recv[k].at[shard, bits >> (k + 1)],
                flip(me, steps[k]),
            )

        def parts_of(k):
            return [high << (k + 1) for high in reversed(range(1 << (count - 1 - k)))]

        def send_first(shard, amount):
            for bits in parts_of(0):
                copy(0, shard, bits | 1).start()

        def own_first(shard, amount):
            for bits in parts_of(0):
                own_copy(shard, bits).start()

        def take_step(k, shard, amount):
            for bits in parts_of(k):
                copy(k, shard, bits | 1 << k).wait_recv()
                arrived = store(k, shard, bits)
                if k == 0:
                    own_copy(shard, bits).wait()
                    mine = own.at[shard, bits >> 1]
                else:
                    mine = store(k - 1, shard, bits)
                add_blocks(arrived, rows_of(mine), rows_of(arrived), rows)
                if k + 1 < count and bits >> (k + 1) & 1:
                    copy(k + 1, shard, bits).start()

        def line_inside(amount):
            there = my_line + amount
            return (there >= 0) & (there < lines)

        def line_copy(amount, shard):
            way = (amount + 1) // 2
            return remote(
                on_line.at[way, shard],
                on_line.at[way, shard],
                line_send.at[way, shard],
                line_recv.at[way, shard],
                along(me, amount),
            )

        def each(distance, work):
            if distance == 0:
                work(my_line, 0)
                return
            for amount in (1, -1):
                shard = my_line + amount * distance
                pl.when((shard >= 0) & (shard < lines))(functools.partial(work, shard, amount))

        def line_step(shard, amount):
            done = held[last].at[shard, 0]
            moving = on_line.at[(amount + 1) // 2, shard]

            @pl.when(line_inside(-amount))
            def _():
                line_copy(amount, shard).wait_recv()
                add_blocks(moving, rows_of(moving), rows_of(done), rows)

            @pl.when(jnp.logical_not(line_inside(-amount)))
            def _():
                add_blocks(moving, rows_of(done), None, rows)

            line_copy(amount, shard).start()

        order = list(reversed(range(lines)))

        def begin():
            for distance in order:
                each(distance, send_first)
            for distance in order:
                each(distance, own_first)

        def tick(number):
            for k in reversed(range(count)):
                index = number - k
                if 0 <= index < lines:
                    each(order[index], functools.partial(take_step, k))
            index = number - count
            if 0 <= index < lines and order[index] > 0:
                each(order[index], line_step)

        def end():
            final = held[last].at[my_line, 0]
            add_blocks(out_ref, rows_of(final), None, rows)
            if lines > 1:
                for amount in (1, -1):

                    @pl.when(line_inside(-amount))
                    def _():
                        line_copy(amount, my_line).wait_recv()
                        moving = on_line.at[(amount + 1) // 2, my_line]
                        add_blocks(out_ref, rows_of(out_ref), rows_of(moving), rows)

                for amount in (1, -1):
                    for distance in range(1, lines):
                        shard = my_line + amount * distance
                        pl.when((shard >= 0) & (shard < lines))(
                            lambda amount=amount, shard=shard: line_copy(amount, shard).wait_send()
                        )
            for k in range(count):
                for shard in range(lines):
                    for bits in parts_of(k):
                        copy(k, shard, bits | 1 << k).wait_send()

        ticks = [functools.partial(tick, number) for number in range(lines + count)]
        return [begin] + ticks + [end]


DIRECT = (("pair",), ("fsdp",), ("pair", "fsdp"))


def move(me, names):
    place = me
    for name in names:
        place = flip(place, name)
    return place


def quarter_of(place):
    return place["fsdp"] * 2 + place["pair"]


class Exchange:
    steps, lines, corner = ("pair", "fsdp"), 1, True

    def __init__(self, values, spread):
        self.spread = spread
        if spread:
            shape = (4, values.shape[0], values.shape[1] // 4)
        else:
            shape = (values.shape[1], values.shape[2] * 4)
        self.out = jax.ShapeDtypeStruct(shape, values.dtype)
        self.in_spec = self.out_spec = pl.BlockSpec(memory_space=pl.ANY)

    def scratch(self):
        return [
            pltpu.SemaphoreType.DMA(()),
            pltpu.SemaphoreType.DMA((3,)),
            pltpu.SemaphoreType.DMA((3,)),
        ]

    def stages(self, me, x_ref, out_ref, own_sem, send, recv):
        def wide(ref, quarter):
            columns = ref.shape[1] // 4
            return ref.at[:, pl.ds(pl.multiple_of(quarter * columns, columns), columns)]

        def narrow(ref, quarter):
            return ref.at[quarter]

        cut, put = (wide, narrow) if self.spread else (narrow, wide)
        copies = []
        for k, names in reversed(list(enumerate(DIRECT))):
            there = move(me, names)
            copies.append(
                remote(
                    cut(x_ref, quarter_of(there)),
                    put(out_ref, quarter_of(me)),
                    send.at[k],
                    recv.at[k],
                    there,
                )
            )
        copies.append(
            pltpu.make_async_copy(
                cut(x_ref, quarter_of(me)), put(out_ref, quarter_of(me)), own_sem
            )
        )

        def begin():
            for one in copies:
                one.start()

        def end():
            for one in copies:
                one.wait()

        return [begin, end]


class Total:
    steps = ("tp", "pair", "fsdp")

    def __init__(self, values, lines):
        self.lines, self.out = lines, jax.ShapeDtypeStruct(values.shape, F32)
        self.in_spec = self.out_spec = pl.BlockSpec(memory_space=pltpu.VMEM)

    def scratch(self):
        shape, lines = self.out.shape, self.lines
        return [
            pltpu.VMEM((3, 2) + shape, F32),
            pltpu.VMEM((lines,) + shape, F32),
            pltpu.SemaphoreType.DMA((3,)),
            pltpu.SemaphoreType.DMA((3,)),
            pltpu.SemaphoreType.DMA((2, lines)),
            pltpu.SemaphoreType.DMA((lines,)),
        ]

    def stages(self, me, x_ref, out_ref, moved, on_line, send, recv, line_send, line_recv):
        lines = self.lines

        def swap(k):
            return remote(
                moved.at[k, 0], moved.at[k, 1], send.at[k], recv.at[k], flip(me, self.steps[k])
            )

        def copy(amount, shard):
            return remote(
                on_line.at[shard],
                on_line.at[shard],
                line_send.at[(amount + 1) // 2, shard],
                line_recv.at[shard],
                along(me, amount),
            )

        def inside(amount):
            there = me["line"] + amount
            return (there >= 0) & (there < lines)

        def begin():
            moved[0, 0] = x_ref[...]
            swap(0).start()

        def after(k):
            swap(k).wait()
            if k < 2:
                moved[k + 1, 0] = moved[k, 0] + moved[k, 1]
                swap(k + 1).start()
                return
            on_line[me["line"]] = moved[k, 0] + moved[k, 1]
            for amount in (1, -1):
                pl.when(inside(amount))(lambda amount=amount: copy(amount, me["line"]).start())

        def hop(distance):
            for amount in (1, -1):
                shard = me["line"] - amount * distance

                @pl.when((shard >= 0) & (shard < lines))
                def _():
                    copy(amount, shard).wait_recv()
                    pl.when(inside(amount))(lambda: copy(amount, shard).start())

        def end():
            total = on_line[0]
            for shard in range(1, lines):
                total = total + on_line[shard]
            out_ref[...] = total
            for amount in (1, -1):
                for distance in range(lines):
                    shard = me["line"] - amount * distance
                    pl.when((shard >= 0) & (shard < lines) & inside(amount))(
                        lambda amount=amount, shard=shard: copy(amount, shard).wait_send()
                    )

        return (
            [begin]
            + [functools.partial(after, k) for k in range(3)]
            + [functools.partial(hop, distance) for distance in range(1, lines)]
            + [end]
        )


def greet(me, programs):
    barrier = pltpu.get_barrier_semaphore()
    lines = max(one.lines for one in programs)
    steps = list(dict.fromkeys(step for one in programs for step in one.steps))
    if SIDE in steps:
        steps = [step for step in steps if step not in ("pair", "fsdp")]
    places = [flip(me, step) for step in steps]
    if any(isinstance(one, Exchange) for one in programs):
        places.append(move(me, ("pair", "fsdp")))
    for place in places:
        pl.semaphore_signal(barrier, inc=1, device_id=place, device_id_type=MESH_ID)
    count = len(places)
    if lines > 1:
        for amount in (-1, 1):
            there = me["line"] + amount
            inside = (there >= 0) & (there < lines)

            @pl.when(inside)
            def _():
                pl.semaphore_signal(
                    barrier, inc=1, device_id=along(me, amount), device_id_type=MESH_ID
                )

            count = count + inside.astype(jnp.int32)
    pl.semaphore_wait(barrier, count)


def split_scratch(programs, refs):
    parts, start = [], 0
    for one in programs:
        size = len(one.scratch())
        parts.append(refs[start : start + size])
        start += size
    return parts


def schedule(programs, x_refs, out_refs, scratch):
    me = here()
    works = [(0.0, functools.partial(greet, me, programs))]
    for one, x_ref, out_ref, held in zip(programs, x_refs, out_refs, split_scratch(programs, scratch)):
        stages = one.stages(me, x_ref, out_ref, *held)
        works += [(k / (len(stages) - 1), stage) for k, stage in enumerate(stages)]
    return sorted(works, key=lambda work: work[0])


def run_programs(programs, arrays, number):
    count = len(programs)

    def kernel(*refs):
        for _, work in schedule(programs, refs[:count], refs[count : 2 * count], refs[2 * count :]):
            work()

    return pl.pallas_call(
        kernel,
        out_shape=[one.out for one in programs],
        in_specs=[one.in_spec for one in programs],
        out_specs=[one.out_spec for one in programs],
        scratch_shapes=[held for one in programs for held in one.scratch()],
        compiler_params=pltpu.CompilerParams(
            collective_id=number, has_side_effects=True, vmem_limit_bytes=VMEM_BYTES
        ),
    )(*arrays)


def by_rows_slot(ref, at):
    return ref.at[at["fsdp"], at["line"], at["pair"]]


def by_plane_slot(ref, at):
    return ref.at[at["fsdp"], at["pair"], at["tp"]]


def by_ctx_slot(ref, at):
    return ref.at[at["line"], at["pair"], at["tp"]]


def rows_gather(values):
    lines = lax.axis_size("line")
    return Gather(values, (SIDE, FRONT), lines, (2, lines, 2) + values.shape, by_rows_slot)


def rows_sum(values):
    lines, (total, columns) = lax.axis_size("line"), values.shape
    rows = total // (4 * lines)
    parts = values.astype(BF16).reshape(2, lines, 2, rows, columns)
    return Sum((FRONT, SIDE), lines, rows, columns, by_rows_slot), parts


def plane_gather(values):
    return Gather(values, (SIDE, FRONT, "tp"), 1, (2, 2, 2) + values.shape, by_plane_slot)


def plane_sum(values):
    rows, columns = values.shape[0] // 8, values.shape[1]
    parts = values.astype(BF16).reshape(2, 2, 2, rows, columns)
    return Sum(("tp", FRONT, SIDE), 1, rows, columns, by_plane_slot), parts


def flat(values):
    return values.reshape(-1, values.shape[-1])


def gather_ctx(values, number):
    lines = lax.axis_size("line")
    one = Gather(values, ("pair", "tp"), lines, (lines, 2, 2) + values.shape, by_ctx_slot)
    return run_programs([one], [values], number)[0]


def sum_ctx(values, number):
    lines, _, _, rows, columns = values.shape
    one = Sum(("tp", "pair"), lines, rows, columns, by_ctx_slot)
    return run_programs([one], [values], number)[0]


def total_of(values):
    size = values.shape[0]
    rows = -(-size // 1024) * 8
    padded = jnp.pad(values, (0, rows * 128 - size)).reshape(rows, 128)
    return Total(padded, lax.axis_size("line")), padded


def swap_tp(values):
    return lax.ppermute(values, "tp", [(0, 1), (1, 0)])


def gather_line(values):
    quarters, rows, columns = values.shape
    every = lax.all_gather(values, "line", axis=0, tiled=False)
    return every.reshape(-1, columns)


def sum_line(values):
    total, columns = values.shape
    lines = lax.axis_size("line")
    summed = lax.psum_scatter(values.astype(BF16), "line", scatter_dimension=0, tiled=True)
    return summed.reshape(4, total // (4 * lines), columns)


def to_line_order(values):
    lines = lax.axis_size("line")
    size = values.shape[1] // (2 * lines)
    cuts = [(half * lines + shard) * size for shard in range(lines) for half in range(2)]
    return jnp.concatenate([values[:, cut : cut + size] for cut in cuts], axis=1)


def from_line_order(values):
    lines = lax.axis_size("line")
    size = values.shape[1] // (2 * lines)
    cuts = [(shard * 2 + half) * size for half in range(2) for shard in range(lines)]
    return jnp.concatenate([values[:, cut : cut + size] for cut in cuts], axis=1)


LOG2E = 1.4426950408889634


def visible_bias(bias_ref, position, chunks):
    prompt = position < PBLK
    row = lax.broadcasted_iota(jnp.int32, (BLK, BLK), 0)
    column = lax.broadcasted_iota(jnp.int32, (BLK, BLK), 1)
    limit = jnp.where(prompt, position * BLK + column, PBLK * BLK)
    for chunk in range(chunks - 1):
        bias_ref[chunk] = jnp.where(row + chunk * BLK <= limit, 0.0, MASKED)
    own_limit = jnp.where(prompt, -1, column)
    bias_ref[chunks - 1] = jnp.where(row <= own_limit, 0.0, MASKED)


def rows_by_rows(left, right):
    return lax.dot_general(left, right, (((1,), (1,)), ((), ())), preferred_element_type=F32)


def beside(programs, in_refs, out_refs, scratch, steps):
    step = pl.program_id(0) * pl.num_programs(1) + pl.program_id(1)
    for place, work in schedule(programs, in_refs, out_refs, scratch):
        pl.when(step == min(steps - 1, int(place * steps)))(work)


def attend_kernel(programs, steps, *refs):
    count = len(programs)
    (position_ref, query_ref, key_ref, value_t_ref), refs = refs[:4], refs[4:]
    others, refs = refs[:count], refs[count:]
    (mixed_ref, logsum_ref), refs = refs[:2], refs[2:]
    other_outs, refs = refs[:count], refs[count:]
    (bias_ref, score_ref), scratch = refs[:2], refs[2:]
    chunks = PBLK + 1
    factor = HD**-0.5 * LOG2E
    beside(programs, others, other_outs, scratch, steps)

    @pl.when(pl.program_id(1) == 0)
    def _():
        visible_bias(bias_ref, position_ref[pl.program_id(0)], chunks)

    query = query_ref[...]
    largest = None
    for chunk in range(chunks):
        keys = key_ref[0, chunk * BLK : (chunk + 1) * BLK, :]
        score = rows_by_rows(keys, query) + bias_ref[chunk]
        score_ref[chunk] = score
        top = jnp.max(score.reshape(BLK // 8, 8, BLK), axis=0)
        largest = top if largest is None else jnp.maximum(largest, top)
    largest = jnp.max(largest, axis=0, keepdims=True)
    total = jnp.zeros((8, BLK), F32)
    mixed = jnp.zeros((HD, BLK), F32)
    for chunk in range(chunks):
        weight = jnp.exp2((score_ref[chunk] - largest) * factor)
        total = total + jnp.sum(weight.reshape(BLK // 8, 8, BLK), axis=0)
        values = value_t_ref[0, :, chunk * BLK : (chunk + 1) * BLK]
        mixed = mixed + jnp.dot(values, weight.astype(BF16), preferred_element_type=F32)
    total = jnp.sum(total, axis=0, keepdims=True)
    mixed_ref[...] = (mixed / total).T.astype(BF16)
    logsum_ref[0, 0] = largest * factor + jnp.log2(total)


def attend(queries, keysets, positions, programs, arrays, number):
    rows, width = queries.shape
    blocks, heads = rows // BLK, width // HD
    keys = keysets[:, :, :HD]
    values_t = keysets[:, :, HD:].transpose(0, 2, 1)
    count = keysets.shape[1]
    out = pl.pallas_call(
        functools.partial(attend_kernel, programs, blocks * heads),
        grid=(blocks, heads),
        out_shape=[
            jax.ShapeDtypeStruct((rows, width), BF16),
            jax.ShapeDtypeStruct((blocks, heads, 1, BLK), F32),
        ]
        + [one.out for one in programs],
        in_specs=[
            pl.BlockSpec(memory_space=pltpu.SMEM),
            pl.BlockSpec((BLK, HD), lambda b, h: (b, h)),
            pl.BlockSpec((1, count, HD), lambda b, h: (b, 0, 0)),
            pl.BlockSpec((1, HD, count), lambda b, h: (b, 0, 0)),
        ]
        + [one.in_spec for one in programs],
        out_specs=[
            pl.BlockSpec((BLK, HD), lambda b, h: (b, h)),
            pl.BlockSpec((1, 1, 1, BLK), lambda b, h: (b, h, 0, 0)),
        ]
        + [one.out_spec for one in programs],
        scratch_shapes=[
            pltpu.VMEM((PBLK + 1, BLK, BLK), F32),
            pltpu.VMEM((PBLK + 1, BLK, BLK), F32),
        ]
        + [held for one in programs for held in one.scratch()],
        compiler_params=pltpu.CompilerParams(
            collective_id=number, has_side_effects=True, vmem_limit_bytes=VMEM_BYTES
        ),
        cost_estimate=pl.CostEstimate(
            flops=4 * rows * width * count,
            bytes_accessed=8 * rows * width,
            transcendentals=rows * heads * count,
        ),
    )(positions, queries, keys, values_t, *arrays)
    return out[0], out[1], out[2:]


def attend_back_kernel(programs, steps, *refs):
    count = len(programs)
    (position_ref, query_ref, grad_ref, mixed_ref, logsum_ref), refs = refs[:5], refs[5:]
    (key_ref, key_t_ref, value_ref), refs = refs[:3], refs[3:]
    others, refs = refs[:count], refs[count:]
    (grad_query_ref, set_ref), refs = refs[:2], refs[2:]
    other_outs, refs = refs[:count], refs[count:]
    bias_ref, scratch = refs[0], refs[1:]
    chunks = PBLK + 1
    scale = HD**-0.5
    block, head = pl.program_id(0), pl.program_id(1)
    beside(programs, others, other_outs, scratch, steps)

    @pl.when(head == 0)
    def _():
        visible_bias(bias_ref, position_ref[block], chunks)
        set_ref[...] = jnp.zeros_like(set_ref)

    query, grad = query_ref[...], grad_ref[...]
    inner = jnp.sum(grad.astype(F32) * mixed_ref[...].astype(F32), axis=1, keepdims=True)
    inner = jnp.broadcast_to(inner, (BLK, HD)).T[:1, :]
    logsum = logsum_ref[0, 0]
    grad_query = jnp.zeros((HD, BLK), F32)
    for chunk in range(chunks):
        cut = slice(chunk * BLK, (chunk + 1) * BLK)
        score = rows_by_rows(key_ref[0, cut, :], query)
        weight = jnp.exp2(score * (scale * LOG2E) + bias_ref[chunk] - logsum)
        grad_weight = rows_by_rows(value_ref[0, cut, :], grad)
        grad_score = (weight * (grad_weight - inner)).astype(BF16)
        set_ref[0, cut, :HD] += jnp.dot(grad_score, query, preferred_element_type=F32)
        set_ref[0, cut, HD:] += jnp.dot(weight.astype(BF16), grad, preferred_element_type=F32)
        grad_query = grad_query + jnp.dot(
            key_t_ref[0, :, cut], grad_score, preferred_element_type=F32
        )
    grad_query_ref[...] = (grad_query * scale).T.astype(BF16)

    @pl.when(head == pl.num_programs(1) - 1)
    def _():
        set_ref[0, :, :HD] = set_ref[0, :, :HD] * scale


def attend_back(queries, grads, mixed, logsums, keysets, positions, programs, arrays, number):
    rows, width = queries.shape
    blocks, heads = rows // BLK, width // HD
    keys, values = keysets[:, :, :HD], keysets[:, :, HD:]
    count = keysets.shape[1]
    by_head = pl.BlockSpec((BLK, HD), lambda b, h: (b, h))
    by_block = pl.BlockSpec((1, count, HD), lambda b, h: (b, 0, 0))
    out = pl.pallas_call(
        functools.partial(attend_back_kernel, programs, blocks * heads),
        grid=(blocks, heads),
        out_shape=[
            jax.ShapeDtypeStruct((rows, width), BF16),
            jax.ShapeDtypeStruct((blocks, count, 2 * HD), F32),
        ]
        + [one.out for one in programs],
        in_specs=[
            pl.BlockSpec(memory_space=pltpu.SMEM),
            by_head,
            by_head,
            by_head,
            pl.BlockSpec((1, 1, 1, BLK), lambda b, h: (b, h, 0, 0)),
            by_block,
            pl.BlockSpec((1, HD, count), lambda b, h: (b, 0, 0)),
            by_block,
        ]
        + [one.in_spec for one in programs],
        out_specs=[by_head, pl.BlockSpec((1, count, 2 * HD), lambda b, h: (b, 0, 0))]
        + [one.out_spec for one in programs],
        scratch_shapes=[pltpu.VMEM((PBLK + 1, BLK, BLK), F32)]
        + [held for one in programs for held in one.scratch()],
        compiler_params=pltpu.CompilerParams(
            collective_id=number, has_side_effects=True, vmem_limit_bytes=VMEM_BYTES
        ),
        cost_estimate=pl.CostEstimate(
            flops=10 * rows * width * count,
            bytes_accessed=16 * rows * width,
            transcendentals=rows * heads * count,
        ),
    )(positions, queries, grads, mixed, logsums, keys, keys.transpose(0, 2, 1), values, *arrays)
    return out[0], out[1], out[2:]


def by_slot_kernel(slot_ref, set_ref, out_ref, table_ref):
    blocks, chunks = slot_ref.shape
    per_device = out_ref.shape[2] // BLK

    def clear(index, carry):
        table_ref[index] = jnp.zeros(table_ref.shape[1:], F32)
        return carry

    def give(index, carry):
        holder, place = index // per_device, index % per_device
        rows = pl.ds(pl.multiple_of(place * BLK, BLK), BLK)
        out_ref[holder, 0, rows, :] = table_ref[index, :, :HD].astype(BF16)
        out_ref[holder, 1, rows, :] = table_ref[index, :, HD:].astype(BF16)
        return carry

    lax.fori_loop(0, table_ref.shape[0], clear, 0)
    for block in range(blocks):
        for chunk in range(chunks):
            cut = slice(chunk * BLK, (chunk + 1) * BLK)
            table_ref[slot_ref[block, chunk]] += set_ref[block, cut, :]
    lax.fori_loop(0, table_ref.shape[0], give, 0)


def by_slot(sets, key_slots, slot_count):
    blocks = sets.shape[0]
    return pl.pallas_call(
        by_slot_kernel,
        out_shape=jax.ShapeDtypeStruct((slot_count // blocks, 2, blocks * BLK, HD), BF16),
        in_specs=[
            pl.BlockSpec(memory_space=pltpu.SMEM),
            pl.BlockSpec(memory_space=pltpu.VMEM),
        ],
        out_specs=pl.BlockSpec(memory_space=pltpu.VMEM),
        scratch_shapes=[pltpu.VMEM((slot_count, BLK, 2 * HD), F32)],
        compiler_params=pltpu.CompilerParams(vmem_limit_bytes=VMEM_BYTES),
    )(key_slots, sets)


def body(
    hidden_in,
    block_order,
    attn_norm_gain,
    attn_norm_bias,
    query_weight,
    query_bias,
    keyval_weight,
    value_bias,
    proj_weight,
    proj_bias,
    mlp_norm_gain,
    mlp_norm_bias,
    up_weight,
    up_bias,
    down_weight,
    down_bias,
    out_cotangent,
):
    rows_dev = hidden_in.shape[0]
    half_rows = rows_dev // 2
    width = hidden_in.shape[1]
    blocks_dev = rows_dev // BLK
    slot_count = block_order.shape[1]
    group_blocks = PBLK + CONTS
    heads_dev = query_bias.shape[0] // HD
    head_width = heads_dev * HD
    core = lax.axis_index("tp")
    quarter = lax.axis_index("fsdp") * lax.axis_size("pair") + lax.axis_index("pair")
    quarters = lax.axis_size("fsdp") * lax.axis_size("pair")
    hidden_dev = up_weight.shape[1] // quarters

    def own_half(values):
        return lax.dynamic_slice_in_dim(values, core * half_rows, half_rows, axis=0)

    def other_half(values):
        return lax.dynamic_slice_in_dim(values, (1 - core) * half_rows, half_rows, axis=0)

    def in_order(mine, other, axis=0):
        first = jnp.where(core == 0, mine, other)
        second = jnp.where(core == 0, other, mine)
        return jnp.concatenate([first, second], axis=axis)

    def sum_halves(values):
        return own_half(values) + swap_tp(other_half(values))

    def join_halves(values):
        return in_order(values, swap_tp(values))

    gain_one = attn_norm_gain.astype(F32)
    shift_one = attn_norm_bias.astype(F32)
    gain_two = mlp_norm_gain.astype(F32)
    shift_two = mlp_norm_bias.astype(F32)

    slot_ids = jnp.arange(slot_count, dtype=jnp.int32)
    ordering = block_order[0]
    inverse = jnp.sum(
        jnp.where(ordering[None, :] == slot_ids[:, None], slot_ids[None, :], 0), axis=1
    )
    ctx_index = lax.axis_index("line") * lax.axis_size("pair") + lax.axis_index("pair")
    first_slot = ctx_index * blocks_dev
    my_slots = first_slot + jnp.arange(blocks_dev, dtype=jnp.int32)
    my_blocks = lax.dynamic_slice_in_dim(ordering, first_slot, blocks_dev)
    positions = my_blocks % group_blocks
    group_base = my_blocks // group_blocks * group_blocks
    prompt_slots = jnp.take(
        inverse, group_base[:, None] + jnp.arange(PBLK, dtype=jnp.int32)[None, :]
    )
    key_slots = jnp.concatenate([prompt_slots, my_slots[:, None]], axis=1)

    keyval_cut = lax.dynamic_slice_in_dim(keyval_weight, core * HD, HD, axis=1)
    first_cut = jnp.concatenate([query_weight, keyval_cut], axis=1)
    down_cut, up_cut, first_all = run_programs(
        [Exchange(down_weight, True), Exchange(up_weight, True), rows_gather(first_cut)],
        [down_weight, up_weight, first_cut],
        1,
    )
    first_all = flat(first_all)

    stream = hidden_in.astype(F32)
    normed_one = layer_norm(stream, gain_one, shift_one).astype(BF16)
    value_shift = jnp.where(core == 1, value_bias.astype(F32), 0.0)
    first_shift = jnp.concatenate([query_bias.astype(F32), value_shift])
    first_low = (jnp.dot(normed_one, first_all, preferred_element_type=F32) + first_shift).astype(
        BF16
    )
    query_low = first_low[:, :head_width]
    part_low = first_low[:, head_width:]
    keyval_every = gather_ctx(part_low, 4)
    keyval_every, down_cut, up_cut = lax.optimization_barrier((keyval_every, down_cut, up_cut))
    down_all = gather_line(down_cut)
    up_all = gather_line(up_cut)
    keyval_low = in_order(part_low, swap_tp(part_low), axis=1)
    keyval_table = keyval_every.transpose(0, 1, 3, 2, 4).reshape(slot_count, BLK, 2 * HD)
    own_table = keyval_low.reshape(blocks_dev, 1, BLK, 2 * HD)
    keysets = jnp.concatenate([keyval_table[prompt_slots], own_table], axis=1)
    keysets = keysets.reshape(blocks_dev, (PBLK + 1) * BLK, 2 * HD)
    cotangent = own_half(out_cotangent)
    cotangent_line = to_line_order(cotangent)
    mixed_low, logsums, (proj_all, cotangent_all) = attend(
        query_low,
        keysets,
        positions,
        [rows_gather(proj_weight), plane_gather(cotangent_line)],
        [proj_weight, cotangent_line],
        2,
    )
    proj_all, cotangent_all = flat(proj_all), flat(cotangent_all)
    proj_part = jnp.einsum("rk,ok->ro", mixed_low, proj_all, preferred_element_type=F32)
    middle = own_half(stream) + sum_halves(proj_part) + proj_bias.astype(F32)

    normed_two = layer_norm(middle, gain_two, shift_two).astype(BF16)
    normed_two_line = to_line_order(normed_two)
    normed_two_all = run_programs([plane_gather(normed_two_line)], [normed_two_line], 6)[0]
    normed_two_all = flat(normed_two_all)
    up_shift = lax.dynamic_slice_in_dim(up_bias, quarter * hidden_dev, hidden_dev).astype(F32)
    grad_act = jnp.dot(cotangent_all, down_all, preferred_element_type=F32)
    pre_act = jnp.dot(normed_two_all, up_all, preferred_element_type=F32) + up_shift
    act, gelu_pull = jax.vjp(gelu_tanh, pre_act)
    act_low = act.astype(BF16)
    grad_pre_wide = gelu_pull(grad_act)[0]
    grad_pre = grad_pre_wide.astype(BF16)
    normed_two_part = jnp.einsum("rf,df->rd", grad_pre, up_all, preferred_element_type=F32)
    plane_two, plane_parts = plane_sum(normed_two_part)
    grad_normed_two = from_line_order(run_programs([plane_two], [plane_parts], 7)[0])
    down_part = jnp.einsum("rf,of->ro", act_low, down_all, preferred_element_type=F32)
    grad_up_bias = jnp.sum(grad_pre, axis=0, dtype=F32)
    down_weight_grad = jnp.einsum("ro,rf->of", cotangent_all, act_low, preferred_element_type=F32)
    up_weight_grad = jnp.einsum("rd,rf->df", normed_two_all, grad_pre, preferred_element_type=F32)
    down_cut_grad = sum_line(down_weight_grad)
    up_cut_grad = sum_line(up_weight_grad)

    norm_two_pull = jax.vjp(layer_norm, middle, gain_two, shift_two)[1]
    grad_mid_norm, grad_mlp_norm_gain, grad_mlp_norm_bias = norm_two_pull(grad_normed_two)
    grad_middle = cotangent.astype(F32) + grad_mid_norm
    grad_down_bias = jnp.sum(cotangent, axis=0, dtype=F32)

    grad_attn_half = grad_middle.astype(BF16)
    grad_proj_bias = jnp.sum(grad_attn_half, axis=0, dtype=F32)
    grad_attn = join_halves(grad_attn_half)
    proj_weight_grad = jnp.einsum("ro,rk->ok", grad_attn, mixed_low, preferred_element_type=F32)
    grad_mixed = jnp.einsum("ro,ok->rk", grad_attn, proj_all, preferred_element_type=F32).astype(
        BF16
    )
    sum_proj, proj_parts = rows_sum(proj_weight_grad)
    sum_down, down_parts = plane_sum(down_part)
    grad_query, grad_sets, (grad_proj_weight, mlp_out) = attend_back(
        query_low,
        grad_mixed,
        mixed_low,
        logsums,
        keysets,
        positions,
        [sum_proj, sum_down],
        [proj_parts, down_parts],
        3,
    )
    mlp_out = from_line_order(mlp_out) + down_bias.astype(F32)
    layer_out = join_halves((middle + mlp_out).astype(BF16))
    grad_table = by_slot(grad_sets, key_slots, slot_count)
    grad_query_bias = jnp.sum(grad_query, axis=0, dtype=F32)
    grad_parts = grad_table.reshape(
        lax.axis_size("line"), lax.axis_size("pair"), 2, rows_dev, HD
    )
    grad_part = sum_ctx(grad_parts, 12).astype(BF16)
    grad_value_bias = jnp.where(core == 1, jnp.sum(grad_part, axis=0, dtype=F32), 0.0)
    grad_first = jnp.concatenate([grad_query, grad_part], axis=1)
    normed_one_part = jnp.einsum("rk,dk->rd", grad_first, first_all, preferred_element_type=F32)
    grad_normed_one = sum_halves(normed_one_part)
    first_weight_grad = jnp.einsum("rd,rk->dk", normed_one, grad_first, preferred_element_type=F32)
    norm_one_pull = jax.vjp(layer_norm, own_half(stream), gain_one, shift_one)[1]
    grad_in_norm, grad_attn_norm_gain, grad_attn_norm_bias = norm_one_pull(grad_normed_one)
    input_grad = join_halves((grad_middle + grad_in_norm).astype(BF16))

    query_slots = jnp.zeros((2 * head_width,), F32)
    query_slots = lax.dynamic_update_slice_in_dim(
        query_slots, grad_query_bias, core * head_width, axis=0
    )
    hidden_slots = jnp.zeros((2 * quarters * hidden_dev,), F32)
    hidden_slots = lax.dynamic_update_slice_in_dim(
        hidden_slots, grad_up_bias, (core * quarters + quarter) * hidden_dev, axis=0
    )
    pieces = [
        grad_attn_norm_gain,
        grad_attn_norm_bias,
        grad_proj_bias,
        grad_mlp_norm_gain,
        grad_mlp_norm_bias,
        grad_down_bias,
        grad_value_bias,
        query_slots,
        hidden_slots,
    ]
    sum_first, first_parts = rows_sum(first_weight_grad)
    total, padded = total_of(jnp.concatenate(pieces))
    grad_first_weight, grad_down_weight, grad_up_weight, summed = run_programs(
        [sum_first, Exchange(down_cut_grad, False), Exchange(up_cut_grad, False), total],
        [first_parts, down_cut_grad, up_cut_grad, padded],
        13,
    )
    grad_down_weight, grad_up_weight = grad_down_weight.astype(F32), grad_up_weight.astype(F32)
    grad_query_weight = grad_first_weight[:, :head_width]
    grad_cut = grad_first_weight[:, head_width:]
    grad_keyval_weight = in_order(grad_cut, swap_tp(grad_cut), axis=1)
    summed = summed.reshape(-1)
    cuts, start = [], 0
    for piece in pieces:
        cuts.append(summed[start : start + piece.shape[0]])
        start += piece.shape[0]
    sum_query = lax.dynamic_slice_in_dim(cuts[7], core * head_width, head_width)
    sum_up = lax.dynamic_slice_in_dim(cuts[8], core * quarters * hidden_dev, quarters * hidden_dev)
    return (
        layer_out,
        input_grad,
        cuts[0],
        cuts[1],
        grad_query_weight,
        sum_query,
        grad_keyval_weight,
        cuts[6],
        grad_proj_weight,
        cuts[2],
        cuts[3],
        cuts[4],
        grad_up_weight,
        sum_up,
        grad_down_weight,
        cuts[5],
    )


def solution(mesh):
    fsdp, ctx, tp = mesh.devices.shape
    grid = Mesh(mesh.devices.reshape(fsdp, ctx // 2, 2, tp), EVERY)
    by_rows = P(ROWS, None)
    by_both = P(ROWS, "tp")
    return jax.shard_map(
        body,
        mesh=grid,
        in_specs=(
            by_rows,
            P("fsdp", None),
            P(),
            P(),
            by_both,
            P("tp"),
            by_rows,
            P(),
            by_both,
            P(),
            P(),
            P(),
            by_both,
            P("tp"),
            by_both,
            P(),
            by_rows,
        ),
        out_specs=(
            by_rows,
            by_rows,
            P(),
            P(),
            by_both,
            P("tp"),
            by_rows,
            P(),
            by_both,
            P(),
            P(),
            P(),
            by_both,
            P("tp"),
            by_both,
            P(),
        ),
        check_vma=False,
    )
```

time: 1430 us -> 726 us (0.51)
  waiting for transfers between devices: 934 us -> 12.1 us
  Pallas kernels: 0 us -> 458 us
  matrix products: 212 us -> 118 us
  other arithmetic: 106 us -> 34.1 us
  local copies, waits for them, and re-layouts: 103 us -> 66.1 us
  loops' own time: 18.5 us -> 0 us
  blocking collectives: 17.4 us -> 0 us
    reduce_scatter x7 -> x2, waiting for transfers between devices: 511 us -> 0.01 us  [sum_line(): lax.psum_scatter(values.astype(BF16), 'line', scatter_dimension=0, tiled=...]
    pallas_call x0 -> x9, Pallas kernels: none -> 458 us  [the longest x6 275 us: run_programs(): pl.pallas_call(kernel, out_shape=[one.out for one in programs], in_specs=...]
    all_gather x5 -> x0, waiting for transfers between devices: 187 us -> none  [the longest x2 92.3 us: gather_plane(): return lax.all_gather(values, PLANE + ('tp',), axis=0, tiled=True)]
    all_gather x2, waiting for transfers between devices: 120 us -> 10.1 us  [gather_line(): every = lax.all_gather(values, 'line', axis=0, tiled=False)]
    psum x1 -> x0, waiting for transfers between devices: 98.6 us -> none  [body(): summed = lax.psum(jnp.concatenate(pieces), EVERY)]
    dot_general x15 -> x0, matrix products: 95.6 us -> none  [the longest x2 24 us: attend_back(): jnp.einsum('hqd,kd->hqk', grad_mixed, value_part, preferred_element_type=...]
    convert_element_type x9 -> x4, other arithmetic: 30.3 us -> 4.02 us  [the longest x1 1.53 us: body(): grad_up_weight.astype(F32)]
    reduce_sum x2 -> x0, other arithmetic: 23.3 us -> none  [attend_block(): row_total = jnp.sum(exponent, axis=-1, keepdims=True)]
  transfers between devices with their start and end apart: 27 -> 11, of which waited for: 19 -> 2; matrix products, arithmetic and copies ran while one was open for 17% -> 22% of each run, Pallas kernels for 0% -> 41%
where the time goes in v3:
time: 726 us; the launch traced here: 720 us
  Pallas kernels  458 us (63%)
  matrix products  118 us (16%)
  local copies, waits for them, and re-layouts  66.1 us (9%)
  other arithmetic  34.1 us (5%)
  starting transfers between devices  17.2 us (2%)
  between operations  15 us (2%)
  waiting for transfers between devices  12.1 us (2%)
    pallas_call x6, Pallas kernels, run_programs(): pl.pallas_call(kernel, out_shape=[one.out for one in programs], in_specs=...  275 us
    pallas_call x1, Pallas kernels, attend_back(): pl.pallas_call(functools.partial(attend_back_kernel, programs, blocks * h...  97.3 us
    pallas_call x1, Pallas kernels, attend(): pl.pallas_call(functools.partial(attend_kernel, programs, blocks * heads)...  80.9 us
    unnamed x132, local copies, waits for them, and re-layouts  30.7 us
    dot_general x1, matrix products, body(): grad_act = jnp.dot(cotangent_all, down_all, preferred_element_type=F32)  18.6 us
    dot_general x1, matrix products, body(): jnp.einsum('rf,of->ro', act_low, down_all, preferred_element_type=F32)  18.2 us
    ppermute x7, starting transfers between devices, swap_tp(): return lax.ppermute(values, 'tp', [(0, 1), (1, 0)])  16.2 us
  transfers between devices with their start and end apart: 11, of which 2 were waited for; matrix products, arithmetic and copies ran while one was open for 22% of the time, Pallas kernels for 41%

profile of v3, /device:TPU:0, one launch (start us, length us, event | category | flops | bytes accessed | tf_op | source)
XLA Modules:
  0.0 720.4 jit_solution(14094854610107276908)
XLA Ops:
  7.3 2.1 convert_reduce_fusion.1
  11.1 66.4 %shard_map.288 = (bf16[4,128,1024]{2,1,0:T(8,128)(2,1)}, bf16[4,128,1024]{2,1,0:T(8,128)(2,1)}, bf16[2,4,2,128,1152]{4,3,2,1,0:T(8,128)(2,1)}) custom-call(bf16[128,4096]{1,0:T(8,128)(2,1)} %refs_0_.1, bf16[128,4096]{1,0:T(8,128)(2,1)} %refs_1_.1, bf16[128,1152]{1,0:T(8,128)(2,1)} %pad_maximum_fusion.9.refs_2_), custom_call_target="tpu_custom_call" | custom-call | tf_op jit(solution)/shard_map/pallas_call | solution.py:577
  77.4 5.3 fusion.7
  83.4 22.1 %shard_map.289 = bf16[4,2,2,512,128]{4,3,2,1,0:T(8,128)(2,1)} custom-call(bf16[512,128]{1,0:T(8,128)(2,1)} %slice.231.refs_0_), custom_call_target="tpu_custom_call" | custom-call | tf_op jit(solution)/shard_map/pallas_call | solution.py:577
  120.4 5.1 copy.44
  125.5 4.4 reshape.316
  129.9 3.6 gather_fusion.1
  137.9 2.1 fusion.23
  140.0 2.4 copy.46.refs_3_
  142.3 80.9 %shard_map.290 = (bf16[512,1024]{1,0:T(8,128)(2,1)}, f32[2,8,1,256]{3,2,1,0:T(1,128)}, bf16[2,4,2,128,1024]{4,3,2,1,0:T(8,128)(2,1)}, bf16[2,2,2,256,2048]{4,3,2,1,0:T(8,128)(2,1)}) custom-call(s32[2]{0:T(128)} %and_select_fusion.3.refs_0_, bf16[512,1024]{1,0:T(8,128)(2,1)} %slice.230.refs_1_, bf16[2,2304,128]{2,1,0:T(8,128)(2,1)} %get-tuple-element.77.refs_2_.refs_5_, ...), custom_call_target="tpu_custom_call" | custom-call | flops 4831838208 | bytes 4194304 | tf_op jit(solution)/shard_map/pallas_call | solution.py:743
  223.3 4.9 fusion.24
  232.2 2.5 convert_element_type.102
  239.9 4.0 fusion.22
  245.9 43.2 %shard_map.291 = bf16[2,2,2,256,2048]{4,3,2,1,0:T(8,128)(2,1)} custom-call(bf16[256,2048]{1,0:T(8,128)(2,1)} %copy-done.12), custom_call_target="tpu_custom_call" | custom-call | tf_op jit(solution)/shard_map/pallas_call | solution.py:577
  289.7 14.4 %fusion.25 = f32[2048,1024]{1,0:T(8,128)} fusion(bf16[2048,2048]{1,0:T(8,128)(2,1)} %bitcast.73, bf16[2048,1024]{1,0:T(8,128)(2,1)} %bitcast.85), kind=kOutput, calls=%fused_computation.165 | convolution fusion | flops 8589934592 | bytes 20971520 | tf_op jit(solution)/shard_map/dot_general | solution.py:1018
  304.1 10.1 %all-gather.5.cloned.1.call-done = bf16[16,128,1024]{2,1,0:T(8,128)(2,1)} async-done(((bf16[4,128,1024]{2,1,0:T(8,128)(2,1)}), bf16[16,128,1024]{2,1,0:T(8,128)(2,1)}) %all-gather.5.cloned.1.call-update) | async-done | bytes 4194320 | tf_op jit(solution)/shard_map/all_gather | solution.py:652
  314.2 18.6 %convert_reduce_fusion = (f32[1024]{0:T(1024)S(1)}, bf16[2048,1024]{1,0:T(8,128)(2,1)S(1)}) fusion(f32[2048,1024]{1,0:T(8,128)} %fusion.25, f32[1024]{0:T(1024)S(1)} %dynamic-slice_convert_fusion, bf16[2048,2048]{1,0:T(8,128)(2,1)} %bitcast.89, bf16[2048,1024]{1,0:T(8,128)(2,1)} %bitcast.87), kind=kOutput, calls=%fused_computation.11 | convolution fusion | flops 8638168064 | bytes 25174016 | tf_op jit(solution)/shard_map/dot_general | solution.py:1017
  332.8 2.1 copy-done.45
  334.9 10.7 %convolution_convert_fusion.4 = bf16[2048,1024]{1,0:T(8,128)(2,1)} fusion(bf16[2048,2048]{1,0:T(8,128)(2,1)S(1)} %bitcast.74, bf16[2048,1024]{1,0:T(8,128)(2,1)S(1)} %get-tuple-element.59), kind=kOutput, calls=%fused_computation.19 | convolution fusion | flops 8592031744 | bytes 16777216 | tf_op jit(solution)/shard_map/rd,rf->df/dot_general | solution.py:1029
  345.7 14.2 %convolution_convert_fusion.2 = bf16[2048,2048]{1,0:T(8,128)(2,1)} fusion(bf16[2048,1024]{1,0:T(8,128)(2,1)} %copy-done.45, bf16[2048,1024]{1,0:T(8,128)(2,1)} %bitcast.86), kind=kOutput, calls=%fused_computation.15 | convolution fusion | flops 8594128896 | bytes 16777216 | tf_op jit(solution)/shard_map/rf,df->rd/dot_general | solution.py:1023
  359.8 42.6 %shard_map.292 = f32[256,2048]{1,0:T(8,128)} custom-call(bf16[2,2,2,256,2048]{4,3,2,1,0:T(8,128)(2,1)} %bitcast.72), custom_call_target="tpu_custom_call" | custom-call | tf_op jit(solution)/shard_map/pallas_call | solution.py:577
  414.9 18.2 %convolution_convert_fusion.1 = bf16[2048,2048]{1,0:T(8,128)(2,1)} fusion(bf16[2048,1024]{1,0:T(8,128)(2,1)S(1)} %bitcast.88, f32[2048,1024]{1,0:T(8,128)} %fusion.25, f32[1024]{0:T(1024)S(1)} %dynamic-slice_convert_fusion), kind=kOutput, calls=%fused_computation.14 | convolution fusion | flops 8615100416 | bytes 20975616 | tf_op jit(solution)/shard_map/rf,of->ro/dot_general | solution.py:1026
  433.1 13.7 %convolution_convert_fusion.5 = bf16[2048,1024]{1,0:T(8,128)(2,1)} fusion(bf16[2048,2048]{1,0:T(8,128)(2,1)S(1)} %bitcast.92, f32[2048,1024]{1,0:T(8,128)} %fusion.25, f32[1024]{0:T(1024)S(1)} %dynamic-slice_convert_fusion), kind=kOutput, calls=%fused_computation.20 | convolution fusion | flops 8613003264 | bytes 20975616 | tf_op jit(solution)/shard_map/ro,rf->of/dot_general | solution.py:1028
  450.0 3.3 convolution_convert_fusion.6.refs_2_
  453.4 4.4 convolution_convert_fusion.3
  457.8 97.3 %shard_map.293 = (bf16[512,1024]{1,0:T(8,128)(2,1)}, f32[2,2304,256]{2,1,0:T(8,128)}, f32[128,1024]{1,0:T(8,128)}, f32[256,2048]{1,0:T(8,128)}) custom-call(s32[2]{0:T(128)} %and_select_fusion.3.refs_0_, bf16[512,1024]{1,0:T(8,128)(2,1)} %slice.230.refs_1_, bf16[512,1024]{1,0:T(8,128)(2,1)} %convolution_convert_fusion.6.refs_2_, ...), custom_call_target="tpu_custom_call" | custom-call | flops 12079595520 | bytes 8388608 | tf_op jit(solution)/shard_map/pallas_call | solution.py:828
  555.0 4.8 shard_map.294
  559.8 26.2 %shard_map.295 = f32[512,128]{1,0:T(8,128)} custom-call(bf16[4,2,2,512,128]{4,3,2,1,0:T(8,128)(2,1)} %bitcast.77), custom_call_target="tpu_custom_call" | custom-call | tf_op jit(solution)/shard_map/pallas_call | solution.py:577
  587.1 5.0 fusion.9
  596.0 4.9 convolution_convert_fusion
  611.0 74.9 %shard_map.296 = (f32[128,1152]{1,0:T(8,128)}, bf16[128,4096]{1,0:T(8,128)(2,1)}, bf16[128,4096]{1,0:T(8,128)(2,1)}, f32[184,128]{1,0:T(8,128)}) custom-call(bf16[2,4,2,128,1152]{4,3,2,1,0:T(8,128)(2,1)} %bitcast.78, bf16[4,128,1024]{2,1,0:T(8,128)(2,1)} %bitcast.81, bf16[4,128,1024]{2,1,0:T(8,128)(2,1)} %bitcast.80, f32[184,128]{1,0:T(8,128)} %pad_bitcast_fusion.refs_3_), custom_call_target="tpu_custom_call" | custom-call | tf_op jit(solution)/shard_map/pallas_call | solution.py:577
  689.1 14.9 %collective-permute-start.6 = (f32[128,128]{1,0:T(8,128)S(1)}, f32[128,128]{1,0:T(8,128)S(1)}, u32[]{:S(2)}, u32[]{:S(2)}) collective-permute-start(f32[128,128]{1,0:T(8,128)S(1)} %slice.213), channel_id=1, source_target_pairs={{0,1},{1,0},{2,3},{3,2},{4,5},{5,4},{6,7},{7,6},{8,9},{9,8},{10,11... | collective-permute-start | bytes 196616 | tf_op jit(solution)/shard_map/ppermute | solution.py:647
  (240 shorter events, 76.4 us)
Async XLA Ops:
  7.2 3.1 copy-start
  7.2 282.4 %all-gather.7.cloned.1.call-start = ((), (), s32[]{:S(2)}) async-start(), calls=%async_computation.5 | async-start | bytes 5242880 | tf_op jit(solution)/shard_map/all_gather | solution.py:652
  9.5 68.0 %copy-start.29 = (f32[512]{0:T(512)}, f32[512]{0:T(512)S(1)}, u32[]{:S(2)}) copy-start(f32[512]{0:T(512)S(1)} %broadcast_multiply_fusion) | copy-start | bytes 6148
  10.2 72.6 %copy-start.38 = (f32[512]{0:T(512)}, f32[512]{0:T(512)S(1)}, u32[]{:S(2)}) copy-start(f32[512]{0:T(512)S(1)} %add_rsqrt_fusion) | copy-start | bytes 6148
  10.2 72.5 %copy-start.19 = (f32[2048]{0:T(1024)}, f32[2048]{0:T(1024)S(1)}, u32[]{:S(2)}) copy-start(f32[2048]{0:T(1024)S(1)} %convert_element_type.103) | copy-start | bytes 24580
  10.2 72.5 %copy-start.27 = (f32[2048]{0:T(1024)}, f32[2048]{0:T(1024)S(1)}, u32[]{:S(2)}) copy-start(f32[2048]{0:T(1024)S(1)} %convert_element_type.104) | copy-start | bytes 24580
  82.8 23.6 %copy-start.40 = (s32[1,16]{1,0:T(1,128)S(1)}, s32[1,16]{1,0:T(1,128)}, u32[]{:S(2)}) copy-start(s32[1,16]{1,0:T(1,128)} %param.18) | copy-start | bytes 196
  83.4 22.5 %copy-start.16 = (bf16[512,128]{1,0:T(8,128)(2,1)S(1)}, bf16[512,128]{1,0:T(8,128)(2,1)}, u32[]{:S(2)}) copy-start(bf16[512,128]{1,0:T(8,128)(2,1)} %slice.231.refs_0_) | copy-start | bytes 393220
  105.6 208.6 %all-gather.5.cloned.1.call-start = ((), (), s32[]{:S(2)}) async-start(), calls=%async_computation.4 | async-start | bytes 5242880 | tf_op jit(solution)/shard_map/all_gather | solution.py:652
  105.9 29.1 %collective-permute-start = (bf16[512,128]{1,0:T(8,128)(2,1)S(1)}, bf16[512,128]{1,0:T(8,128)(2,1)}, u32[]{:S(2)}, u32[]{:S(2)}) collective-permute-start(bf16[512,128]{1,0:T(8,128)(2,1)S(1)} %copy-done.16), channel_id=1, source_target_pairs={{0,1},{1,0},{2,3},{3,2},{4,5},{5,4},{6,7},{7,6},{8,9},{9,8},{10,11... | collective-permute-start | bytes 393224 | tf_op jit(solution)/shard_map/ppermute | solution.py:647
  230.8 9.0 %collective-permute-start.1 = (f32[256,2048]{1,0:T(8,128)}, f32[256,2048]{1,0:T(8,128)}, u32[]{:S(2)}, u32[]{:S(2)}) collective-permute-start(f32[256,2048]{1,0:T(8,128)} %constant_dynamic-slice_fusion.1), channel_id=1, source_target_pairs={{0,1},{1,0},{2,3},{3,2},{4,5},{5,4},{6,7},{7,6},{8,9},{9,8},{10,11... | collective-permute-start | bytes 6291464 | tf_op jit(solution)/shard_map/ppermute | solution.py:647
  231.5 379.6 %reduce-scatter.5.cloned.1.call-start = ((), (), s32[]{:S(2)}) async-start(), calls=%async_computation.3 | async-start | bytes 5242880 | tf_op jit(solution)/shard_map/reduce_scatter | solution.py:659
  238.5 5.4 copy-start.22
  243.8 45.3 %copy-start.24 = (f32[256]{0:T(256)}, f32[256]{0:T(256)S(1)}, u32[]{:S(2)}) copy-start(f32[256]{0:T(256)S(1)} %get-tuple-element.73) | copy-start | bytes 3076
  314.1 20.7 %copy-start.7 = (bf16[2,2,2,256,2048]{4,3,2,1,0:T(8,128)(2,1)S(1)}, bf16[2,2,2,256,2048]{4,3,2,1,0:T(8,128)(2,1)}, u32[]{:S(2)}) copy-start(bf16[2,2,2,256,2048]{4,3,2,1,0:T(8,128)(2,1)} %shard_map.291) | copy-start | bytes 25165828
  345.6 265.4 %reduce-scatter.3.cloned.1.call-start = ((), (), s32[]{:S(2)}) async-start(), calls=%async_computation.2 | async-start | bytes 5242880 | tf_op jit(solution)/shard_map/reduce_scatter | solution.py:659
  413.1 20.0 %slice-start = ((s8[8388608]{0:T(1024)(128)(4,1)}), s8[4194304]{0:T(1024)(128)(4,1)S(1)}, s32[]{:S(2)}) async-start(s8[8388608]{0:T(1024)(128)(4,1)} %bitcast.90), calls=%async_computation.6 | async-start | bytes 8388608
  413.1 20.0 %slice-start.1 = ((s8[8388608]{0:T(1024)(128)(4,1)}), s8[4194304]{0:T(1024)(128)(4,1)S(1)}, s32[]{:S(2)}) async-start(s8[8388608]{0:T(1024)(128)(4,1)} %bitcast.90), calls=%async_computation.7 | async-start | bytes 8388608
  413.2 34.4 %collective-permute-start.2 = (bf16[256,2048]{1,0:T(8,128)(2,1)S(1)}, bf16[256,2048]{1,0:T(8,128)(2,1)}, u32[]{:S(2)}, u32[]{:S(2)}) collective-permute-start(bf16[256,2048]{1,0:T(8,128)(2,1)S(1)} %get-tuple-element.63), channel_id=1, source_target_pairs={{0,1},{1,0},{2,3},{3,2},{4,5},{5,4},{6,7},{7,6},{8,9},{9,8},{10,11... | collective-permute-start | bytes 3145736 | tf_op jit(solution)/shard_map/ppermute | solution.py:647
  450.0 3.3 copy-start.44
  559.8 27.2 %copy-start.15 = (bf16[512,1024]{1,0:T(8,128)(2,1)S(1)}, bf16[512,1024]{1,0:T(8,128)(2,1)}, u32[]{:S(2)}) copy-start(bf16[512,1024]{1,0:T(8,128)(2,1)} %get-tuple-element.45) | copy-start | bytes 3145732
  592.3 8.6 %collective-permute-start.4 = (f32[256,2048]{1,0:T(8,128)S(1)}, f32[256,2048]{1,0:T(8,128)S(1)}, u32[]{:S(2)}, u32[]{:S(2)}) collective-permute-start(f32[256,2048]{1,0:T(8,128)S(1)} %constant_dynamic-slice_fusion), channel_id=1, source_target_pairs={{0,1},{1,0},{2,3},{3,2},{4,5},{5,4},{6,7},{7,6},{8,9},{9,8},{10,11... | collective-permute-start | bytes 6291464 | tf_op jit(solution)/shard_map/ppermute | solution.py:647
  594.7 11.0 %collective-permute-start.3 = (bf16[256,2048]{1,0:T(8,128)(2,1)S(1)}, bf16[256,2048]{1,0:T(8,128)(2,1)S(1)}, u32[]{:S(2)}, u32[]{:S(2)}) collective-permute-start(bf16[256,2048]{1,0:T(8,128)(2,1)S(1)} %add_convert_fusion.2), channel_id=1, source_target_pairs={{0,1},{1,0},{2,3},{3,2},{4,5},{5,4},{6,7},{7,6},{8,9},{9,8},{10,11... | collective-permute-start | bytes 3145736 | tf_op jit(solution)/shard_map/ppermute | solution.py:647
  595.9 5.0 copy-start.2
  596.0 5.0 copy-start.23
  596.0 5.0 copy-start.26
  604.9 2.7 collective-permute-start.5
  686.0 21.8 %copy-start.14 = (bf16[128,4096]{1,0:T(8,128)(2,1)S(1)}, bf16[128,4096]{1,0:T(8,128)(2,1)}, u32[]{:S(2)}) copy-start(bf16[128,4096]{1,0:T(8,128)(2,1)} %get-tuple-element.50) | copy-start | bytes 3145732
  689.1 22.3 %collective-permute-start.6 = (f32[128,128]{1,0:T(8,128)S(1)}, f32[128,128]{1,0:T(8,128)S(1)}, u32[]{:S(2)}, u32[]{:S(2)}) collective-permute-start(f32[128,128]{1,0:T(8,128)S(1)} %slice.213), channel_id=1, source_target_pairs={{0,1},{1,0},{2,3},{3,2},{4,5},{5,4},{6,7},{7,6},{8,9},{9,8},{10,11... | collective-permute-start | bytes 196616 | tf_op jit(solution)/shard_map/ppermute | solution.py:647
  705.2 4.1 copy-start.13
  709.3 3.7 copy-start.17
  709.3 4.5 copy-start.1
  (27 other events, 55.4 us)
Sparse Core Ops, SparseCore 0:
  105.7 89.8 all-gather.6
  231.6 82.5 all-gather.4
  345.7 75.2 reduce-scatter.4
  446.9 74.3 reduce-scatter.2

commit v4 on v3

--- a/solution.py
+++ b/solution.py
@@ -26,10 +26,6 @@
     return centered * lax.rsqrt(spread + EPSILON) * norm_gain + norm_shift
 
 
-def gelu_tanh(values):
-    return jax.nn.gelu(values, approximate=True)
-
-
 MESH_ID = pl.DeviceIdType.MESH
 VMEM_BYTES = 60 * 1024 * 1024
 SIDE = ("pair", "fsdp")
@@ -100,7 +96,7 @@
             pltpu.SemaphoreType.DMA(()),
             pltpu.SemaphoreType.DMA((2, self.lines)),
             pltpu.SemaphoreType.DMA((self.lines,)),
-            pltpu.SemaphoreType.DMA((self.lines, len(self.steps) * parts)),
+            pltpu.SemaphoreType.DMA((self.lines, max(1, len(self.steps)) * parts)),
             pltpu.SemaphoreType.DMA((self.lines, parts)),
         ]
 
@@ -208,10 +204,10 @@
 
 
 class Sum:
-    def __init__(self, steps, lines, rows, columns, slot):
+    def __init__(self, steps, lines, rows, columns, slot, shared=0):
         self.steps, self.lines, self.rows, self.columns = steps, lines, rows, columns
-        self.slot = slot
-        self.out = jax.ShapeDtypeStruct((rows, columns), F32)
+        self.slot, self.shared = slot, shared
+        self.out = jax.ShapeDtypeStruct((rows, columns + shared), F32)
         self.in_spec = pl.BlockSpec(memory_space=pl.ANY)
         self.out_spec = pl.BlockSpec(memory_space=pltpu.VMEM)
 
@@ -226,14 +222,17 @@
             + [pltpu.SemaphoreType.DMA((lines, sizes[0]))]
             + [pltpu.SemaphoreType.DMA((lines, size)) for size in sizes] * 2
             + [pltpu.SemaphoreType.DMA((2, lines))] * 2
+            + [pltpu.SemaphoreType.DMA((2,))]
         )
 
-    def stages(self, me, x_ref, out_ref, own, *rest):
+    def stages(self, me, x_ref, whole_ref, own, *rest):
+        out_ref = whole_ref.at[:, : self.columns] if self.shared else whole_ref
         steps, lines, rows, slot = self.steps, self.lines, self.rows, self.slot
         count = len(steps)
         held, rest = rest[:count], rest[count:]
         on_line, own_sem, rest = rest[0], rest[1], rest[2:]
-        send, recv, (line_send, line_recv) = rest[:count], rest[count : 2 * count], rest[2 * count :]
+        send, recv = rest[:count], rest[count : 2 * count]
+        line_send, line_recv, share_sem = rest[2 * count :]
         my_line = me["line"] if lines > 1 else 0
         last = count - 1
 
@@ -275,8 +274,8 @@
             for bits in parts_of(0):
                 own_copy(shard, bits).start()
 
-        def take_step(k, shard, amount):
-            for bits in parts_of(k):
+        def take_step(k, shard, amount, parts=None):
+            for bits in parts or parts_of(k):
                 copy(k, shard, bits | 1 << k).wait_recv()
                 arrived = store(k, shard, bits)
                 if k == 0:
@@ -360,12 +359,27 @@
                         pl.when((shard >= 0) & (shard < lines))(
                             lambda amount=amount, shard=shard: line_copy(amount, shard).wait_send()
                         )
+            if self.shared:
+                share = remote(
+                    whole_ref.at[:, self.columns - self.shared : self.columns],
+                    whole_ref.at[:, self.columns :],
+                    share_sem.at[0],
+                    share_sem.at[1],
+                    flip(me, "tp"),
+                )
+                share.start()
+                share.wait()
             for k in range(count):
                 for shard in range(lines):
                     for bits in parts_of(k):
                         copy(k, shard, bits | 1 << k).wait_send()
 
-        ticks = [functools.partial(tick, number) for number in range(lines + count)]
+        if lines == 1:
+            ticks = [
+                functools.partial(take_step, k, 0, 0, [bits]) for k in range(count) for bits in parts_of(k)
+            ]
+        else:
+            ticks = [functools.partial(tick, number) for number in range(lines + count)]
         return [begin] + ticks + [end]
 
 
@@ -563,27 +577,49 @@
     works = [(0.0, functools.partial(greet, me, programs))]
     for one, x_ref, out_ref, held in zip(programs, x_refs, out_refs, split_scratch(programs, scratch)):
         stages = one.stages(me, x_ref, out_ref, *held)
-        works += [(k / (len(stages) - 1), stage) for k, stage in enumerate(stages)]
+        places = getattr(one, "places", (0.0, 1.0))
+        if len(places) == 2:
+            places = spaced(places[0], places[1], len(stages))
+        last = len(places) - 2
+        works += [
+            (places[-1] if k == len(stages) - 1 else places[min(k, last)], stage)
+            for k, stage in enumerate(stages)
+        ]
     return sorted(works, key=lambda work: work[0])
+
+
+def placed(program, *places):
+    program.places = list(places)
+    return program
+
+
+def spaced(start, stop, count):
+    return [start + (stop - start) * k / (count - 1) for k in range(count)]
 
 
 def run_programs(programs, arrays, number):
     count = len(programs)
+    given = [k for k, array in enumerate(arrays) if not callable(array)]
 
     def kernel(*refs):
-        for _, work in schedule(programs, refs[:count], refs[count : 2 * count], refs[2 * count :]):
+        in_refs, out_refs = refs[: len(given)], refs[len(given) : len(given) + count]
+        in_refs = [
+            array(out_refs) if callable(array) else in_refs[given.index(k)]
+            for k, array in enumerate(arrays)
+        ]
+        for _, work in schedule(programs, in_refs, out_refs, refs[len(given) + count :]):
             work()
 
     return pl.pallas_call(
         kernel,
         out_shape=[one.out for one in programs],
-        in_specs=[one.in_spec for one in programs],
+        in_specs=[programs[k].in_spec for k in given],
         out_specs=[one.out_spec for one in programs],
         scratch_shapes=[held for one in programs for held in one.scratch()],
         compiler_params=pltpu.CompilerParams(
             collective_id=number, has_side_effects=True, vmem_limit_bytes=VMEM_BYTES
         ),
-    )(*arrays)
+    )(*[arrays[k] for k in given])
 
 
 def by_rows_slot(ref, at):
@@ -595,7 +631,7 @@
 
 
 def by_ctx_slot(ref, at):
-    return ref.at[at["line"], at["pair"], at["tp"]]
+    return ref.at[at["tp"], at["line"], at["pair"]]
 
 
 def rows_gather(values):
@@ -603,11 +639,24 @@
     return Gather(values, (SIDE, FRONT), lines, (2, lines, 2) + values.shape, by_rows_slot)
 
 
-def rows_sum(values):
+def line_gather(shape, kind):
+    lines = lax.axis_size("line")
+    like = jax.ShapeDtypeStruct(shape, kind)
+    return Gather(like, (), lines, (lines,) + shape, lambda ref, at: ref.at[at["line"]])
+
+
+def columns_gather(values):
+    lines, rows, columns = values.shape
+    return Gather(
+        values, (SIDE, FRONT), 1, (2, lines, 2, rows, columns), lambda ref, at: ref.at[at["fsdp"], :, at["pair"]]
+    )
+
+
+def rows_sum(values, shared=0):
     lines, (total, columns) = lax.axis_size("line"), values.shape
     rows = total // (4 * lines)
     parts = values.astype(BF16).reshape(2, lines, 2, rows, columns)
-    return Sum((FRONT, SIDE), lines, rows, columns, by_rows_slot), parts
+    return Sum((FRONT, SIDE), lines, rows, columns, by_rows_slot, shared), parts
 
 
 def plane_gather(values):
@@ -626,14 +675,13 @@
 
 def gather_ctx(values, number):
     lines = lax.axis_size("line")
-    one = Gather(values, ("pair", "tp"), lines, (lines, 2, 2) + values.shape, by_ctx_slot)
+    one = Gather(values, ("pair", "tp"), lines, (2, lines, 2) + values.shape, by_ctx_slot)
     return run_programs([one], [values], number)[0]
 
 
-def sum_ctx(values, number):
-    lines, _, _, rows, columns = values.shape
-    one = Sum(("tp", "pair"), lines, rows, columns, by_ctx_slot)
-    return run_programs([one], [values], number)[0]
+def ctx_sum(values):
+    _, lines, _, rows, columns = values.shape
+    return Sum(("tp", "pair"), lines, rows, columns, by_ctx_slot)
 
 
 def total_of(values):
@@ -641,37 +689,6 @@
     rows = -(-size // 1024) * 8
     padded = jnp.pad(values, (0, rows * 128 - size)).reshape(rows, 128)
     return Total(padded, lax.axis_size("line")), padded
-
-
-def swap_tp(values):
-    return lax.ppermute(values, "tp", [(0, 1), (1, 0)])
-
-
-def gather_line(values):
-    quarters, rows, columns = values.shape
-    every = lax.all_gather(values, "line", axis=0, tiled=False)
-    return every.reshape(-1, columns)
-
-
-def sum_line(values):
-    total, columns = values.shape
-    lines = lax.axis_size("line")
-    summed = lax.psum_scatter(values.astype(BF16), "line", scatter_dimension=0, tiled=True)
-    return summed.reshape(4, total // (4 * lines), columns)
-
-
-def to_line_order(values):
-    lines = lax.axis_size("line")
-    size = values.shape[1] // (2 * lines)
-    cuts = [(half * lines + shard) * size for shard in range(lines) for half in range(2)]
-    return jnp.concatenate([values[:, cut : cut + size] for cut in cuts], axis=1)
-
-
-def from_line_order(values):
-    lines = lax.axis_size("line")
-    size = values.shape[1] // (2 * lines)
-    cuts = [(shard * 2 + half) * size for half in range(2) for shard in range(lines)]
-    return jnp.concatenate([values[:, cut : cut + size] for cut in cuts], axis=1)
 
 
 LOG2E = 1.4426950408889634
@@ -692,31 +709,46 @@
     return lax.dot_general(left, right, (((1,), (1,)), ((), ())), preferred_element_type=F32)
 
 
-def beside(programs, in_refs, out_refs, scratch, steps):
-    step = pl.program_id(0) * pl.num_programs(1) + pl.program_id(1)
+def beside(programs, in_refs, out_refs, scratch, step, steps):
+    late = []
     for place, work in schedule(programs, in_refs, out_refs, scratch):
-        pl.when(step == min(steps - 1, int(place * steps)))(work)
+        if place < 1:
+            pl.when(step == int(place * steps))(work)
+        else:
+            late.append(work)
+
+    def finish():
+        @pl.when(step == steps - 1)
+        def _():
+            for work in late:
+                work()
+
+    return finish
 
 
 def attend_kernel(programs, steps, *refs):
     count = len(programs)
-    (position_ref, query_ref, key_ref, value_t_ref), refs = refs[:4], refs[4:]
+    (position_ref, slot_ref, query_ref, table_ref), refs = refs[:4], refs[4:]
     others, refs = refs[:count], refs[count:]
     (mixed_ref, logsum_ref), refs = refs[:2], refs[2:]
     other_outs, refs = refs[:count], refs[count:]
-    (bias_ref, score_ref), scratch = refs[:2], refs[2:]
+    (bias_ref, score_ref, value_t_ref), scratch = refs[:3], refs[3:]
     chunks = PBLK + 1
+    block = pl.program_id(0)
     factor = HD**-0.5 * LOG2E
-    beside(programs, others, other_outs, scratch, steps)
+    step = pl.program_id(0) * pl.num_programs(1) + pl.program_id(1)
+    finish = beside(programs, others, other_outs, scratch, step, steps)
 
     @pl.when(pl.program_id(1) == 0)
     def _():
-        visible_bias(bias_ref, position_ref[pl.program_id(0)], chunks)
+        visible_bias(bias_ref, position_ref[block], chunks)
+        for chunk in range(chunks):
+            value_t_ref[chunk] = table_ref[1, slot_ref[block, chunk]].astype(F32).T.astype(BF16)
 
     query = query_ref[...]
     largest = None
     for chunk in range(chunks):
-        keys = key_ref[0, chunk * BLK : (chunk + 1) * BLK, :]
+        keys = table_ref[0, slot_ref[block, chunk]]
         score = rows_by_rows(keys, query) + bias_ref[chunk]
         score_ref[chunk] = score
         top = jnp.max(score.reshape(BLK // 8, 8, BLK), axis=0)
@@ -727,19 +759,19 @@
     for chunk in range(chunks):
         weight = jnp.exp2((score_ref[chunk] - largest) * factor)
         total = total + jnp.sum(weight.reshape(BLK // 8, 8, BLK), axis=0)
-        values = value_t_ref[0, :, chunk * BLK : (chunk + 1) * BLK]
-        mixed = mixed + jnp.dot(values, weight.astype(BF16), preferred_element_type=F32)
+        mixed = mixed + jnp.dot(
+            value_t_ref[chunk], weight.astype(BF16), preferred_element_type=F32
+        )
     total = jnp.sum(total, axis=0, keepdims=True)
     mixed_ref[...] = (mixed / total).T.astype(BF16)
     logsum_ref[0, 0] = largest * factor + jnp.log2(total)
-
-
-def attend(queries, keysets, positions, programs, arrays, number):
+    finish()
+
+
+def attend(queries, table, positions, key_slots, programs, arrays, number):
     rows, width = queries.shape
     blocks, heads = rows // BLK, width // HD
-    keys = keysets[:, :, :HD]
-    values_t = keysets[:, :, HD:].transpose(0, 2, 1)
-    count = keysets.shape[1]
+    count = (PBLK + 1) * BLK
     out = pl.pallas_call(
         functools.partial(attend_kernel, programs, blocks * heads),
         grid=(blocks, heads),
@@ -750,9 +782,9 @@
         + [one.out for one in programs],
         in_specs=[
             pl.BlockSpec(memory_space=pltpu.SMEM),
+            pl.BlockSpec(memory_space=pltpu.SMEM),
             pl.BlockSpec((BLK, HD), lambda b, h: (b, h)),
-            pl.BlockSpec((1, count, HD), lambda b, h: (b, 0, 0)),
-            pl.BlockSpec((1, HD, count), lambda b, h: (b, 0, 0)),
+            pl.BlockSpec(memory_space=pltpu.VMEM),
         ]
         + [one.in_spec for one in programs],
         out_specs=[
@@ -763,6 +795,7 @@
         scratch_shapes=[
             pltpu.VMEM((PBLK + 1, BLK, BLK), F32),
             pltpu.VMEM((PBLK + 1, BLK, BLK), F32),
+            pltpu.VMEM((PBLK + 1, HD, BLK), BF16),
         ]
         + [held for one in programs for held in one.scratch()],
         compiler_params=pltpu.CompilerParams(
@@ -773,27 +806,30 @@
             bytes_accessed=8 * rows * width,
             transcendentals=rows * heads * count,
         ),
-    )(positions, queries, keys, values_t, *arrays)
+    )(positions, key_slots, queries, table, *arrays)
     return out[0], out[1], out[2:]
 
 
 def attend_back_kernel(programs, steps, *refs):
     count = len(programs)
-    (position_ref, query_ref, grad_ref, mixed_ref, logsum_ref), refs = refs[:5], refs[5:]
-    (key_ref, key_t_ref, value_ref), refs = refs[:3], refs[3:]
+    (position_ref, slot_ref, query_ref, grad_ref, mixed_ref), refs = refs[:5], refs[5:]
+    (logsum_ref, table_ref), refs = refs[:2], refs[2:]
     others, refs = refs[:count], refs[count:]
     (grad_query_ref, set_ref), refs = refs[:2], refs[2:]
     other_outs, refs = refs[:count], refs[count:]
-    bias_ref, scratch = refs[0], refs[1:]
+    (bias_ref, key_t_ref), scratch = refs[:2], refs[2:]
     chunks = PBLK + 1
     scale = HD**-0.5
     block, head = pl.program_id(0), pl.program_id(1)
-    beside(programs, others, other_outs, scratch, steps)
+    step = pl.program_id(0) * pl.num_programs(1) + pl.program_id(1)
+    finish = beside(programs, others, other_outs, scratch, step, steps)
 
     @pl.when(head == 0)
     def _():
         visible_bias(bias_ref, position_ref[block], chunks)
         set_ref[...] = jnp.zeros_like(set_ref)
+        for chunk in range(chunks):
+            key_t_ref[chunk] = table_ref[0, slot_ref[block, chunk]].astype(F32).T.astype(BF16)
 
     query, grad = query_ref[...], grad_ref[...]
     inner = jnp.sum(grad.astype(F32) * mixed_ref[...].astype(F32), axis=1, keepdims=True)
@@ -802,14 +838,15 @@
     grad_query = jnp.zeros((HD, BLK), F32)
     for chunk in range(chunks):
         cut = slice(chunk * BLK, (chunk + 1) * BLK)
-        score = rows_by_rows(key_ref[0, cut, :], query)
+        slot = slot_ref[block, chunk]
+        score = rows_by_rows(table_ref[0, slot], query)
         weight = jnp.exp2(score * (scale * LOG2E) + bias_ref[chunk] - logsum)
-        grad_weight = rows_by_rows(value_ref[0, cut, :], grad)
+        grad_weight = rows_by_rows(table_ref[1, slot], grad)
         grad_score = (weight * (grad_weight - inner)).astype(BF16)
         set_ref[0, cut, :HD] += jnp.dot(grad_score, query, preferred_element_type=F32)
         set_ref[0, cut, HD:] += jnp.dot(weight.astype(BF16), grad, preferred_element_type=F32)
         grad_query = grad_query + jnp.dot(
-            key_t_ref[0, :, cut], grad_score, preferred_element_type=F32
+            key_t_ref[chunk], grad_score, preferred_element_type=F32
         )
     grad_query_ref[...] = (grad_query * scale).T.astype(BF16)
 
@@ -817,14 +854,16 @@
     def _():
         set_ref[0, :, :HD] = set_ref[0, :, :HD] * scale
 
-
-def attend_back(queries, grads, mixed, logsums, keysets, positions, programs, arrays, number):
+    finish()
+
+
+def attend_back(
+    queries, grads, mixed, logsums, table, positions, key_slots, programs, arrays, number
+):
     rows, width = queries.shape
     blocks, heads = rows // BLK, width // HD
-    keys, values = keysets[:, :, :HD], keysets[:, :, HD:]
-    count = keysets.shape[1]
+    count = (PBLK + 1) * BLK
     by_head = pl.BlockSpec((BLK, HD), lambda b, h: (b, h))
-    by_block = pl.BlockSpec((1, count, HD), lambda b, h: (b, 0, 0))
     out = pl.pallas_call(
         functools.partial(attend_back_kernel, programs, blocks * heads),
         grid=(blocks, heads),
@@ -835,18 +874,20 @@
         + [one.out for one in programs],
         in_specs=[
             pl.BlockSpec(memory_space=pltpu.SMEM),
+            pl.BlockSpec(memory_space=pltpu.SMEM),
             by_head,
             by_head,
             by_head,
             pl.BlockSpec((1, 1, 1, BLK), lambda b, h: (b, h, 0, 0)),
-            by_block,
-            pl.BlockSpec((1, HD, count), lambda b, h: (b, 0, 0)),
-            by_block,
+            pl.BlockSpec(memory_space=pltpu.VMEM),
         ]
         + [one.in_spec for one in programs],
         out_specs=[by_head, pl.BlockSpec((1, count, 2 * HD), lambda b, h: (b, 0, 0))]
         + [one.out_spec for one in programs],
-        scratch_shapes=[pltpu.VMEM((PBLK + 1, BLK, BLK), F32)]
+        scratch_shapes=[
+            pltpu.VMEM((PBLK + 1, BLK, BLK), F32),
+            pltpu.VMEM((PBLK + 1, HD, BLK), BF16),
+        ]
         + [held for one in programs for held in one.scratch()],
         compiler_params=pltpu.CompilerParams(
             collective_id=number, has_side_effects=True, vmem_limit_bytes=VMEM_BYTES
@@ -856,23 +897,20 @@
             bytes_accessed=16 * rows * width,
             transcendentals=rows * heads * count,
         ),
-    )(positions, queries, grads, mixed, logsums, keys, keys.transpose(0, 2, 1), values, *arrays)
+    )(positions, key_slots, queries, grads, mixed, logsums, table, *arrays)
     return out[0], out[1], out[2:]
 
 
 def by_slot_kernel(slot_ref, set_ref, out_ref, table_ref):
     blocks, chunks = slot_ref.shape
-    per_device = out_ref.shape[2] // BLK
 
     def clear(index, carry):
         table_ref[index] = jnp.zeros(table_ref.shape[1:], F32)
         return carry
 
     def give(index, carry):
-        holder, place = index // per_device, index % per_device
-        rows = pl.ds(pl.multiple_of(place * BLK, BLK), BLK)
-        out_ref[holder, 0, rows, :] = table_ref[index, :, :HD].astype(BF16)
-        out_ref[holder, 1, rows, :] = table_ref[index, :, HD:].astype(BF16)
+        out_ref[0, index] = table_ref[index, :, :HD].astype(BF16)
+        out_ref[1, index] = table_ref[index, :, HD:].astype(BF16)
         return carry
 
     lax.fori_loop(0, table_ref.shape[0], clear, 0)
@@ -884,10 +922,9 @@
 
 
 def by_slot(sets, key_slots, slot_count):
-    blocks = sets.shape[0]
     return pl.pallas_call(
         by_slot_kernel,
-        out_shape=jax.ShapeDtypeStruct((slot_count // blocks, 2, blocks * BLK, HD), BF16),
+        out_shape=jax.ShapeDtypeStruct((2, slot_count, BLK, HD), BF16),
         in_specs=[
             pl.BlockSpec(memory_space=pltpu.SMEM),
             pl.BlockSpec(memory_space=pltpu.VMEM),
@@ -896,6 +933,728 @@
         scratch_shapes=[pltpu.VMEM((slot_count, BLK, 2 * HD), F32)],
         compiler_params=pltpu.CompilerParams(vmem_limit_bytes=VMEM_BYTES),
     )(key_slots, sets)
+
+
+GELU_OUTER = 0.7978845608028654
+GELU_INNER = 0.044715
+
+
+def down_copies(piece_ref, rest_ref, down_own, sems):
+    first, rows = piece_ref.shape[2], down_own.shape[2]
+    return [
+        pltpu.make_async_copy(piece_ref, down_own.at[:, :, :first], sems.at[0]),
+        pltpu.make_async_copy(
+            rest_ref.at[:, :, : rows - first], down_own.at[:, :, first:], sems.at[1]
+        ),
+    ]
+
+
+def forward_kernel(
+    x_ref,
+    cotangent_ref,
+    piece_ref,
+    rest_ref,
+    shift_ref,
+    all_ref,
+    act_ref,
+    pre_ref,
+    part_ref,
+    bias_ref,
+    up_own,
+    down_own,
+    rows_own,
+    cotangent_own,
+    act_own,
+    pre_own,
+    part_own,
+    weight_sem,
+    load_sem,
+    store_sem,
+    own_sem,
+    send,
+    recv,
+):
+    me = here()
+    steps = (SIDE, FRONT, "tp")
+    half, width = x_ref.shape
+    hidden = rest_ref.shape[3]
+
+    def place(bits):
+        at = me
+        for k in (2, 1, 0):
+            if bits >> k & 1:
+                at = flip(at, steps[k])
+        return at
+
+    def block(bits):
+        return by_plane_slot(all_ref, place(bits))
+
+    def to_step(k, bits):
+        source = block(bits) if bits else x_ref
+        return remote(
+            source, block(bits), send.at[k, bits], recv.at[bits | 1 << k], flip(me, steps[k])
+        )
+
+    def arrived(bits):
+        remote(block(bits), block(bits), send.at[0, 0], recv.at[bits], me).wait_recv()
+
+    def loads(number):
+        slot, copies = number % 2, []
+        for side, bits in enumerate((number, number + 4)):
+            rows = pl.ds(side * half, half)
+            copies.append(
+                pltpu.make_async_copy(
+                    by_plane_slot(cotangent_ref, place(bits)),
+                    cotangent_own.at[slot, rows],
+                    load_sem.at[slot, 0, side],
+                )
+            )
+            copies.append(
+                pltpu.make_async_copy(
+                    block(bits) if bits else x_ref,
+                    rows_own.at[slot, rows],
+                    load_sem.at[slot, 1, side],
+                )
+            )
+        return copies
+
+    def stores(number, kind):
+        slot = number % 2
+        source, target = ((act_own, act_ref), (pre_own, pre_ref), (part_own, part_ref))[kind]
+        return [
+            pltpu.make_async_copy(
+                source.at[slot, pl.ds(side * half, half)],
+                by_plane_slot(target, place(bits)),
+                store_sem.at[slot, kind, side],
+            )
+            for side, bits in enumerate((number, number + 4))
+        ]
+
+    def products(number):
+        slot = number % 2
+        tile = 256
+
+        def one(index, carry):
+            cut = pl.ds(pl.multiple_of(index * tile, tile), tile)
+            down = down_own[:, :, :, cut].reshape(width, tile)
+            up = up_own[:, :, :, cut].reshape(width, tile)
+            grad_act = jnp.dot(cotangent_own[slot], down, preferred_element_type=F32)
+            value = jnp.dot(rows_own[slot], up, preferred_element_type=F32)
+            value = value + shift_ref[:, cut]
+            square = value * value
+            bend = jnp.tanh(GELU_OUTER * value * (1.0 + GELU_INNER * square))
+            act_own[slot, :, cut] = (0.5 * value * (1.0 + bend)).astype(BF16)
+            slope = 0.5 * (1.0 + bend) + 0.5 * GELU_OUTER * value * (1.0 - bend * bend) * (
+                1.0 + 3.0 * GELU_INNER * square
+            )
+            grad_pre = (grad_act * slope).astype(BF16)
+            pre_own[slot, :, cut] = grad_pre
+            bias_ref[:, cut] += jnp.sum(
+                grad_pre.astype(F32).reshape(2 * half // 8, 8, tile), axis=0
+            )
+            return carry
+
+        lax.fori_loop(0, hidden // tile, one, 0)
+
+    def back(number):
+        slot = number % 2
+        tile = up_own.shape[1] * up_own.shape[2]
+
+        def one(index, carry):
+            cut = pl.ds(pl.multiple_of(index * tile, tile), tile)
+            up = up_own[index].reshape(tile, hidden)
+            part_own[slot, :, cut] = rows_by_rows(pre_own[slot], up).astype(BF16)
+            return carry
+
+        lax.fori_loop(0, width // tile, one, 0)
+
+    def pass_on(bits, *ways):
+        arrived(bits)
+        for k in ways:
+            to_step(k, bits).start()
+
+    def second():
+        to_step(0, 0).wait_send()
+        to_step(1, 0).start()
+
+    between = [
+        second,
+        functools.partial(pass_on, 2, 2),
+        functools.partial(pass_on, 3, 2),
+        lambda: None,
+    ]
+    barrier = pltpu.get_barrier_semaphore()
+    for step in steps:
+        pl.semaphore_signal(barrier, inc=1, device_id=flip(me, step), device_id_type=MESH_ID)
+    pl.semaphore_wait(barrier, 3)
+    to_step(0, 0).start()
+    to_step(2, 0).start()
+    own = pltpu.make_async_copy(x_ref, block(0), own_sem)
+    own.start()
+    weights = down_copies(piece_ref, rest_ref, down_own, weight_sem)
+    weights.append(
+        pltpu.make_async_copy(
+            rest_ref.at[:, :, rest_ref.shape[2] - up_own.shape[2] :], up_own, weight_sem.at[2]
+        )
+    )
+    for one in weights:
+        one.start()
+    bias_ref[...] = jnp.zeros_like(bias_ref)
+    for number in range(4):
+        if number == 1:
+            pass_on(1, 1, 2)
+        arrived(4 + number)
+        copies = loads(number)
+        for one in copies:
+            one.start()
+        if number == 0:
+            for one in weights:
+                one.wait()
+        if number >= 2:
+            for kind in range(3):
+                for one in stores(number - 2, kind):
+                    one.wait()
+        for one in copies:
+            one.wait()
+        products(number)
+        between[number]()
+        for kind in range(2):
+            for one in stores(number, kind):
+                one.start()
+        back(number)
+        for one in stores(number, 2):
+            one.start()
+    for number in (2, 3):
+        for kind in range(3):
+            for one in stores(number, kind):
+                one.wait()
+    own.wait()
+    for k, bits in ((1, 0), (2, 0), (1, 1), (2, 1), (2, 2), (2, 3)):
+        to_step(k, bits).wait_send()
+
+
+def forward_products(rows, cotangent_all, piece, rest, shift, number):
+    half, width = rows.shape
+    lines, quarters, _, hidden = rest.shape
+    weights = (lines, quarters, width // (lines * quarters), hidden)
+    anywhere = pl.BlockSpec(memory_space=pl.ANY)
+    inside = pl.BlockSpec(memory_space=pltpu.VMEM)
+    lead = (2, 2, 2, half)
+    return pl.pallas_call(
+        forward_kernel,
+        out_shape=[
+            jax.ShapeDtypeStruct(lead + (width,), BF16),
+            jax.ShapeDtypeStruct(lead + (hidden,), BF16),
+            jax.ShapeDtypeStruct(lead + (hidden,), BF16),
+            jax.ShapeDtypeStruct(lead + (width,), BF16),
+            jax.ShapeDtypeStruct((8, hidden), F32),
+        ],
+        in_specs=[anywhere] * 4 + [inside],
+        out_specs=[anywhere] * 4 + [inside],
+        scratch_shapes=[
+            pltpu.VMEM(weights, BF16),
+            pltpu.VMEM(weights, BF16),
+            pltpu.VMEM((2, 2 * half, width), BF16),
+            pltpu.VMEM((2, 2 * half, width), BF16),
+            pltpu.VMEM((2, 2 * half, hidden), BF16),
+            pltpu.VMEM((2, 2 * half, hidden), BF16),
+            pltpu.VMEM((2, 2 * half, width), BF16),
+            pltpu.SemaphoreType.DMA((3,)),
+            pltpu.SemaphoreType.DMA((2, 2, 2)),
+            pltpu.SemaphoreType.DMA((2, 3, 2)),
+            pltpu.SemaphoreType.DMA(()),
+            pltpu.SemaphoreType.DMA((3, 4)),
+            pltpu.SemaphoreType.DMA((8,)),
+        ],
+        compiler_params=pltpu.CompilerParams(
+            collective_id=number, has_side_effects=True, vmem_limit_bytes=VMEM_BYTES
+        ),
+        cost_estimate=pl.CostEstimate(
+            flops=48 * half * width * hidden,
+            bytes_accessed=32 * half * width * 3,
+            transcendentals=8 * half * hidden,
+        ),
+    )(rows, cotangent_all, piece, rest, shift)
+
+
+def grads_kernel(programs, steps, *refs):
+    count = len(programs)
+    (cotangent_ref, rows_ref, act_ref, pre_ref, piece_ref, rest_ref), refs = refs[:6], refs[6:]
+    others, refs = refs[:count], refs[count:]
+    (down_part_ref, weight_grad_ref), refs = refs[:2], refs[2:]
+    other_outs, refs = refs[:count], refs[count:]
+    (act_own, pre_own, down_own, load_sem), scratch = refs[:4], refs[4:]
+    step = pl.program_id(0)
+    finish = beside(programs, others, other_outs, scratch, step, steps)
+
+    @pl.when(step == 0)
+    def _():
+        copies = [
+            pltpu.make_async_copy(act_ref, act_own, load_sem.at[2]),
+            pltpu.make_async_copy(pre_ref, pre_own, load_sem.at[3]),
+        ] + down_copies(piece_ref, rest_ref, down_own, load_sem)
+        for one in copies:
+            one.start()
+        for one in copies:
+            one.wait()
+
+    def by_columns(left, right):
+        return lax.dot_general(left, right, (((0,), (0,)), ((), ())), preferred_element_type=F32)
+
+    tile = down_part_ref.shape[0]
+    rows = pl.ds(pl.multiple_of(step * tile, tile), tile)
+    shards, _, shard_rows, hidden = weight_grad_ref.shape
+    for kind, (left, right) in enumerate(((cotangent_ref, act_own), (rows_ref, pre_own))):
+        grad = by_columns(left[...], right[...]).astype(BF16)
+        weight_grad_ref[:, kind] = grad.reshape(shards, shard_rows, hidden)
+    down = down_own[...].reshape(down_part_ref.shape[1], hidden)
+    down_part_ref[...] = rows_by_rows(act_own[rows, :], down).astype(BF16)
+    finish()
+
+
+def grad_products(cotangent_all, rows_all, act, grad_pre, piece, rest, programs, arrays, number):
+    rows, width = cotangent_all.shape
+    hidden = act.shape[1]
+    lines, quarters = rest.shape[:2]
+    shards, shard_rows = lines * quarters, width // (lines * quarters)
+    steps = 8
+    columns = pl.BlockSpec((rows, width // steps), lambda i: (0, i))
+    anywhere = pl.BlockSpec(memory_space=pl.ANY)
+    grads = pl.BlockSpec((shards // steps, 2, shard_rows, hidden), lambda i: (i, 0, 0, 0))
+    out = pl.pallas_call(
+        functools.partial(grads_kernel, programs, steps),
+        grid=(steps,),
+        out_shape=[
+            jax.ShapeDtypeStruct((rows, width), BF16),
+            jax.ShapeDtypeStruct((shards, 2, shard_rows, hidden), BF16),
+        ]
+        + [one.out for one in programs],
+        in_specs=[columns, columns] + [anywhere] * 4 + [one.in_spec for one in programs],
+        out_specs=[pl.BlockSpec((rows // steps, width), lambda i: (i, 0)), grads]
+        + [one.out_spec for one in programs],
+        scratch_shapes=[
+            pltpu.VMEM((rows, hidden), BF16),
+            pltpu.VMEM((rows, hidden), BF16),
+            pltpu.VMEM((lines, quarters, shard_rows, hidden), BF16),
+            pltpu.SemaphoreType.DMA((4,)),
+        ]
+        + [held for one in programs for held in one.scratch()],
+        compiler_params=pltpu.CompilerParams(
+            collective_id=number, has_side_effects=True, vmem_limit_bytes=VMEM_BYTES
+        ),
+        cost_estimate=pl.CostEstimate(
+            flops=6 * rows * width * hidden,
+            bytes_accessed=8 * rows * width,
+            transcendentals=0,
+        ),
+    )(cotangent_all, rows_all, act, grad_pre, piece, rest, *arrays)
+    return out[0], out[1], out[2:]
+
+
+def reorder_kernel(cuts, size, x_ref, out_ref):
+    for index, cut in enumerate(cuts):
+        out_ref[:, index * size : (index + 1) * size] = x_ref[:, cut : cut + size]
+
+
+def reorder(values, cuts):
+    size = values.shape[1] // len(cuts)
+    if size % 128:
+        return jnp.concatenate([values[:, cut : cut + size] for cut in cuts], axis=1)
+    return pl.pallas_call(
+        functools.partial(reorder_kernel, cuts, size),
+        out_shape=jax.ShapeDtypeStruct(values.shape, values.dtype),
+        compiler_params=pltpu.CompilerParams(vmem_limit_bytes=VMEM_BYTES),
+    )(values)
+
+
+def to_line_order(values):
+    lines = lax.axis_size("line")
+    size = values.shape[1] // (2 * lines)
+    return reorder(
+        values, [(half * lines + shard) * size for shard in range(lines) for half in range(2)]
+    )
+
+
+def from_line_order(values):
+    lines = lax.axis_size("line")
+    size = values.shape[1] // (2 * lines)
+    return reorder(
+        values, [(shard * 2 + half) * size for half in range(2) for shard in range(lines)]
+    )
+
+
+def meet_sibling(me):
+    barrier = pltpu.get_barrier_semaphore()
+    pl.semaphore_signal(barrier, inc=1, device_id=flip(me, "tp"), device_id_type=MESH_ID)
+    pl.semaphore_wait(barrier, 1)
+
+
+def half_rows_of(core, rows):
+    return pl.ds(pl.multiple_of(core * rows, rows), rows)
+
+
+def each_rows(total, tile, work):
+    def one(index, carry):
+        work(pl.ds(pl.multiple_of(index * tile, tile), tile))
+        return carry
+
+    lax.fori_loop(0, total // tile, one, 0)
+
+
+def each_columns(total, tile, work):
+    each_rows(total, tile, work)
+
+
+def moments(values):
+    centered = values - jnp.mean(values, axis=1, keepdims=True)
+    spread = jnp.mean(centered * centered, axis=1, keepdims=True)
+    return centered, lax.rsqrt(spread + EPSILON)
+
+
+def norm_back(values, gain, grad):
+    centered, rstd = moments(values)
+    xhat = centered * rstd
+    scaled = grad * gain
+    inner = jnp.mean(scaled * xhat, axis=1, keepdims=True)
+    return xhat, rstd * (scaled - jnp.mean(scaled, axis=1, keepdims=True) - xhat * inner)
+
+
+def fold_rows(values):
+    return jnp.sum(values.reshape(values.shape[0] // 8, 8, values.shape[1]), axis=0)
+
+
+def shuffled(cuts, ref, rows):
+    if cuts is None:
+        return ref[rows, :]
+    size = ref.shape[1] // len(cuts)
+    return jnp.concatenate([ref[rows, cut : cut + size] for cut in cuts], axis=1)
+
+
+def project_kernel(
+    cuts,
+    mixed_ref,
+    proj_ref,
+    stream_ref,
+    bias_ref,
+    gain_ref,
+    shift_ref,
+    middle_ref,
+    normed_ref,
+    sent_ref,
+    got_ref,
+    sems,
+):
+    me = here()
+    half, width = middle_ref.shape
+    mine, other = half_rows_of(me["tp"], half), half_rows_of(1 - me["tp"], half)
+    tile = 512
+    meet_sibling(me)
+    copy = remote(sent_ref, got_ref, sems.at[0], sems.at[1], flip(me, "tp"))
+
+    def part(rows, target):
+        def work(cut):
+            target[:, cut] = rows_by_rows(mixed_ref[rows, :], proj_ref[cut, :])
+
+        each_columns(width, tile, work)
+
+    part(other, sent_ref)
+    copy.start()
+    part(mine, middle_ref)
+    copy.wait_recv()
+    bias, gain = bias_ref[...].astype(F32), gain_ref[...].astype(F32)
+    shift = shift_ref[...].astype(F32)
+    few = 32
+
+    def finish(rows):
+        start = pl.multiple_of(me["tp"] * half + rows.start, few)
+        stream = stream_ref[pl.ds(start, few), :].astype(F32)
+        middle = stream + (middle_ref[rows, :] + got_ref[rows, :] + bias)
+        middle_ref[rows, :] = middle
+        centered, rstd = moments(middle)
+        normed = (centered * rstd * gain + shift).astype(BF16)
+        if cuts is None:
+            normed_ref[rows, :] = normed
+            return
+        size = width // len(cuts)
+        for index, cut in enumerate(cuts):
+            normed_ref[rows, index * size : (index + 1) * size] = normed[:, cut : cut + size]
+
+    each_rows(half, few, finish)
+    copy.wait_send()
+
+
+def in_vmem(count):
+    return [pl.BlockSpec(memory_space=pltpu.VMEM)] * count
+
+
+def kernel_params(number):
+    return pltpu.CompilerParams(
+        collective_id=number, has_side_effects=True, vmem_limit_bytes=VMEM_BYTES
+    )
+
+
+def line_cuts(width, back):
+    lines = lax.axis_size("line")
+    size = width // (2 * lines)
+    if size % 128:
+        return None
+    if back:
+        return [(shard * 2 + half) * size for half in range(2) for shard in range(lines)]
+    return [(half * lines + shard) * size for shard in range(lines) for half in range(2)]
+
+
+def project(mixed, proj_all, stream, bias, gain, shift, number):
+    rows, width = stream.shape
+    half = rows // 2
+    cuts = line_cuts(width, False)
+    middle, normed = pl.pallas_call(
+        functools.partial(project_kernel, cuts),
+        out_shape=[
+            jax.ShapeDtypeStruct((half, width), F32),
+            jax.ShapeDtypeStruct((half, width), BF16),
+        ],
+        in_specs=in_vmem(6),
+        out_specs=in_vmem(2),
+        scratch_shapes=[
+            pltpu.VMEM((half, width), F32),
+            pltpu.VMEM((half, width), F32),
+            pltpu.SemaphoreType.DMA((2,)),
+        ],
+        compiler_params=kernel_params(number),
+        cost_estimate=pl.CostEstimate(
+            flops=2 * rows * width * mixed.shape[1], bytes_accessed=8 * rows * width, transcendentals=0
+        ),
+    )(mixed, proj_all, stream, bias[None], gain[None], shift[None])
+    return middle, normed if cuts else to_line_order(normed)
+
+
+def middle_back_kernel(
+    cuts,
+    sum_ref,
+    middle_ref,
+    cotangent_ref,
+    mixed_ref,
+    proj_ref,
+    gain_ref,
+    grad_middle_ref,
+    grad_mixed_ref,
+    proj_grad_ref,
+    sums_ref,
+    attn_ref,
+    sums_own,
+    sems,
+):
+    me = here()
+    half, width = middle_ref.shape
+    mine, other = half_rows_of(me["tp"], half), half_rows_of(1 - me["tp"], half)
+    few = 32
+    gain = gain_ref[...].astype(F32)
+    meet_sibling(me)
+    sums_own[...] = jnp.zeros_like(sums_own)
+
+    def norm(rows):
+        start = pl.multiple_of(me["tp"] * half + rows.start, few)
+        cotangent = cotangent_ref[pl.ds(start, few), :].astype(F32)
+        grad = shuffled(cuts, sum_ref, rows)
+        xhat, back = norm_back(middle_ref[rows, :], gain, grad)
+        grad_middle = cotangent + back
+        grad_middle_ref[rows, :] = grad_middle
+        attn = grad_middle.astype(BF16)
+        attn_ref[pl.ds(start, few), :] = attn
+        sums_own[0] += fold_rows(grad * xhat)
+        sums_own[1] += fold_rows(grad)
+        sums_own[2] += fold_rows(attn.astype(F32))
+        sums_own[3] += fold_rows(cotangent)
+
+    each_rows(half, few, norm)
+    copy = remote(attn_ref.at[mine], attn_ref.at[mine], sems.at[0], sems.at[1], flip(me, "tp"))
+    copy.start()
+
+    def to_heads(rows):
+        def work(cut):
+            grad = jnp.dot(attn_ref[rows, :], proj_ref[:, cut], preferred_element_type=F32)
+            grad_mixed_ref[rows, cut] = grad.astype(BF16)
+
+        each_columns(proj_ref.shape[1], 256, work)
+
+    to_heads(mine)
+    for kind in range(4):
+        sums_ref[kind : kind + 1, :] = jnp.sum(sums_own[kind], axis=0, keepdims=True)
+    sums_ref[4:8, :] = jnp.zeros((4, width), F32)
+    copy.wait_recv()
+    to_heads(other)
+
+    def weight(cut):
+        grad = lax.dot_general(
+            attn_ref[:, cut], mixed_ref[...], (((0,), (0,)), ((), ())), preferred_element_type=F32
+        )
+        proj_grad_ref[cut, :] = grad.astype(BF16)
+
+    each_columns(width, 256, weight)
+    copy.wait_send()
+
+
+def middle_back(grad_sum, middle, cotangent, mixed, proj_all, gain, number):
+    rows, width = cotangent.shape
+    half, heads = rows // 2, mixed.shape[1]
+    cuts = line_cuts(width, True)
+    return pl.pallas_call(
+        functools.partial(middle_back_kernel, cuts),
+        out_shape=[
+            jax.ShapeDtypeStruct((half, width), F32),
+            jax.ShapeDtypeStruct((rows, heads), BF16),
+            jax.ShapeDtypeStruct((width, heads), BF16),
+            jax.ShapeDtypeStruct((8, width), F32),
+        ],
+        in_specs=in_vmem(6),
+        out_specs=in_vmem(4),
+        scratch_shapes=[
+            pltpu.VMEM((rows, width), BF16),
+            pltpu.VMEM((4, 8, width), F32),
+            pltpu.SemaphoreType.DMA((2,)),
+        ],
+        compiler_params=kernel_params(number),
+        cost_estimate=pl.CostEstimate(
+            flops=4 * rows * width * heads, bytes_accessed=16 * rows * width, transcendentals=0
+        ),
+    )(grad_sum if cuts else from_line_order(grad_sum), middle, cotangent, mixed, proj_all, gain[None])
+
+
+def first_back_kernel(
+    cuts,
+    grad_query_ref,
+    grad_part_ref,
+    first_ref,
+    stream_ref,
+    normed_ref,
+    gain_ref,
+    grad_middle_ref,
+    mlp_ref,
+    middle_ref,
+    bias_ref,
+    input_ref,
+    layer_ref,
+    weight_ref,
+    sums_ref,
+    query_sums_ref,
+    part_sums_ref,
+    sent_ref,
+    got_ref,
+    grad_first_ref,
+    sums_own,
+    sems,
+):
+    me = here()
+    rows, width = stream_ref.shape
+    half, heads = rows // 2, grad_query_ref.shape[1]
+    mine, other = half_rows_of(me["tp"], half), half_rows_of(1 - me["tp"], half)
+    few = 32
+    sibling = flip(me, "tp")
+    meet_sibling(me)
+
+    grad_first_ref[:, :heads] = grad_query_ref[...]
+    grad_first_ref[:, heads:] = grad_part_ref[...].astype(BF16)
+
+    def part(at, target):
+        def work(cut):
+            target[:, cut] = rows_by_rows(grad_first_ref[at, :], first_ref[cut, :])
+
+        each_columns(width, 512, work)
+
+    part(other, sent_ref)
+    sums_copy = remote(sent_ref, got_ref, sems.at[0], sems.at[1], sibling)
+    sums_copy.start()
+    bias = bias_ref[...].astype(F32)
+
+    def layer(at):
+        start = pl.multiple_of(me["tp"] * half + at.start, few)
+        out = middle_ref[at, :] + (shuffled(cuts, mlp_ref, at) + bias)
+        layer_ref[pl.ds(start, few), :] = out.astype(BF16)
+
+    each_rows(half, few, layer)
+    layer_copy = remote(layer_ref.at[mine], layer_ref.at[mine], sems.at[2], sems.at[3], sibling)
+    layer_copy.start()
+    part(mine, grad_own := sums_own.at[0])
+    sums_copy.wait_recv()
+    gain = gain_ref[...].astype(F32)
+    folded = sums_own.at[1]
+    folded[0:16, :] = jnp.zeros((16, width), F32)
+
+    def norm(at):
+        start = pl.multiple_of(me["tp"] * half + at.start, few)
+        grad = grad_own[at, :] + got_ref[at, :]
+        xhat, back = norm_back(stream_ref[pl.ds(start, few), :].astype(F32), gain, grad)
+        input_ref[pl.ds(start, few), :] = (grad_middle_ref[at, :] + back).astype(BF16)
+        folded[0:8, :] += fold_rows(grad * xhat)
+        folded[8:16, :] += fold_rows(grad)
+
+    each_rows(half, few, norm)
+    input_copy = remote(input_ref.at[mine], input_ref.at[mine], sems.at[4], sems.at[5], sibling)
+    input_copy.start()
+    sums_ref[0:1, :] = jnp.sum(folded[0:8, :], axis=0, keepdims=True)
+    sums_ref[1:2, :] = jnp.sum(folded[8:16, :], axis=0, keepdims=True)
+    sums_ref[2:8, :] = jnp.zeros((6, width), F32)
+
+    def weight(cut):
+        grad = lax.dot_general(
+            normed_ref[:, cut],
+            grad_first_ref[:, heads:],
+            (((0,), (0,)), ((), ())),
+            preferred_element_type=F32,
+        )
+        weight_ref[cut, :] = grad.astype(BF16)
+
+    each_columns(width, 512, weight)
+    query_sums_ref[...] = fold_rows(grad_query_ref[...].astype(F32))
+    part_sums_ref[...] = fold_rows(grad_first_ref[:, heads:].astype(F32))
+    layer_copy.wait()
+    input_copy.wait()
+    sums_copy.wait_send()
+
+
+def first_back(
+    grad_query, grad_part, first_all, stream, normed, gain, grad_middle, mlp_sum, middle, bias, number
+):
+    rows, width = stream.shape
+    half, heads, part = rows // 2, grad_query.shape[1], grad_part.shape[1]
+    cuts = line_cuts(width, True)
+    return pl.pallas_call(
+        functools.partial(first_back_kernel, cuts),
+        out_shape=[
+            jax.ShapeDtypeStruct((rows, width), BF16),
+            jax.ShapeDtypeStruct((rows, width), BF16),
+            jax.ShapeDtypeStruct((width, part), BF16),
+            jax.ShapeDtypeStruct((8, width), F32),
+            jax.ShapeDtypeStruct((8, heads), F32),
+            jax.ShapeDtypeStruct((8, part), F32),
+        ],
+        in_specs=in_vmem(10),
+        out_specs=in_vmem(6),
+        scratch_shapes=[
+            pltpu.VMEM((half, width), F32),
+            pltpu.VMEM((half, width), F32),
+            pltpu.VMEM((rows, heads + part), BF16),
+            pltpu.VMEM((2, half, width), F32),
+            pltpu.SemaphoreType.DMA((6,)),
+        ],
+        compiler_params=kernel_params(number),
+        cost_estimate=pl.CostEstimate(
+            flops=2 * rows * width * (heads + 2 * part),
+            bytes_accessed=24 * rows * width,
+            transcendentals=0,
+        ),
+    )(
+        grad_query,
+        grad_part,
+        first_all,
+        stream,
+        normed,
+        gain[None],
+        grad_middle,
+        mlp_sum if cuts else from_line_order(mlp_sum),
+        middle,
+        bias[None],
+    )
 
 
 def body(
@@ -933,24 +1692,13 @@
     def own_half(values):
         return lax.dynamic_slice_in_dim(values, core * half_rows, half_rows, axis=0)
 
-    def other_half(values):
-        return lax.dynamic_slice_in_dim(values, (1 - core) * half_rows, half_rows, axis=0)
-
     def in_order(mine, other, axis=0):
         first = jnp.where(core == 0, mine, other)
         second = jnp.where(core == 0, other, mine)
         return jnp.concatenate([first, second], axis=axis)
 
-    def sum_halves(values):
-        return own_half(values) + swap_tp(other_half(values))
-
-    def join_halves(values):
-        return in_order(values, swap_tp(values))
-
     gain_one = attn_norm_gain.astype(F32)
     shift_one = attn_norm_bias.astype(F32)
-    gain_two = mlp_norm_gain.astype(F32)
-    shift_two = mlp_norm_bias.astype(F32)
 
     slot_ids = jnp.arange(slot_count, dtype=jnp.int32)
     ordering = block_order[0]
@@ -970,9 +1718,26 @@
 
     keyval_cut = lax.dynamic_slice_in_dim(keyval_weight, core * HD, HD, axis=1)
     first_cut = jnp.concatenate([query_weight, keyval_cut], axis=1)
-    down_cut, up_cut, first_all = run_programs(
-        [Exchange(down_weight, True), Exchange(up_weight, True), rows_gather(first_cut)],
-        [down_weight, up_weight, first_cut],
+    mlp_weights = jnp.concatenate([down_weight, up_weight], axis=0)
+    shard_rows = down_weight.shape[0]
+    first_rows = shard_rows // 2
+    first_line = line_gather(first_cut.shape, BF16)
+    first_like = jax.ShapeDtypeStruct(first_line.out.shape, BF16)
+    _, mlp_cut, proj_line, mlp_piece, first_all = run_programs(
+        [
+            placed(first_line, 0.0, 0.17),
+            placed(Exchange(mlp_weights, True), 0.0, 0.18),
+            placed(line_gather(proj_weight.shape, BF16), 0.06, 0.28),
+            placed(line_gather((quarters, first_rows, hidden_dev), BF16), 0.3, 0.5, 0.65, 0.8, 0.8, 1.0),
+            placed(columns_gather(first_like), 0.19, 0.4, 0.7, 1.0),
+        ],
+        [
+            first_cut,
+            mlp_weights,
+            proj_weight,
+            lambda outs: outs[1].at[:, :first_rows],
+            lambda outs: outs[0],
+        ],
         1,
     )
     first_all = flat(first_all)
@@ -987,60 +1752,50 @@
     query_low = first_low[:, :head_width]
     part_low = first_low[:, head_width:]
     keyval_every = gather_ctx(part_low, 4)
-    keyval_every, down_cut, up_cut = lax.optimization_barrier((keyval_every, down_cut, up_cut))
-    down_all = gather_line(down_cut)
-    up_all = gather_line(up_cut)
-    keyval_low = in_order(part_low, swap_tp(part_low), axis=1)
-    keyval_table = keyval_every.transpose(0, 1, 3, 2, 4).reshape(slot_count, BLK, 2 * HD)
-    own_table = keyval_low.reshape(blocks_dev, 1, BLK, 2 * HD)
-    keysets = jnp.concatenate([keyval_table[prompt_slots], own_table], axis=1)
-    keysets = keysets.reshape(blocks_dev, (PBLK + 1) * BLK, 2 * HD)
-    cotangent = own_half(out_cotangent)
-    cotangent_line = to_line_order(cotangent)
+    keyval_every, mlp_cut = lax.optimization_barrier((keyval_every, mlp_cut))
+    mlp_rest = lax.all_gather(mlp_cut[:, first_rows:], "line", axis=0, tiled=False)
+    table = keyval_every.reshape(2, slot_count, BLK, HD)
+    cotangent_line = to_line_order(own_half(out_cotangent))
     mixed_low, logsums, (proj_all, cotangent_all) = attend(
         query_low,
-        keysets,
+        table,
         positions,
-        [rows_gather(proj_weight), plane_gather(cotangent_line)],
-        [proj_weight, cotangent_line],
+        key_slots,
+        [
+            placed(columns_gather(proj_line), 0.0, 0.9, 1.0, 1.0),
+            placed(plane_gather(cotangent_line), 0.0, 0.9, 1.0, 1.0),
+        ],
+        [proj_line, cotangent_line],
         2,
     )
-    proj_all, cotangent_all = flat(proj_all), flat(cotangent_all)
-    proj_part = jnp.einsum("rk,ok->ro", mixed_low, proj_all, preferred_element_type=F32)
-    middle = own_half(stream) + sum_halves(proj_part) + proj_bias.astype(F32)
-
-    normed_two = layer_norm(middle, gain_two, shift_two).astype(BF16)
-    normed_two_line = to_line_order(normed_two)
-    normed_two_all = run_programs([plane_gather(normed_two_line)], [normed_two_line], 6)[0]
-    normed_two_all = flat(normed_two_all)
+    proj_all = flat(proj_all)
+    middle, normed_two_line = project(
+        mixed_low, proj_all, hidden_in, proj_bias, mlp_norm_gain, mlp_norm_bias, 5
+    )
+
     up_shift = lax.dynamic_slice_in_dim(up_bias, quarter * hidden_dev, hidden_dev).astype(F32)
-    grad_act = jnp.dot(cotangent_all, down_all, preferred_element_type=F32)
-    pre_act = jnp.dot(normed_two_all, up_all, preferred_element_type=F32) + up_shift
-    act, gelu_pull = jax.vjp(gelu_tanh, pre_act)
-    act_low = act.astype(BF16)
-    grad_pre_wide = gelu_pull(grad_act)[0]
-    grad_pre = grad_pre_wide.astype(BF16)
-    normed_two_part = jnp.einsum("rf,df->rd", grad_pre, up_all, preferred_element_type=F32)
-    plane_two, plane_parts = plane_sum(normed_two_part)
-    grad_normed_two = from_line_order(run_programs([plane_two], [plane_parts], 7)[0])
-    down_part = jnp.einsum("rf,of->ro", act_low, down_all, preferred_element_type=F32)
-    grad_up_bias = jnp.sum(grad_pre, axis=0, dtype=F32)
-    down_weight_grad = jnp.einsum("ro,rf->of", cotangent_all, act_low, preferred_element_type=F32)
-    up_weight_grad = jnp.einsum("rd,rf->df", normed_two_all, grad_pre, preferred_element_type=F32)
-    down_cut_grad = sum_line(down_weight_grad)
-    up_cut_grad = sum_line(up_weight_grad)
-
-    norm_two_pull = jax.vjp(layer_norm, middle, gain_two, shift_two)[1]
-    grad_mid_norm, grad_mlp_norm_gain, grad_mlp_norm_bias = norm_two_pull(grad_normed_two)
-    grad_middle = cotangent.astype(F32) + grad_mid_norm
-    grad_down_bias = jnp.sum(cotangent, axis=0, dtype=F32)
-
-    grad_attn_half = grad_middle.astype(BF16)
-    grad_proj_bias = jnp.sum(grad_attn_half, axis=0, dtype=F32)
-    grad_attn = join_halves(grad_attn_half)
-    proj_weight_grad = jnp.einsum("ro,rk->ok", grad_attn, mixed_low, preferred_element_type=F32)
-    grad_mixed = jnp.einsum("ro,ok->rk", grad_attn, proj_all, preferred_element_type=F32).astype(
-        BF16
+    normed_two_all, act_low, grad_pre, normed_two_part, up_bias_parts = forward_products(
+        normed_two_line, cotangent_all, mlp_piece, mlp_rest, up_shift[None], 6
+    )
+    plane_two, plane_parts = plane_sum(flat(normed_two_part))
+    placed(plane_two, 0.0, 0.13, 0.13, 0.13, 0.13, 0.38, 0.8, 1.0, 1.0)
+    down_part, mlp_weight_grad, (grad_normed_two,) = grad_products(
+        flat(cotangent_all),
+        flat(normed_two_all),
+        flat(act_low),
+        flat(grad_pre),
+        mlp_piece,
+        mlp_rest,
+        [plane_two],
+        [plane_parts],
+        7,
+    )
+    grad_up_bias = jnp.sum(up_bias_parts, axis=0)
+    mlp_cut_grad = lax.psum_scatter(mlp_weight_grad, "line", scatter_dimension=0, tiled=True)
+    mlp_cut_grad = mlp_cut_grad.reshape(quarters, 2 * shard_rows, hidden_dev)
+
+    grad_middle, grad_mixed, proj_weight_grad, middle_sums = middle_back(
+        grad_normed_two, middle, out_cotangent, mixed_low, proj_all, mlp_norm_gain, 8
     )
     sum_proj, proj_parts = rows_sum(proj_weight_grad)
     sum_down, down_parts = plane_sum(down_part)
@@ -1049,28 +1804,40 @@
         grad_mixed,
         mixed_low,
         logsums,
-        keysets,
+        table,
         positions,
-        [sum_proj, sum_down],
+        key_slots,
+        [
+            placed(sum_proj, 0.0, 0.13, 0.26, 0.38, 0.51, 0.63, 0.7, 0.9),
+            placed(sum_down, 0.0, 0.45, 0.45, 0.45, 0.45, 0.76, 0.95, 1.0, 1.0),
+        ],
         [proj_parts, down_parts],
         3,
     )
-    mlp_out = from_line_order(mlp_out) + down_bias.astype(F32)
-    layer_out = join_halves((middle + mlp_out).astype(BF16))
     grad_table = by_slot(grad_sets, key_slots, slot_count)
-    grad_query_bias = jnp.sum(grad_query, axis=0, dtype=F32)
     grad_parts = grad_table.reshape(
-        lax.axis_size("line"), lax.axis_size("pair"), 2, rows_dev, HD
-    )
-    grad_part = sum_ctx(grad_parts, 12).astype(BF16)
-    grad_value_bias = jnp.where(core == 1, jnp.sum(grad_part, axis=0, dtype=F32), 0.0)
-    grad_first = jnp.concatenate([grad_query, grad_part], axis=1)
-    normed_one_part = jnp.einsum("rk,dk->rd", grad_first, first_all, preferred_element_type=F32)
-    grad_normed_one = sum_halves(normed_one_part)
-    first_weight_grad = jnp.einsum("rd,rk->dk", normed_one, grad_first, preferred_element_type=F32)
-    norm_one_pull = jax.vjp(layer_norm, own_half(stream), gain_one, shift_one)[1]
-    grad_in_norm, grad_attn_norm_gain, grad_attn_norm_bias = norm_one_pull(grad_normed_one)
-    input_grad = join_halves((grad_middle + grad_in_norm).astype(BF16))
+        2, lax.axis_size("line"), lax.axis_size("pair"), rows_dev, HD
+    )
+    query_weight_grad = jnp.einsum("rd,rk->dk", normed_one, grad_query, preferred_element_type=F32)
+    sum_query, query_parts = rows_sum(query_weight_grad)
+    grad_part, grad_query_weight = run_programs(
+        [ctx_sum(grad_parts), sum_query], [grad_parts, query_parts], 12
+    )
+    input_grad, layer_out, part_weight_grad, first_sums, query_sums, part_sums = first_back(
+        grad_query,
+        grad_part,
+        first_all,
+        hidden_in,
+        normed_one,
+        attn_norm_gain,
+        grad_middle,
+        mlp_out,
+        middle,
+        down_bias,
+        9,
+    )
+    grad_query_bias = jnp.sum(query_sums, axis=0)
+    grad_value_bias = jnp.where(core == 1, jnp.sum(part_sums, axis=0), 0.0)
 
     query_slots = jnp.zeros((2 * head_width,), F32)
     query_slots = lax.dynamic_update_slice_in_dim(
@@ -1081,27 +1848,26 @@
         hidden_slots, grad_up_bias, (core * quarters + quarter) * hidden_dev, axis=0
     )
     pieces = [
-        grad_attn_norm_gain,
-        grad_attn_norm_bias,
-        grad_proj_bias,
-        grad_mlp_norm_gain,
-        grad_mlp_norm_bias,
-        grad_down_bias,
+        first_sums[0],
+        first_sums[1],
+        middle_sums[2],
+        middle_sums[0],
+        middle_sums[1],
+        middle_sums[3],
         grad_value_bias,
         query_slots,
         hidden_slots,
     ]
-    sum_first, first_parts = rows_sum(first_weight_grad)
+    sum_part, weight_parts = rows_sum(part_weight_grad, HD)
     total, padded = total_of(jnp.concatenate(pieces))
-    grad_first_weight, grad_down_weight, grad_up_weight, summed = run_programs(
-        [sum_first, Exchange(down_cut_grad, False), Exchange(up_cut_grad, False), total],
-        [first_parts, down_cut_grad, up_cut_grad, padded],
+    summed, grad_part_weight, mlp_grads = run_programs(
+        [placed(total, 0.0, 0.8), placed(sum_part, 0.1, 0.9), placed(Exchange(mlp_cut_grad, False), 0.3, 1.0)],
+        [padded, weight_parts, mlp_cut_grad],
         13,
     )
-    grad_down_weight, grad_up_weight = grad_down_weight.astype(F32), grad_up_weight.astype(F32)
-    grad_query_weight = grad_first_weight[:, :head_width]
-    grad_cut = grad_first_weight[:, head_width:]
-    grad_keyval_weight = in_order(grad_cut, swap_tp(grad_cut), axis=1)
+    grad_down_weight = mlp_grads[:shard_rows].astype(F32)
+    grad_up_weight = mlp_grads[shard_rows:].astype(F32)
+    grad_keyval_weight = in_order(grad_part_weight[:, :HD], grad_part_weight[:, HD:], axis=1)
     summed = summed.reshape(-1)
     cuts, start = [], 0
     for piece in pieces:

time: 726 us -> 651 us (0.90)
  Pallas kernels: 458 us -> 568 us
  matrix products: 118 us -> 10.3 us
  local copies, waits for them, and re-layouts: 66.1 us -> 20.2 us
  other arithmetic: 34.1 us -> 17 us
  starting transfers between devices: 17.2 us -> 0.25 us
    pallas_call x1 -> x7, Pallas kernels: 4.78 us -> 182 us  [the longest x1 59 us: forward_products(): pl.pallas_call(forward_kernel, out_shape=[jax.ShapeDtypeStruct(lead + (wi...]
    dot_general x11 -> x1, matrix products: 112 us -> 4.36 us  [body(): jnp.einsum('rd,rk->dk', normed_one, grad_query, preferred_element_type=F32)]
    pallas_call x6 -> x4, Pallas kernels: 275 us -> 230 us  [run_programs(): pl.pallas_call(kernel, out_shape=[one.out for one in programs], in_specs=...]
    unnamed x132 -> x61, local copies, waits for them, and re-layouts: 30.7 us -> 5.48 us
    pallas_call x1, Pallas kernels: 97.3 us -> 79.3 us  [attend_back(): pl.pallas_call(functools.partial(attend_back_kernel, programs, blocks * h...]
    ppermute x7 -> x0, starting transfers between devices: 16.2 us -> none  [swap_tp(): return lax.ppermute(values, 'tp', [(0, 1), (1, 0)])]
    transpose x3 -> x0, local copies, waits for them, and re-layouts: 8.83 us -> none  [the longest x1 5.07 us: body(): keyval_every.transpose(0, 1, 3, 2, 4).reshape(slot_count, BLK, 2 * HD)]
    all_gather x2 -> x1, waiting for transfers between devices: 10.1 us -> 14.8 us  [body(): lax.all_gather(mlp_cut[:, first_rows:], 'line', axis=0, tiled=False)]
  transfers between devices with their start and end apart: 11 -> 2, of which waited for: 2 -> 1; matrix products, arithmetic and copies ran while one was open for 22% -> 3% of each run, Pallas kernels for 41% -> 45%
where the time goes in v4:
time: 651 us; the launch traced here: 645 us
  Pallas kernels  568 us (87%)
  local copies, waits for them, and re-layouts  20.2 us (3%)
  other arithmetic  17 us (3%)
  between operations  14.9 us (2%)
  waiting for transfers between devices  14.8 us (2%)
  matrix products  10.3 us (2%)
    pallas_call x4, Pallas kernels, run_programs(): pl.pallas_call(kernel, out_shape=[one.out for one in programs], in_specs=...  230 us
    pallas_call x1, Pallas kernels, attend_back(): pl.pallas_call(functools.partial(attend_back_kernel, programs, blocks * h...  79.3 us
    pallas_call x1, Pallas kernels, attend(): pl.pallas_call(functools.partial(attend_kernel, programs, blocks * heads)...  76.4 us
    pallas_call x1, Pallas kernels, forward_products(): pl.pallas_call(forward_kernel, out_shape=[jax.ShapeDtypeStruct(lead + (wi...  59 us
    pallas_call x1, Pallas kernels, grad_products(): pl.pallas_call(functools.partial(grads_kernel, programs, steps), grid=(st...  57.1 us
    pallas_call x1, Pallas kernels, first_back(): pl.pallas_call(functools.partial(first_back_kernel, cuts), out_shape=[jax...  25.3 us
    pallas_call x1, Pallas kernels, middle_back(): pl.pallas_call(functools.partial(middle_back_kernel, cuts), out_shape=[ja...  19.6 us
    all_gather x1, waiting for transfers between devices, body(): lax.all_gather(mlp_cut[:, first_rows:], 'line', axis=0, tiled=False)  14.8 us
  transfers between devices with their start and end apart: 2, of which 1 were waited for; matrix products, arithmetic and copies ran while one was open for 3% of the time, Pallas kernels for 45%

profile of v4, /device:TPU:0, one launch (start us, length us, event | category | flops | bytes accessed | tf_op | source)
XLA Modules:
  0.0 645.3 jit_solution(6978799448036864108)
XLA Ops:
  7.3 0.8 convert_element_type.37
  8.1 2.0 convert_reduce_fusion
  11.7 2.7 pad_maximum_fusion.refs_1_
  14.4 93.5 %shard_map.288 = (bf16[4,128,1152]{2,1,0:T(8,128)(2,1)}, bf16[4,256,1024]{2,1,0:T(8,128)(2,1)}, bf16[4,128,1024]{2,1,0:T(8,128)(2,1)}, bf16[4,4,64,1024]{3,2,1,0:T(8,128)(2,1)}, bf16[2,4,2,128,1152]{4,3,2,1,0:T(8,128)(2,1)}) custom-call(bf16[128,1152]{1,0:T(8,128)(2,1)} %pad_maximum_fusion.1.refs_0_, bf16[256,4096]{1,0:T(8,128)(2,1)} %pad_maximum_fusion.refs_1_, ...), custom_call_target="tpu_custom_call" | custom-call | tf_op jit(solution)/shard_map/pallas_call | solution.py:613
  107.9 0.8 fusion.5.normed_ref
  108.8 6.0 fusion.6
  115.4 19.6 %shard_map.289 = bf16[2,4,2,512,128]{4,3,2,1,0:T(8,128)(2,1)} custom-call(bf16[512,128]{1,0:T(8,128)(2,1)} %slice.127.refs_0_), custom_call_target="tpu_custom_call" | custom-call | tf_op jit(solution)/shard_map/pallas_call | solution.py:613
  135.0 1.3 slice.95
  136.6 1.1 slice.126.refs_2_
  138.8 1.0 constant_dynamic-slice_fusion.x_ref
  139.9 2.3 shard_map.290.refs_5_
  144.7 1.3 dynamic-slice_convert_fusion
  146.5 76.4 %shard_map.291 = (bf16[512,1024]{1,0:T(8,128)(2,1)}, f32[2,8,1,256]{3,2,1,0:T(1,128)}, bf16[2,4,2,128,1024]{4,3,2,1,0:T(8,128)(2,1)}, bf16[2,2,2,256,2048]{4,3,2,1,0:T(8,128)(2,1)}) custom-call(s32[2]{0:T(128)} %and_select_fusion.2.refs_0_, s32[2,9]{1,0:T(2,128)} %pad_add_fusion.refs_1_.slot_ref, bf16[512,1024]{1,0:T(8,128)(2,1)} %slice.126.refs_2_, ...), custom_call_target="tpu_custom_call" | custom-call | flops 4831838208 | bytes 4194304 | tf_op jit(solution)/shard_map/pallas_call | solution.py:775
  222.9 13.3 %shard_map.292 = (f32[256,2048]{1,0:T(8,128)}, bf16[256,2048]{1,0:T(8,128)(2,1)}) custom-call(bf16[512,1024]{1,0:T(8,128)(2,1)} %get-tuple-element.60.mixed_ref.refs_4_, bf16[2048,1024]{1,0:T(8,128)(2,1)} %bitcast.76, bf16[512,2048]{1,0:T(8,128)(2,1)} %stream_ref.3, bf16[1,2048]{1,0:T(2,128)(2,1)} %broadcast_in_dim.59.bias_ref, ...), custom_call_target="tpu_custom_call" | custom-call | flops 2147483648 | bytes 8388608 | tf_op jit(solution)/shard_map/pallas_call | solution.py:1410
  236.2 14.8 %all-gather.3.cloned.1.call-done = bf16[16,192,1024]{2,1,0:T(8,128)(2,1)} async-done(((bf16[4,192,1024]{2,1,0:T(8,128)(2,1)}), bf16[16,192,1024]{2,1,0:T(8,128)(2,1)}) %all-gather.3.cloned.1.call-update) | async-done | bytes 6291472 | tf_op jit(solution)/shard_map/all_gather | solution.py:1756
  251.0 59.0 %shard_map.293 = (bf16[2,2,2,256,2048]{4,3,2,1,0:T(8,128)(2,1)}, bf16[2,2,2,256,1024]{4,3,2,1,0:T(8,128)(2,1)}, bf16[2,2,2,256,1024]{4,3,2,1,0:T(8,128)(2,1)}, b...) custom-call(bf16[256,2048]{1,0:T(8,128)(2,1)} %get-tuple-element.62.x_ref, ...), custom_call_target="tpu_custom_call" | custom-call | flops 25769803776 | bytes 50331648 | tf_op jit(solution)/shard_map/pallas_call | solution.py:1143
  310.0 57.1 %shard_map.294 = (bf16[2048,2048]{1,0:T(8,128)(2,1)}, bf16[16,2,128,1024]{3,2,1,0:T(8,128)(2,1)}, f32[256,2048]{1,0:T(8,128)}) custom-call(bf16[2048,2048]{1,0:T(8,128)(2,1)} %bitcast.74, bf16[2048,2048]{1,0:T(8,128)(2,1)} %bitcast.75, bf16[2048,1024]{1,0:T(8,128)(2,1)} %bitcast.79, bf16[2048,1024]{1,0:T(8,128)(2,1)} %bitcast.80, ...), custom_call_target="tpu_custom_call" | custom-call | flops 25769803776 | bytes 33554432 | tf_op jit(solution)/shard_map/pallas_call | solution.py:1224
  368.4 19.6 %shard_map.295 = (f32[256,2048]{1,0:T(8,128)}, bf16[512,1024]{1,0:T(8,128)(2,1)}, bf16[2048,1024]{1,0:T(8,128)(2,1)}, f32[8,2048]{1,0:T(8,128)}) custom-call(f32[256,2048]{1,0:T(8,128)} %get-tuple-element.69.sum_ref, f32[256,2048]{1,0:T(8,128)} %get-tuple-element.70.middle_ref, bf16[512,2048]{1,0:T(8,128)(2,1)} %cotangent_ref.1, ...), custom_call_target="tpu_custom_call" | custom-call | flops 4294967296 | bytes 16777216 | tf_op jit(solution)/shard_map/pallas_call | solution.py:1501
  388.0 79.3 %shard_map.296 = (bf16[512,1024]{1,0:T(8,128)(2,1)}, f32[2,2304,256]{2,1,0:T(8,128)}, f32[128,1024]{1,0:T(8,128)}, f32[256,2048]{1,0:T(8,128)}) custom-call(s32[2]{0:T(128)} %and_select_fusion.2.refs_0_, s32[2,9]{1,0:T(2,128)} %pad_add_fusion.refs_1_.slot_ref, bf16[512,1024]{1,0:T(8,128)(2,1)} %slice.126.refs_2_, ...), custom_call_target="tpu_custom_call" | custom-call | flops 12079595520 | bytes 8388608 | tf_op jit(solution)/shard_map/pallas_call | solution.py:867
  467.3 5.2 shard_map.297
  472.5 4.4 convolution_convert_fusion
  476.9 70.9 %shard_map.298 = (f32[512,128]{1,0:T(8,128)}, f32[128,1024]{1,0:T(8,128)}) custom-call(bf16[2,4,2,512,128]{4,3,2,1,0:T(8,128)(2,1)} %bitcast.55, bf16[2,4,2,128,1024]{4,3,2,1,0:T(8,128)(2,1)} %bitcast.58), custom_call_target="tpu_custom_call" | custom-call | tf_op jit(solution)/shard_map/pallas_call | solution.py:613
  547.8 25.3 %shard_map.299 = (bf16[512,2048]{1,0:T(8,128)(2,1)}, bf16[512,2048]{1,0:T(8,128)(2,1)}, bf16[2048,128]{1,0:T(8,128)(2,1)}, f32[8,2048]{1,0:T(8,128)}, f32[8,1024]{1,0:T(8,128)}, /*index=5*/f32[8,128]{1,0:T(8,128)}) custom-call(bf16[512,1024]{1,0:T(8,128)(2,1)} %get-tuple-element.75.grad_query_ref, f32[512,128]{1,0:T(8,128)} %get-tuple-element.77.grad_part_ref, ...), custom_call_target="tpu_custom_call" | custom-call | flops 2684354560 | bytes 25165824 | tf_op jit(solution)/shard_map/pallas_call | solution.py:1621
  575.2 0.9 fusion.10
  576.9 46.3 %shard_map.300 = (f32[184,128]{1,0:T(8,128)}, f32[128,256]{1,0:T(8,128)}, bf16[256,4096]{1,0:T(8,128)(2,1)}) custom-call(f32[184,128]{1,0:T(8,128)} %pad_bitcast_fusion.refs_0_, bf16[2,4,2,128,128]{4,3,2,1,0:T(8,128)(2,1)} %bitcast.62, bf16[4,256,1024]{2,1,0:T(8,128)(2,1)} %bitcast.61), custom_call_target="tpu_custom_call" | custom-call | tf_op jit(solution)/shard_map/pallas_call | solution.py:613
  623.2 1.4 slice_bitcast_fusion.1
  625.4 1.2 slice_bitcast_fusion.8
  626.6 4.2 slice_convert_fusion
  632.7 1.3 copy.47
  634.0 1.0 copy-done.5
  635.0 1.3 copy.48
  637.2 0.8 copy.50
  (104 shorter events, 14.2 us)
Async XLA Ops:
  7.2 3.7 copy-start
  7.2 3.0 copy-start.2
  7.2 243.8 %all-gather.3.cloned.1.call-start = ((), (), s32[]{:S(2)}) async-start(), calls=%async_computation.2 | async-start | bytes 7864320 | tf_op jit(solution)/shard_map/all_gather | solution.py:1756
  8.1 2.8 copy-start.16
  8.1 2.8 copy-start.18
  8.1 2.8 copy-start.13
  8.1 3.6 copy-start.9
  11.7 2.7 copy-start.24
  108.8 6.0 copy-start.3
  114.8 20.3 %copy-start.7 = (bf16[4,256,1024]{2,1,0:T(8,128)(2,1)S(1)}, bf16[4,256,1024]{2,1,0:T(8,128)(2,1)}, u32[]{:S(2)}) copy-start(bf16[4,256,1024]{2,1,0:T(8,128)(2,1)} %get-tuple-element.64) | copy-start | bytes 6291460
  136.3 1.4 copy-start.23
  136.3 2.5 copy-start.10
  136.3 440.6 %reduce-scatter.2.cloned.1.call-start = ((), (), s32[]{:S(2)}) async-start(), calls=%async_computation.1 | async-start | bytes 10485760 | tf_op jit(solution)/shard_map/reduce_scatter | solution.py:1794
  138.8 3.4 copy-start.19
  138.8 4.0 copy-start.20
  138.8 4.6 copy-start.21
  367.1 0.7 copy-start.22
  467.3 5.2 copy-start.4
  467.3 5.2 copy-start.8
  547.8 26.8 %copy-start.15 = (f32[8,1024]{1,0:T(8,128)S(1)}, f32[8,1024]{1,0:T(8,128)}, u32[]{:S(2)}) copy-start(f32[8,1024]{1,0:T(8,128)} %get-tuple-element.86) | copy-start | bytes 98308
  547.8 28.3 %copy-start.17 = (f32[8,2048]{1,0:T(8,128)S(1)}, f32[8,2048]{1,0:T(8,128)}, u32[]{:S(2)}) copy-start(f32[8,2048]{1,0:T(8,128)} %get-tuple-element.83) | copy-start | bytes 196612
  626.6 4.8 copy-start.14
  626.6 6.1 copy-start.6
  632.7 2.3 copy-start.5
  635.0 1.4 copy-start.12
  635.0 2.2 copy-start.11
  635.0 3.0 copy-start.1
Sparse Core Ops, SparseCore 0:
  136.5 114.4 all-gather.2
  367.2 168.0 reduce-scatter.1

commit v5 on v4

--- a/solution.py
+++ b/solution.py
@@ -19,15 +19,9 @@
 EVERY = ("fsdp", "line", "pair", "tp")
 
 
-def layer_norm(values, norm_gain, norm_shift):
-    average = jnp.mean(values, axis=-1, keepdims=True)
-    centered = values - average
-    spread = jnp.mean(centered * centered, axis=-1, keepdims=True)
-    return centered * lax.rsqrt(spread + EPSILON) * norm_gain + norm_shift
-
-
 MESH_ID = pl.DeviceIdType.MESH
 VMEM_BYTES = 60 * 1024 * 1024
+SMALL = pl.CostEstimate(flops=1, bytes_accessed=1, transcendentals=0)
 SIDE = ("pair", "fsdp")
 FRONT = ("fsdp", "pair")
 
@@ -174,14 +168,6 @@
                     me,
                 ).wait_recv()
                 send_on(bits, shard, block(bits, shard))
-
-        def tick(number):
-            if number < lines:
-                at_distance(number, line_arrival)
-            for level in range(count):
-                distance = number - 1 - level
-                if 0 <= distance < lines:
-                    at_distance(distance, functools.partial(level_arrival, level))
 
         def end():
             own.wait()
@@ -199,8 +185,14 @@
                     for k in range(top_bit(bits) + 1, count):
                         to_step(k, bits, shard, block(bits, shard)).wait_send()
 
-        ticks = [functools.partial(tick, number) for number in range(1, lines + count)]
-        return [begin] + ticks + [end]
+        line = [functools.partial(at_distance, number, line_arrival) for number in range(1, lines)]
+        levels = [
+            functools.partial(at_distance, number - level, functools.partial(level_arrival, level))
+            for number in range(lines + count - 1)
+            for level in range(count)
+            if 0 <= number - level < lines
+        ]
+        return [begin] + line + levels + [end]
 
 
 class Sum:
@@ -398,50 +390,35 @@
 
 
 class Exchange:
-    steps, lines, corner = ("pair", "fsdp"), 1, True
-
-    def __init__(self, values, spread):
-        self.spread = spread
-        if spread:
-            shape = (4, values.shape[0], values.shape[1] // 4)
-        else:
-            shape = (values.shape[1], values.shape[2] * 4)
-        self.out = jax.ShapeDtypeStruct(shape, values.dtype)
+    steps, lines = ("pair", "fsdp"), 1
+
+    def __init__(self, moves, shape, kind):
+        self.moves = moves
+        self.out = jax.ShapeDtypeStruct(shape, kind)
         self.in_spec = self.out_spec = pl.BlockSpec(memory_space=pl.ANY)
 
     def scratch(self):
+        count = len(self.moves)
         return [
-            pltpu.SemaphoreType.DMA(()),
-            pltpu.SemaphoreType.DMA((3,)),
-            pltpu.SemaphoreType.DMA((3,)),
+            pltpu.SemaphoreType.DMA((count,)),
+            pltpu.SemaphoreType.DMA((count, 3)),
+            pltpu.SemaphoreType.DMA((count, 3)),
         ]
 
-    def stages(self, me, x_ref, out_ref, own_sem, send, recv):
-        def wide(ref, quarter):
-            columns = ref.shape[1] // 4
-            return ref.at[:, pl.ds(pl.multiple_of(quarter * columns, columns), columns)]
-
-        def narrow(ref, quarter):
-            return ref.at[quarter]
-
-        cut, put = (wide, narrow) if self.spread else (narrow, wide)
+    def stages(self, me, x_refs, out_ref, own_sem, send, recv):
         copies = []
-        for k, names in reversed(list(enumerate(DIRECT))):
-            there = move(me, names)
+        for n, (source, target) in enumerate(self.moves):
+            there_ref = target(out_ref, quarter_of(me))
+            for k, names in reversed(list(enumerate(DIRECT))):
+                there = move(me, names)
+                copies.append(
+                    remote(
+                        source(x_refs, quarter_of(there)), there_ref, send.at[n, k], recv.at[n, k], there
+                    )
+                )
             copies.append(
-                remote(
-                    cut(x_ref, quarter_of(there)),
-                    put(out_ref, quarter_of(me)),
-                    send.at[k],
-                    recv.at[k],
-                    there,
-                )
+                pltpu.make_async_copy(source(x_refs, quarter_of(me)), there_ref, own_sem.at[n])
             )
-        copies.append(
-            pltpu.make_async_copy(
-                cut(x_ref, quarter_of(me)), put(out_ref, quarter_of(me)), own_sem
-            )
-        )
 
         def begin():
             for one in copies:
@@ -452,6 +429,53 @@
                 one.wait()
 
         return [begin, end]
+
+
+def half_quarter(ref, quarter, half, rows=None):
+    columns = ref.shape[1] // 8
+    cut = pl.ds(pl.multiple_of((quarter * 2 + half) * columns, columns), columns)
+    return ref.at[:, cut] if rows is None else ref.at[rows, cut]
+
+
+def spread_halves(pieces, columns, kind):
+    moves, start = [], 0
+    for index, rows, half in pieces:
+        count = rows.stop - rows.start
+        moves.append(
+            (
+                lambda refs, quarter, index=index, rows=rows, half=half: half_quarter(
+                    refs[index], quarter, half, rows
+                ),
+                lambda ref, quarter, start=start, count=count: ref.at[quarter, start : start + count],
+            )
+        )
+        start += count
+    return Exchange(moves, (4, start, columns // 8), kind)
+
+
+def join_halves(rows, columns, kind):
+    moves = [
+        (
+            lambda refs, quarter, half=half: refs[half].at[quarter],
+            lambda ref, quarter, half=half: half_quarter(ref, quarter, half),
+        )
+        for half in range(2)
+    ]
+    return Exchange(moves, (rows, columns), kind)
+
+
+class Work:
+    steps, lines = (), 1
+
+    def __init__(self, work, shape, kind):
+        self.work, self.out = work, jax.ShapeDtypeStruct(shape, kind)
+        self.in_spec = self.out_spec = pl.BlockSpec(memory_space=pltpu.VMEM)
+
+    def scratch(self):
+        return []
+
+    def stages(self, me, x_refs, out_ref):
+        return [functools.partial(self.work, me, x_refs, out_ref), lambda: None]
 
 
 class Total:
@@ -536,11 +560,12 @@
         )
 
 
-def greet(me, programs):
+def greet(me, programs, partners=()):
     barrier = pltpu.get_barrier_semaphore()
     lines = max(one.lines for one in programs)
-    steps = list(dict.fromkeys(step for one in programs for step in one.steps))
-    if SIDE in steps:
+    steps = list(dict.fromkeys([step for one in programs for step in one.steps] + list(partners)))
+    if SIDE in steps or FRONT in steps:
+        steps = [SIDE, FRONT] + [step for step in steps if step not in (SIDE, FRONT)]
         steps = [step for step in steps if step not in ("pair", "fsdp")]
     places = [flip(me, step) for step in steps]
     if any(isinstance(one, Exchange) for one in programs):
@@ -572,9 +597,9 @@
     return parts
 
 
-def schedule(programs, x_refs, out_refs, scratch):
+def schedule(programs, x_refs, out_refs, scratch, partners=()):
     me = here()
-    works = [(0.0, functools.partial(greet, me, programs))]
+    works = [(0.0, functools.partial(greet, me, programs, partners))]
     for one, x_ref, out_ref, held in zip(programs, x_refs, out_refs, split_scratch(programs, scratch)):
         stages = one.stages(me, x_ref, out_ref, *held)
         places = getattr(one, "places", (0.0, 1.0))
@@ -597,14 +622,16 @@
     return [start + (stop - start) * k / (count - 1) for k in range(count)]
 
 
-def run_programs(programs, arrays, number):
+def run_programs(programs, arrays, number, near=(), far=()):
     count = len(programs)
     given = [k for k, array in enumerate(arrays) if not callable(array)]
+    others = len(near) + len(far)
 
     def kernel(*refs):
-        in_refs, out_refs = refs[: len(given)], refs[len(given) : len(given) + count]
+        (more, refs) = refs[:others], refs[others:]
+        plain, out_refs = refs[: len(given)], refs[len(given) : len(given) + count]
         in_refs = [
-            array(out_refs) if callable(array) else in_refs[given.index(k)]
+            array(more, out_refs) if callable(array) else plain[given.index(k)]
             for k, array in enumerate(arrays)
         ]
         for _, work in schedule(programs, in_refs, out_refs, refs[len(given) + count :]):
@@ -613,13 +640,16 @@
     return pl.pallas_call(
         kernel,
         out_shape=[one.out for one in programs],
-        in_specs=[programs[k].in_spec for k in given],
+        in_specs=[pl.BlockSpec(memory_space=pltpu.VMEM)] * len(near)
+        + [pl.BlockSpec(memory_space=pl.ANY)] * len(far)
+        + [programs[k].in_spec for k in given],
         out_specs=[one.out_spec for one in programs],
         scratch_shapes=[held for one in programs for held in one.scratch()],
         compiler_params=pltpu.CompilerParams(
             collective_id=number, has_side_effects=True, vmem_limit_bytes=VMEM_BYTES
         ),
-    )(*[arrays[k] for k in given])
+        cost_estimate=SMALL,
+    )(*near, *far, *[arrays[k] for k in given])
 
 
 def by_rows_slot(ref, at):
@@ -673,22 +703,15 @@
     return values.reshape(-1, values.shape[-1])
 
 
-def gather_ctx(values, number):
+def ctx_gather(shape, kind):
     lines = lax.axis_size("line")
-    one = Gather(values, ("pair", "tp"), lines, (2, lines, 2) + values.shape, by_ctx_slot)
-    return run_programs([one], [values], number)[0]
+    like = jax.ShapeDtypeStruct(shape, kind)
+    return Gather(like, ("pair", "tp"), lines, (2, lines, 2) + shape, by_ctx_slot)
 
 
 def ctx_sum(values):
     _, lines, _, rows, columns = values.shape
     return Sum(("tp", "pair"), lines, rows, columns, by_ctx_slot)
-
-
-def total_of(values):
-    size = values.shape[0]
-    rows = -(-size // 1024) * 8
-    padded = jnp.pad(values, (0, rows * 128 - size)).reshape(rows, 128)
-    return Total(padded, lax.axis_size("line")), padded
 
 
 LOG2E = 1.4426950408889634
@@ -801,11 +824,7 @@
         compiler_params=pltpu.CompilerParams(
             collective_id=number, has_side_effects=True, vmem_limit_bytes=VMEM_BYTES
         ),
-        cost_estimate=pl.CostEstimate(
-            flops=4 * rows * width * count,
-            bytes_accessed=8 * rows * width,
-            transcendentals=rows * heads * count,
-        ),
+        cost_estimate=SMALL,
     )(positions, key_slots, queries, table, *arrays)
     return out[0], out[1], out[2:]
 
@@ -892,11 +911,7 @@
         compiler_params=pltpu.CompilerParams(
             collective_id=number, has_side_effects=True, vmem_limit_bytes=VMEM_BYTES
         ),
-        cost_estimate=pl.CostEstimate(
-            flops=10 * rows * width * count,
-            bytes_accessed=16 * rows * width,
-            transcendentals=rows * heads * count,
-        ),
+        cost_estimate=SMALL,
     )(positions, key_slots, queries, grads, mixed, logsums, table, *arrays)
     return out[0], out[1], out[2:]
 
@@ -932,6 +947,7 @@
         out_specs=pl.BlockSpec(memory_space=pltpu.VMEM),
         scratch_shapes=[pltpu.VMEM((slot_count, BLK, 2 * HD), F32)],
         compiler_params=pltpu.CompilerParams(vmem_limit_bytes=VMEM_BYTES),
+        cost_estimate=SMALL,
     )(key_slots, sets)
 
 
@@ -939,21 +955,47 @@
 GELU_INNER = 0.044715
 
 
-def down_copies(piece_ref, rest_ref, down_own, sems):
-    first, rows = piece_ref.shape[2], down_own.shape[2]
-    return [
-        pltpu.make_async_copy(piece_ref, down_own.at[:, :, :first], sems.at[0]),
-        pltpu.make_async_copy(
-            rest_ref.at[:, :, : rows - first], down_own.at[:, :, first:], sems.at[1]
-        ),
-    ]
+def weight_copies(parts, target, sems):
+    copies, start = [], 0
+    for number, (ref, rows) in enumerate(parts):
+        count = rows.stop - rows.start
+        copies.append(
+            pltpu.make_async_copy(
+                ref.at[:, :, rows], target.at[:, :, start : start + count], sems.at[number]
+            )
+        )
+        start += count
+    return copies
+
+
+def first_half(rows, first, refs):
+    piece, early = refs[0], refs[1]
+    down = [(piece, slice(0, first)), (early, slice(0, rows - first))]
+    return down, [(early, slice(rows - first, 2 * rows - first))]
+
+
+def second_half(rows, first, refs):
+    early, late = refs[1], refs[2]
+    start = 2 * rows - first
+    there = early.shape[2] - start
+    down = [(early, slice(start, start + there)), (late, slice(0, rows - there))]
+    return down, [(late, slice(rows - there, 2 * rows - there))]
+
+
+def gelu_both(value, grad_act):
+    square = value * value
+    bend = jnp.tanh(GELU_OUTER * value * (1.0 + GELU_INNER * square))
+    slope = 0.5 * (1.0 + bend) + 0.5 * GELU_OUTER * value * (1.0 - bend * bend) * (
+        1.0 + 3.0 * GELU_INNER * square
+    )
+    return 0.5 * value * (1.0 + bend), grad_act * slope
 
 
 def forward_kernel(
     x_ref,
     cotangent_ref,
     piece_ref,
-    rest_ref,
+    early_ref,
     shift_ref,
     all_ref,
     act_ref,
@@ -977,7 +1019,7 @@
     me = here()
     steps = (SIDE, FRONT, "tp")
     half, width = x_ref.shape
-    hidden = rest_ref.shape[3]
+    hidden = early_ref.shape[3]
 
     def place(bits):
         at = me
@@ -1041,13 +1083,9 @@
             grad_act = jnp.dot(cotangent_own[slot], down, preferred_element_type=F32)
             value = jnp.dot(rows_own[slot], up, preferred_element_type=F32)
             value = value + shift_ref[:, cut]
-            square = value * value
-            bend = jnp.tanh(GELU_OUTER * value * (1.0 + GELU_INNER * square))
-            act_own[slot, :, cut] = (0.5 * value * (1.0 + bend)).astype(BF16)
-            slope = 0.5 * (1.0 + bend) + 0.5 * GELU_OUTER * value * (1.0 - bend * bend) * (
-                1.0 + 3.0 * GELU_INNER * square
-            )
-            grad_pre = (grad_act * slope).astype(BF16)
+            act, grad_pre = gelu_both(value, grad_act)
+            act_own[slot, :, cut] = act.astype(BF16)
+            grad_pre = grad_pre.astype(BF16)
             pre_own[slot, :, cut] = grad_pre
             bias_ref[:, cut] += jnp.sum(
                 grad_pre.astype(F32).reshape(2 * half // 8, 8, tile), axis=0
@@ -1091,12 +1129,9 @@
     to_step(2, 0).start()
     own = pltpu.make_async_copy(x_ref, block(0), own_sem)
     own.start()
-    weights = down_copies(piece_ref, rest_ref, down_own, weight_sem)
-    weights.append(
-        pltpu.make_async_copy(
-            rest_ref.at[:, :, rest_ref.shape[2] - up_own.shape[2] :], up_own, weight_sem.at[2]
-        )
-    )
+    down_parts, up_parts = first_half(up_own.shape[2], piece_ref.shape[2], (piece_ref, early_ref))
+    weights = weight_copies(down_parts, down_own, weight_sem)
+    weights += weight_copies(up_parts, up_own, weight_sem.at[2:])
     for one in weights:
         one.start()
     bias_ref[...] = jnp.zeros_like(bias_ref)
@@ -1133,9 +1168,9 @@
         to_step(k, bits).wait_send()
 
 
-def forward_products(rows, cotangent_all, piece, rest, shift, number):
+def forward_products(rows, cotangent_all, piece, early, shift, number):
     half, width = rows.shape
-    lines, quarters, _, hidden = rest.shape
+    lines, quarters, _, hidden = early.shape
     weights = (lines, quarters, width // (lines * quarters), hidden)
     anywhere = pl.BlockSpec(memory_space=pl.ANY)
     inside = pl.BlockSpec(memory_space=pltpu.VMEM)
@@ -1169,53 +1204,170 @@
         compiler_params=pltpu.CompilerParams(
             collective_id=number, has_side_effects=True, vmem_limit_bytes=VMEM_BYTES
         ),
-        cost_estimate=pl.CostEstimate(
-            flops=48 * half * width * hidden,
-            bytes_accessed=32 * half * width * 3,
-            transcendentals=8 * half * hidden,
-        ),
-    )(rows, cotangent_all, piece, rest, shift)
+        cost_estimate=SMALL,
+    )(rows, cotangent_all, piece, early, shift)
+
+
+def second_kernel(
+    rows_ref,
+    cotangent_ref,
+    before_ref,
+    piece_ref,
+    early_ref,
+    late_ref,
+    shift_ref,
+    act_ref,
+    pre_ref,
+    part_ref,
+    bias_ref,
+    up_own,
+    down_own,
+    weight_sem,
+):
+    step = pl.program_id(0)
+    width, hidden = rows_ref.shape[1], act_ref.shape[1]
+
+    @pl.when(step == 0)
+    def _():
+        down_parts, up_parts = second_half(
+            up_own.shape[2], piece_ref.shape[2], (piece_ref, early_ref, late_ref)
+        )
+        weights = weight_copies(down_parts, down_own, weight_sem)
+        weights += weight_copies(up_parts, up_own, weight_sem.at[2:])
+        for one in weights:
+            one.start()
+        bias_ref[...] = jnp.zeros_like(bias_ref)
+        for one in weights:
+            one.wait()
+
+    tile = 256
+
+    def one(index, carry):
+        cut = pl.ds(pl.multiple_of(index * tile, tile), tile)
+        down = down_own[:, :, :, cut].reshape(width, tile)
+        up = up_own[:, :, :, cut].reshape(width, tile)
+        grad_act = jnp.dot(cotangent_ref[...], down, preferred_element_type=F32)
+        value = jnp.dot(rows_ref[...], up, preferred_element_type=F32) + shift_ref[:, cut]
+        act, grad_pre = gelu_both(value, grad_act)
+        act_ref[:, cut] = act.astype(BF16)
+        grad_pre = grad_pre.astype(BF16)
+        pre_ref[:, cut] = grad_pre
+        bias_ref[:, cut] += fold_rows(grad_pre.astype(F32))
+        return carry
+
+    lax.fori_loop(0, hidden // tile, one, 0)
+    tile_back = up_own.shape[1] * up_own.shape[2]
+
+    def back(index, carry):
+        cut = pl.ds(pl.multiple_of(index * tile_back, tile_back), tile_back)
+        up = up_own[index].reshape(tile_back, hidden)
+        part = before_ref[:, cut].astype(F32) + rows_by_rows(pre_ref[...], up)
+        part_ref[:, cut] = part.astype(BF16)
+        return carry
+
+    lax.fori_loop(0, width // tile_back, back, 0)
+
+
+def second_products(rows_all, cotangent_all, before, piece, early, late, shift):
+    rows, width = rows_all.shape
+    lines, quarters, _, hidden = late.shape
+    weights = (lines, quarters, width // (lines * quarters), hidden)
+    steps = 4
+    wide = pl.BlockSpec((rows // steps, width), lambda i: (i, 0))
+    narrow = pl.BlockSpec((rows // steps, hidden), lambda i: (i, 0))
+    anywhere = pl.BlockSpec(memory_space=pl.ANY)
+    return pl.pallas_call(
+        second_kernel,
+        grid=(steps,),
+        out_shape=[
+            jax.ShapeDtypeStruct((rows, hidden), BF16),
+            jax.ShapeDtypeStruct((rows, hidden), BF16),
+            jax.ShapeDtypeStruct((rows, width), BF16),
+            jax.ShapeDtypeStruct((8, hidden), F32),
+        ],
+        in_specs=[wide] * 3 + [anywhere] * 3 + [pl.BlockSpec((1, hidden), lambda i: (0, 0))],
+        out_specs=[narrow, narrow, wide, pl.BlockSpec((8, hidden), lambda i: (0, 0))],
+        scratch_shapes=[
+            pltpu.VMEM(weights, BF16),
+            pltpu.VMEM(weights, BF16),
+            pltpu.SemaphoreType.DMA((3,)),
+        ],
+        compiler_params=pltpu.CompilerParams(vmem_limit_bytes=VMEM_BYTES),
+        cost_estimate=SMALL,
+    )(rows_all, cotangent_all, before, piece, early, late, shift)
+
+
+def by_columns(left, right):
+    return lax.dot_general(left, right, (((0,), (0,)), ((), ())), preferred_element_type=F32)
+
+
+def weight_kernel(cotangent_ref, rows_ref, act_ref, pre_ref, out_ref):
+    shards, _, shard_rows, hidden = out_ref.shape
+    for kind, (left, right) in enumerate(((cotangent_ref, act_ref), (rows_ref, pre_ref))):
+        grad = by_columns(left[...], right[...]).astype(BF16)
+        out_ref[:, kind] = grad.reshape(shards, shard_rows, hidden)
+
+
+def weight_products(cotangent_all, rows_all, act, pre, shards):
+    rows, width = rows_all.shape
+    hidden, steps = act.shape[1], 8
+    columns = pl.BlockSpec((rows, width // steps), lambda i: (0, i))
+    whole = pl.BlockSpec((rows, hidden), lambda i: (0, 0))
+    return pl.pallas_call(
+        weight_kernel,
+        grid=(steps,),
+        out_shape=jax.ShapeDtypeStruct((shards, 2, width // shards, hidden), BF16),
+        in_specs=[columns, columns, whole, whole],
+        out_specs=pl.BlockSpec((shards // steps, 2, width // shards, hidden), lambda i: (i, 0, 0, 0)),
+        compiler_params=pltpu.CompilerParams(vmem_limit_bytes=VMEM_BYTES),
+        cost_estimate=SMALL,
+    )(cotangent_all, rows_all, act, pre)
 
 
 def grads_kernel(programs, steps, *refs):
     count = len(programs)
-    (cotangent_ref, rows_ref, act_ref, pre_ref, piece_ref, rest_ref), refs = refs[:6], refs[6:]
+    (cotangent_ref, rows_ref, act_a_ref, act_b_ref, pre_ref), refs = refs[:5], refs[5:]
+    (piece_ref, early_ref, late_ref), refs = refs[:3], refs[3:]
     others, refs = refs[:count], refs[count:]
     (down_part_ref, weight_grad_ref), refs = refs[:2], refs[2:]
     other_outs, refs = refs[:count], refs[count:]
-    (act_own, pre_own, down_own, load_sem), scratch = refs[:4], refs[4:]
+    (acts, pre_own, downs, load_sem, weight_sem), scratch = refs[:5], refs[5:]
     step = pl.program_id(0)
     finish = beside(programs, others, other_outs, scratch, step, steps)
 
     @pl.when(step == 0)
     def _():
+        rows, first = downs.shape[3], piece_ref.shape[2]
+        places = (piece_ref, early_ref, late_ref)
         copies = [
-            pltpu.make_async_copy(act_ref, act_own, load_sem.at[2]),
-            pltpu.make_async_copy(pre_ref, pre_own, load_sem.at[3]),
-        ] + down_copies(piece_ref, rest_ref, down_own, load_sem)
+            pltpu.make_async_copy(act_a_ref, acts.at[0], load_sem.at[0]),
+            pltpu.make_async_copy(act_b_ref, acts.at[1], load_sem.at[1]),
+            pltpu.make_async_copy(pre_ref, pre_own, load_sem.at[2]),
+        ]
+        copies += weight_copies(first_half(rows, first, places)[0], downs.at[0], weight_sem.at[0])
+        copies += weight_copies(second_half(rows, first, places)[0], downs.at[1], weight_sem.at[1])
         for one in copies:
             one.start()
         for one in copies:
             one.wait()
 
-    def by_columns(left, right):
-        return lax.dot_general(left, right, (((0,), (0,)), ((), ())), preferred_element_type=F32)
-
-    tile = down_part_ref.shape[0]
+    tile, width = down_part_ref.shape
     rows = pl.ds(pl.multiple_of(step * tile, tile), tile)
     shards, _, shard_rows, hidden = weight_grad_ref.shape
-    for kind, (left, right) in enumerate(((cotangent_ref, act_own), (rows_ref, pre_own))):
+    for kind, (left, right) in enumerate(((cotangent_ref, acts.at[1]), (rows_ref, pre_own))):
         grad = by_columns(left[...], right[...]).astype(BF16)
         weight_grad_ref[:, kind] = grad.reshape(shards, shard_rows, hidden)
-    down = down_own[...].reshape(down_part_ref.shape[1], hidden)
-    down_part_ref[...] = rows_by_rows(act_own[rows, :], down).astype(BF16)
+    part = rows_by_rows(acts[0, rows, :], downs[0].reshape(width, hidden))
+    part = part + rows_by_rows(acts[1, rows, :], downs[1].reshape(width, hidden))
+    down_part_ref[...] = part.astype(BF16)
     finish()
 
 
-def grad_products(cotangent_all, rows_all, act, grad_pre, piece, rest, programs, arrays, number):
-    rows, width = cotangent_all.shape
-    hidden = act.shape[1]
-    lines, quarters = rest.shape[:2]
+def grad_products(
+    cotangent_all, rows_all, act_a, act_b, pre, piece, early, late, programs, arrays, number
+):
+    rows, width = rows_all.shape
+    lines, quarters, _, hidden = late.shape
     shards, shard_rows = lines * quarters, width // (lines * quarters)
     steps = 8
     columns = pl.BlockSpec((rows, width // steps), lambda i: (0, i))
@@ -1229,25 +1381,22 @@
             jax.ShapeDtypeStruct((shards, 2, shard_rows, hidden), BF16),
         ]
         + [one.out for one in programs],
-        in_specs=[columns, columns] + [anywhere] * 4 + [one.in_spec for one in programs],
+        in_specs=[columns, columns] + [anywhere] * 6 + [one.in_spec for one in programs],
         out_specs=[pl.BlockSpec((rows // steps, width), lambda i: (i, 0)), grads]
         + [one.out_spec for one in programs],
         scratch_shapes=[
+            pltpu.VMEM((2, rows, hidden), BF16),
             pltpu.VMEM((rows, hidden), BF16),
-            pltpu.VMEM((rows, hidden), BF16),
-            pltpu.VMEM((lines, quarters, shard_rows, hidden), BF16),
-            pltpu.SemaphoreType.DMA((4,)),
+            pltpu.VMEM((2, lines, quarters, shard_rows, hidden), BF16),
+            pltpu.SemaphoreType.DMA((3,)),
+            pltpu.SemaphoreType.DMA((2, 2)),
         ]
         + [held for one in programs for held in one.scratch()],
         compiler_params=pltpu.CompilerParams(
             collective_id=number, has_side_effects=True, vmem_limit_bytes=VMEM_BYTES
         ),
-        cost_estimate=pl.CostEstimate(
-            flops=6 * rows * width * hidden,
-            bytes_accessed=8 * rows * width,
-            transcendentals=0,
-        ),
-    )(cotangent_all, rows_all, act, grad_pre, piece, rest, *arrays)
+        cost_estimate=SMALL,
+    )(cotangent_all, rows_all, act_a, act_b, pre, piece, early, late, *arrays)
     return out[0], out[1], out[2:]
 
 
@@ -1264,6 +1413,7 @@
         functools.partial(reorder_kernel, cuts, size),
         out_shape=jax.ShapeDtypeStruct(values.shape, values.dtype),
         compiler_params=pltpu.CompilerParams(vmem_limit_bytes=VMEM_BYTES),
+        cost_estimate=SMALL,
     )(values)
 
 
@@ -1328,6 +1478,48 @@
         return ref[rows, :]
     size = ref.shape[1] // len(cuts)
     return jnp.concatenate([ref[rows, cut : cut + size] for cut in cuts], axis=1)
+
+
+def norm_work(me, refs, out_ref):
+    stream_ref, gain_ref, shift_ref = refs
+    gain, shift = gain_ref[...].astype(F32), shift_ref[...].astype(F32)
+
+    def work(rows):
+        centered, rstd = moments(stream_ref[rows, :].astype(F32))
+        out_ref[rows, :] = (centered * rstd * gain + shift).astype(BF16)
+
+    each_rows(out_ref.shape[0], 32, work)
+
+
+def reorder_work(cuts, me, x_ref, out_ref):
+    half, size = out_ref.shape[0], out_ref.shape[1] // len(cuts)
+    few = 64
+
+    def work(rows):
+        start = pl.multiple_of(me["tp"] * half + rows.start, few)
+        for index, cut in enumerate(cuts):
+            out_ref[rows, index * size : (index + 1) * size] = x_ref[
+                pl.ds(start, few), cut : cut + size
+            ]
+
+    each_rows(half, few, work)
+
+
+def part_work(me, refs, out_ref):
+    normed_ref, weight_ref, shift_ref = refs
+    heads = weight_ref.shape[1] - out_ref.shape[1]
+    part = jnp.dot(normed_ref[...], weight_ref[:, heads:], preferred_element_type=F32)
+    out_ref[...] = (part + shift_ref[:, heads:]).astype(BF16)
+
+
+def query_work(me, refs, out_ref):
+    normed_ref, weight_ref, shift_ref = refs
+
+    def work(cut):
+        query = jnp.dot(normed_ref[...], weight_ref[:, cut], preferred_element_type=F32)
+        out_ref[:, cut] = (query + shift_ref[:, cut]).astype(BF16)
+
+    each_columns(out_ref.shape[1], 256, work)
 
 
 def project_kernel(
@@ -1421,9 +1613,7 @@
             pltpu.SemaphoreType.DMA((2,)),
         ],
         compiler_params=kernel_params(number),
-        cost_estimate=pl.CostEstimate(
-            flops=2 * rows * width * mixed.shape[1], bytes_accessed=8 * rows * width, transcendentals=0
-        ),
+        cost_estimate=SMALL,
     )(mixed, proj_all, stream, bias[None], gain[None], shift[None])
     return middle, normed if cuts else to_line_order(normed)
 
@@ -1514,86 +1704,56 @@
             pltpu.SemaphoreType.DMA((2,)),
         ],
         compiler_params=kernel_params(number),
-        cost_estimate=pl.CostEstimate(
-            flops=4 * rows * width * heads, bytes_accessed=16 * rows * width, transcendentals=0
-        ),
+        cost_estimate=SMALL,
     )(grad_sum if cuts else from_line_order(grad_sum), middle, cotangent, mixed, proj_all, gain[None])
 
 
-def first_back_kernel(
-    cuts,
-    grad_query_ref,
-    grad_part_ref,
-    first_ref,
-    stream_ref,
-    normed_ref,
-    gain_ref,
-    grad_middle_ref,
-    mlp_ref,
-    middle_ref,
-    bias_ref,
-    input_ref,
-    layer_ref,
-    weight_ref,
-    sums_ref,
-    query_sums_ref,
-    part_sums_ref,
-    sent_ref,
-    got_ref,
-    grad_first_ref,
-    sums_own,
-    sems,
-):
+def first_back_kernel(cuts, programs, *refs):
+    (
+        grad_query_ref,
+        grad_part_ref,
+        first_ref,
+        stream_ref,
+        normed_ref,
+        gain_ref,
+        grad_middle_ref,
+        mlp_ref,
+        middle_ref,
+        bias_ref,
+        middle_sums_ref,
+        hidden_sums_ref,
+        cut_a_ref,
+        cut_b_ref,
+    ), refs = refs[:14], refs[14:]
+    (input_ref, layer_ref, down_out, up_out, part_out, total_out), refs = refs[:6], refs[6:]
+    (weight_ref, vector_ref, sent_ref, got_ref, grad_first_ref, held_ref, sems), scratch = refs[:7], refs[7:]
     me = here()
     rows, width = stream_ref.shape
     half, heads = rows // 2, grad_query_ref.shape[1]
+    shard_rows = part_out.shape[0]
     mine, other = half_rows_of(me["tp"], half), half_rows_of(1 - me["tp"], half)
     few = 32
     sibling = flip(me, "tp")
-    meet_sibling(me)
-
+    works = schedule(
+        programs,
+        (
+            (cut_a_ref.at[:, :shard_rows], cut_b_ref.at[:, :shard_rows]),
+            (cut_a_ref.at[:, shard_rows:], cut_b_ref.at[:, shard_rows:]),
+            weight_ref.reshape(2, -1, 2, shard_rows, weight_ref.shape[1]),
+            vector_ref,
+        ),
+        (down_out, up_out, part_out, total_out),
+        scratch,
+        ("tp",),
+    )
+
+    def run_until(stop):
+        while works and works[0][0] < stop:
+            works.pop(0)[1]()
+
+    run_until(0.1)
     grad_first_ref[:, :heads] = grad_query_ref[...]
     grad_first_ref[:, heads:] = grad_part_ref[...].astype(BF16)
-
-    def part(at, target):
-        def work(cut):
-            target[:, cut] = rows_by_rows(grad_first_ref[at, :], first_ref[cut, :])
-
-        each_columns(width, 512, work)
-
-    part(other, sent_ref)
-    sums_copy = remote(sent_ref, got_ref, sems.at[0], sems.at[1], sibling)
-    sums_copy.start()
-    bias = bias_ref[...].astype(F32)
-
-    def layer(at):
-        start = pl.multiple_of(me["tp"] * half + at.start, few)
-        out = middle_ref[at, :] + (shuffled(cuts, mlp_ref, at) + bias)
-        layer_ref[pl.ds(start, few), :] = out.astype(BF16)
-
-    each_rows(half, few, layer)
-    layer_copy = remote(layer_ref.at[mine], layer_ref.at[mine], sems.at[2], sems.at[3], sibling)
-    layer_copy.start()
-    part(mine, grad_own := sums_own.at[0])
-    sums_copy.wait_recv()
-    gain = gain_ref[...].astype(F32)
-    folded = sums_own.at[1]
-    folded[0:16, :] = jnp.zeros((16, width), F32)
-
-    def norm(at):
-        start = pl.multiple_of(me["tp"] * half + at.start, few)
-        grad = grad_own[at, :] + got_ref[at, :]
-        xhat, back = norm_back(stream_ref[pl.ds(start, few), :].astype(F32), gain, grad)
-        input_ref[pl.ds(start, few), :] = (grad_middle_ref[at, :] + back).astype(BF16)
-        folded[0:8, :] += fold_rows(grad * xhat)
-        folded[8:16, :] += fold_rows(grad)
-
-    each_rows(half, few, norm)
-    input_copy = remote(input_ref.at[mine], input_ref.at[mine], sems.at[4], sems.at[5], sibling)
-    input_copy.start()
-    sums_ref[0:1, :] = jnp.sum(folded[0:8, :], axis=0, keepdims=True)
-    sums_ref[1:2, :] = jnp.sum(folded[8:16, :], axis=0, keepdims=True)
-    sums_ref[2:8, :] = jnp.zeros((6, width), F32)
 
     def weight(cut):
         grad = lax.dot_general(
@@ -1605,44 +1765,128 @@
         weight_ref[cut, :] = grad.astype(BF16)
 
     each_columns(width, 512, weight)
-    query_sums_ref[...] = fold_rows(grad_query_ref[...].astype(F32))
-    part_sums_ref[...] = fold_rows(grad_first_ref[:, heads:].astype(F32))
+    run_until(0.2)
+
+    def part(at, target):
+        def work(cut):
+            target[:, cut] = rows_by_rows(grad_first_ref[at, :], first_ref[cut, :])
+
+        each_columns(width, 512, work)
+
+    part(other, sent_ref)
+    sums_copy = remote(sent_ref, got_ref, sems.at[0], sems.at[1], sibling)
+    sums_copy.start()
+    run_until(0.3)
+    bias = bias_ref[...].astype(F32)
+
+    def layer(at):
+        start = pl.multiple_of(me["tp"] * half + at.start, few)
+        out = middle_ref[at, :] + (shuffled(cuts, mlp_ref, at) + bias)
+        layer_ref[pl.ds(start, few), :] = out.astype(BF16)
+
+    each_rows(half, few, layer)
+    layer_copy = remote(layer_ref.at[mine], layer_ref.at[mine], sems.at[2], sems.at[3], sibling)
+    layer_copy.start()
+    run_until(0.4)
+    grad_own, folded = held_ref.at[0], held_ref.at[1]
+    part(mine, grad_own)
+    run_until(0.5)
+    sums_copy.wait_recv()
+    gain = gain_ref[...].astype(F32)
+    folded[0:16, :] = jnp.zeros((16, width), F32)
+
+    def norm(at):
+        start = pl.multiple_of(me["tp"] * half + at.start, few)
+        grad = grad_own[at, :] + got_ref[at, :]
+        xhat, back = norm_back(stream_ref[pl.ds(start, few), :].astype(F32), gain, grad)
+        input_ref[pl.ds(start, few), :] = (grad_middle_ref[at, :] + back).astype(BF16)
+        folded[0:8, :] += fold_rows(grad * xhat)
+        folded[8:16, :] += fold_rows(grad)
+
+    each_rows(half, few, norm)
+    input_copy = remote(input_ref.at[mine], input_ref.at[mine], sems.at[4], sems.at[5], sibling)
+    input_copy.start()
+    vector_ref[...] = jnp.zeros_like(vector_ref)
+    vector_ref[0:1, :width] = jnp.sum(folded[0:8, :], axis=0, keepdims=True)
+    vector_ref[0:1, width : 2 * width] = jnp.sum(folded[8:16, :], axis=0, keepdims=True)
+    for kind in range(4):
+        at = slice(kind % 2 * width, (kind % 2 + 1) * width)
+        vector_ref[1 + kind // 2 : 2 + kind // 2, at] = middle_sums_ref[kind : kind + 1, :]
+    query_sums = jnp.sum(fold_rows(grad_query_ref[...].astype(F32)), axis=0, keepdims=True)
+    part_sums = jnp.sum(
+        fold_rows(grad_first_ref[:, heads:].astype(F32)), axis=0, keepdims=True
+    )
+    hidden_sums = jnp.sum(hidden_sums_ref[...], axis=0, keepdims=True)
+    hidden, part_width = hidden_sums.shape[1], part_sums.shape[1]
+    for core in range(2):
+        own = me["tp"] == core
+        vector_ref[3:4, core * heads : (core + 1) * heads] = jnp.where(own, query_sums, 0.0)
+        for quarter in range(4):
+            here_too = own & (quarter_of(me) == quarter)
+            vector_ref[4 + core : 5 + core, quarter * hidden : (quarter + 1) * hidden] = jnp.where(
+                here_too, hidden_sums, 0.0
+            )
+    vector_ref[3:4, 2 * heads : 2 * heads + part_width] = jnp.where(me["tp"] == 1, part_sums, 0.0)
+    run_until(2.0)
     layer_copy.wait()
     input_copy.wait()
     sums_copy.wait_send()
 
 
 def first_back(
-    grad_query, grad_part, first_all, stream, normed, gain, grad_middle, mlp_sum, middle, bias, number
+    grad_query,
+    grad_part,
+    first_all,
+    stream,
+    normed,
+    gain,
+    grad_middle,
+    mlp_sum,
+    middle,
+    bias,
+    middle_sums,
+    hidden_sums,
+    cut_a,
+    cut_b,
+    number,
 ):
     rows, width = stream.shape
     half, heads, part = rows // 2, grad_query.shape[1], grad_part.shape[1]
+    lines, hidden = lax.axis_size("line"), hidden_sums.shape[1]
     cuts = line_cuts(width, True)
+    shard_rows = width // (4 * lines)
+    vector = (8, max(2 * width, 4 * hidden, 2 * heads + part))
+    programs = [
+        placed(join_halves(shard_rows, 8 * cut_a.shape[2], BF16), 0.0, 1.0),
+        placed(join_halves(shard_rows, 8 * cut_a.shape[2], BF16), 0.0, 1.0),
+        placed(
+            Sum((FRONT, SIDE), lines, shard_rows, part, by_rows_slot, part),
+            0.1, *spaced(0.9, 0.99, lines + 3),
+        ),
+        placed(Total(jax.ShapeDtypeStruct(vector, F32), lines), 0.9, 0.99),
+    ]
+    anywhere = [pl.BlockSpec(memory_space=pl.ANY)] * 2
     return pl.pallas_call(
-        functools.partial(first_back_kernel, cuts),
+        functools.partial(first_back_kernel, cuts, programs),
         out_shape=[
             jax.ShapeDtypeStruct((rows, width), BF16),
             jax.ShapeDtypeStruct((rows, width), BF16),
-            jax.ShapeDtypeStruct((width, part), BF16),
-            jax.ShapeDtypeStruct((8, width), F32),
-            jax.ShapeDtypeStruct((8, heads), F32),
-            jax.ShapeDtypeStruct((8, part), F32),
-        ],
-        in_specs=in_vmem(10),
-        out_specs=in_vmem(6),
+        ]
+        + [one.out for one in programs],
+        in_specs=in_vmem(12) + anywhere,
+        out_specs=in_vmem(2) + [one.out_spec for one in programs],
         scratch_shapes=[
+            pltpu.VMEM((width, part), BF16),
+            pltpu.VMEM(vector, F32),
             pltpu.VMEM((half, width), F32),
             pltpu.VMEM((half, width), F32),
             pltpu.VMEM((rows, heads + part), BF16),
             pltpu.VMEM((2, half, width), F32),
             pltpu.SemaphoreType.DMA((6,)),
-        ],
+        ]
+        + [held for one in programs for held in one.scratch()],
         compiler_params=kernel_params(number),
-        cost_estimate=pl.CostEstimate(
-            flops=2 * rows * width * (heads + 2 * part),
-            bytes_accessed=24 * rows * width,
-            transcendentals=0,
-        ),
+        cost_estimate=SMALL,
     )(
         grad_query,
         grad_part,
@@ -1654,6 +1898,10 @@
         mlp_sum if cuts else from_line_order(mlp_sum),
         middle,
         bias[None],
+        middle_sums,
+        hidden_sums,
+        cut_a,
+        cut_b,
     )
 
 
@@ -1697,8 +1945,6 @@
         second = jnp.where(core == 0, other, mine)
         return jnp.concatenate([first, second], axis=axis)
 
-    gain_one = attn_norm_gain.astype(F32)
-    shift_one = attn_norm_bias.astype(F32)
 
     slot_ids = jnp.arange(slot_count, dtype=jnp.int32)
     ordering = block_order[0]
@@ -1718,44 +1964,73 @@
 
     keyval_cut = lax.dynamic_slice_in_dim(keyval_weight, core * HD, HD, axis=1)
     first_cut = jnp.concatenate([query_weight, keyval_cut], axis=1)
-    mlp_weights = jnp.concatenate([down_weight, up_weight], axis=0)
     shard_rows = down_weight.shape[0]
-    first_rows = shard_rows // 2
-    first_line = line_gather(first_cut.shape, BF16)
-    first_like = jax.ShapeDtypeStruct(first_line.out.shape, BF16)
-    _, mlp_cut, proj_line, mlp_piece, first_all = run_programs(
+    hidden_half = hidden_dev // 2
+    columns = down_weight.shape[1]
+    first_rows = shard_rows * 3 // 4 // 16 * 16
+    early_rows = shard_rows // 2
+    cuts = line_cuts(width, False)
+    lines = lax.axis_size("line")
+    first_pieces = [(0, slice(0, first_rows), 0)]
+    early_pieces = [
+        (0, slice(first_rows, shard_rows), 0),
+        (1, slice(0, shard_rows), 0),
+        (0, slice(0, early_rows), 1),
+    ]
+    late_pieces = [(0, slice(early_rows, shard_rows), 1), (1, slice(0, shard_rows), 1)]
+    hops = [0.1 * k for k in range(1, 4)] if lines == 4 else spaced(0.1, 0.3, lines - 1)
+    levels = spaced(0.4, 0.98, 2 * lines)
+    piece_hops = spaced(0.35, 0.75, lines - 1)
+    _, first_all, early_cut, late_cut, mlp_piece, normed_one, cotangent_line = run_programs(
         [
-            placed(first_line, 0.0, 0.17),
-            placed(Exchange(mlp_weights, True), 0.0, 0.18),
-            placed(line_gather(proj_weight.shape, BF16), 0.06, 0.28),
-            placed(line_gather((quarters, first_rows, hidden_dev), BF16), 0.3, 0.5, 0.65, 0.8, 0.8, 1.0),
-            placed(columns_gather(first_like), 0.19, 0.4, 0.7, 1.0),
+            placed(spread_halves(first_pieces, columns, BF16), 0.0, 0.05),
+            placed(rows_gather(first_cut), 0.01, *hops, *levels, 1.0),
+            placed(spread_halves(early_pieces, columns, BF16), 0.06, 1.0),
+            placed(spread_halves(late_pieces, columns, BF16), 0.061, 1.0),
+            placed(line_gather((quarters, first_rows, hidden_half), BF16), 0.07, *piece_hops, 1.0),
+            placed(Work(norm_work, hidden_in.shape, BF16), 0.31, 0.31),
+            placed(Work(functools.partial(reorder_work, cuts or [0]), (half_rows, width), BF16), 0.32, 0.32),
         ],
         [
-            first_cut,
-            mlp_weights,
-            proj_weight,
-            lambda outs: outs[1].at[:, :first_rows],
-            lambda outs: outs[0],
+            lambda more, outs: more[4:6],
+            lambda more, outs: more[6],
+            lambda more, outs: more[4:6],
+            lambda more, outs: more[4:6],
+            lambda more, outs: outs[0],
+            lambda more, outs: more[:3],
+            lambda more, outs: more[3],
         ],
         1,
-    )
+        near=[hidden_in, attn_norm_gain[None], attn_norm_bias[None], out_cotangent],
+        far=[down_weight, up_weight, first_cut],
+    )
+    if cuts is None:
+        cotangent_line = to_line_order(own_half(out_cotangent))
     first_all = flat(first_all)
 
-    stream = hidden_in.astype(F32)
-    normed_one = layer_norm(stream, gain_one, shift_one).astype(BF16)
     value_shift = jnp.where(core == 1, value_bias.astype(F32), 0.0)
     first_shift = jnp.concatenate([query_bias.astype(F32), value_shift])
-    first_low = (jnp.dot(normed_one, first_all, preferred_element_type=F32) + first_shift).astype(
-        BF16
-    )
-    query_low = first_low[:, :head_width]
-    part_low = first_low[:, head_width:]
-    keyval_every = gather_ctx(part_low, 4)
-    keyval_every, mlp_cut = lax.optimization_barrier((keyval_every, mlp_cut))
-    mlp_rest = lax.all_gather(mlp_cut[:, first_rows:], "line", axis=0, tiled=False)
+    part_like = (rows_dev, HD)
+    _, query_low, keyval_every, proj_line = run_programs(
+        [
+            placed(Work(part_work, part_like, BF16), 0.0, 0.0),
+            placed(Work(query_work, (rows_dev, head_width), BF16), 0.2, 0.2),
+            placed(ctx_gather(part_like, BF16), 0.1, 1.0),
+            placed(line_gather(proj_weight.shape, BF16), 0.11, 1.0),
+        ],
+        [
+            lambda more, outs: more[:3],
+            lambda more, outs: more[:3],
+            lambda more, outs: outs[0],
+            lambda more, outs: more[3],
+        ],
+        4,
+        near=[normed_one, first_all, first_shift[None]],
+        far=[proj_weight],
+    )
+    keyval_every, early_cut = lax.optimization_barrier((keyval_every, early_cut))
+    mlp_early = lax.all_gather(early_cut, "line", axis=0, tiled=False)
     table = keyval_every.reshape(2, slot_count, BLK, HD)
-    cotangent_line = to_line_order(own_half(out_cotangent))
     mixed_low, logsums, (proj_all, cotangent_all) = attend(
         query_low,
         table,
@@ -1769,34 +2044,56 @@
         2,
     )
     proj_all = flat(proj_all)
+    mixed_low, mlp_early, late_cut = lax.optimization_barrier((mixed_low, mlp_early, late_cut))
+    mlp_late = lax.all_gather(late_cut, "line", axis=0, tiled=False)
     middle, normed_two_line = project(
         mixed_low, proj_all, hidden_in, proj_bias, mlp_norm_gain, mlp_norm_bias, 5
     )
 
     up_shift = lax.dynamic_slice_in_dim(up_bias, quarter * hidden_dev, hidden_dev).astype(F32)
-    normed_two_all, act_low, grad_pre, normed_two_part, up_bias_parts = forward_products(
-        normed_two_line, cotangent_all, mlp_piece, mlp_rest, up_shift[None], 6
-    )
-    plane_two, plane_parts = plane_sum(flat(normed_two_part))
-    placed(plane_two, 0.0, 0.13, 0.13, 0.13, 0.13, 0.38, 0.8, 1.0, 1.0)
-    down_part, mlp_weight_grad, (grad_normed_two,) = grad_products(
-        flat(cotangent_all),
-        flat(normed_two_all),
-        flat(act_low),
-        flat(grad_pre),
+    up_shift = up_shift[None]
+    shards = lines * quarters
+    rows_all, act_a, pre_a, back_a, bias_a = forward_products(
+        normed_two_line, cotangent_all, mlp_piece, mlp_early, up_shift[:, :hidden_half], 6
+    )
+    rows_all, act_a, pre_a, back_a = flat(rows_all), flat(act_a), flat(pre_a), flat(back_a)
+    cotangent_all = flat(cotangent_all)
+    weight_grad_a = weight_products(cotangent_all, rows_all, act_a, pre_a, shards)
+    cut_a = lax.psum_scatter(weight_grad_a, "line", scatter_dimension=0, tiled=True)
+    rows_all, weight_grad_a = lax.optimization_barrier((rows_all, weight_grad_a))
+    act_b, pre_b, back_both, bias_b = second_products(
+        rows_all,
+        cotangent_all,
+        back_a,
         mlp_piece,
-        mlp_rest,
+        mlp_early,
+        mlp_late,
+        up_shift[:, hidden_half:],
+    )
+    plane_two, plane_parts = plane_sum(back_both)
+    placed(plane_two, 0.0, 0.13, 0.13, 0.13, 0.13, 0.51, 0.9, 1.0, 1.0)
+    down_part, weight_grad_b, (grad_normed_two,) = grad_products(
+        cotangent_all,
+        rows_all,
+        act_a,
+        act_b,
+        pre_b,
+        mlp_piece,
+        mlp_early,
+        mlp_late,
         [plane_two],
         [plane_parts],
         7,
     )
-    grad_up_bias = jnp.sum(up_bias_parts, axis=0)
-    mlp_cut_grad = lax.psum_scatter(mlp_weight_grad, "line", scatter_dimension=0, tiled=True)
-    mlp_cut_grad = mlp_cut_grad.reshape(quarters, 2 * shard_rows, hidden_dev)
+    cut_b = lax.psum_scatter(weight_grad_b, "line", scatter_dimension=0, tiled=True)
+    cut_a = cut_a.reshape(quarters, 2 * shard_rows, hidden_half)
+    cut_b = cut_b.reshape(quarters, 2 * shard_rows, hidden_half)
+    up_bias_parts = jnp.concatenate([bias_a, bias_b], axis=1)
 
     grad_middle, grad_mixed, proj_weight_grad, middle_sums = middle_back(
         grad_normed_two, middle, out_cotangent, mixed_low, proj_all, mlp_norm_gain, 8
     )
+    grad_mixed, cut_a = lax.optimization_barrier((grad_mixed, cut_a))
     sum_proj, proj_parts = rows_sum(proj_weight_grad)
     sum_down, down_parts = plane_sum(down_part)
     grad_query, grad_sets, (grad_proj_weight, mlp_out) = attend_back(
@@ -1823,7 +2120,7 @@
     grad_part, grad_query_weight = run_programs(
         [ctx_sum(grad_parts), sum_query], [grad_parts, query_parts], 12
     )
-    input_grad, layer_out, part_weight_grad, first_sums, query_sums, part_sums = first_back(
+    input_grad, layer_out, down_wide, up_wide, grad_part_weight, summed = first_back(
         grad_query,
         grad_part,
         first_all,
@@ -1834,64 +2131,33 @@
         mlp_out,
         middle,
         down_bias,
+        middle_sums,
+        up_bias_parts,
+        cut_a,
+        cut_b,
         9,
     )
-    grad_query_bias = jnp.sum(query_sums, axis=0)
-    grad_value_bias = jnp.where(core == 1, jnp.sum(part_sums, axis=0), 0.0)
-
-    query_slots = jnp.zeros((2 * head_width,), F32)
-    query_slots = lax.dynamic_update_slice_in_dim(
-        query_slots, grad_query_bias, core * head_width, axis=0
-    )
-    hidden_slots = jnp.zeros((2 * quarters * hidden_dev,), F32)
-    hidden_slots = lax.dynamic_update_slice_in_dim(
-        hidden_slots, grad_up_bias, (core * quarters + quarter) * hidden_dev, axis=0
-    )
-    pieces = [
-        first_sums[0],
-        first_sums[1],
-        middle_sums[2],
-        middle_sums[0],
-        middle_sums[1],
-        middle_sums[3],
-        grad_value_bias,
-        query_slots,
-        hidden_slots,
-    ]
-    sum_part, weight_parts = rows_sum(part_weight_grad, HD)
-    total, padded = total_of(jnp.concatenate(pieces))
-    summed, grad_part_weight, mlp_grads = run_programs(
-        [placed(total, 0.0, 0.8), placed(sum_part, 0.1, 0.9), placed(Exchange(mlp_cut_grad, False), 0.3, 1.0)],
-        [padded, weight_parts, mlp_cut_grad],
-        13,
-    )
-    grad_down_weight = mlp_grads[:shard_rows].astype(F32)
-    grad_up_weight = mlp_grads[shard_rows:].astype(F32)
+    grad_down_weight, grad_up_weight = down_wide.astype(F32), up_wide.astype(F32)
     grad_keyval_weight = in_order(grad_part_weight[:, :HD], grad_part_weight[:, HD:], axis=1)
-    summed = summed.reshape(-1)
-    cuts, start = [], 0
-    for piece in pieces:
-        cuts.append(summed[start : start + piece.shape[0]])
-        start += piece.shape[0]
-    sum_query = lax.dynamic_slice_in_dim(cuts[7], core * head_width, head_width)
-    sum_up = lax.dynamic_slice_in_dim(cuts[8], core * quarters * hidden_dev, quarters * hidden_dev)
+    sum_query = lax.dynamic_slice_in_dim(summed[3], core * head_width, head_width)
+    sum_up = jnp.where(core == 0, summed[4], summed[5])[: quarters * hidden_dev]
     return (
         layer_out,
         input_grad,
-        cuts[0],
-        cuts[1],
+        summed[0, :width],
+        summed[0, width : 2 * width],
         grad_query_weight,
         sum_query,
         grad_keyval_weight,
-        cuts[6],
+        summed[3, 2 * head_width : 2 * head_width + HD],
         grad_proj_weight,
-        cuts[2],
-        cuts[3],
-        cuts[4],
+        summed[2, :width],
+        summed[1, :width],
+        summed[1, width : 2 * width],
         grad_up_weight,
         sum_up,
         grad_down_weight,
-        cuts[5],
+        summed[2, width : 2 * width],
     )
 
 

time: 651 us -> 620 us (0.952)
  waiting for transfers between devices: 14.8 us -> 0.13 us
    pallas_call x2 -> x3, Pallas kernels: 27.6 us -> 120 us  [the longest x1 75.9 us: first_back(): pl.pallas_call(functools.partial(first_back_kernel, cuts, programs), out_...]
    pallas_call x4 -> x3, Pallas kernels: 230 us -> 155 us  [run_programs(): pl.pallas_call(kernel, out_shape=[one.out for one in programs], in_specs=...]
    all_gather x1 -> x2, waiting for transfers between devices: 14.8 us -> 0.04 us  [the longest x1 0.02 us: body(): mlp_early = lax.all_gather(early_cut, 'line', axis=0, tiled=False)]
    pallas_call x1, Pallas kernels: 59 us -> 51.8 us  [forward_products(): pl.pallas_call(forward_kernel, out_shape=[jax.ShapeDtypeStruct(lead + (wi...]
  transfers between devices with their start and end apart: 2 -> 4, of which waited for: 1 -> 0; matrix products, arithmetic and copies ran while one was open for 3% -> 2% of each run, Pallas kernels for 45% -> 63%
where the time goes in v5:
time: 620 us
  Pallas kernels  570 us (92%)
  local copies, waits for them, and re-layouts  16.6 us (3%)
  between operations  14 us (2%)
  other arithmetic  13.4 us (2%)
    pallas_call x3, Pallas kernels, run_programs(): pl.pallas_call(kernel, out_shape=[one.out for one in programs], in_specs=...  155 us
    pallas_call x1, Pallas kernels, attend_back(): pl.pallas_call(functools.partial(attend_back_kernel, programs, blocks * h...  78.1 us
    pallas_call x1, Pallas kernels, attend(): pl.pallas_call(functools.partial(attend_kernel, programs, blocks * heads)...  76.2 us
    pallas_call x1, Pallas kernels, first_back(): pl.pallas_call(functools.partial(first_back_kernel, cuts, programs), out_...  75.9 us
    pallas_call x1, Pallas kernels, forward_products(): pl.pallas_call(forward_kernel, out_shape=[jax.ShapeDtypeStruct(lead + (wi...  51.8 us
    pallas_call x1, Pallas kernels, grad_products(): pl.pallas_call(functools.partial(grads_kernel, programs, steps), grid=(st...  50.8 us
    pallas_call x1, Pallas kernels, second_products(): pl.pallas_call(second_kernel, grid=(steps,), out_shape=[jax.ShapeDtypeStr...  28.6 us
    pallas_call x1, Pallas kernels, middle_back(): pl.pallas_call(functools.partial(middle_back_kernel, cuts), out_shape=[ja...  19.6 us
  transfers between devices with their start and end apart: 4, of which 0 were waited for; matrix products, arithmetic and copies ran while one was open for 2% of the time, Pallas kernels for 63%

profile of v5, /device:TPU:0, one launch (start us, length us, event | category | flops | bytes accessed | tf_op | source)
XLA Modules:
  0.0 619.6 jit_solution(15970403497349574478)
XLA Ops:
  7.2 0.7 convert_element_type.16
  9.2 1.3 broadcast_in_dim.54.refs_1_.refs_5_
  10.5 1.3 broadcast_in_dim.55.refs_2_
  11.8 1.7 pad_maximum_fusion.refs_6_
  13.5 70.8 %shard_map.288 = (bf16[4,96,512]{2,1,0:T(8,128)(2,1)}, bf16[2,4,2,128,1152]{4,3,2,1,0:T(8,128)(2,1)}, bf16[4,224,512]{2,1,0:T(8,128)(2,1)}, bf16[4,192,512]{2,1,...) custom-call(bf16[512,2048]{1,0:T(8,128)(2,1)} %refs_3_.5, ...), custom_call_target="tpu_custom_call" | custom-call | flops 1 | bytes 1 | tf_op jit(solution)/shard_map/pallas_call | solution.py:640
  84.3 36.5 %shard_map.289 = (bf16[512,128]{1,0:T(8,128)(2,1)}, bf16[512,1024]{1,0:T(8,128)(2,1)}, bf16[2,4,2,512,128]{4,3,2,1,0:T(8,128)(2,1)}, bf16[4,128,1024]{2,1,0:T(8,128)(2,1)}) custom-call(bf16[512,2048]{1,0:T(8,128)(2,1)} %get-tuple-element.67.refs_0_.refs_4_, bf16[2048,1152]{1,0:T(8,128)(2,1)} %bitcast.49, f32[1,1152]{1,0:T(1,128)} %broadcast_in_dim.57.refs_2_, ...), custom_call_target="tpu_custom_call" | custom-call | flops 1 | bytes 1 | tf_op jit(solution)/shard_map/pallas_call | solution.py:640
  121.2 0.7 gather_fusion
  123.2 76.2 %shard_map.290 = (bf16[512,1024]{1,0:T(8,128)(2,1)}, f32[2,8,1,256]{3,2,1,0:T(1,128)}, bf16[2,4,2,128,1024]{4,3,2,1,0:T(8,128)(2,1)}, bf16[2,2,2,256,2048]{4,3,2,1,0:T(8,128)(2,1)}) custom-call(s32[2]{0:T(128)} %and_select_fusion.2.refs_0_, s32[2,9]{1,0:T(2,128)} %pad_add_fusion.refs_1_.slot_ref, bf16[512,1024]{1,0:T(8,128)(2,1)} %get-tuple-element.69.refs_2_, ...), custom_call_target="tpu_custom_call" | custom-call | flops 1 | bytes 1 | tf_op jit(solution)/shard_map/pallas_call | solution.py:798
  201.6 0.7 dynamic-slice_convert_fusion
  202.8 13.7 %shard_map.291 = (f32[256,2048]{1,0:T(8,128)}, bf16[256,2048]{1,0:T(8,128)(2,1)}) custom-call(bf16[512,1024]{1,0:T(8,128)(2,1)} %get-tuple-element.79.mixed_ref.refs_4_, bf16[2048,1024]{1,0:T(8,128)(2,1)} %bitcast.51, bf16[512,2048]{1,0:T(8,128)(2,1)} %refs_3_.5, bf16[1,2048]{1,0:T(2,128)(2,1)} %broadcast_in_dim.58.bias_ref, ...), custom_call_target="tpu_custom_call" | custom-call | flops 1 | bytes 1 | tf_op jit(solution)/shard_map/pallas_call | solution.py:1602
  216.5 51.8 %shard_map.292 = (bf16[2,2,2,256,2048]{4,3,2,1,0:T(8,128)(2,1)}, bf16[2,2,2,256,512]{4,3,2,1,0:T(8,128)(2,1)}, bf16[2,2,2,256,512]{4,3,2,1,0:T(8,128)(2,1)}, bf1...) custom-call(bf16[256,2048]{1,0:T(8,128)(2,1)} %get-tuple-element.81.x_ref, ...), custom_call_target="tpu_custom_call" | custom-call | flops 1 | bytes 1 | tf_op jit(solution)/shard_map/pallas_call | solution.py:1178
  268.3 15.7 %shard_map.293 = bf16[16,2,128,512]{3,2,1,0:T(8,128)(2,1)} custom-call(bf16[2048,2048]{1,0:T(8,128)(2,1)} %bitcast.40, bf16[2048,2048]{1,0:T(8,128)(2,1)} %bitcast.43, bf16[2048,512]{1,0:T(8,128)(2,1)} %bitcast.56, bf16[2048,512]{1,0:T(8,128)(2,1)} %bitcast.65), custom_call_target="tpu_custom_call" | custom-call | flops 1 | bytes 1 | tf_op jit(solution)/shard_map/pallas_call | solution.py:1316
  284.3 28.6 %shard_map.294 = (bf16[2048,512]{1,0:T(8,128)(2,1)}, bf16[2048,512]{1,0:T(8,128)(2,1)}, bf16[2048,2048]{1,0:T(8,128)(2,1)}, f32[8,512]{1,0:T(8,128)}) custom-call(bf16[2048,2048]{1,0:T(8,128)(2,1)} %bitcast.44, bf16[2048,2048]{1,0:T(8,128)(2,1)} %bitcast.41, bf16[2048,2048]{1,0:T(8,128)(2,1)} %bitcast.62, ...), custom_call_target="tpu_custom_call" | custom-call | flops 1 | bytes 1 | tf_op jit(solution)/shard_map/pallas_call | solution.py:1279
  313.0 50.8 %shard_map.295 = (bf16[2048,2048]{1,0:T(8,128)(2,1)}, bf16[16,2,128,512]{3,2,1,0:T(8,128)(2,1)}, f32[256,2048]{1,0:T(8,128)}) custom-call(bf16[2048,2048]{1,0:T(8,128)(2,1)} %bitcast.42, bf16[2048,2048]{1,0:T(8,128)(2,1)} %bitcast.45, bf16[2048,512]{1,0:T(8,128)(2,1)} %bitcast.57, bf16[2048,512]{1,0:T(8,128)(2,1)} %get-tuple-element.90.refs_3_, ...), custom_call_target="tpu_custom_call" | custom-call | flops 1 | bytes 1 | tf_op jit(solution)/shard_map/pallas_call | solution.py:1376
  365.1 19.6 %shard_map.296 = (f32[256,2048]{1,0:T(8,128)}, bf16[512,1024]{1,0:T(8,128)(2,1)}, bf16[2048,1024]{1,0:T(8,128)(2,1)}, f32[8,2048]{1,0:T(8,128)}) custom-call(f32[256,2048]{1,0:T(8,128)} %get-tuple-element.93.sum_ref, f32[256,2048]{1,0:T(8,128)} %get-tuple-element.94.middle_ref.refs_8_, bf16[512,2048]{1,0:T(8,128)(2,1)} %cotangent_ref.1, ...), custom_call_target="tpu_custom_call" | custom-call | flops 1 | bytes 1 | tf_op jit(solution)/shard_map/pallas_call | solution.py:1691
  385.3 78.1 %shard_map.297 = (bf16[512,1024]{1,0:T(8,128)(2,1)}, f32[2,2304,256]{2,1,0:T(8,128)}, f32[128,1024]{1,0:T(8,128)}, f32[256,2048]{1,0:T(8,128)}) custom-call(s32[2]{0:T(128)} %and_select_fusion.2.refs_0_, s32[2,9]{1,0:T(2,128)} %pad_add_fusion.refs_1_.slot_ref, bf16[512,1024]{1,0:T(8,128)(2,1)} %get-tuple-element.69.refs_2_, ...), custom_call_target="tpu_custom_call" | custom-call | flops 1 | bytes 1 | tf_op jit(solution)/shard_map/pallas_call | solution.py:886
  463.4 5.2 shard_map.298
  468.6 4.4 convolution_convert_fusion
  473.0 47.7 %shard_map.299 = (f32[512,128]{1,0:T(8,128)}, f32[128,1024]{1,0:T(8,128)}) custom-call(bf16[2,4,2,512,128]{4,3,2,1,0:T(8,128)(2,1)} %bitcast.60, bf16[2,4,2,128,1024]{4,3,2,1,0:T(8,128)(2,1)} %bitcast.64), custom_call_target="tpu_custom_call" | custom-call | flops 1 | bytes 1 | tf_op jit(solution)/shard_map/pallas_call | solution.py:640
  520.7 75.9 %shard_map.300 = (bf16[512,2048]{1,0:T(8,128)(2,1)}, bf16[512,2048]{1,0:T(8,128)(2,1)}, bf16[128,4096]{1,0:T(8,128)(2,1)}, bf16[128,4096]{1,0:T(8,128)(2,1)}, f32[128,256]{1,0:T(8,128)}, /*index=5*/f32[8,4096]{1,0:T(8,128)}) custom-call(bf16[512,1024]{1,0:T(8,128)(2,1)} %get-tuple-element.100.refs_0_, f32[512,128]{1,0:T(8,128)} %get-tuple-element.102.refs_1_, ...), custom_call_target="tpu_custom_call" | custom-call | flops 1 | bytes 1 | tf_op jit(solution)/shard_map/pallas_call | solution.py:1869
  596.6 1.3 slice_bitcast_fusion
  597.8 1.7 fusion.2
  599.6 1.7 broadcast_select_fusion
  601.3 0.9 slice_select_fusion.1
  602.2 2.8 convert_element_type.19
  604.9 1.5 convert_element_type.20
  606.5 0.7 pad_maximum_fusion.1
  607.7 1.3 copy.37
  609.0 1.0 copy-done.3
  610.1 1.3 copy.38
  611.4 0.8 copy.39
  612.2 0.8 copy.40
  (64 shorter events, 8.6 us)
Async XLA Ops:
  7.2 4.6 copy-start
  7.2 192.3 %all-gather.5.cloned.1.call-start = ((), (), s32[]{:S(2)}) async-start(), calls=%async_computation.4 | async-start | bytes 4587520 | tf_op jit(solution)/shard_map/all_gather | solution.py:2032
  84.3 36.6 %copy-start.15 = (s32[1,16]{1,0:T(1,128)S(1)}, s32[1,16]{1,0:T(1,128)}, u32[]{:S(2)}) copy-start(s32[1,16]{1,0:T(1,128)} %param.18) | copy-start | bytes 196
  120.8 163.5 %all-gather.7.cloned.1.call-start = ((), (), s32[]{:S(2)}) async-start(), calls=%async_computation.5 | async-start | bytes 3932160 | tf_op jit(solution)/shard_map/all_gather | solution.py:2048
  123.2 76.5 %copy-start.11 = (bf16[2048]{0:T(1024)(128)(2,1)S(1)}, bf16[2048]{0:T(1024)(128)(2,1)}, u32[]{:S(2)}) copy-start(bf16[2048]{0:T(1024)(128)(2,1)} %param.27) | copy-start | bytes 12292
  123.2 77.1 %copy-start.12 = (bf16[2048]{0:T(1024)(128)(2,1)S(1)}, bf16[2048]{0:T(1024)(128)(2,1)}, u32[]{:S(2)}) copy-start(bf16[2048]{0:T(1024)(128)(2,1)} %param.26) | copy-start | bytes 12292
  123.2 77.7 %copy-start.13 = (bf16[2048]{0:T(1024)(128)(2,1)S(1)}, bf16[2048]{0:T(1024)(128)(2,1)}, u32[]{:S(2)}) copy-start(bf16[2048]{0:T(1024)(128)(2,1)} %param.28) | copy-start | bytes 12292
  199.5 185.8 %reduce-scatter.3.cloned.1.call-start = ((), (), s32[]{:S(2)}) async-start(), calls=%async_computation.2 | async-start | bytes 5242880 | tf_op jit(solution)/shard_map/reduce_scatter | solution.py:2062
  284.0 236.6 %reduce-scatter.5.cloned.1.call-start = ((), (), s32[]{:S(2)}) async-start(), calls=%async_computation.3 | async-start | bytes 5242880 | tf_op jit(solution)/shard_map/reduce_scatter | solution.py:2088
  363.8 0.7 copy-start.14
  365.1 19.6 %copy-start.9 = (f32[8,512]{1,0:T(8,128)S(1)}, f32[8,512]{1,0:T(8,128)}, u32[]{:S(2)}) copy-start(f32[8,512]{1,0:T(8,128)} %get-tuple-element.106) | copy-start | bytes 49156
  365.1 19.6 %copy-start.10 = (f32[8,512]{1,0:T(8,128)S(1)}, f32[8,512]{1,0:T(8,128)}, u32[]{:S(2)}) copy-start(f32[8,512]{1,0:T(8,128)} %get-tuple-element.107) | copy-start | bytes 49156
  463.4 5.2 copy-start.2
  463.4 5.2 copy-start.6
  596.6 8.4 %copy-start.5 = (bf16[128,4096]{1,0:T(8,128)(2,1)S(1)}, bf16[128,4096]{1,0:T(8,128)(2,1)}, u32[]{:S(2)}) copy-start(bf16[128,4096]{1,0:T(8,128)(2,1)} %get-tuple-element.117) | copy-start | bytes 3145732
  604.9 2.8 copy-start.4
  607.7 2.3 copy-start.3
  610.1 1.4 copy-start.8
  610.1 2.2 copy-start.7
  610.1 3.0 copy-start.1
Sparse Core Ops, SparseCore 0:
  120.9 70.3 all-gather.4
  199.6 61.5 all-gather.6
  284.2 74.3 reduce-scatter.2
  364.0 90.6 reduce-scatter.4

commit v6 on v5

--- a/solution.py
+++ b/solution.py
@@ -196,10 +196,10 @@
 
 
 class Sum:
-    def __init__(self, steps, lines, rows, columns, slot, shared=0):
+    def __init__(self, steps, lines, rows, columns, slot, kind=F32):
         self.steps, self.lines, self.rows, self.columns = steps, lines, rows, columns
-        self.slot, self.shared = slot, shared
-        self.out = jax.ShapeDtypeStruct((rows, columns + shared), F32)
+        self.slot = slot
+        self.out = jax.ShapeDtypeStruct((rows, columns), kind)
         self.in_spec = pl.BlockSpec(memory_space=pl.ANY)
         self.out_spec = pl.BlockSpec(memory_space=pltpu.VMEM)
 
@@ -214,17 +214,15 @@
             + [pltpu.SemaphoreType.DMA((lines, sizes[0]))]
             + [pltpu.SemaphoreType.DMA((lines, size)) for size in sizes] * 2
             + [pltpu.SemaphoreType.DMA((2, lines))] * 2
-            + [pltpu.SemaphoreType.DMA((2,))]
         )
 
-    def stages(self, me, x_ref, whole_ref, own, *rest):
-        out_ref = whole_ref.at[:, : self.columns] if self.shared else whole_ref
+    def stages(self, me, x_ref, out_ref, own, *rest):
         steps, lines, rows, slot = self.steps, self.lines, self.rows, self.slot
         count = len(steps)
         held, rest = rest[:count], rest[count:]
         on_line, own_sem, rest = rest[0], rest[1], rest[2:]
         send, recv = rest[:count], rest[count : 2 * count]
-        line_send, line_recv, share_sem = rest[2 * count :]
+        line_send, line_recv = rest[2 * count :]
         my_line = me["line"] if lines > 1 else 0
         last = count - 1
 
@@ -335,15 +333,26 @@
 
         def end():
             final = held[last].at[my_line, 0]
-            add_blocks(out_ref, rows_of(final), None, rows)
-            if lines > 1:
-                for amount in (1, -1):
+            if lines == 1:
+                add_blocks(out_ref, rows_of(final), None, rows)
+            else:
+                for way, amount in enumerate((-1, 1)):
 
                     @pl.when(line_inside(-amount))
                     def _():
                         line_copy(amount, my_line).wait_recv()
-                        moving = on_line.at[(amount + 1) // 2, my_line]
-                        add_blocks(out_ref, rows_of(out_ref), rows_of(moving), rows)
+
+                    @pl.when(jnp.logical_not(line_inside(-amount)))
+                    def _():
+                        add_blocks(on_line.at[way, my_line], lambda cut: jnp.zeros_like(final[cut, :]), None, rows)
+
+                left, right = on_line.at[0, my_line], on_line.at[1, my_line]
+                add_blocks(
+                    out_ref,
+                    lambda cut: final[cut, :].astype(F32) + left[cut, :].astype(F32),
+                    rows_of(right),
+                    rows,
+                )
 
                 for amount in (1, -1):
                     for distance in range(1, lines):
@@ -351,16 +360,6 @@
                         pl.when((shard >= 0) & (shard < lines))(
                             lambda amount=amount, shard=shard: line_copy(amount, shard).wait_send()
                         )
-            if self.shared:
-                share = remote(
-                    whole_ref.at[:, self.columns - self.shared : self.columns],
-                    whole_ref.at[:, self.columns :],
-                    share_sem.at[0],
-                    share_sem.at[1],
-                    flip(me, "tp"),
-                )
-                share.start()
-                share.wait()
             for k in range(count):
                 for shard in range(lines):
                     for bits in parts_of(k):
@@ -478,113 +477,213 @@
         return [functools.partial(self.work, me, x_refs, out_ref), lambda: None]
 
 
+class Direct:
+    steps, rows_too = ("tp",), True
+
+    def __init__(self, lines, rows, columns, shared):
+        self.lines, self.rows, self.columns, self.shared = lines, rows, columns, shared
+        self.out = jax.ShapeDtypeStruct((rows, columns + shared), F32)
+        self.in_spec = self.out_spec = pl.BlockSpec(memory_space=pltpu.VMEM)
+
+    def scratch(self):
+        lines = self.lines
+        return [
+            pltpu.VMEM((2, lines, 2, self.rows, self.columns), BF16),
+            pltpu.SemaphoreType.DMA((4, 2, lines)),
+            pltpu.SemaphoreType.DMA((2, lines, 2)),
+            pltpu.SemaphoreType.DMA((2,)),
+        ]
+
+    def stages(self, me, x_ref, out_ref, held, send, recv, share_sem):
+        def on_others(work):
+            for side in range(4):
+                for distance in range(self.lines):
+                    for way, amount in enumerate((1, -1) if distance else (1,)):
+                        if side or distance:
+                            place = along(plane_partner(me, side * 2), amount * distance)
+                            inside = (place["line"] >= 0) & (place["line"] < self.lines)
+                            pl.when(inside)(
+                                functools.partial(work, place, send.at[side, way, distance])
+                            )
+
+        def copy(place, sem):
+            return remote(
+                by_rows_slot(x_ref, place),
+                by_rows_slot(held, me),
+                sem,
+                by_rows_slot(recv, me),
+                place,
+            )
+
+        def arrived(place, sem):
+            slot = by_rows_slot(held, place)
+            remote(slot, slot, sem, by_rows_slot(recv, place), me).wait_recv()
+
+        def begin():
+            on_others(lambda place, sem: copy(place, sem).start())
+            held[me["fsdp"], me["line"], me["pair"]] = x_ref[me["fsdp"], me["line"], me["pair"]]
+
+        def end():
+            on_others(arrived)
+            total = jnp.zeros((self.rows, self.columns), F32)
+            for half in range(2):
+                for shard in range(self.lines):
+                    for side in range(2):
+                        total = total + held[half, shard, side].astype(F32)
+            out_ref[:, : self.columns] = total
+            share = remote(
+                out_ref.at[:, : self.columns],
+                out_ref.at[:, self.columns :],
+                share_sem.at[0],
+                share_sem.at[1],
+                flip(me, "tp"),
+            )
+            share.start()
+            share.wait()
+            on_others(lambda place, sem: copy(place, sem).wait_send())
+
+        return [begin, end]
+
+
 class Total:
-    steps = ("tp", "pair", "fsdp")
-
-    def __init__(self, values, lines):
-        self.lines, self.out = lines, jax.ShapeDtypeStruct(values.shape, F32)
+    steps, everyone = (), True
+
+    def __init__(self, shape, lines, special, heads):
+        self.lines, self.shape, self.special, self.heads = lines, shape, special, heads
+        self.out = jax.ShapeDtypeStruct((shape[0], 2 * shape[1]), F32)
         self.in_spec = self.out_spec = pl.BlockSpec(memory_space=pltpu.VMEM)
 
     def scratch(self):
-        shape, lines = self.out.shape, self.lines
+        shape, lines = self.shape, self.lines
         return [
-            pltpu.VMEM((3, 2) + shape, F32),
             pltpu.VMEM((lines,) + shape, F32),
-            pltpu.SemaphoreType.DMA((3,)),
-            pltpu.SemaphoreType.DMA((3,)),
+            pltpu.VMEM((8,) + shape, F32),
             pltpu.SemaphoreType.DMA((2, lines)),
             pltpu.SemaphoreType.DMA((lines,)),
+            pltpu.SemaphoreType.DMA((8,)),
+            pltpu.SemaphoreType.DMA((8,)),
         ]
 
-    def stages(self, me, x_ref, out_ref, moved, on_line, send, recv, line_send, line_recv):
-        lines = self.lines
-
-        def swap(k):
+    def stages(self, me, x_ref, out_ref, on_line, on_plane, line_send, line_recv, send, recv):
+        lines, mine = self.lines, me["line"]
+        number = plane_number(me)
+
+        def on_others(work):
+            for distance in range(1, lines):
+                for way, amount in enumerate((1, -1)):
+                    there = mine + amount * distance
+                    pl.when((there >= 0) & (there < lines))(
+                        functools.partial(work, way, amount, distance, there)
+                    )
+
+        def to_line(way, amount, distance):
             return remote(
-                moved.at[k, 0], moved.at[k, 1], send.at[k], recv.at[k], flip(me, self.steps[k])
+                on_line.at[mine],
+                on_line.at[mine],
+                line_send.at[way, distance],
+                line_recv.at[mine],
+                along(me, amount * distance),
             )
 
-        def copy(amount, shard):
+        def to_plane(bits):
             return remote(
-                on_line.at[shard],
-                on_line.at[shard],
-                line_send.at[(amount + 1) // 2, shard],
-                line_recv.at[shard],
-                along(me, amount),
+                on_plane.at[number],
+                on_plane.at[number],
+                send.at[bits],
+                recv.at[number],
+                plane_partner(me, bits),
             )
 
-        def inside(amount):
-            there = me["line"] + amount
-            return (there >= 0) & (there < lines)
-
         def begin():
-            moved[0, 0] = x_ref[...]
-            swap(0).start()
-
-        def after(k):
-            swap(k).wait()
-            if k < 2:
-                moved[k + 1, 0] = moved[k, 0] + moved[k, 1]
-                swap(k + 1).start()
-                return
-            on_line[me["line"]] = moved[k, 0] + moved[k, 1]
-            for amount in (1, -1):
-                pl.when(inside(amount))(lambda amount=amount: copy(amount, me["line"]).start())
-
-        def hop(distance):
-            for amount in (1, -1):
-                shard = me["line"] - amount * distance
-
-                @pl.when((shard >= 0) & (shard < lines))
-                def _():
-                    copy(amount, shard).wait_recv()
-                    pl.when(inside(amount))(lambda: copy(amount, shard).start())
-
-        def end():
+            on_line[mine] = x_ref[...]
+            on_others(lambda way, amount, distance, there: to_line(way, amount, distance).start())
+
+        def arrived(way, amount, distance, there):
+            remote(
+                on_line.at[there], on_line.at[there], line_send.at[0, 0], line_recv.at[there], me
+            ).wait_recv()
+
+        def middle():
+            on_others(arrived)
             total = on_line[0]
             for shard in range(1, lines):
                 total = total + on_line[shard]
-            out_ref[...] = total
-            for amount in (1, -1):
-                for distance in range(lines):
-                    shard = me["line"] - amount * distance
-                    pl.when((shard >= 0) & (shard < lines) & inside(amount))(
-                        lambda amount=amount, shard=shard: copy(amount, shard).wait_send()
-                    )
-
-        return (
-            [begin]
-            + [functools.partial(after, k) for k in range(3)]
-            + [functools.partial(hop, distance) for distance in range(1, lines)]
-            + [end]
-        )
+            on_plane[number] = total
+            for bits in range(1, 8):
+                to_plane(bits).start()
+
+        def end():
+            for bits in range(1, 8):
+                there = plane_number(plane_partner(me, bits))
+                remote(
+                    on_plane.at[there], on_plane.at[there], send.at[0], recv.at[there], me
+                ).wait_recv()
+            total = on_plane[0]
+            for other in range(1, 8):
+                total = total + on_plane[other]
+            width, row, heads = self.shape[1], slice(self.special, self.special + 1), self.heads
+            out_ref[...] = jnp.zeros_like(out_ref)
+            out_ref[:, :width] = total
+            same = [on_plane[quarter * 2 + me["tp"], row, :] for quarter in range(4)]
+            out_ref[row, :heads] = sum(part[:, :heads] for part in same)
+            for quarter, part in enumerate(same):
+                out_ref[quarter : quarter + 1, width : 2 * width - heads] = part[:, heads:]
+            for bits in range(1, 8):
+                to_plane(bits).wait_send()
+            on_others(lambda way, amount, distance, there: to_line(way, amount, distance).wait_send())
+
+        return [begin, middle, end]
+
+
+def plane_number(place):
+    return (place["fsdp"] * 2 + place["pair"]) * 2 + place["tp"]
+
+
+def plane_partner(me, bits):
+    place = me
+    for bit, name in ((1, "tp"), (2, "pair"), (4, "fsdp")):
+        if bits & bit:
+            place = flip(place, name)
+    return place
 
 
 def greet(me, programs, partners=()):
     barrier = pltpu.get_barrier_semaphore()
-    lines = max(one.lines for one in programs)
-    steps = list(dict.fromkeys([step for one in programs for step in one.steps] + list(partners)))
-    if SIDE in steps or FRONT in steps:
-        steps = [SIDE, FRONT] + [step for step in steps if step not in (SIDE, FRONT)]
-        steps = [step for step in steps if step not in ("pair", "fsdp")]
-    places = [flip(me, step) for step in steps]
-    if any(isinstance(one, Exchange) for one in programs):
-        places.append(move(me, ("pair", "fsdp")))
-    for place in places:
-        pl.semaphore_signal(barrier, inc=1, device_id=place, device_id_type=MESH_ID)
-    count = len(places)
-    if lines > 1:
-        for amount in (-1, 1):
+    plane, reach, lines, corners = set(), 0, 1, False
+    for one in programs:
+        lines = max(lines, one.lines)
+        if one.lines > 1:
+            reach = max(reach, one.lines - 1 if hasattr(one, "everyone") else 1)
+        if hasattr(one, "everyone"):
+            plane |= set(range(1, 8))
+        if isinstance(one, Exchange) or hasattr(one, "rows_too"):
+            plane |= {2, 4, 6}
+        if hasattr(one, "rows_too"):
+            reach, corners = one.lines - 1, True
+    for step in [step for one in programs for step in one.steps] + list(partners):
+        plane |= {"tp": {1}, "pair": {2}, "fsdp": {4}}.get(step, {2, 4})
+    for bits in sorted(plane):
+        pl.semaphore_signal(
+            barrier, inc=1, device_id=plane_partner(me, bits), device_id_type=MESH_ID
+        )
+    count = len(plane)
+    for distance in range(1, reach + 1):
+        for amount in (-distance, distance):
             there = me["line"] + amount
             inside = (there >= 0) & (there < lines)
 
-            @pl.when(inside)
-            def _():
-                pl.semaphore_signal(
-                    barrier, inc=1, device_id=along(me, amount), device_id_type=MESH_ID
-                )
-
-            count = count + inside.astype(jnp.int32)
+            for bits in (0, 2, 4, 6) if corners else (0,):
+
+                @pl.when(inside)
+                def _():
+                    pl.semaphore_signal(
+                        barrier,
+                        inc=1,
+                        device_id=along(plane_partner(me, bits), amount),
+                        device_id_type=MESH_ID,
+                    )
+
+                count = count + inside.astype(jnp.int32)
     pl.semaphore_wait(barrier, count)
 
 
@@ -682,11 +781,11 @@
     )
 
 
-def rows_sum(values, shared=0):
+def rows_sum(values):
     lines, (total, columns) = lax.axis_size("line"), values.shape
     rows = total // (4 * lines)
     parts = values.astype(BF16).reshape(2, lines, 2, rows, columns)
-    return Sum((FRONT, SIDE), lines, rows, columns, by_rows_slot, shared), parts
+    return Sum((FRONT, SIDE), lines, rows, columns, by_rows_slot), parts
 
 
 def plane_gather(values):
@@ -709,9 +808,13 @@
     return Gather(like, ("pair", "tp"), lines, (2, lines, 2) + shape, by_ctx_slot)
 
 
-def ctx_sum(values):
-    _, lines, _, rows, columns = values.shape
-    return Sum(("tp", "pair"), lines, rows, columns, by_ctx_slot)
+def ctx_sums(values):
+    _, lines, rows, columns = values.shape
+    along_line = Sum(
+        ("tp",), lines, rows, columns, lambda ref, at: ref.at[at["tp"], at["line"]], BF16
+    )
+    over_pair = Sum(("pair",), 1, rows // 2, columns, lambda ref, at: ref.at[at["pair"]])
+    return along_line, over_pair
 
 
 LOG2E = 1.4426950408889634
@@ -1002,8 +1105,10 @@
     pre_ref,
     part_ref,
     bias_ref,
+    weight_grad_ref,
     up_own,
     down_own,
+    grads_own,
     rows_own,
     cotangent_own,
     act_own,
@@ -1106,6 +1211,28 @@
 
         lax.fori_loop(0, width // tile, one, 0)
 
+    def grads(number):
+        slot = number % 2
+        tile = 256
+        shard_rows = weight_grad_ref.shape[2]
+
+        def one(index, carry):
+            cut = pl.ds(pl.multiple_of(index * tile, tile), tile)
+            for kind, (left, right) in enumerate(((cotangent_own, act_own), (rows_own, pre_own))):
+                grad = by_columns(left[slot, :, cut], right[slot])
+                if number > 0:
+                    grad = grads_own[kind, cut, :] + grad
+                if number < 3:
+                    grads_own[kind, cut, :] = grad
+                else:
+                    count = tile // shard_rows
+                    shards = pl.ds(pl.multiple_of(index * count, count), count)
+                    grad = grad.astype(BF16).reshape(count, shard_rows, hidden)
+                    weight_grad_ref[shards, kind] = grad
+            return carry
+
+        lax.fori_loop(0, width // tile, one, 0)
+
     def pass_on(bits, *ways):
         arrived(bits)
         for k in ways:
@@ -1115,12 +1242,12 @@
         to_step(0, 0).wait_send()
         to_step(1, 0).start()
 
-    between = [
-        second,
-        functools.partial(pass_on, 2, 2),
-        functools.partial(pass_on, 3, 2),
-        lambda: None,
-    ]
+    def third():
+        to_step(1, 0).wait_send()
+        to_step(1, 1).start()
+        pass_on(2, 2)
+
+    between = [second, third, functools.partial(pass_on, 3, 2), lambda: None]
     barrier = pltpu.get_barrier_semaphore()
     for step in steps:
         pl.semaphore_signal(barrier, inc=1, device_id=flip(me, step), device_id_type=MESH_ID)
@@ -1137,7 +1264,7 @@
     bias_ref[...] = jnp.zeros_like(bias_ref)
     for number in range(4):
         if number == 1:
-            pass_on(1, 1, 2)
+            pass_on(1, 2)
         arrived(4 + number)
         copies = loads(number)
         for one in copies:
@@ -1159,12 +1286,13 @@
         back(number)
         for one in stores(number, 2):
             one.start()
+        grads(number)
     for number in (2, 3):
         for kind in range(3):
             for one in stores(number, kind):
                 one.wait()
     own.wait()
-    for k, bits in ((1, 0), (2, 0), (1, 1), (2, 1), (2, 2), (2, 3)):
+    for k, bits in ((2, 0), (1, 1), (2, 1), (2, 2), (2, 3)):
         to_step(k, bits).wait_send()
 
 
@@ -1183,12 +1311,14 @@
             jax.ShapeDtypeStruct(lead + (hidden,), BF16),
             jax.ShapeDtypeStruct(lead + (width,), BF16),
             jax.ShapeDtypeStruct((8, hidden), F32),
+            jax.ShapeDtypeStruct((lines * quarters, 2, weights[2], hidden), BF16),
         ],
         in_specs=[anywhere] * 4 + [inside],
-        out_specs=[anywhere] * 4 + [inside],
+        out_specs=[anywhere] * 4 + [inside] * 2,
         scratch_shapes=[
             pltpu.VMEM(weights, BF16),
             pltpu.VMEM(weights, BF16),
+            pltpu.VMEM((2, width, hidden), F32),
             pltpu.VMEM((2, 2 * half, width), BF16),
             pltpu.VMEM((2, 2 * half, width), BF16),
             pltpu.VMEM((2, 2 * half, hidden), BF16),
@@ -1299,29 +1429,6 @@
 
 def by_columns(left, right):
     return lax.dot_general(left, right, (((0,), (0,)), ((), ())), preferred_element_type=F32)
-
-
-def weight_kernel(cotangent_ref, rows_ref, act_ref, pre_ref, out_ref):
-    shards, _, shard_rows, hidden = out_ref.shape
-    for kind, (left, right) in enumerate(((cotangent_ref, act_ref), (rows_ref, pre_ref))):
-        grad = by_columns(left[...], right[...]).astype(BF16)
-        out_ref[:, kind] = grad.reshape(shards, shard_rows, hidden)
-
-
-def weight_products(cotangent_all, rows_all, act, pre, shards):
-    rows, width = rows_all.shape
-    hidden, steps = act.shape[1], 8
-    columns = pl.BlockSpec((rows, width // steps), lambda i: (0, i))
-    whole = pl.BlockSpec((rows, hidden), lambda i: (0, 0))
-    return pl.pallas_call(
-        weight_kernel,
-        grid=(steps,),
-        out_shape=jax.ShapeDtypeStruct((shards, 2, width // shards, hidden), BF16),
-        in_specs=[columns, columns, whole, whole],
-        out_specs=pl.BlockSpec((shards // steps, 2, width // shards, hidden), lambda i: (i, 0, 0, 0)),
-        compiler_params=pltpu.CompilerParams(vmem_limit_bytes=VMEM_BYTES),
-        cost_estimate=SMALL,
-    )(cotangent_all, rows_all, act, pre)
 
 
 def grads_kernel(programs, steps, *refs):
@@ -1626,10 +1733,12 @@
     mixed_ref,
     proj_ref,
     gain_ref,
+    hidden_a_ref,
+    hidden_b_ref,
     grad_middle_ref,
     grad_mixed_ref,
     proj_grad_ref,
-    sums_ref,
+    vector_ref,
     attn_ref,
     sums_own,
     sems,
@@ -1668,9 +1777,13 @@
         each_columns(proj_ref.shape[1], 256, work)
 
     to_heads(mine)
+    vector_ref[...] = jnp.zeros_like(vector_ref)
     for kind in range(4):
-        sums_ref[kind : kind + 1, :] = jnp.sum(sums_own[kind], axis=0, keepdims=True)
-    sums_ref[4:8, :] = jnp.zeros((4, width), F32)
+        vector_ref[2 + kind : 3 + kind, :] = jnp.sum(sums_own[kind], axis=0, keepdims=True)
+    size = hidden_a_ref.shape[1]
+    for number, hidden_ref in enumerate((hidden_a_ref, hidden_b_ref)):
+        start = width - (2 - number) * size
+        vector_ref[6:7, start : start + size] = jnp.sum(hidden_ref[...], axis=0, keepdims=True)
     copy.wait_recv()
     to_heads(other)
 
@@ -1684,7 +1797,7 @@
     copy.wait_send()
 
 
-def middle_back(grad_sum, middle, cotangent, mixed, proj_all, gain, number):
+def middle_back(grad_sum, middle, cotangent, mixed, proj_all, gain, hidden_a, hidden_b, number):
     rows, width = cotangent.shape
     half, heads = rows // 2, mixed.shape[1]
     cuts = line_cuts(width, True)
@@ -1696,7 +1809,7 @@
             jax.ShapeDtypeStruct((width, heads), BF16),
             jax.ShapeDtypeStruct((8, width), F32),
         ],
-        in_specs=in_vmem(6),
+        in_specs=in_vmem(8),
         out_specs=in_vmem(4),
         scratch_shapes=[
             pltpu.VMEM((rows, width), BF16),
@@ -1705,7 +1818,16 @@
         ],
         compiler_params=kernel_params(number),
         cost_estimate=SMALL,
-    )(grad_sum if cuts else from_line_order(grad_sum), middle, cotangent, mixed, proj_all, gain[None])
+    )(
+        grad_sum if cuts else from_line_order(grad_sum),
+        middle,
+        cotangent,
+        mixed,
+        proj_all,
+        gain[None],
+        hidden_a,
+        hidden_b,
+    )
 
 
 def first_back_kernel(cuts, programs, *refs):
@@ -1720,11 +1842,10 @@
         mlp_ref,
         middle_ref,
         bias_ref,
-        middle_sums_ref,
-        hidden_sums_ref,
+        early_ref,
         cut_a_ref,
         cut_b_ref,
-    ), refs = refs[:14], refs[14:]
+    ), refs = refs[:13], refs[13:]
     (input_ref, layer_ref, down_out, up_out, part_out, total_out), refs = refs[:6], refs[6:]
     (weight_ref, vector_ref, sent_ref, got_ref, grad_first_ref, held_ref, sems), scratch = refs[:7], refs[7:]
     me = here()
@@ -1806,27 +1927,17 @@
     each_rows(half, few, norm)
     input_copy = remote(input_ref.at[mine], input_ref.at[mine], sems.at[4], sems.at[5], sibling)
     input_copy.start()
-    vector_ref[...] = jnp.zeros_like(vector_ref)
-    vector_ref[0:1, :width] = jnp.sum(folded[0:8, :], axis=0, keepdims=True)
-    vector_ref[0:1, width : 2 * width] = jnp.sum(folded[8:16, :], axis=0, keepdims=True)
-    for kind in range(4):
-        at = slice(kind % 2 * width, (kind % 2 + 1) * width)
-        vector_ref[1 + kind // 2 : 2 + kind // 2, at] = middle_sums_ref[kind : kind + 1, :]
-    query_sums = jnp.sum(fold_rows(grad_query_ref[...].astype(F32)), axis=0, keepdims=True)
+    vector_ref[...] = early_ref[...]
+    for kind in range(2):
+        total = jnp.sum(folded[kind * 8 : kind * 8 + 8, :], axis=0, keepdims=True)
+        vector_ref[kind : kind + 1, :] = total
+    vector_ref[6:7, :heads] = jnp.sum(
+        fold_rows(grad_query_ref[...].astype(F32)), axis=0, keepdims=True
+    )
     part_sums = jnp.sum(
         fold_rows(grad_first_ref[:, heads:].astype(F32)), axis=0, keepdims=True
     )
-    hidden_sums = jnp.sum(hidden_sums_ref[...], axis=0, keepdims=True)
-    hidden, part_width = hidden_sums.shape[1], part_sums.shape[1]
-    for core in range(2):
-        own = me["tp"] == core
-        vector_ref[3:4, core * heads : (core + 1) * heads] = jnp.where(own, query_sums, 0.0)
-        for quarter in range(4):
-            here_too = own & (quarter_of(me) == quarter)
-            vector_ref[4 + core : 5 + core, quarter * hidden : (quarter + 1) * hidden] = jnp.where(
-                here_too, hidden_sums, 0.0
-            )
-    vector_ref[3:4, 2 * heads : 2 * heads + part_width] = jnp.where(me["tp"] == 1, part_sums, 0.0)
+    vector_ref[7:8, : part_sums.shape[1]] = jnp.where(me["tp"] == 1, part_sums, 0.0)
     run_until(2.0)
     layer_copy.wait()
     input_copy.wait()
@@ -1844,26 +1955,22 @@
     mlp_sum,
     middle,
     bias,
-    middle_sums,
-    hidden_sums,
+    early,
     cut_a,
     cut_b,
     number,
 ):
     rows, width = stream.shape
     half, heads, part = rows // 2, grad_query.shape[1], grad_part.shape[1]
-    lines, hidden = lax.axis_size("line"), hidden_sums.shape[1]
+    lines = lax.axis_size("line")
     cuts = line_cuts(width, True)
     shard_rows = width // (4 * lines)
-    vector = (8, max(2 * width, 4 * hidden, 2 * heads + part))
+    vector = early.shape
     programs = [
         placed(join_halves(shard_rows, 8 * cut_a.shape[2], BF16), 0.0, 1.0),
         placed(join_halves(shard_rows, 8 * cut_a.shape[2], BF16), 0.0, 1.0),
-        placed(
-            Sum((FRONT, SIDE), lines, shard_rows, part, by_rows_slot, part),
-            0.1, *spaced(0.9, 0.99, lines + 3),
-        ),
-        placed(Total(jax.ShapeDtypeStruct(vector, F32), lines), 0.9, 0.99),
+        placed(Direct(lines, shard_rows, part, part), 0.1, 0.95),
+        placed(Total(vector, lines, 6, heads), 0.9, 0.93, 0.97),
     ]
     anywhere = [pl.BlockSpec(memory_space=pl.ANY)] * 2
     return pl.pallas_call(
@@ -1873,7 +1980,7 @@
             jax.ShapeDtypeStruct((rows, width), BF16),
         ]
         + [one.out for one in programs],
-        in_specs=in_vmem(12) + anywhere,
+        in_specs=in_vmem(11) + anywhere,
         out_specs=in_vmem(2) + [one.out_spec for one in programs],
         scratch_shapes=[
             pltpu.VMEM((width, part), BF16),
@@ -1898,8 +2005,7 @@
         mlp_sum if cuts else from_line_order(mlp_sum),
         middle,
         bias[None],
-        middle_sums,
-        hidden_sums,
+        early,
         cut_a,
         cut_b,
     )
@@ -1967,7 +2073,7 @@
     shard_rows = down_weight.shape[0]
     hidden_half = hidden_dev // 2
     columns = down_weight.shape[1]
-    first_rows = shard_rows * 3 // 4 // 16 * 16
+    first_rows = shard_rows // 2
     early_rows = shard_rows // 2
     cuts = line_cuts(width, False)
     lines = lax.axis_size("line")
@@ -1981,7 +2087,7 @@
     hops = [0.1 * k for k in range(1, 4)] if lines == 4 else spaced(0.1, 0.3, lines - 1)
     levels = spaced(0.4, 0.98, 2 * lines)
     piece_hops = spaced(0.35, 0.75, lines - 1)
-    _, first_all, early_cut, late_cut, mlp_piece, normed_one, cotangent_line = run_programs(
+    _, first_all, early_cut, late_cut, mlp_piece, normed_one, cotangent_line, proj_line = run_programs(
         [
             placed(spread_halves(first_pieces, columns, BF16), 0.0, 0.05),
             placed(rows_gather(first_cut), 0.01, *hops, *levels, 1.0),
@@ -1990,6 +2096,7 @@
             placed(line_gather((quarters, first_rows, hidden_half), BF16), 0.07, *piece_hops, 1.0),
             placed(Work(norm_work, hidden_in.shape, BF16), 0.31, 0.31),
             placed(Work(functools.partial(reorder_work, cuts or [0]), (half_rows, width), BF16), 0.32, 0.32),
+            placed(line_gather(proj_weight.shape, BF16), 0.305, *spaced(0.48, 0.88, lines - 1), 1.0),
         ],
         [
             lambda more, outs: more[4:6],
@@ -1999,10 +2106,11 @@
             lambda more, outs: outs[0],
             lambda more, outs: more[:3],
             lambda more, outs: more[3],
+            lambda more, outs: more[7],
         ],
         1,
         near=[hidden_in, attn_norm_gain[None], attn_norm_bias[None], out_cotangent],
-        far=[down_weight, up_weight, first_cut],
+        far=[down_weight, up_weight, first_cut, proj_weight],
     )
     if cuts is None:
         cotangent_line = to_line_order(own_half(out_cotangent))
@@ -2011,22 +2119,19 @@
     value_shift = jnp.where(core == 1, value_bias.astype(F32), 0.0)
     first_shift = jnp.concatenate([query_bias.astype(F32), value_shift])
     part_like = (rows_dev, HD)
-    _, query_low, keyval_every, proj_line = run_programs(
+    _, query_low, keyval_every = run_programs(
         [
             placed(Work(part_work, part_like, BF16), 0.0, 0.0),
             placed(Work(query_work, (rows_dev, head_width), BF16), 0.2, 0.2),
             placed(ctx_gather(part_like, BF16), 0.1, 1.0),
-            placed(line_gather(proj_weight.shape, BF16), 0.11, 1.0),
         ],
         [
             lambda more, outs: more[:3],
             lambda more, outs: more[:3],
             lambda more, outs: outs[0],
-            lambda more, outs: more[3],
         ],
         4,
         near=[normed_one, first_all, first_shift[None]],
-        far=[proj_weight],
     )
     keyval_every, early_cut = lax.optimization_barrier((keyval_every, early_cut))
     mlp_early = lax.all_gather(early_cut, "line", axis=0, tiled=False)
@@ -2052,13 +2157,11 @@
 
     up_shift = lax.dynamic_slice_in_dim(up_bias, quarter * hidden_dev, hidden_dev).astype(F32)
     up_shift = up_shift[None]
-    shards = lines * quarters
-    rows_all, act_a, pre_a, back_a, bias_a = forward_products(
+    rows_all, act_a, pre_a, back_a, bias_a, weight_grad_a = forward_products(
         normed_two_line, cotangent_all, mlp_piece, mlp_early, up_shift[:, :hidden_half], 6
     )
     rows_all, act_a, pre_a, back_a = flat(rows_all), flat(act_a), flat(pre_a), flat(back_a)
     cotangent_all = flat(cotangent_all)
-    weight_grad_a = weight_products(cotangent_all, rows_all, act_a, pre_a, shards)
     cut_a = lax.psum_scatter(weight_grad_a, "line", scatter_dimension=0, tiled=True)
     rows_all, weight_grad_a = lax.optimization_barrier((rows_all, weight_grad_a))
     act_b, pre_b, back_both, bias_b = second_products(
@@ -2088,10 +2191,9 @@
     cut_b = lax.psum_scatter(weight_grad_b, "line", scatter_dimension=0, tiled=True)
     cut_a = cut_a.reshape(quarters, 2 * shard_rows, hidden_half)
     cut_b = cut_b.reshape(quarters, 2 * shard_rows, hidden_half)
-    up_bias_parts = jnp.concatenate([bias_a, bias_b], axis=1)
-
-    grad_middle, grad_mixed, proj_weight_grad, middle_sums = middle_back(
-        grad_normed_two, middle, out_cotangent, mixed_low, proj_all, mlp_norm_gain, 8
+
+    grad_middle, grad_mixed, proj_weight_grad, vector = middle_back(
+        grad_normed_two, middle, out_cotangent, mixed_low, proj_all, mlp_norm_gain, bias_a, bias_b, 8
     )
     grad_mixed, cut_a = lax.optimization_barrier((grad_mixed, cut_a))
     sum_proj, proj_parts = rows_sum(proj_weight_grad)
@@ -2112,13 +2214,22 @@
         3,
     )
     grad_table = by_slot(grad_sets, key_slots, slot_count)
-    grad_parts = grad_table.reshape(
-        2, lax.axis_size("line"), lax.axis_size("pair"), rows_dev, HD
-    )
+    grad_parts = grad_table.reshape(2, lines, 2 * rows_dev, HD)
+    along_line, over_pair = ctx_sums(grad_parts)
     query_weight_grad = jnp.einsum("rd,rk->dk", normed_one, grad_query, preferred_element_type=F32)
     sum_query, query_parts = rows_sum(query_weight_grad)
-    grad_part, grad_query_weight = run_programs(
-        [ctx_sum(grad_parts), sum_query], [grad_parts, query_parts], 12
+    _, grad_part, grad_query_weight = run_programs(
+        [
+            placed(along_line, 0.01, 0.75),
+            placed(over_pair, 0.76, 0.86, 0.97),
+            placed(sum_query, 0.0, 1.0),
+        ],
+        [
+            grad_parts,
+            lambda more, outs: outs[0].reshape(2, rows_dev, HD),
+            query_parts,
+        ],
+        12,
     )
     input_grad, layer_out, down_wide, up_wide, grad_part_weight, summed = first_back(
         grad_query,
@@ -2131,33 +2242,31 @@
         mlp_out,
         middle,
         down_bias,
-        middle_sums,
-        up_bias_parts,
+        vector,
         cut_a,
         cut_b,
         9,
     )
     grad_down_weight, grad_up_weight = down_wide.astype(F32), up_wide.astype(F32)
     grad_keyval_weight = in_order(grad_part_weight[:, :HD], grad_part_weight[:, HD:], axis=1)
-    sum_query = lax.dynamic_slice_in_dim(summed[3], core * head_width, head_width)
-    sum_up = jnp.where(core == 0, summed[4], summed[5])[: quarters * hidden_dev]
+    sum_up = summed[:quarters, width : 2 * width - head_width].reshape(quarters * hidden_dev)
     return (
         layer_out,
         input_grad,
         summed[0, :width],
-        summed[0, width : 2 * width],
+        summed[1, :width],
         grad_query_weight,
-        sum_query,
+        summed[6, :head_width],
         grad_keyval_weight,
-        summed[3, 2 * head_width : 2 * head_width + HD],
+        summed[7, :HD],
         grad_proj_weight,
+        summed[4, :width],
         summed[2, :width],
-        summed[1, :width],
-        summed[1, width : 2 * width],
+        summed[3, :width],
         grad_up_weight,
         sum_up,
         grad_down_weight,
-        summed[2, width : 2 * width],
+        summed[5, :width],
     )
 
 

time: 620 us -> 580 us (0.935)
  Pallas kernels: 570 us -> 531 us
    pallas_call x1, Pallas kernels: 75.9 us -> 46.2 us  [first_back(): pl.pallas_call(functools.partial(first_back_kernel, cuts, programs), out_...]
    pallas_call x1 -> x0, Pallas kernels: 15.7 us -> none  [weight_products(): pl.pallas_call(weight_kernel, grid=(steps,), out_shape=jax.ShapeDtypeStru...]
    pallas_call x1, Pallas kernels: 51.8 us -> 61.4 us  [forward_products(): pl.pallas_call(forward_kernel, out_shape=[jax.ShapeDtypeStruct(lead + (wi...]
  transfers between devices with their start and end apart: 4 -> 4, of which waited for: 0 -> 0; matrix products, arithmetic and copies ran while one was open for 2% -> 2% of each run, Pallas kernels for 63% -> 67%
where the time goes in v6:
time: 580 us; the launch traced here: 579 us
  Pallas kernels  531 us (92%)
  local copies, waits for them, and re-layouts  19 us (3%)
  between operations  14 us (2%)
  other arithmetic  10.2 us (2%)
    pallas_call x3, Pallas kernels, run_programs(): pl.pallas_call(kernel, out_shape=[one.out for one in programs], in_specs=...  151 us
    pallas_call x1, Pallas kernels, attend_back(): pl.pallas_call(functools.partial(attend_back_kernel, programs, blocks * h...  79.1 us
    pallas_call x1, Pallas kernels, attend(): pl.pallas_call(functools.partial(attend_kernel, programs, blocks * heads)...  76.4 us
    pallas_call x1, Pallas kernels, forward_products(): pl.pallas_call(forward_kernel, out_shape=[jax.ShapeDtypeStruct(lead + (wi...  61.4 us
    pallas_call x1, Pallas kernels, grad_products(): pl.pallas_call(functools.partial(grads_kernel, programs, steps), grid=(st...  50.5 us
    pallas_call x1, Pallas kernels, first_back(): pl.pallas_call(functools.partial(first_back_kernel, cuts, programs), out_...  46.2 us
    pallas_call x1, Pallas kernels, second_products(): pl.pallas_call(second_kernel, grid=(steps,), out_shape=[jax.ShapeDtypeStr...  28.5 us
    pallas_call x1, Pallas kernels, middle_back(): pl.pallas_call(functools.partial(middle_back_kernel, cuts), out_shape=[ja...  19.6 us
  transfers between devices with their start and end apart: 4, of which 0 were waited for; matrix products, arithmetic and copies ran while one was open for 2% of the time, Pallas kernels for 67%

profile of v6, /device:TPU:0, one launch (start us, length us, event | category | flops | bytes accessed | tf_op | source)
XLA Modules:
  0.0 579.3 jit_solution(13092749892883122067)
XLA Ops:
  7.2 0.7 convert_element_type.16
  7.9 0.7 broadcast_select_fusion
  9.2 1.3 broadcast_in_dim.54.refs_1_.refs_5_
  10.5 1.3 broadcast_in_dim.55.refs_2_
  11.8 1.7 pad_maximum_fusion.refs_6_
  13.5 71.0 %shard_map.288 = (bf16[4,64,512]{2,1,0:T(8,128)(2,1)}, bf16[2,4,2,128,1152]{4,3,2,1,0:T(8,128)(2,1)}, bf16[4,256,512]{2,1,0:T(8,128)(2,1)}, bf16[4,192,512]{2,1,...) custom-call(bf16[512,2048]{1,0:T(8,128)(2,1)} %refs_3_.3, ...), custom_call_target="tpu_custom_call" | custom-call | flops 1 | bytes 1 | tf_op jit(solution)/shard_map/pallas_call | solution.py:739
  84.5 26.6 %shard_map.289 = (bf16[512,128]{1,0:T(8,128)(2,1)}, bf16[512,1024]{1,0:T(8,128)(2,1)}, bf16[2,4,2,512,128]{4,3,2,1,0:T(8,128)(2,1)}) custom-call(bf16[512,2048]{1,0:T(8,128)(2,1)} %get-tuple-element.67.refs_0_.refs_4_, bf16[2048,1152]{1,0:T(8,128)(2,1)} %bitcast.57, f32[1,1152]{1,0:T(1,128)} %broadcast_in_dim.57.refs_2_), custom_call_target="tpu_custom_call" | custom-call | flops 1 | bytes 1 | tf_op jit(solution)/shard_map/pallas_call | solution.py:739
  111.6 0.7 gather_fusion
  113.6 76.4 %shard_map.290 = (bf16[512,1024]{1,0:T(8,128)(2,1)}, f32[2,8,1,256]{3,2,1,0:T(1,128)}, bf16[2,4,2,128,1024]{4,3,2,1,0:T(8,128)(2,1)}, bf16[2,2,2,256,2048]{4,3,2,1,0:T(8,128)(2,1)}) custom-call(s32[2]{0:T(128)} %and_select_fusion.2.refs_0_, s32[2,9]{1,0:T(2,128)} %pad_add_fusion.refs_1_.slot_ref, bf16[512,1024]{1,0:T(8,128)(2,1)} %get-tuple-element.69.refs_2_, ...), custom_call_target="tpu_custom_call" | custom-call | flops 1 | bytes 1 | tf_op jit(solution)/shard_map/pallas_call | solution.py:901
  192.1 0.7 dynamic-slice_convert_fusion
  193.4 13.2 %shard_map.291 = (f32[256,2048]{1,0:T(8,128)}, bf16[256,2048]{1,0:T(8,128)(2,1)}) custom-call(bf16[512,1024]{1,0:T(8,128)(2,1)} %get-tuple-element.79.mixed_ref.refs_4_, bf16[2048,1024]{1,0:T(8,128)(2,1)} %bitcast.59, bf16[512,2048]{1,0:T(8,128)(2,1)} %refs_3_.3, bf16[1,2048]{1,0:T(2,128)(2,1)} %broadcast_in_dim.58.bias_ref, ...), custom_call_target="tpu_custom_call" | custom-call | flops 1 | bytes 1 | tf_op jit(solution)/shard_map/pallas_call | solution.py:1709
  206.6 61.4 %shard_map.292 = (bf16[2,2,2,256,2048]{4,3,2,1,0:T(8,128)(2,1)}, bf16[2,2,2,256,512]{4,3,2,1,0:T(8,128)(2,1)}, bf16[2,2,2,256,512]{4,3,2,1,0:T(8,128)(2,1)}, bf1...) custom-call(bf16[256,2048]{1,0:T(8,128)(2,1)} %get-tuple-element.81.x_ref, ...), custom_call_target="tpu_custom_call" | custom-call | flops 1 | bytes 1 | tf_op jit(solution)/shard_map/pallas_call | solution.py:1306
  268.3 28.5 %shard_map.293 = (bf16[2048,512]{1,0:T(8,128)(2,1)}, bf16[2048,512]{1,0:T(8,128)(2,1)}, bf16[2048,2048]{1,0:T(8,128)(2,1)}, f32[8,512]{1,0:T(8,128)}) custom-call(bf16[2048,2048]{1,0:T(8,128)(2,1)} %bitcast.55, bf16[2048,2048]{1,0:T(8,128)(2,1)} %bitcast.50, bf16[2048,2048]{1,0:T(8,128)(2,1)} %bitcast.68, ...), custom_call_target="tpu_custom_call" | custom-call | flops 1 | bytes 1 | tf_op jit(solution)/shard_map/pallas_call | solution.py:1409
  296.8 50.5 %shard_map.294 = (bf16[2048,2048]{1,0:T(8,128)(2,1)}, bf16[16,2,128,512]{3,2,1,0:T(8,128)(2,1)}, f32[256,2048]{1,0:T(8,128)}) custom-call(bf16[2048,2048]{1,0:T(8,128)(2,1)} %bitcast.51, bf16[2048,2048]{1,0:T(8,128)(2,1)} %bitcast.56, bf16[2048,512]{1,0:T(8,128)(2,1)} %bitcast.71, bf16[2048,512]{1,0:T(8,128)(2,1)} %get-tuple-element.90.refs_3_, ...), custom_call_target="tpu_custom_call" | custom-call | flops 1 | bytes 1 | tf_op jit(solution)/shard_map/pallas_call | solution.py:1483
  348.6 19.6 %shard_map.295 = (f32[256,2048]{1,0:T(8,128)}, bf16[512,1024]{1,0:T(8,128)(2,1)}, bf16[2048,1024]{1,0:T(8,128)(2,1)}, f32[8,2048]{1,0:T(8,128)}) custom-call(f32[256,2048]{1,0:T(8,128)} %get-tuple-element.93.sum_ref, f32[256,2048]{1,0:T(8,128)} %get-tuple-element.94.middle_ref.refs_8_, bf16[512,2048]{1,0:T(8,128)(2,1)} %cotangent_ref.1, ...), custom_call_target="tpu_custom_call" | custom-call | flops 1 | bytes 1 | tf_op jit(solution)/shard_map/pallas_call | solution.py:1804
  368.2 79.1 %shard_map.296 = (bf16[512,1024]{1,0:T(8,128)(2,1)}, f32[2,2304,256]{2,1,0:T(8,128)}, f32[128,1024]{1,0:T(8,128)}, f32[256,2048]{1,0:T(8,128)}) custom-call(s32[2]{0:T(128)} %and_select_fusion.2.refs_0_, s32[2,9]{1,0:T(2,128)} %pad_add_fusion.refs_1_.slot_ref, bf16[512,1024]{1,0:T(8,128)(2,1)} %get-tuple-element.69.refs_2_, ...), custom_call_target="tpu_custom_call" | custom-call | flops 1 | bytes 1 | tf_op jit(solution)/shard_map/pallas_call | solution.py:989
  447.3 5.2 shard_map.297
  452.5 4.4 convolution_convert_fusion
  456.8 53.4 %shard_map.298 = (bf16[1024,128]{1,0:T(8,128)(2,1)}, f32[512,128]{1,0:T(8,128)}, f32[128,1024]{1,0:T(8,128)}) custom-call(bf16[2,4,1024,128]{3,2,1,0:T(8,128)(2,1)} %bitcast.66, bf16[2,4,2,128,1024]{4,3,2,1,0:T(8,128)(2,1)} %bitcast.70), custom_call_target="tpu_custom_call" | custom-call | flops 1 | bytes 1 | tf_op jit(solution)/shard_map/pallas_call | solution.py:739
  510.3 46.2 %shard_map.299 = (bf16[512,2048]{1,0:T(8,128)(2,1)}, bf16[512,2048]{1,0:T(8,128)(2,1)}, bf16[128,4096]{1,0:T(8,128)(2,1)}, bf16[128,4096]{1,0:T(8,128)(2,1)}, f32[128,256]{1,0:T(8,128)}, /*index=5*/f32[8,4096]{1,0:T(8,128)}) custom-call(bf16[512,1024]{1,0:T(8,128)(2,1)} %get-tuple-element.102.refs_0_, f32[512,128]{1,0:T(8,128)} %get-tuple-element.104.refs_1_, ...), custom_call_target="tpu_custom_call" | custom-call | flops 1 | bytes 1 | tf_op jit(solution)/shard_map/pallas_call | solution.py:1976
  556.5 1.3 slice_bitcast_fusion.1
  557.8 1.4 slice.43
  559.2 0.8 slice_bitcast_fusion
  559.9 1.7 fusion.1
  562.3 2.8 convert_element_type.19
  565.0 1.5 convert_element_type.20
  566.6 0.7 pad_maximum_fusion.1
  567.5 1.3 copy.40
  568.8 1.0 copy-done.3
  569.8 1.3 copy.41
  571.2 0.8 copy.42
  572.0 0.8 copy.43
  (61 shorter events, 7.6 us)
Async XLA Ops:
  7.2 4.6 copy-start
  7.2 182.8 %all-gather.5.cloned.1.call-start = ((), (), s32[]{:S(2)}) async-start(), calls=%async_computation.4 | async-start | bytes 5242880 | tf_op jit(solution)/shard_map/all_gather | solution.py:2137
  84.5 26.7 %copy-start.14 = (s32[1,16]{1,0:T(1,128)S(1)}, s32[1,16]{1,0:T(1,128)}, u32[]{:S(2)}) copy-start(s32[1,16]{1,0:T(1,128)} %param.18) | copy-start | bytes 196
  111.1 157.1 %all-gather.7.cloned.1.call-start = ((), (), s32[]{:S(2)}) async-start(), calls=%async_computation.5 | async-start | bytes 3932160 | tf_op jit(solution)/shard_map/all_gather | solution.py:2153
  113.6 76.7 %copy-start.10 = (bf16[2048]{0:T(1024)(128)(2,1)S(1)}, bf16[2048]{0:T(1024)(128)(2,1)}, u32[]{:S(2)}) copy-start(bf16[2048]{0:T(1024)(128)(2,1)} %param.27) | copy-start | bytes 12292
  113.6 77.3 %copy-start.11 = (bf16[2048]{0:T(1024)(128)(2,1)S(1)}, bf16[2048]{0:T(1024)(128)(2,1)}, u32[]{:S(2)}) copy-start(bf16[2048]{0:T(1024)(128)(2,1)} %param.26) | copy-start | bytes 12292
  113.6 78.0 %copy-start.12 = (bf16[2048]{0:T(1024)(128)(2,1)S(1)}, bf16[2048]{0:T(1024)(128)(2,1)}, u32[]{:S(2)}) copy-start(bf16[2048]{0:T(1024)(128)(2,1)} %param.28) | copy-start | bytes 12292
  190.1 178.1 %reduce-scatter.3.cloned.1.call-start = ((), (), s32[]{:S(2)}) async-start(), calls=%async_computation.2 | async-start | bytes 5242880 | tf_op jit(solution)/shard_map/reduce_scatter | solution.py:2165
  268.0 242.3 %reduce-scatter.5.cloned.1.call-start = ((), (), s32[]{:S(2)}) async-start(), calls=%async_computation.3 | async-start | bytes 5242880 | tf_op jit(solution)/shard_map/reduce_scatter | solution.py:2191
  347.3 0.7 copy-start.13
  447.3 5.2 copy-start.2
  447.3 5.2 copy-start.6
  556.5 8.5 %copy-start.5 = (bf16[128,4096]{1,0:T(8,128)(2,1)S(1)}, bf16[128,4096]{1,0:T(8,128)(2,1)}, u32[]{:S(2)}) copy-start(bf16[128,4096]{1,0:T(8,128)(2,1)} %get-tuple-element.117) | copy-start | bytes 3145732
  565.0 1.5 copy-start.9
  565.0 2.4 copy-start.4
  567.4 2.3 copy-start.3
  569.8 1.4 copy-start.8
  569.8 2.2 copy-start.7
  569.8 3.0 copy-start.1
Sparse Core Ops, SparseCore 0:
  111.3 78.7 all-gather.4
  191.6 62.1 all-gather.6
  268.1 74.9 reduce-scatter.2
  347.5 91.5 reduce-scatter.4

commit v7 on v6

--- a/solution.py
+++ b/solution.py
@@ -196,6 +196,8 @@
 
 
 class Sum:
+    far_line = True
+
     def __init__(self, steps, lines, rows, columns, slot, kind=F32):
         self.steps, self.lines, self.rows, self.columns = steps, lines, rows, columns
         self.slot = slot
@@ -210,10 +212,10 @@
         return (
             [pltpu.VMEM((lines, sizes[0]) + block, BF16)]
             + [pltpu.VMEM((lines, size) + block, BF16) for size in sizes]
-            + [pltpu.VMEM((2, lines) + (block if lines > 1 else (16, 128)), BF16)]
+            + [pltpu.VMEM((lines,) + (block if lines > 1 else (16, 128)), BF16)]
             + [pltpu.SemaphoreType.DMA((lines, sizes[0]))]
             + [pltpu.SemaphoreType.DMA((lines, size)) for size in sizes] * 2
-            + [pltpu.SemaphoreType.DMA((2, lines))] * 2
+            + [pltpu.SemaphoreType.DMA((lines,))] * 2
         )
 
     def stages(self, me, x_ref, out_ref, own, *rest):
@@ -277,18 +279,13 @@
                 if k + 1 < count and bits >> (k + 1) & 1:
                     copy(k + 1, shard, bits).start()
 
-        def line_inside(amount):
-            there = my_line + amount
-            return (there >= 0) & (there < lines)
-
-        def line_copy(amount, shard):
-            way = (amount + 1) // 2
+        def line_copy(shard):
             return remote(
-                on_line.at[way, shard],
-                on_line.at[way, shard],
-                line_send.at[way, shard],
-                line_recv.at[way, shard],
-                along(me, amount),
+                held[last].at[shard, 0],
+                on_line.at[my_line],
+                line_send.at[shard],
+                line_recv.at[my_line],
+                along(me, shard - my_line),
             )
 
         def each(distance, work):
@@ -299,21 +296,6 @@
                 shard = my_line + amount * distance
                 pl.when((shard >= 0) & (shard < lines))(functools.partial(work, shard, amount))
 
-        def line_step(shard, amount):
-            done = held[last].at[shard, 0]
-            moving = on_line.at[(amount + 1) // 2, shard]
-
-            @pl.when(line_inside(-amount))
-            def _():
-                line_copy(amount, shard).wait_recv()
-                add_blocks(moving, rows_of(moving), rows_of(done), rows)
-
-            @pl.when(jnp.logical_not(line_inside(-amount)))
-            def _():
-                add_blocks(moving, rows_of(done), None, rows)
-
-            line_copy(amount, shard).start()
-
         order = list(reversed(range(lines)))
 
         def begin():
@@ -327,39 +309,31 @@
                 index = number - k
                 if 0 <= index < lines:
                     each(order[index], functools.partial(take_step, k))
-            index = number - count
-            if 0 <= index < lines and order[index] > 0:
-                each(order[index], line_step)
+                    if k == last and order[index] > 0:
+                        each(order[index], lambda shard, amount: line_copy(shard).start())
 
         def end():
             final = held[last].at[my_line, 0]
             if lines == 1:
                 add_blocks(out_ref, rows_of(final), None, rows)
             else:
-                for way, amount in enumerate((-1, 1)):
-
-                    @pl.when(line_inside(-amount))
-                    def _():
-                        line_copy(amount, my_line).wait_recv()
-
-                    @pl.when(jnp.logical_not(line_inside(-amount)))
-                    def _():
-                        add_blocks(on_line.at[way, my_line], lambda cut: jnp.zeros_like(final[cut, :]), None, rows)
-
-                left, right = on_line.at[0, my_line], on_line.at[1, my_line]
+                add_blocks(on_line.at[my_line], rows_of(final), None, rows)
+
+                def arrived(shard, amount):
+                    remote(
+                        on_line.at[shard], on_line.at[shard], line_send.at[0], line_recv.at[shard], me
+                    ).wait_recv()
+
+                for distance in range(1, lines):
+                    each(distance, arrived)
                 add_blocks(
                     out_ref,
-                    lambda cut: final[cut, :].astype(F32) + left[cut, :].astype(F32),
-                    rows_of(right),
+                    lambda cut: sum(on_line[shard, cut, :].astype(F32) for shard in range(lines)),
+                    None,
                     rows,
                 )
-
-                for amount in (1, -1):
-                    for distance in range(1, lines):
-                        shard = my_line + amount * distance
-                        pl.when((shard >= 0) & (shard < lines))(
-                            lambda amount=amount, shard=shard: line_copy(amount, shard).wait_send()
-                        )
+                for distance in range(1, lines):
+                    each(distance, lambda shard, amount: line_copy(shard).wait_send())
             for k in range(count):
                 for shard in range(lines):
                     for bits in parts_of(k):
@@ -370,7 +344,7 @@
                 functools.partial(take_step, k, 0, 0, [bits]) for k in range(count) for bits in parts_of(k)
             ]
         else:
-            ticks = [functools.partial(tick, number) for number in range(lines + count)]
+            ticks = [functools.partial(tick, number) for number in range(lines + count - 1)]
         return [begin] + ticks + [end]
 
 
@@ -653,7 +627,8 @@
     for one in programs:
         lines = max(lines, one.lines)
         if one.lines > 1:
-            reach = max(reach, one.lines - 1 if hasattr(one, "everyone") else 1)
+            far = hasattr(one, "everyone") or hasattr(one, "far_line")
+            reach = max(reach, one.lines - 1 if far else 1)
         if hasattr(one, "everyone"):
             plane |= set(range(1, 8))
         if isinstance(one, Exchange) or hasattr(one, "rows_too"):
@@ -841,12 +816,14 @@
         if place < 1:
             pl.when(step == int(place * steps))(work)
         else:
-            late.append(work)
-
-    def finish():
+            late.append((place, work))
+
+    def finish(own=None):
         @pl.when(step == steps - 1)
         def _():
-            for work in late:
+            early = [work for place, work in late if place < 1.05]
+            rest = [work for place, work in late if place >= 1.05]
+            for work in early + ([own] if own else []) + rest:
                 work()
 
     return finish
@@ -935,11 +912,11 @@
 def attend_back_kernel(programs, steps, *refs):
     count = len(programs)
     (position_ref, slot_ref, query_ref, grad_ref, mixed_ref), refs = refs[:5], refs[5:]
-    (logsum_ref, table_ref), refs = refs[:2], refs[2:]
+    (logsum_ref, table_ref, normed_ref), refs = refs[:3], refs[3:]
     others, refs = refs[:count], refs[count:]
-    (grad_query_ref, set_ref), refs = refs[:2], refs[2:]
+    (grad_query_ref, set_ref, weight_ref), refs = refs[:3], refs[3:]
     other_outs, refs = refs[:count], refs[count:]
-    (bias_ref, key_t_ref), scratch = refs[:2], refs[2:]
+    (bias_ref, key_t_ref, kept_ref), scratch = refs[:3], refs[3:]
     chunks = PBLK + 1
     scale = HD**-0.5
     block, head = pl.program_id(0), pl.program_id(1)
@@ -970,17 +947,31 @@
         grad_query = grad_query + jnp.dot(
             key_t_ref[chunk], grad_score, preferred_element_type=F32
         )
-    grad_query_ref[...] = (grad_query * scale).T.astype(BF16)
+    grad_query = (grad_query * scale).T.astype(BF16)
+    grad_query_ref[...] = grad_query
+    kept_ref[block, head] = grad_query
 
     @pl.when(head == pl.num_programs(1) - 1)
     def _():
         set_ref[0, :, :HD] = set_ref[0, :, :HD] * scale
 
-    finish()
+    def weights():
+        blocks, heads = kept_ref.shape[:2]
+        kept = [
+            jnp.concatenate([kept_ref[b, h] for h in range(heads)], axis=1) for b in range(blocks)
+        ]
+        kept = jnp.concatenate(kept, axis=0)
+
+        def work(cut):
+            weight_ref[cut, :] = by_columns(normed_ref[:, cut], kept).astype(BF16)
+
+        each_columns(weight_ref.shape[0], 256, work)
+
+    finish(weights)
 
 
 def attend_back(
-    queries, grads, mixed, logsums, table, positions, key_slots, programs, arrays, number
+    queries, grads, mixed, logsums, table, normed, positions, key_slots, programs, arrays, number
 ):
     rows, width = queries.shape
     blocks, heads = rows // BLK, width // HD
@@ -992,6 +983,7 @@
         out_shape=[
             jax.ShapeDtypeStruct((rows, width), BF16),
             jax.ShapeDtypeStruct((blocks, count, 2 * HD), F32),
+            jax.ShapeDtypeStruct((normed.shape[1], width), BF16),
         ]
         + [one.out for one in programs],
         in_specs=[
@@ -1002,21 +994,27 @@
             by_head,
             pl.BlockSpec((1, 1, 1, BLK), lambda b, h: (b, h, 0, 0)),
             pl.BlockSpec(memory_space=pltpu.VMEM),
+            pl.BlockSpec(memory_space=pltpu.VMEM),
         ]
         + [one.in_spec for one in programs],
-        out_specs=[by_head, pl.BlockSpec((1, count, 2 * HD), lambda b, h: (b, 0, 0))]
+        out_specs=[
+            by_head,
+            pl.BlockSpec((1, count, 2 * HD), lambda b, h: (b, 0, 0)),
+            pl.BlockSpec(memory_space=pltpu.VMEM),
+        ]
         + [one.out_spec for one in programs],
         scratch_shapes=[
             pltpu.VMEM((PBLK + 1, BLK, BLK), F32),
             pltpu.VMEM((PBLK + 1, HD, BLK), BF16),
+            pltpu.VMEM((blocks, heads, BLK, HD), BF16),
         ]
         + [held for one in programs for held in one.scratch()],
         compiler_params=pltpu.CompilerParams(
             collective_id=number, has_side_effects=True, vmem_limit_bytes=VMEM_BYTES
         ),
         cost_estimate=SMALL,
-    )(positions, key_slots, queries, grads, mixed, logsums, table, *arrays)
-    return out[0], out[1], out[2:]
+    )(positions, key_slots, queries, grads, mixed, logsums, table, normed, *arrays)
+    return out[0], out[1], out[2], out[3:]
 
 
 def by_slot_kernel(slot_ref, set_ref, out_ref, table_ref):
@@ -1197,7 +1195,7 @@
             )
             return carry
 
-        lax.fori_loop(0, hidden // tile, one, 0)
+        lax.fori_loop(0, hidden // tile, one, 0, unroll=True)
 
     def back(number):
         slot = number % 2
@@ -1209,7 +1207,7 @@
             part_own[slot, :, cut] = rows_by_rows(pre_own[slot], up).astype(BF16)
             return carry
 
-        lax.fori_loop(0, width // tile, one, 0)
+        lax.fori_loop(0, width // tile, one, 0, unroll=2)
 
     def grads(number):
         slot = number % 2
@@ -1231,7 +1229,7 @@
                     weight_grad_ref[shards, kind] = grad
             return carry
 
-        lax.fori_loop(0, width // tile, one, 0)
+        lax.fori_loop(0, width // tile, one, 0, unroll=2)
 
     def pass_on(bits, *ways):
         arrived(bits)
@@ -1338,173 +1336,269 @@
     )(rows, cotangent_all, piece, early, shift)
 
 
+CHIPS = ((1, 1), (1, 0), (0, 1), (0, 0))
+
+
 def second_kernel(
     rows_ref,
     cotangent_ref,
     before_ref,
+    rows_columns_ref,
+    cotangent_columns_ref,
+    act_a_ref,
     piece_ref,
     early_ref,
     late_ref,
     shift_ref,
-    act_ref,
-    pre_ref,
-    part_ref,
+    down_part_ref,
+    weight_grad_ref,
     bias_ref,
+    sum_ref,
     up_own,
-    down_own,
+    downs,
+    acts,
+    pre_own,
+    rows_own,
+    cotangent_own,
+    before_own,
+    part_own,
+    over_core,
+    over_front,
+    over_side,
     weight_sem,
+    load_sem,
+    core_send,
+    core_recv,
+    front_send,
+    front_recv,
+    side_sem,
 ):
     step = pl.program_id(0)
-    width, hidden = rows_ref.shape[1], act_ref.shape[1]
-
-    @pl.when(step == 0)
+    me = here()
+    core = me["tp"]
+    width, hidden = rows_ref.shape[1], pre_own.shape[1]
+    count = rows_ref.shape[0] // 4
+    half = count // 2
+    tile = 256
+    places = (piece_ref, early_ref, late_ref)
+    shard_rows, first = up_own.shape[2], piece_ref.shape[2]
+
+    def chip(number):
+        up, side = CHIPS[number]
+        fsdp = me["fsdp"] + up * (1 - 2 * me["fsdp"])
+        return fsdp, me["pair"] + side * (1 - 2 * me["pair"])
+
+    def rows_of_chip(number):
+        fsdp, pair = chip(number)
+        return pl.ds(pl.multiple_of((fsdp * 2 + pair) * count, count), count)
+
+    def loads(number):
+        slot, rows = number % 2, rows_of_chip(number)
+        pairs = ((rows_ref, rows_own), (cotangent_ref, cotangent_own), (before_ref, before_own))
+        return [
+            pltpu.make_async_copy(source.at[rows], target.at[slot], load_sem.at[slot, kind])
+            for kind, (source, target) in enumerate(pairs)
+        ]
+
+    def second_weights():
+        down_parts, up_parts = second_half(shard_rows, first, places)
+        copies = weight_copies(down_parts, downs.at[1], weight_sem.at[0])
+        return copies + weight_copies(up_parts, up_own, weight_sem.at[1])
+
+    def first_weights():
+        copies = weight_copies(first_half(shard_rows, first, places)[0], downs.at[0], weight_sem.at[2])
+        return copies + [pltpu.make_async_copy(act_a_ref, acts.at[0], weight_sem.at[1, 1])]
+
+    def to_core(number):
+        fsdp, pair = chip(number)
+        up, side = CHIPS[number]
+        return remote(
+            part_own.at[fsdp, pair, 1 - core],
+            over_core.at[up, side],
+            core_send.at[up, side],
+            core_recv.at[up, side],
+            flip(me, "tp"),
+        )
+
+    def take_core(number):
+        fsdp, pair = chip(number)
+        to_core(number).wait_recv()
+        held = over_core.at[CHIPS[number]]
+        add_blocks(held, rows_of(part_own.at[fsdp, pair, core]), rows_of(held), half)
+
+    def to_front(corner):
+        source = over_core.at[1, 1] if corner else over_core.at[1 - core, core]
+        return remote(
+            source, over_front.at[corner], front_send.at[corner], front_recv.at[corner], flip(me, FRONT)
+        )
+
+    def to_side():
+        return remote(over_front.at[1], over_side, side_sem.at[0], side_sem.at[1], flip(me, SIDE))
+
+    def take_front(corner):
+        to_front(corner).wait_recv()
+        held = over_front.at[corner]
+        mine = over_core.at[core, 1 - core] if corner else over_core.at[0, 0]
+        add_blocks(held, rows_of(mine), rows_of(held), half)
+
+    def products(number):
+        slot, rows = number % 2, rows_of_chip(number)
+
+        def one(index, carry):
+            cut = pl.ds(pl.multiple_of(index * tile, tile), tile)
+            down = downs[1, :, :, :, cut].reshape(width, tile)
+            up = up_own[:, :, :, cut].reshape(width, tile)
+            grad_act = jnp.dot(cotangent_own[slot], down, preferred_element_type=F32)
+            value = jnp.dot(rows_own[slot], up, preferred_element_type=F32) + shift_ref[:, cut]
+            act, grad_pre = gelu_both(value, grad_act)
+            acts[1, rows, cut] = act.astype(BF16)
+            grad_pre = grad_pre.astype(BF16)
+            pre_own[rows, cut] = grad_pre
+            bias_ref[:, cut] += fold_rows(grad_pre.astype(F32))
+            return carry
+
+        lax.fori_loop(0, hidden // tile, one, 0, unroll=True)
+        tile_back = up_own.shape[1] * shard_rows
+        fsdp, pair = chip(number)
+
+        def back(index, carry):
+            cut = pl.ds(pl.multiple_of(index * tile_back, tile_back), tile_back)
+            up = up_own[index].reshape(tile_back, hidden)
+            part = before_own[slot, :, cut].astype(F32) + rows_by_rows(pre_own[rows, :], up)
+            part_own[fsdp, pair, :, :, cut] = part.astype(BF16).reshape(2, half, tile_back)
+            return carry
+
+        lax.fori_loop(0, width // tile_back, back, 0, unroll=2)
+
+    def chunk_step(number):
+        if number == 0:
+            barrier = pltpu.get_barrier_semaphore()
+            for bits in (1, 2, 4):
+                pl.semaphore_signal(
+                    barrier, inc=1, device_id=plane_partner(me, bits), device_id_type=MESH_ID
+                )
+            for one in loads(0) + second_weights() + first_weights():
+                one.start()
+            bias_ref[...] = jnp.zeros_like(bias_ref)
+            for one in second_weights():
+                one.wait()
+            pl.semaphore_wait(barrier, 3)
+        for one in loads(number):
+            one.wait()
+        if number < 3:
+            for one in loads(number + 1):
+                one.start()
+        products(number)
+        to_core(number).start()
+        if number > 0:
+            take_core(number - 1)
+        if number == 1:
+            to_front(1).start()
+        if number == 2:
+            pl.when(core == 0)(lambda: to_front(0).start())
+        if number == 3:
+            pl.when(core == 1)(lambda: to_front(0).start())
+            for one in first_weights():
+                one.wait()
+
+    for number in range(4):
+        pl.when(step == number)(functools.partial(chunk_step, number))
+
+    @pl.when(step == 4)
     def _():
-        down_parts, up_parts = second_half(
-            up_own.shape[2], piece_ref.shape[2], (piece_ref, early_ref, late_ref)
-        )
-        weights = weight_copies(down_parts, down_own, weight_sem)
-        weights += weight_copies(up_parts, up_own, weight_sem.at[2:])
-        for one in weights:
-            one.start()
-        bias_ref[...] = jnp.zeros_like(bias_ref)
-        for one in weights:
-            one.wait()
-
-    tile = 256
-
-    def one(index, carry):
-        cut = pl.ds(pl.multiple_of(index * tile, tile), tile)
-        down = down_own[:, :, :, cut].reshape(width, tile)
-        up = up_own[:, :, :, cut].reshape(width, tile)
-        grad_act = jnp.dot(cotangent_ref[...], down, preferred_element_type=F32)
-        value = jnp.dot(rows_ref[...], up, preferred_element_type=F32) + shift_ref[:, cut]
-        act, grad_pre = gelu_both(value, grad_act)
-        act_ref[:, cut] = act.astype(BF16)
-        grad_pre = grad_pre.astype(BF16)
-        pre_ref[:, cut] = grad_pre
-        bias_ref[:, cut] += fold_rows(grad_pre.astype(F32))
-        return carry
-
-    lax.fori_loop(0, hidden // tile, one, 0)
-    tile_back = up_own.shape[1] * up_own.shape[2]
-
-    def back(index, carry):
-        cut = pl.ds(pl.multiple_of(index * tile_back, tile_back), tile_back)
-        up = up_own[index].reshape(tile_back, hidden)
-        part = before_ref[:, cut].astype(F32) + rows_by_rows(pre_ref[...], up)
-        part_ref[:, cut] = part.astype(BF16)
-        return carry
-
-    lax.fori_loop(0, width // tile_back, back, 0)
-
-
-def second_products(rows_all, cotangent_all, before, piece, early, late, shift):
+        take_core(3)
+
+    @pl.when(step == 5)
+    def _():
+        take_front(1)
+        to_side().start()
+
+    @pl.when(step == 9)
+    def _():
+        take_front(0)
+
+    @pl.when(step >= 4)
+    def _():
+        rows_here = down_part_ref.shape[0]
+        rows = pl.ds(pl.multiple_of((step - 4) * rows_here, rows_here), rows_here)
+        shards = weight_grad_ref.shape[0]
+        for kind, (left, right) in enumerate(
+            ((cotangent_columns_ref, acts.at[1]), (rows_columns_ref, pre_own))
+        ):
+            grad = by_columns(left[...], right[...]).astype(BF16)
+            weight_grad_ref[:, kind] = grad.reshape(shards, shard_rows, hidden)
+        part = rows_by_rows(acts[0, rows, :], downs[0].reshape(width, hidden))
+        part = part + rows_by_rows(acts[1, rows, :], downs[1].reshape(width, hidden))
+        down_part_ref[...] = part.astype(BF16)
+
+    @pl.when(step == pl.num_programs(0) - 1)
+    def _():
+        to_side().wait_recv()
+        final = over_front.at[0]
+        add_blocks(sum_ref, rows_of(final), rows_of(over_side), half)
+        for number in range(4):
+            to_core(number).wait_send()
+        for corner in range(2):
+            to_front(corner).wait_send()
+        to_side().wait_send()
+
+
+def second_products(rows_all, cotangent_all, before, act_a, piece, early, late, shift, number):
     rows, width = rows_all.shape
     lines, quarters, _, hidden = late.shape
-    weights = (lines, quarters, width // (lines * quarters), hidden)
-    steps = 4
-    wide = pl.BlockSpec((rows // steps, width), lambda i: (i, 0))
-    narrow = pl.BlockSpec((rows // steps, hidden), lambda i: (i, 0))
+    shards, shard_rows = lines * quarters, width // (lines * quarters)
+    weights = (lines, quarters, shard_rows, hidden)
+    steps, tiles, half = 12, 8, rows // 8
+
+    def tile(i):
+        return jnp.maximum(i - 4, 0)
+
+    columns = pl.BlockSpec((rows, width // tiles), lambda i: (0, tile(i)))
     anywhere = pl.BlockSpec(memory_space=pl.ANY)
+    fixed = lambda shape: pl.BlockSpec(shape, lambda i: (0,) * len(shape))
     return pl.pallas_call(
         second_kernel,
         grid=(steps,),
         out_shape=[
-            jax.ShapeDtypeStruct((rows, hidden), BF16),
-            jax.ShapeDtypeStruct((rows, hidden), BF16),
             jax.ShapeDtypeStruct((rows, width), BF16),
+            jax.ShapeDtypeStruct((shards, 2, shard_rows, hidden), BF16),
             jax.ShapeDtypeStruct((8, hidden), F32),
+            jax.ShapeDtypeStruct((half, width), F32),
         ],
-        in_specs=[wide] * 3 + [anywhere] * 3 + [pl.BlockSpec((1, hidden), lambda i: (0, 0))],
-        out_specs=[narrow, narrow, wide, pl.BlockSpec((8, hidden), lambda i: (0, 0))],
+        in_specs=[anywhere] * 3 + [columns] * 2 + [anywhere] * 4 + [fixed((1, hidden))],
+        out_specs=[
+            pl.BlockSpec((rows // tiles, width), lambda i: (tile(i), 0)),
+            pl.BlockSpec((shards // tiles, 2, shard_rows, hidden), lambda i: (tile(i), 0, 0, 0)),
+            fixed((8, hidden)),
+            fixed((half, width)),
+        ],
         scratch_shapes=[
             pltpu.VMEM(weights, BF16),
-            pltpu.VMEM(weights, BF16),
-            pltpu.SemaphoreType.DMA((3,)),
+            pltpu.VMEM((2,) + weights, BF16),
+            pltpu.VMEM((2, rows, hidden), BF16),
+            pltpu.VMEM((rows, hidden), BF16),
+            pltpu.VMEM((2, 2 * half, width), BF16),
+            pltpu.VMEM((2, 2 * half, width), BF16),
+            pltpu.VMEM((2, 2 * half, width), BF16),
+            pltpu.VMEM((2, 2, 2, half, width), BF16),
+            pltpu.VMEM((2, 2, half, width), BF16),
+            pltpu.VMEM((2, half, width), BF16),
+            pltpu.VMEM((half, width), BF16),
+            pltpu.SemaphoreType.DMA((3, 2)),
+            pltpu.SemaphoreType.DMA((2, 3)),
+            pltpu.SemaphoreType.DMA((2, 2)),
+            pltpu.SemaphoreType.DMA((2, 2)),
+            pltpu.SemaphoreType.DMA((2,)),
+            pltpu.SemaphoreType.DMA((2,)),
+            pltpu.SemaphoreType.DMA((2,)),
         ],
-        compiler_params=pltpu.CompilerParams(vmem_limit_bytes=VMEM_BYTES),
+        compiler_params=kernel_params(number),
         cost_estimate=SMALL,
-    )(rows_all, cotangent_all, before, piece, early, late, shift)
+    )(rows_all, cotangent_all, before, rows_all, cotangent_all, act_a, piece, early, late, shift)
 
 
 def by_columns(left, right):
     return lax.dot_general(left, right, (((0,), (0,)), ((), ())), preferred_element_type=F32)
-
-
-def grads_kernel(programs, steps, *refs):
-    count = len(programs)
-    (cotangent_ref, rows_ref, act_a_ref, act_b_ref, pre_ref), refs = refs[:5], refs[5:]
-    (piece_ref, early_ref, late_ref), refs = refs[:3], refs[3:]
-    others, refs = refs[:count], refs[count:]
-    (down_part_ref, weight_grad_ref), refs = refs[:2], refs[2:]
-    other_outs, refs = refs[:count], refs[count:]
-    (acts, pre_own, downs, load_sem, weight_sem), scratch = refs[:5], refs[5:]
-    step = pl.program_id(0)
-    finish = beside(programs, others, other_outs, scratch, step, steps)
-
-    @pl.when(step == 0)
-    def _():
-        rows, first = downs.shape[3], piece_ref.shape[2]
-        places = (piece_ref, early_ref, late_ref)
-        copies = [
-            pltpu.make_async_copy(act_a_ref, acts.at[0], load_sem.at[0]),
-            pltpu.make_async_copy(act_b_ref, acts.at[1], load_sem.at[1]),
-            pltpu.make_async_copy(pre_ref, pre_own, load_sem.at[2]),
-        ]
-        copies += weight_copies(first_half(rows, first, places)[0], downs.at[0], weight_sem.at[0])
-        copies += weight_copies(second_half(rows, first, places)[0], downs.at[1], weight_sem.at[1])
-        for one in copies:
-            one.start()
-        for one in copies:
-            one.wait()
-
-    tile, width = down_part_ref.shape
-    rows = pl.ds(pl.multiple_of(step * tile, tile), tile)
-    shards, _, shard_rows, hidden = weight_grad_ref.shape
-    for kind, (left, right) in enumerate(((cotangent_ref, acts.at[1]), (rows_ref, pre_own))):
-        grad = by_columns(left[...], right[...]).astype(BF16)
-        weight_grad_ref[:, kind] = grad.reshape(shards, shard_rows, hidden)
-    part = rows_by_rows(acts[0, rows, :], downs[0].reshape(width, hidden))
-    part = part + rows_by_rows(acts[1, rows, :], downs[1].reshape(width, hidden))
-    down_part_ref[...] = part.astype(BF16)
-    finish()
-
-
-def grad_products(
-    cotangent_all, rows_all, act_a, act_b, pre, piece, early, late, programs, arrays, number
-):
-    rows, width = rows_all.shape
-    lines, quarters, _, hidden = late.shape
-    shards, shard_rows = lines * quarters, width // (lines * quarters)
-    steps = 8
-    columns = pl.BlockSpec((rows, width // steps), lambda i: (0, i))
-    anywhere = pl.BlockSpec(memory_space=pl.ANY)
-    grads = pl.BlockSpec((shards // steps, 2, shard_rows, hidden), lambda i: (i, 0, 0, 0))
-    out = pl.pallas_call(
-        functools.partial(grads_kernel, programs, steps),
-        grid=(steps,),
-        out_shape=[
-            jax.ShapeDtypeStruct((rows, width), BF16),
-            jax.ShapeDtypeStruct((shards, 2, shard_rows, hidden), BF16),
-        ]
-        + [one.out for one in programs],
-        in_specs=[columns, columns] + [anywhere] * 6 + [one.in_spec for one in programs],
-        out_specs=[pl.BlockSpec((rows // steps, width), lambda i: (i, 0)), grads]
-        + [one.out_spec for one in programs],
-        scratch_shapes=[
-            pltpu.VMEM((2, rows, hidden), BF16),
-            pltpu.VMEM((rows, hidden), BF16),
-            pltpu.VMEM((2, lines, quarters, shard_rows, hidden), BF16),
-            pltpu.SemaphoreType.DMA((3,)),
-            pltpu.SemaphoreType.DMA((2, 2)),
-        ]
-        + [held for one in programs for held in one.scratch()],
-        compiler_params=pltpu.CompilerParams(
-            collective_id=number, has_side_effects=True, vmem_limit_bytes=VMEM_BYTES
-        ),
-        cost_estimate=SMALL,
-    )(cotangent_all, rows_all, act_a, act_b, pre, piece, early, late, *arrays)
-    return out[0], out[1], out[2:]
 
 
 def reorder_kernel(cuts, size, x_ref, out_ref):
@@ -1588,8 +1682,8 @@
 
 
 def norm_work(me, refs, out_ref):
-    stream_ref, gain_ref, shift_ref = refs
-    gain, shift = gain_ref[...].astype(F32), shift_ref[...].astype(F32)
+    stream_ref, vectors_ref = refs
+    gain, shift = vectors_ref[0:1, :], vectors_ref[1:2, :]
 
     def work(rows):
         centered, rstd = moments(stream_ref[rows, :].astype(F32))
@@ -1634,9 +1728,7 @@
     mixed_ref,
     proj_ref,
     stream_ref,
-    bias_ref,
-    gain_ref,
-    shift_ref,
+    vectors_ref,
     middle_ref,
     normed_ref,
     sent_ref,
@@ -1660,8 +1752,7 @@
     copy.start()
     part(mine, middle_ref)
     copy.wait_recv()
-    bias, gain = bias_ref[...].astype(F32), gain_ref[...].astype(F32)
-    shift = shift_ref[...].astype(F32)
+    bias, gain, shift = vectors_ref[2:3, :], vectors_ref[3:4, :], vectors_ref[4:5, :]
     few = 32
 
     def finish(rows):
@@ -1702,7 +1793,7 @@
     return [(half * lines + shard) * size for shard in range(lines) for half in range(2)]
 
 
-def project(mixed, proj_all, stream, bias, gain, shift, number):
+def project(mixed, proj_all, stream, vectors, number):
     rows, width = stream.shape
     half = rows // 2
     cuts = line_cuts(width, False)
@@ -1712,7 +1803,7 @@
             jax.ShapeDtypeStruct((half, width), F32),
             jax.ShapeDtypeStruct((half, width), BF16),
         ],
-        in_specs=in_vmem(6),
+        in_specs=in_vmem(4),
         out_specs=in_vmem(2),
         scratch_shapes=[
             pltpu.VMEM((half, width), F32),
@@ -1721,7 +1812,7 @@
         ],
         compiler_params=kernel_params(number),
         cost_estimate=SMALL,
-    )(mixed, proj_all, stream, bias[None], gain[None], shift[None])
+    )(mixed, proj_all, stream, vectors)
     return middle, normed if cuts else to_line_order(normed)
 
 
@@ -1732,7 +1823,7 @@
     cotangent_ref,
     mixed_ref,
     proj_ref,
-    gain_ref,
+    vectors_ref,
     hidden_a_ref,
     hidden_b_ref,
     grad_middle_ref,
@@ -1747,7 +1838,7 @@
     half, width = middle_ref.shape
     mine, other = half_rows_of(me["tp"], half), half_rows_of(1 - me["tp"], half)
     few = 32
-    gain = gain_ref[...].astype(F32)
+    gain = vectors_ref[3:4, :]
     meet_sibling(me)
     sums_own[...] = jnp.zeros_like(sums_own)
 
@@ -1797,7 +1888,7 @@
     copy.wait_send()
 
 
-def middle_back(grad_sum, middle, cotangent, mixed, proj_all, gain, hidden_a, hidden_b, number):
+def middle_back(grad_sum, middle, cotangent, mixed, proj_all, vectors, hidden_a, hidden_b, number):
     rows, width = cotangent.shape
     half, heads = rows // 2, mixed.shape[1]
     cuts = line_cuts(width, True)
@@ -1824,7 +1915,7 @@
         cotangent,
         mixed,
         proj_all,
-        gain[None],
+        vectors,
         hidden_a,
         hidden_b,
     )
@@ -1837,15 +1928,14 @@
         first_ref,
         stream_ref,
         normed_ref,
-        gain_ref,
+        vectors_ref,
         grad_middle_ref,
         mlp_ref,
         middle_ref,
-        bias_ref,
         early_ref,
         cut_a_ref,
         cut_b_ref,
-    ), refs = refs[:13], refs[13:]
+    ), refs = refs[:12], refs[12:]
     (input_ref, layer_ref, down_out, up_out, part_out, total_out), refs = refs[:6], refs[6:]
     (weight_ref, vector_ref, sent_ref, got_ref, grad_first_ref, held_ref, sems), scratch = refs[:7], refs[7:]
     me = here()
@@ -1898,7 +1988,7 @@
     sums_copy = remote(sent_ref, got_ref, sems.at[0], sems.at[1], sibling)
     sums_copy.start()
     run_until(0.3)
-    bias = bias_ref[...].astype(F32)
+    bias = vectors_ref[5:6, :]
 
     def layer(at):
         start = pl.multiple_of(me["tp"] * half + at.start, few)
@@ -1913,7 +2003,7 @@
     part(mine, grad_own)
     run_until(0.5)
     sums_copy.wait_recv()
-    gain = gain_ref[...].astype(F32)
+    gain = vectors_ref[0:1, :]
     folded[0:16, :] = jnp.zeros((16, width), F32)
 
     def norm(at):
@@ -1950,11 +2040,10 @@
     first_all,
     stream,
     normed,
-    gain,
+    vectors,
     grad_middle,
     mlp_sum,
     middle,
-    bias,
     early,
     cut_a,
     cut_b,
@@ -1980,7 +2069,7 @@
             jax.ShapeDtypeStruct((rows, width), BF16),
         ]
         + [one.out for one in programs],
-        in_specs=in_vmem(11) + anywhere,
+        in_specs=in_vmem(10) + anywhere,
         out_specs=in_vmem(2) + [one.out_spec for one in programs],
         scratch_shapes=[
             pltpu.VMEM((width, part), BF16),
@@ -2000,11 +2089,10 @@
         first_all,
         stream,
         normed,
-        gain[None],
+        vectors,
         grad_middle,
         mlp_sum if cuts else from_line_order(mlp_sum),
         middle,
-        bias[None],
         early,
         cut_a,
         cut_b,
@@ -2068,6 +2156,16 @@
     )
     key_slots = jnp.concatenate([prompt_slots, my_slots[:, None]], axis=1)
 
+    vectors = [
+        attn_norm_gain,
+        attn_norm_bias,
+        proj_bias,
+        mlp_norm_gain,
+        mlp_norm_bias,
+        down_bias,
+    ]
+    vectors = jnp.stack(vectors + [jnp.zeros_like(down_bias)] * 2).astype(F32)
+
     keyval_cut = lax.dynamic_slice_in_dim(keyval_weight, core * HD, HD, axis=1)
     first_cut = jnp.concatenate([query_weight, keyval_cut], axis=1)
     shard_rows = down_weight.shape[0]
@@ -2099,17 +2197,17 @@
             placed(line_gather(proj_weight.shape, BF16), 0.305, *spaced(0.48, 0.88, lines - 1), 1.0),
         ],
         [
-            lambda more, outs: more[4:6],
+            lambda more, outs: more[3:5],
+            lambda more, outs: more[5],
+            lambda more, outs: more[3:5],
+            lambda more, outs: more[3:5],
+            lambda more, outs: outs[0],
+            lambda more, outs: more[:2],
+            lambda more, outs: more[2],
             lambda more, outs: more[6],
-            lambda more, outs: more[4:6],
-            lambda more, outs: more[4:6],
-            lambda more, outs: outs[0],
-            lambda more, outs: more[:3],
-            lambda more, outs: more[3],
-            lambda more, outs: more[7],
         ],
         1,
-        near=[hidden_in, attn_norm_gain[None], attn_norm_bias[None], out_cotangent],
+        near=[hidden_in, vectors, out_cotangent],
         far=[down_weight, up_weight, first_cut, proj_weight],
     )
     if cuts is None:
@@ -2152,7 +2250,7 @@
     mixed_low, mlp_early, late_cut = lax.optimization_barrier((mixed_low, mlp_early, late_cut))
     mlp_late = lax.all_gather(late_cut, "line", axis=0, tiled=False)
     middle, normed_two_line = project(
-        mixed_low, proj_all, hidden_in, proj_bias, mlp_norm_gain, mlp_norm_bias, 5
+        mixed_low, proj_all, hidden_in, vectors, 5
     )
 
     up_shift = lax.dynamic_slice_in_dim(up_bias, quarter * hidden_dev, hidden_dev).astype(F32)
@@ -2164,28 +2262,15 @@
     cotangent_all = flat(cotangent_all)
     cut_a = lax.psum_scatter(weight_grad_a, "line", scatter_dimension=0, tiled=True)
     rows_all, weight_grad_a = lax.optimization_barrier((rows_all, weight_grad_a))
-    act_b, pre_b, back_both, bias_b = second_products(
+    down_part, weight_grad_b, bias_b, grad_normed_two = second_products(
         rows_all,
         cotangent_all,
         back_a,
+        act_a,
         mlp_piece,
         mlp_early,
         mlp_late,
         up_shift[:, hidden_half:],
-    )
-    plane_two, plane_parts = plane_sum(back_both)
-    placed(plane_two, 0.0, 0.13, 0.13, 0.13, 0.13, 0.51, 0.9, 1.0, 1.0)
-    down_part, weight_grad_b, (grad_normed_two,) = grad_products(
-        cotangent_all,
-        rows_all,
-        act_a,
-        act_b,
-        pre_b,
-        mlp_piece,
-        mlp_early,
-        mlp_late,
-        [plane_two],
-        [plane_parts],
         7,
     )
     cut_b = lax.psum_scatter(weight_grad_b, "line", scatter_dimension=0, tiled=True)
@@ -2193,22 +2278,23 @@
     cut_b = cut_b.reshape(quarters, 2 * shard_rows, hidden_half)
 
     grad_middle, grad_mixed, proj_weight_grad, vector = middle_back(
-        grad_normed_two, middle, out_cotangent, mixed_low, proj_all, mlp_norm_gain, bias_a, bias_b, 8
+        grad_normed_two, middle, out_cotangent, mixed_low, proj_all, vectors, bias_a, bias_b, 8
     )
     grad_mixed, cut_a = lax.optimization_barrier((grad_mixed, cut_a))
     sum_proj, proj_parts = rows_sum(proj_weight_grad)
     sum_down, down_parts = plane_sum(down_part)
-    grad_query, grad_sets, (grad_proj_weight, mlp_out) = attend_back(
+    grad_query, grad_sets, query_weight_grad, (grad_proj_weight, mlp_out) = attend_back(
         query_low,
         grad_mixed,
         mixed_low,
         logsums,
         table,
+        normed_one,
         positions,
         key_slots,
         [
-            placed(sum_proj, 0.0, 0.13, 0.26, 0.38, 0.51, 0.63, 0.7, 0.9),
-            placed(sum_down, 0.0, 0.45, 0.45, 0.45, 0.45, 0.76, 0.95, 1.0, 1.0),
+            placed(sum_proj, 0.0, *spaced(0.13, 0.51, lines), 0.63, 1.06),
+            placed(sum_down, 0.0, 0.45, 0.45, 0.45, 0.45, 0.76, 0.95, 1.1, 1.2),
         ],
         [proj_parts, down_parts],
         3,
@@ -2216,7 +2302,6 @@
     grad_table = by_slot(grad_sets, key_slots, slot_count)
     grad_parts = grad_table.reshape(2, lines, 2 * rows_dev, HD)
     along_line, over_pair = ctx_sums(grad_parts)
-    query_weight_grad = jnp.einsum("rd,rk->dk", normed_one, grad_query, preferred_element_type=F32)
     sum_query, query_parts = rows_sum(query_weight_grad)
     _, grad_part, grad_query_weight = run_programs(
         [
@@ -2237,11 +2322,10 @@
         first_all,
         hidden_in,
         normed_one,
-        attn_norm_gain,
+        vectors,
         grad_middle,
         mlp_out,
         middle,
-        down_bias,
         vector,
         cut_a,
         cut_b,

time: 580 us -> 564 us (0.972)
  Pallas kernels: 531 us -> 515 us
    pallas_call x1 -> x0, Pallas kernels: 50.5 us -> none  [grad_products(): pl.pallas_call(functools.partial(grads_kernel, programs, steps), grid=(st...]
    pallas_call x1, Pallas kernels: 28.5 us -> 59.4 us  [second_products(): pl.pallas_call(second_kernel, grid=(steps,), out_shape=[jax.ShapeDtypeStr...]
  transfers between devices with their start and end apart: 4 -> 4, of which waited for: 0 -> 1; matrix products, arithmetic and copies ran while one was open for 2% -> 1% of each run, Pallas kernels for 67% -> 65%
where the time goes in v7:
time: 564 us; the launch traced here: 558 us
  Pallas kernels  515 us (91%)
  local copies, waits for them, and re-layouts  17.7 us (3%)
  between operations  14.2 us (3%)
  other arithmetic  10.8 us (2%)
    pallas_call x3, Pallas kernels, run_programs(): pl.pallas_call(kernel, out_shape=[one.out for one in programs], in_specs=...  147 us
    pallas_call x1, Pallas kernels, attend_back(): pl.pallas_call(functools.partial(attend_back_kernel, programs, blocks * h...  84.3 us
    pallas_call x1, Pallas kernels, attend(): pl.pallas_call(functools.partial(attend_kernel, programs, blocks * heads)...  76.4 us
    pallas_call x1, Pallas kernels, second_products(): pl.pallas_call(second_kernel, grid=(steps,), out_shape=[jax.ShapeDtypeStr...  59.4 us
    pallas_call x1, Pallas kernels, forward_products(): pl.pallas_call(forward_kernel, out_shape=[jax.ShapeDtypeStruct(lead + (wi...  58.8 us
    pallas_call x1, Pallas kernels, first_back(): pl.pallas_call(functools.partial(first_back_kernel, cuts, programs), out_...  51.6 us
    pallas_call x1, Pallas kernels, middle_back(): pl.pallas_call(functools.partial(middle_back_kernel, cuts), out_shape=[ja...  18.7 us
    pallas_call x1, Pallas kernels, project(): pl.pallas_call(functools.partial(project_kernel, cuts), out_shape=[jax.Sh...  13.1 us
  transfers between devices with their start and end apart: 4, of which 1 were waited for; matrix products, arithmetic and copies ran while one was open for 1% of the time, Pallas kernels for 65%

profile of v7, /device:TPU:0, one launch (start us, length us, event | category | flops | bytes accessed | tf_op | source)
XLA Modules:
  0.0 557.9 jit_solution(12810568822033609303)
XLA Ops:
  7.2 0.7 convert_element_type.17
  9.2 0.7 stack.24
  9.9 0.7 stack.25
  10.6 0.7 stack.26
  11.3 0.7 stack.27
  12.0 0.7 stack.28
  12.7 0.7 stack.29
  14.1 1.7 pad_maximum_fusion.refs_5_
  15.8 71.0 %shard_map.288 = (bf16[4,64,512]{2,1,0:T(8,128)(2,1)}, bf16[2,4,2,128,1152]{4,3,2,1,0:T(8,128)(2,1)}, bf16[4,256,512]{2,1,0:T(8,128)(2,1)}, bf16[4,192,512]{2,1,...) custom-call(bf16[512,2048]{1,0:T(8,128)(2,1)} %refs_3_.3, ...), custom_call_target="tpu_custom_call" | custom-call | flops 1 | bytes 1 | tf_op jit(solution)/shard_map/pallas_call | solution.py:714
  86.8 26.7 %shard_map.289 = (bf16[512,128]{1,0:T(8,128)(2,1)}, bf16[512,1024]{1,0:T(8,128)(2,1)}, bf16[2,4,2,512,128]{4,3,2,1,0:T(8,128)(2,1)}) custom-call(bf16[512,2048]{1,0:T(8,128)(2,1)} %get-tuple-element.65.refs_0_.refs_7_.refs_4_, bf16[2048,1152]{1,0:T(8,128)(2,1)} %bitcast.51, f32[1,1152]{1,0:T(1,128)} %broadcast_in_dim.35.refs_2_), custom_call_target="tpu_custom_call" | custom-call | flops 1 | bytes 1 | tf_op jit(solution)/shard_map/pallas_call | solution.py:714
  115.9 76.4 %shard_map.290 = (bf16[512,1024]{1,0:T(8,128)(2,1)}, f32[2,8,1,256]{3,2,1,0:T(1,128)}, bf16[2,4,2,128,1024]{4,3,2,1,0:T(8,128)(2,1)}, bf16[2,2,2,256,2048]{4,3,2,1,0:T(8,128)(2,1)}) custom-call(s32[2]{0:T(128)} %and_select_fusion.2.refs_0_, s32[2,9]{1,0:T(2,128)} %pad_add_fusion.refs_1_.slot_ref, bf16[512,1024]{1,0:T(8,128)(2,1)} %get-tuple-element.67.refs_2_, ...), custom_call_target="tpu_custom_call" | custom-call | flops 1 | bytes 1 | tf_op jit(solution)/shard_map/pallas_call | solution.py:878
  192.6 0.7 dynamic-slice_convert_fusion
  193.9 13.1 %shard_map.291 = (f32[256,2048]{1,0:T(8,128)}, bf16[256,2048]{1,0:T(8,128)(2,1)}) custom-call(bf16[512,1024]{1,0:T(8,128)(2,1)} %get-tuple-element.76.mixed_ref.refs_4_, bf16[2048,1024]{1,0:T(8,128)(2,1)} %bitcast.55, bf16[512,2048]{1,0:T(8,128)(2,1)} %refs_3_.3, f32[8,2048]{1,0:T(8,128)} %convert_element_type.16.refs_1_.vectors_ref.refs_5_), custom_call_target="tpu_custom_call" | custom-call | flops 1 | bytes 1 | tf_op jit(solution)/shard_map/pallas_call | solution.py:1800
  207.0 58.8 %shard_map.292 = (bf16[2,2,2,256,2048]{4,3,2,1,0:T(8,128)(2,1)}, bf16[2,2,2,256,512]{4,3,2,1,0:T(8,128)(2,1)}, bf16[2,2,2,256,512]{4,3,2,1,0:T(8,128)(2,1)}, bf1...) custom-call(bf16[256,2048]{1,0:T(8,128)(2,1)} %get-tuple-element.78.x_ref, ...), custom_call_target="tpu_custom_call" | custom-call | flops 1 | bytes 1 | tf_op jit(solution)/shard_map/pallas_call | solution.py:1304
  265.9 59.4 %shard_map.293 = (bf16[2048,2048]{1,0:T(8,128)(2,1)}, bf16[16,2,128,512]{3,2,1,0:T(8,128)(2,1)}, f32[8,512]{1,0:T(8,128)}, f32[256,2048]{1,0:T(8,128)}) custom-call(bf16[2048,2048]{1,0:T(8,128)(2,1)} %bitcast.49, bf16[2048,2048]{1,0:T(8,128)(2,1)} %bitcast.47, bf16[2048,2048]{1,0:T(8,128)(2,1)} %bitcast.58, bf16[2048,2048]{1,0:T(8,128)(2,1)} %bitcast.50, ...), custom_call_target="tpu_custom_call" | custom-call | flops 1 | bytes 1 | tf_op jit(solution)/shard_map/pallas_call | solution.py:1559
  325.4 18.7 %shard_map.294 = (f32[256,2048]{1,0:T(8,128)}, bf16[512,1024]{1,0:T(8,128)(2,1)}, bf16[2048,1024]{1,0:T(8,128)(2,1)}, f32[8,2048]{1,0:T(8,128)}) custom-call(f32[256,2048]{1,0:T(8,128)} %get-tuple-element.88.sum_ref, f32[256,2048]{1,0:T(8,128)} %get-tuple-element.89.middle_ref.refs_8_, bf16[512,2048]{1,0:T(8,128)(2,1)} %cotangent_ref.1, ...), custom_call_target="tpu_custom_call" | custom-call | flops 1 | bytes 1 | tf_op jit(solution)/shard_map/pallas_call | solution.py:1895
  344.1 84.3 %shard_map.295 = (bf16[512,1024]{1,0:T(8,128)(2,1)}, f32[2,2304,256]{2,1,0:T(8,128)}, bf16[2048,1024]{1,0:T(8,128)(2,1)}, f32[128,1024]{1,0:T(8,128)}, f32[256,2048]{1,0:T(8,128)}) custom-call(s32[2]{0:T(128)} %and_select_fusion.2.refs_0_, s32[2,9]{1,0:T(2,128)} %pad_add_fusion.refs_1_.slot_ref, bf16[512,1024]{1,0:T(8,128)(2,1)} %get-tuple-element.67.refs_2_, ...), custom_call_target="tpu_custom_call" | custom-call | flops 1 | bytes 1 | tf_op jit(solution)/shard_map/pallas_call | solution.py:980
  428.5 4.7 shard_map.296
  433.2 49.8 %shard_map.297 = (bf16[1024,128]{1,0:T(8,128)(2,1)}, f32[512,128]{1,0:T(8,128)}, f32[128,1024]{1,0:T(8,128)}) custom-call(bf16[2,4,1024,128]{3,2,1,0:T(8,128)(2,1)} %bitcast.61, bf16[2,4,2,128,1024]{4,3,2,1,0:T(8,128)(2,1)} %bitcast.63), custom_call_target="tpu_custom_call" | custom-call | flops 1 | bytes 1 | tf_op jit(solution)/shard_map/pallas_call | solution.py:714
  483.1 51.6 %shard_map.298 = (bf16[512,2048]{1,0:T(8,128)(2,1)}, bf16[512,2048]{1,0:T(8,128)(2,1)}, bf16[128,4096]{1,0:T(8,128)(2,1)}, bf16[128,4096]{1,0:T(8,128)(2,1)}, f32[128,256]{1,0:T(8,128)}, /*index=5*/f32[8,4096]{1,0:T(8,128)}) custom-call(bf16[512,1024]{1,0:T(8,128)(2,1)} %get-tuple-element.97.refs_0_, f32[512,128]{1,0:T(8,128)} %get-tuple-element.100.refs_1_, ...), custom_call_target="tpu_custom_call" | custom-call | flops 1 | bytes 1 | tf_op jit(solution)/shard_map/pallas_call | solution.py:2065
  534.8 1.3 slice_bitcast_fusion.1
  536.0 1.4 slice.43
  537.4 0.8 slice_bitcast_fusion
  538.1 1.9 fusion.1
  540.6 2.8 convert_element_type.19
  543.4 1.5 convert_element_type.20
  544.9 0.7 pad_maximum_fusion.1
  545.8 1.3 copy.40
  547.1 1.0 copy-done.2
  548.2 1.3 copy.41
  549.5 0.8 copy.42
  550.3 0.8 copy.43
  (50 shorter events, 6.4 us)
Async XLA Ops:
  7.2 6.9 %copy-start = (bf16[128,256]{1,0:T(8,128)(2,1)S(1)}, bf16[128,256]{1,0:T(8,128)(2,1)}, u32[]{:S(2)}) copy-start(bf16[128,256]{1,0:T(8,128)(2,1)} %param.23) | copy-start | bytes 196612
  7.2 185.2 %all-gather.5.cloned.1.call-start = ((), (), s32[]{:S(2)}) async-start(), calls=%async_computation.4 | async-start | bytes 5242880 | tf_op jit(solution)/shard_map/all_gather | solution.py:2235
  86.8 26.8 %copy-start.8 = (s32[1,16]{1,0:T(1,128)S(1)}, s32[1,16]{1,0:T(1,128)}, u32[]{:S(2)}) copy-start(s32[1,16]{1,0:T(1,128)} %param.18) | copy-start | bytes 196
  113.5 152.4 %all-gather.7.cloned.1.call-start = ((), (), s32[]{:S(2)}) async-start(), calls=%async_computation.5 | async-start | bytes 3932160 | tf_op jit(solution)/shard_map/all_gather | solution.py:2251
  192.4 151.7 %reduce-scatter.3.cloned.1.call-start = ((), (), s32[]{:S(2)}) async-start(), calls=%async_computation.2 | async-start | bytes 5242880 | tf_op jit(solution)/shard_map/reduce_scatter | solution.py:2263
  265.9 217.2 %reduce-scatter.5.cloned.1.call-start = ((), (), s32[]{:S(2)}) async-start(), calls=%async_computation.3 | async-start | bytes 5242880 | tf_op jit(solution)/shard_map/reduce_scatter | solution.py:2276
  534.7 8.7 %copy-start.4 = (bf16[128,4096]{1,0:T(8,128)(2,1)S(1)}, bf16[128,4096]{1,0:T(8,128)(2,1)}, u32[]{:S(2)}) copy-start(bf16[128,4096]{1,0:T(8,128)(2,1)} %get-tuple-element.113) | copy-start | bytes 3145732
  543.4 1.5 copy-start.7
  543.4 2.4 copy-start.3
  545.8 2.3 copy-start.2
  548.2 1.4 copy-start.6
  548.2 2.2 copy-start.5
  548.2 3.0 copy-start.1
Sparse Core Ops, SparseCore 0:
  113.6 78.7 all-gather.4
  193.9 62.0 all-gather.6
  266.0 74.4 reduce-scatter.2
  342.7 94.1 reduce-scatter.4

commit v8 on v7

--- a/solution.py
+++ b/solution.py
@@ -426,15 +426,36 @@
     return Exchange(moves, (4, start, columns // 8), kind)
 
 
-def join_halves(rows, columns, kind):
-    moves = [
-        (
-            lambda refs, quarter, half=half: refs[half].at[quarter],
-            lambda ref, quarter, half=half: half_quarter(ref, quarter, half),
-        )
-        for half in range(2)
-    ]
-    return Exchange(moves, (rows, columns), kind)
+def return_half(cut, kind):
+    quarters, rows, columns = cut.shape
+
+    def place(ref, quarter):
+        return ref.at[:, pl.ds(pl.multiple_of(quarter * columns, columns), columns)]
+
+    return Exchange(
+        [(lambda ref, quarter: ref.at[quarter], place)], (rows, quarters * columns), kind
+    )
+
+
+def widen_kernel(a_ref, b_ref, down_ref, up_ref):
+    rows, columns = down_ref.shape[0], a_ref.shape[1] // 4
+    for start, out_ref in ((0, down_ref), (rows, up_ref)):
+        for quarter in range(4):
+            for half, ref in enumerate((a_ref, b_ref)):
+                at = (quarter * 2 + half) * columns
+                cut = slice(quarter * columns, (quarter + 1) * columns)
+                out_ref[:, at : at + columns] = ref[start : start + rows, cut].astype(F32)
+
+
+def widen(half_a, half_b):
+    rows, columns = half_a.shape
+    shape = jax.ShapeDtypeStruct((rows // 2, 2 * columns), F32)
+    return pl.pallas_call(
+        widen_kernel,
+        out_shape=[shape, shape],
+        compiler_params=pltpu.CompilerParams(vmem_limit_bytes=VMEM_BYTES),
+        cost_estimate=SMALL,
+    )(half_a, half_b)
 
 
 class Work:
@@ -1069,17 +1090,16 @@
     return copies
 
 
-def first_half(rows, first, refs):
-    piece, early = refs[0], refs[1]
-    down = [(piece, slice(0, first)), (early, slice(0, rows - first))]
-    return down, [(early, slice(rows - first, 2 * rows - first))]
-
-
-def second_half(rows, first, refs):
-    early, late = refs[1], refs[2]
-    start = 2 * rows - first
-    there = early.shape[2] - start
-    down = [(early, slice(start, start + there)), (late, slice(0, rows - there))]
+def first_half(rows, refs):
+    piece, other, early = refs[:3]
+    first = piece.shape[2]
+    return [(piece, slice(0, first)), (other, slice(0, rows - first))], [(early, slice(0, rows))]
+
+
+def second_half(rows, refs):
+    early, late = refs[2:]
+    there = early.shape[2] - rows
+    down = [(early, slice(rows, rows + there)), (late, slice(0, rows - there))]
     return down, [(late, slice(rows - there, 2 * rows - there))]
 
 
@@ -1096,6 +1116,7 @@
     x_ref,
     cotangent_ref,
     piece_ref,
+    other_ref,
     early_ref,
     shift_ref,
     all_ref,
@@ -1210,23 +1231,23 @@
         lax.fori_loop(0, width // tile, one, 0, unroll=2)
 
     def grads(number):
-        slot = number % 2
         tile = 256
         shard_rows = weight_grad_ref.shape[2]
+        rows = 4 * half
 
         def one(index, carry):
             cut = pl.ds(pl.multiple_of(index * tile, tile), tile)
             for kind, (left, right) in enumerate(((cotangent_own, act_own), (rows_own, pre_own))):
-                grad = by_columns(left[slot, :, cut], right[slot])
-                if number > 0:
-                    grad = grads_own[kind, cut, :] + grad
-                if number < 3:
+                grad = by_columns(
+                    left[:, :, cut].reshape(rows, tile), right[...].reshape(rows, hidden)
+                )
+                if number == 1:
                     grads_own[kind, cut, :] = grad
                 else:
                     count = tile // shard_rows
                     shards = pl.ds(pl.multiple_of(index * count, count), count)
-                    grad = grad.astype(BF16).reshape(count, shard_rows, hidden)
-                    weight_grad_ref[shards, kind] = grad
+                    grad = (grads_own[kind, cut, :] + grad).astype(BF16)
+                    weight_grad_ref[shards, kind] = grad.reshape(count, shard_rows, hidden)
             return carry
 
         lax.fori_loop(0, width // tile, one, 0, unroll=2)
@@ -1254,7 +1275,7 @@
     to_step(2, 0).start()
     own = pltpu.make_async_copy(x_ref, block(0), own_sem)
     own.start()
-    down_parts, up_parts = first_half(up_own.shape[2], piece_ref.shape[2], (piece_ref, early_ref))
+    down_parts, up_parts = first_half(up_own.shape[2], (piece_ref, other_ref, early_ref))
     weights = weight_copies(down_parts, down_own, weight_sem)
     weights += weight_copies(up_parts, up_own, weight_sem.at[2:])
     for one in weights:
@@ -1284,7 +1305,8 @@
         back(number)
         for one in stores(number, 2):
             one.start()
-        grads(number)
+        if number % 2:
+            grads(number)
     for number in (2, 3):
         for kind in range(3):
             for one in stores(number, kind):
@@ -1294,7 +1316,7 @@
         to_step(k, bits).wait_send()
 
 
-def forward_products(rows, cotangent_all, piece, early, shift, number):
+def forward_products(rows, cotangent_all, piece, other, early, shift, number):
     half, width = rows.shape
     lines, quarters, _, hidden = early.shape
     weights = (lines, quarters, width // (lines * quarters), hidden)
@@ -1311,7 +1333,7 @@
             jax.ShapeDtypeStruct((8, hidden), F32),
             jax.ShapeDtypeStruct((lines * quarters, 2, weights[2], hidden), BF16),
         ],
-        in_specs=[anywhere] * 4 + [inside],
+        in_specs=[anywhere] * 5 + [inside],
         out_specs=[anywhere] * 4 + [inside] * 2,
         scratch_shapes=[
             pltpu.VMEM(weights, BF16),
@@ -1333,7 +1355,7 @@
             collective_id=number, has_side_effects=True, vmem_limit_bytes=VMEM_BYTES
         ),
         cost_estimate=SMALL,
-    )(rows, cotangent_all, piece, early, shift)
+    )(rows, cotangent_all, piece, other, early, shift)
 
 
 CHIPS = ((1, 1), (1, 0), (0, 1), (0, 0))
@@ -1347,6 +1369,7 @@
     cotangent_columns_ref,
     act_a_ref,
     piece_ref,
+    other_ref,
     early_ref,
     late_ref,
     shift_ref,
@@ -1380,8 +1403,8 @@
     count = rows_ref.shape[0] // 4
     half = count // 2
     tile = 256
-    places = (piece_ref, early_ref, late_ref)
-    shard_rows, first = up_own.shape[2], piece_ref.shape[2]
+    places = (piece_ref, other_ref, early_ref, late_ref)
+    shard_rows = up_own.shape[2]
 
     def chip(number):
         up, side = CHIPS[number]
@@ -1401,12 +1424,12 @@
         ]
 
     def second_weights():
-        down_parts, up_parts = second_half(shard_rows, first, places)
+        down_parts, up_parts = second_half(shard_rows, places)
         copies = weight_copies(down_parts, downs.at[1], weight_sem.at[0])
         return copies + weight_copies(up_parts, up_own, weight_sem.at[1])
 
     def first_weights():
-        copies = weight_copies(first_half(shard_rows, first, places)[0], downs.at[0], weight_sem.at[2])
+        copies = weight_copies(first_half(shard_rows, places)[0], downs.at[0], weight_sem.at[2])
         return copies + [pltpu.make_async_copy(act_a_ref, acts.at[0], weight_sem.at[1, 1])]
 
     def to_core(number):
@@ -1543,9 +1566,9 @@
         to_side().wait_send()
 
 
-def second_products(rows_all, cotangent_all, before, act_a, piece, early, late, shift, number):
+def second_products(rows_all, cotangent_all, before, act_a, pieces, shift, number):
     rows, width = rows_all.shape
-    lines, quarters, _, hidden = late.shape
+    lines, quarters, _, hidden = pieces[-1].shape
     shards, shard_rows = lines * quarters, width // (lines * quarters)
     weights = (lines, quarters, shard_rows, hidden)
     steps, tiles, half = 12, 8, rows // 8
@@ -1565,7 +1588,7 @@
             jax.ShapeDtypeStruct((8, hidden), F32),
             jax.ShapeDtypeStruct((half, width), F32),
         ],
-        in_specs=[anywhere] * 3 + [columns] * 2 + [anywhere] * 4 + [fixed((1, hidden))],
+        in_specs=[anywhere] * 3 + [columns] * 2 + [anywhere] * 5 + [fixed((1, hidden))],
         out_specs=[
             pl.BlockSpec((rows // tiles, width), lambda i: (tile(i), 0)),
             pl.BlockSpec((shards // tiles, 2, shard_rows, hidden), lambda i: (tile(i), 0, 0, 0)),
@@ -1594,7 +1617,7 @@
         ],
         compiler_params=kernel_params(number),
         cost_estimate=SMALL,
-    )(rows_all, cotangent_all, before, rows_all, cotangent_all, act_a, piece, early, late, shift)
+    )(rows_all, cotangent_all, before, rows_all, cotangent_all, act_a, *pieces, shift)
 
 
 def by_columns(left, right):
@@ -1726,7 +1749,8 @@
 def project_kernel(
     cuts,
     mixed_ref,
-    proj_ref,
+    proj_a_ref,
+    proj_b_ref,
     stream_ref,
     vectors_ref,
     middle_ref,
@@ -1744,7 +1768,9 @@
 
     def part(rows, target):
         def work(cut):
-            target[:, cut] = rows_by_rows(mixed_ref[rows, :], proj_ref[cut, :])
+            heads = proj_a_ref.shape[1]
+            part = rows_by_rows(mixed_ref[rows, :heads], proj_a_ref[cut, :])
+            target[:, cut] = part + rows_by_rows(mixed_ref[rows, heads:], proj_b_ref[cut, :])
 
         each_columns(width, tile, work)
 
@@ -1793,7 +1819,7 @@
     return [(half * lines + shard) * size for shard in range(lines) for half in range(2)]
 
 
-def project(mixed, proj_all, stream, vectors, number):
+def project(mixed, proj_a, proj_b, stream, vectors, number):
     rows, width = stream.shape
     half = rows // 2
     cuts = line_cuts(width, False)
@@ -1803,7 +1829,7 @@
             jax.ShapeDtypeStruct((half, width), F32),
             jax.ShapeDtypeStruct((half, width), BF16),
         ],
-        in_specs=in_vmem(4),
+        in_specs=in_vmem(5),
         out_specs=in_vmem(2),
         scratch_shapes=[
             pltpu.VMEM((half, width), F32),
@@ -1812,7 +1838,7 @@
         ],
         compiler_params=kernel_params(number),
         cost_estimate=SMALL,
-    )(mixed, proj_all, stream, vectors)
+    )(mixed, proj_a, proj_b, stream, vectors)
     return middle, normed if cuts else to_line_order(normed)
 
 
@@ -1822,7 +1848,8 @@
     middle_ref,
     cotangent_ref,
     mixed_ref,
-    proj_ref,
+    proj_a_ref,
+    proj_b_ref,
     vectors_ref,
     hidden_a_ref,
     hidden_b_ref,
@@ -1861,11 +1888,15 @@
     copy.start()
 
     def to_heads(rows):
-        def work(cut):
-            grad = jnp.dot(attn_ref[rows, :], proj_ref[:, cut], preferred_element_type=F32)
-            grad_mixed_ref[rows, cut] = grad.astype(BF16)
-
-        each_columns(proj_ref.shape[1], 256, work)
+        for number, proj_ref in enumerate((proj_a_ref, proj_b_ref)):
+            heads = proj_ref.shape[1]
+            grad_ref = grad_mixed_ref.at[:, number * heads : (number + 1) * heads]
+
+            def work(cut):
+                grad = jnp.dot(attn_ref[rows, :], proj_ref[:, cut], preferred_element_type=F32)
+                grad_ref[rows, cut] = grad.astype(BF16)
+
+            each_columns(heads, 256, work)
 
     to_heads(mine)
     vector_ref[...] = jnp.zeros_like(vector_ref)
@@ -1888,7 +1919,7 @@
     copy.wait_send()
 
 
-def middle_back(grad_sum, middle, cotangent, mixed, proj_all, vectors, hidden_a, hidden_b, number):
+def middle_back(grad_sum, middle, cotangent, mixed, proj_a, proj_b, vectors, hidden_a, hidden_b, number):
     rows, width = cotangent.shape
     half, heads = rows // 2, mixed.shape[1]
     cuts = line_cuts(width, True)
@@ -1900,7 +1931,7 @@
             jax.ShapeDtypeStruct((width, heads), BF16),
             jax.ShapeDtypeStruct((8, width), F32),
         ],
-        in_specs=in_vmem(8),
+        in_specs=in_vmem(9),
         out_specs=in_vmem(4),
         scratch_shapes=[
             pltpu.VMEM((rows, width), BF16),
@@ -1914,7 +1945,8 @@
         middle,
         cotangent,
         mixed,
-        proj_all,
+        proj_a,
+        proj_b,
         vectors,
         hidden_a,
         hidden_b,
@@ -1933,10 +1965,9 @@
         mlp_ref,
         middle_ref,
         early_ref,
-        cut_a_ref,
         cut_b_ref,
-    ), refs = refs[:12], refs[12:]
-    (input_ref, layer_ref, down_out, up_out, part_out, total_out), refs = refs[:6], refs[6:]
+    ), refs = refs[:11], refs[11:]
+    (input_ref, layer_ref, mlp_out, part_out, total_out), refs = refs[:5], refs[5:]
     (weight_ref, vector_ref, sent_ref, got_ref, grad_first_ref, held_ref, sems), scratch = refs[:7], refs[7:]
     me = here()
     rows, width = stream_ref.shape
@@ -1948,12 +1979,11 @@
     works = schedule(
         programs,
         (
-            (cut_a_ref.at[:, :shard_rows], cut_b_ref.at[:, :shard_rows]),
-            (cut_a_ref.at[:, shard_rows:], cut_b_ref.at[:, shard_rows:]),
+            cut_b_ref,
             weight_ref.reshape(2, -1, 2, shard_rows, weight_ref.shape[1]),
             vector_ref,
         ),
-        (down_out, up_out, part_out, total_out),
+        (mlp_out, part_out, total_out),
         scratch,
         ("tp",),
     )
@@ -2045,7 +2075,6 @@
     mlp_sum,
     middle,
     early,
-    cut_a,
     cut_b,
     number,
 ):
@@ -2056,12 +2085,11 @@
     shard_rows = width // (4 * lines)
     vector = early.shape
     programs = [
-        placed(join_halves(shard_rows, 8 * cut_a.shape[2], BF16), 0.0, 1.0),
-        placed(join_halves(shard_rows, 8 * cut_a.shape[2], BF16), 0.0, 1.0),
+        placed(return_half(cut_b, BF16), 0.0, 1.0),
         placed(Direct(lines, shard_rows, part, part), 0.1, 0.95),
         placed(Total(vector, lines, 6, heads), 0.9, 0.93, 0.97),
     ]
-    anywhere = [pl.BlockSpec(memory_space=pl.ANY)] * 2
+    anywhere = [pl.BlockSpec(memory_space=pl.ANY)]
     return pl.pallas_call(
         functools.partial(first_back_kernel, cuts, programs),
         out_shape=[
@@ -2094,7 +2122,6 @@
         mlp_sum if cuts else from_line_order(mlp_sum),
         middle,
         early,
-        cut_a,
         cut_b,
     )
 
@@ -2176,19 +2203,17 @@
     cuts = line_cuts(width, False)
     lines = lax.axis_size("line")
     first_pieces = [(0, slice(0, first_rows), 0)]
-    early_pieces = [
-        (0, slice(first_rows, shard_rows), 0),
-        (1, slice(0, shard_rows), 0),
-        (0, slice(0, early_rows), 1),
-    ]
+    other_pieces = [(0, slice(first_rows, shard_rows), 0)]
+    early_pieces = [(1, slice(0, shard_rows), 0), (0, slice(0, early_rows), 1)]
     late_pieces = [(0, slice(early_rows, shard_rows), 1), (1, slice(0, shard_rows), 1)]
     hops = [0.1 * k for k in range(1, 4)] if lines == 4 else spaced(0.1, 0.3, lines - 1)
     levels = spaced(0.4, 0.98, 2 * lines)
     piece_hops = spaced(0.35, 0.75, lines - 1)
-    _, first_all, early_cut, late_cut, mlp_piece, normed_one, cotangent_line, proj_line = run_programs(
+    _, first_all, other_cut, early_cut, late_cut, mlp_piece, normed_one, cotangent_line, proj_line = run_programs(
         [
             placed(spread_halves(first_pieces, columns, BF16), 0.0, 0.05),
             placed(rows_gather(first_cut), 0.01, *hops, *levels, 1.0),
+            placed(spread_halves(other_pieces, columns, BF16), 0.06, 1.0),
             placed(spread_halves(early_pieces, columns, BF16), 0.06, 1.0),
             placed(spread_halves(late_pieces, columns, BF16), 0.061, 1.0),
             placed(line_gather((quarters, first_rows, hidden_half), BF16), 0.07, *piece_hops, 1.0),
@@ -2201,6 +2226,7 @@
             lambda more, outs: more[5],
             lambda more, outs: more[3:5],
             lambda more, outs: more[3:5],
+            lambda more, outs: more[3:5],
             lambda more, outs: outs[0],
             lambda more, outs: more[:2],
             lambda more, outs: more[2],
@@ -2217,46 +2243,58 @@
     value_shift = jnp.where(core == 1, value_bias.astype(F32), 0.0)
     first_shift = jnp.concatenate([query_bias.astype(F32), value_shift])
     part_like = (rows_dev, HD)
-    _, query_low, keyval_every = run_programs(
+    head_half = head_width // 2
+    half_line = jax.ShapeDtypeStruct((lines, shard_rows, head_half), BF16)
+    _, query_low, keyval_every, mlp_other, proj_a = run_programs(
         [
             placed(Work(part_work, part_like, BF16), 0.0, 0.0),
             placed(Work(query_work, (rows_dev, head_width), BF16), 0.2, 0.2),
-            placed(ctx_gather(part_like, BF16), 0.1, 1.0),
+            placed(ctx_gather(part_like, BF16), 0.1, *spaced(0.25, 0.5, lines - 1), *spaced(0.52, 0.9, 2 * lines), 1.0),
+            placed(
+                line_gather((quarters, shard_rows - first_rows, hidden_half), BF16),
+                0.11,
+                *spaced(0.3, 0.62, lines - 1),
+                1.0,
+            ),
+            placed(columns_gather(half_line), 0.001, 0.45, 0.85, 1.0),
         ],
         [
             lambda more, outs: more[:3],
             lambda more, outs: more[:3],
             lambda more, outs: outs[0],
+            lambda more, outs: more[3],
+            lambda more, outs: more[4].at[:, :, :head_half],
         ],
         4,
         near=[normed_one, first_all, first_shift[None]],
+        far=[other_cut, proj_line],
     )
     keyval_every, early_cut = lax.optimization_barrier((keyval_every, early_cut))
     mlp_early = lax.all_gather(early_cut, "line", axis=0, tiled=False)
     table = keyval_every.reshape(2, slot_count, BLK, HD)
-    mixed_low, logsums, (proj_all, cotangent_all) = attend(
+    mixed_low, logsums, (proj_b, cotangent_all) = attend(
         query_low,
         table,
         positions,
         key_slots,
         [
-            placed(columns_gather(proj_line), 0.0, 0.9, 1.0, 1.0),
+            placed(columns_gather(half_line), 0.0, 0.9, 1.0, 1.0),
             placed(plane_gather(cotangent_line), 0.0, 0.9, 1.0, 1.0),
         ],
-        [proj_line, cotangent_line],
+        [proj_line[:, :, head_half:], cotangent_line],
         2,
     )
-    proj_all = flat(proj_all)
+    proj_a, proj_b = flat(proj_a), flat(proj_b)
     mixed_low, mlp_early, late_cut = lax.optimization_barrier((mixed_low, mlp_early, late_cut))
     mlp_late = lax.all_gather(late_cut, "line", axis=0, tiled=False)
     middle, normed_two_line = project(
-        mixed_low, proj_all, hidden_in, vectors, 5
+        mixed_low, proj_a, proj_b, hidden_in, vectors, 5
     )
 
     up_shift = lax.dynamic_slice_in_dim(up_bias, quarter * hidden_dev, hidden_dev).astype(F32)
     up_shift = up_shift[None]
     rows_all, act_a, pre_a, back_a, bias_a, weight_grad_a = forward_products(
-        normed_two_line, cotangent_all, mlp_piece, mlp_early, up_shift[:, :hidden_half], 6
+        normed_two_line, cotangent_all, mlp_piece, mlp_other, mlp_early, up_shift[:, :hidden_half], 6
     )
     rows_all, act_a, pre_a, back_a = flat(rows_all), flat(act_a), flat(pre_a), flat(back_a)
     cotangent_all = flat(cotangent_all)
@@ -2267,9 +2305,7 @@
         cotangent_all,
         back_a,
         act_a,
-        mlp_piece,
-        mlp_early,
-        mlp_late,
+        (mlp_piece, mlp_other, mlp_early, mlp_late),
         up_shift[:, hidden_half:],
         7,
     )
@@ -2278,7 +2314,7 @@
     cut_b = cut_b.reshape(quarters, 2 * shard_rows, hidden_half)
 
     grad_middle, grad_mixed, proj_weight_grad, vector = middle_back(
-        grad_normed_two, middle, out_cotangent, mixed_low, proj_all, vectors, bias_a, bias_b, 8
+        grad_normed_two, middle, out_cotangent, mixed_low, proj_a, proj_b, vectors, bias_a, bias_b, 8
     )
     grad_mixed, cut_a = lax.optimization_barrier((grad_mixed, cut_a))
     sum_proj, proj_parts = rows_sum(proj_weight_grad)
@@ -2303,20 +2339,22 @@
     grad_parts = grad_table.reshape(2, lines, 2 * rows_dev, HD)
     along_line, over_pair = ctx_sums(grad_parts)
     sum_query, query_parts = rows_sum(query_weight_grad)
-    _, grad_part, grad_query_weight = run_programs(
+    _, grad_part, grad_query_weight, mlp_grad_a = run_programs(
         [
             placed(along_line, 0.01, 0.75),
             placed(over_pair, 0.76, 0.86, 0.97),
             placed(sum_query, 0.0, 1.0),
+            placed(return_half(cut_a, BF16), 0.02, 1.0),
         ],
         [
             grad_parts,
             lambda more, outs: outs[0].reshape(2, rows_dev, HD),
             query_parts,
+            cut_a,
         ],
         12,
     )
-    input_grad, layer_out, down_wide, up_wide, grad_part_weight, summed = first_back(
+    input_grad, layer_out, mlp_grad_b, grad_part_weight, summed = first_back(
         grad_query,
         grad_part,
         first_all,
@@ -2327,11 +2365,10 @@
         mlp_out,
         middle,
         vector,
-        cut_a,
         cut_b,
         9,
     )
-    grad_down_weight, grad_up_weight = down_wide.astype(F32), up_wide.astype(F32)
+    grad_down_weight, grad_up_weight = widen(mlp_grad_a, mlp_grad_b)
     grad_keyval_weight = in_order(grad_part_weight[:, :HD], grad_part_weight[:, HD:], axis=1)
     sum_up = summed[:quarters, width : 2 * width - head_width].reshape(quarters * hidden_dev)
     return (

time: 564 us -> 552 us (0.979)
  Pallas kernels: 515 us -> 505 us
    pallas_call x1, Pallas kernels: 76.4 us -> 59 us  [attend(): pl.pallas_call(functools.partial(attend_kernel, programs, blocks * heads)...]
    pallas_call x3, Pallas kernels: 147 us -> 162 us  [run_programs(): pl.pallas_call(kernel, out_shape=[one.out for one in programs], in_specs=...]
    pallas_call x1, Pallas kernels: 51.6 us -> 41.5 us  [first_back(): pl.pallas_call(functools.partial(first_back_kernel, cuts, programs), out_...]
  transfers between devices with their start and end apart: 4 -> 4, of which waited for: 1 -> 1; matrix products, arithmetic and copies ran while one was open for 1% -> 1% of each run, Pallas kernels for 65% -> 64%
where the time goes in v8:
time: 552 us; the launch traced here: 546 us
  Pallas kernels  505 us (91%)
  local copies, waits for them, and re-layouts  18.2 us (3%)
  between operations  14.2 us (3%)
  other arithmetic  7.42 us (1%)
    pallas_call x3, Pallas kernels, run_programs(): pl.pallas_call(kernel, out_shape=[one.out for one in programs], in_specs=...  162 us
    pallas_call x1, Pallas kernels, attend_back(): pl.pallas_call(functools.partial(attend_back_kernel, programs, blocks * h...  84.5 us
    pallas_call x1, Pallas kernels, second_products(): pl.pallas_call(second_kernel, grid=(steps,), out_shape=[jax.ShapeDtypeStr...  59.4 us
    pallas_call x1, Pallas kernels, attend(): pl.pallas_call(functools.partial(attend_kernel, programs, blocks * heads)...  59 us
    pallas_call x1, Pallas kernels, forward_products(): pl.pallas_call(forward_kernel, out_shape=[jax.ShapeDtypeStruct(lead + (wi...  58.6 us
    pallas_call x1, Pallas kernels, first_back(): pl.pallas_call(functools.partial(first_back_kernel, cuts, programs), out_...  41.5 us
    pallas_call x1, Pallas kernels, middle_back(): pl.pallas_call(functools.partial(middle_back_kernel, cuts), out_shape=[ja...  18.6 us
    pallas_call x1, Pallas kernels, project(): pl.pallas_call(functools.partial(project_kernel, cuts), out_shape=[jax.Sh...  13.1 us
  transfers between devices with their start and end apart: 4, of which 1 were waited for; matrix products, arithmetic and copies ran while one was open for 1% of the time, Pallas kernels for 64%

profile of v8, /device:TPU:0, one launch (start us, length us, event | category | flops | bytes accessed | tf_op | source)
XLA Modules:
  0.0 545.9 jit_solution(16408027899722575708)
XLA Ops:
  9.2 0.7 stack.24
  9.9 0.7 stack.25
  10.6 0.7 stack.26
  11.3 0.7 stack.27
  12.0 0.7 stack.28
  12.7 0.7 stack.29
  14.1 1.7 pad_maximum_fusion.refs_5_
  15.8 71.0 %shard_map.288 = (bf16[4,64,512]{2,1,0:T(8,128)(2,1)}, bf16[2,4,2,128,1152]{4,3,2,1,0:T(8,128)(2,1)}, bf16[4,64,512]{2,1,0:T(8,128)(2,1)}, bf16[4,192,512]{2,1,0...) custom-call(bf16[512,2048]{1,0:T(8,128)(2,1)} %refs_3_.3, ...), custom_call_target="tpu_custom_call" | custom-call | flops 1 | bytes 1 | tf_op jit(solution)/shard_map/pallas_call | solution.py:735
  86.8 38.8 %shard_map.289 = (bf16[512,128]{1,0:T(8,128)(2,1)}, bf16[512,1024]{1,0:T(8,128)(2,1)}, bf16[2,4,2,512,128]{4,3,2,1,0:T(8,128)(2,1)}, bf16[4,4,64,512]{3,2,1,0:T(8,128)(2,1)}, bf16[2,4,2,128,512]{4,3,2,1,0:T(8,128)(2,1)}) custom-call(bf16[512,2048]{1,0:T(8,128)(2,1)} %get-tuple-element.70.refs_0_.refs_7_.refs_4_, bf16[2048,1152]{1,0:T(8,128)(2,1)} %bitcast.52, ...), custom_call_target="tpu_custom_call" | custom-call | flops 1 | bytes 1 | tf_op jit(solution)/shard_map/pallas_call | solution.py:735
  125.7 0.8 slice.42.refs_4_
  128.9 59.0 %shard_map.290 = (bf16[512,1024]{1,0:T(8,128)(2,1)}, f32[2,8,1,256]{3,2,1,0:T(1,128)}, bf16[2,4,2,128,512]{4,3,2,1,0:T(8,128)(2,1)}, bf16[2,2,2,256,2048]{4,3,2,1,0:T(8,128)(2,1)}) custom-call(s32[2]{0:T(128)} %and_select_fusion.2.refs_0_, s32[2,9]{1,0:T(2,128)} %pad_add_fusion.refs_1_.slot_ref, bf16[512,1024]{1,0:T(8,128)(2,1)} %get-tuple-element.74.refs_2_, ...), custom_call_target="tpu_custom_call" | custom-call | flops 1 | bytes 1 | tf_op jit(solution)/shard_map/pallas_call | solution.py:899
  187.9 0.7 all-gather.5.cloned.1.call-done
  188.9 0.7 dynamic-slice_convert_fusion
  190.2 13.1 %shard_map.291 = (f32[256,2048]{1,0:T(8,128)}, bf16[256,2048]{1,0:T(8,128)(2,1)}) custom-call(bf16[512,1024]{1,0:T(8,128)(2,1)} %get-tuple-element.82.mixed_ref.refs_4_, bf16[2048,512]{1,0:T(8,128)(2,1)} %bitcast.61, bf16[2048,512]{1,0:T(8,128)(2,1)} %bitcast.63, bf16[512,2048]{1,0:T(8,128)(2,1)} %refs_3_.3, ...), custom_call_target="tpu_custom_call" | custom-call | flops 1 | bytes 1 | tf_op jit(solution)/shard_map/pallas_call | solution.py:1826
  203.3 58.6 %shard_map.292 = (bf16[2,2,2,256,2048]{4,3,2,1,0:T(8,128)(2,1)}, bf16[2,2,2,256,512]{4,3,2,1,0:T(8,128)(2,1)}, bf16[2,2,2,256,512]{4,3,2,1,0:T(8,128)(2,1)}, bf1...) custom-call(bf16[256,2048]{1,0:T(8,128)(2,1)} %get-tuple-element.85.x_ref, ...), custom_call_target="tpu_custom_call" | custom-call | flops 1 | bytes 1 | tf_op jit(solution)/shard_map/pallas_call | solution.py:1326
  262.0 59.4 %shard_map.293 = (bf16[2048,2048]{1,0:T(8,128)(2,1)}, bf16[16,2,128,512]{3,2,1,0:T(8,128)(2,1)}, f32[8,512]{1,0:T(8,128)}, f32[256,2048]{1,0:T(8,128)}) custom-call(bf16[2048,2048]{1,0:T(8,128)(2,1)} %bitcast.50, bf16[2048,2048]{1,0:T(8,128)(2,1)} %bitcast.48, bf16[2048,2048]{1,0:T(8,128)(2,1)} %bitcast.57, bf16[2048,2048]{1,0:T(8,128)(2,1)} %bitcast.51, ...), custom_call_target="tpu_custom_call" | custom-call | flops 1 | bytes 1 | tf_op jit(solution)/shard_map/pallas_call | solution.py:1582
  321.4 18.6 %shard_map.294 = (f32[256,2048]{1,0:T(8,128)}, bf16[512,1024]{1,0:T(8,128)(2,1)}, bf16[2048,1024]{1,0:T(8,128)(2,1)}, f32[8,2048]{1,0:T(8,128)}) custom-call(f32[256,2048]{1,0:T(8,128)} %get-tuple-element.96.sum_ref, f32[256,2048]{1,0:T(8,128)} %get-tuple-element.97.middle_ref.refs_8_, bf16[512,2048]{1,0:T(8,128)(2,1)} %cotangent_ref.1, ...), custom_call_target="tpu_custom_call" | custom-call | flops 1 | bytes 1 | tf_op jit(solution)/shard_map/pallas_call | solution.py:1926
  340.1 84.5 %shard_map.295 = (bf16[512,1024]{1,0:T(8,128)(2,1)}, f32[2,2304,256]{2,1,0:T(8,128)}, bf16[2048,1024]{1,0:T(8,128)(2,1)}, f32[128,1024]{1,0:T(8,128)}, f32[256,2048]{1,0:T(8,128)}) custom-call(s32[2]{0:T(128)} %and_select_fusion.2.refs_0_, s32[2,9]{1,0:T(2,128)} %pad_add_fusion.refs_1_.slot_ref, bf16[512,1024]{1,0:T(8,128)(2,1)} %get-tuple-element.74.refs_2_, ...), custom_call_target="tpu_custom_call" | custom-call | flops 1 | bytes 1 | tf_op jit(solution)/shard_map/pallas_call | solution.py:1001
  424.6 4.7 shard_map.296
  429.4 51.9 %shard_map.297 = (bf16[1024,128]{1,0:T(8,128)(2,1)}, f32[512,128]{1,0:T(8,128)}, f32[128,1024]{1,0:T(8,128)}, bf16[256,2048]{1,0:T(8,128)(2,1)}) custom-call(bf16[2,4,1024,128]{3,2,1,0:T(8,128)(2,1)} %bitcast.60, bf16[2,4,2,128,1024]{4,3,2,1,0:T(8,128)(2,1)} %bitcast.66, bf16[4,256,512]{2,1,0:T(8,128)(2,1)} %bitcast.69), custom_call_target="tpu_custom_call" | custom-call | flops 1 | bytes 1 | tf_op jit(solution)/shard_map/pallas_call | solution.py:735
  481.3 41.5 %shard_map.298 = (bf16[512,2048]{1,0:T(8,128)(2,1)}, bf16[512,2048]{1,0:T(8,128)(2,1)}, bf16[256,2048]{1,0:T(8,128)(2,1)}, f32[128,256]{1,0:T(8,128)}, f32[8,4096]{1,0:T(8,128)}) custom-call(bf16[512,1024]{1,0:T(8,128)(2,1)} %get-tuple-element.105.refs_0_, f32[512,128]{1,0:T(8,128)} %get-tuple-element.109.refs_1_, bf16[2048,1152]{1,0:T(8,128)(2,1)} %bitcast.53, ...), custom_call_target="tpu_custom_call" | custom-call | flops 1 | bytes 1 | tf_op jit(solution)/shard_map/pallas_call | solution.py:2093
  522.8 1.3 slice_bitcast_fusion.1
  524.1 1.4 slice.47
  525.5 0.8 slice_bitcast_fusion
  526.3 1.7 fusion.1
  528.6 0.9 slice_select_fusion.1
  530.1 3.7 shard_map.299
  533.8 1.3 copy.40
  535.2 1.0 copy-done.3
  536.2 1.3 copy.41
  537.6 0.8 copy.42
  538.4 0.8 copy.43
  (48 shorter events, 7.4 us)
Async XLA Ops:
  7.2 6.9 %copy-start = (bf16[128,256]{1,0:T(8,128)(2,1)S(1)}, bf16[128,256]{1,0:T(8,128)(2,1)}, u32[]{:S(2)}) copy-start(bf16[128,256]{1,0:T(8,128)(2,1)} %param.23) | copy-start | bytes 196612
  7.2 181.5 %all-gather.5.cloned.1.call-start = ((), (), s32[]{:S(2)}) async-start(), calls=%async_computation.4 | async-start | bytes 3932160 | tf_op jit(solution)/shard_map/all_gather | solution.py:2273
  86.8 38.9 %copy-start.2 = (bf16[4,128,1024]{2,1,0:T(8,128)(2,1)S(1)}, bf16[4,128,1024]{2,1,0:T(8,128)(2,1)}, u32[]{:S(2)}) copy-start(bf16[4,128,1024]{2,1,0:T(8,128)(2,1)} %get-tuple-element.73.refs_4_) | copy-start | bytes 3145732
  86.8 39.7 %copy-start.7 = (s32[1,16]{1,0:T(1,128)S(1)}, s32[1,16]{1,0:T(1,128)}, u32[]{:S(2)}) copy-start(s32[1,16]{1,0:T(1,128)} %param.18) | copy-start | bytes 196
  125.7 136.3 %all-gather.7.cloned.1.call-start = ((), (), s32[]{:S(2)}) async-start(), calls=%async_computation.5 | async-start | bytes 3932160 | tf_op jit(solution)/shard_map/all_gather | solution.py:2289
  188.7 151.4 %reduce-scatter.3.cloned.1.call-start = ((), (), s32[]{:S(2)}) async-start(), calls=%async_computation.2 | async-start | bytes 5242880 | tf_op jit(solution)/shard_map/reduce_scatter | solution.py:2301
  261.9 219.4 %reduce-scatter.5.cloned.1.call-start = ((), (), s32[]{:S(2)}) async-start(), calls=%async_computation.3 | async-start | bytes 5242880 | tf_op jit(solution)/shard_map/reduce_scatter | solution.py:2312
  522.8 11.0 %copy-start.4 = (bf16[512,2048]{1,0:T(8,128)(2,1)S(1)}, bf16[512,2048]{1,0:T(8,128)(2,1)}, u32[]{:S(2)}) copy-start(bf16[512,2048]{1,0:T(8,128)(2,1)} %get-tuple-element.152) | copy-start | bytes 6291460
  533.8 2.3 copy-start.3
  536.2 1.4 copy-start.6
  536.2 2.2 copy-start.5
  536.2 3.0 copy-start.1
Sparse Core Ops, SparseCore 0:
  125.8 62.8 all-gather.4
  190.2 62.1 all-gather.6
  262.0 74.9 reduce-scatter.2
  339.2 94.1 reduce-scatter.4

commit v9 on v8

--- a/solution.py
+++ b/solution.py
@@ -1746,7 +1746,21 @@
     each_columns(out_ref.shape[1], 256, work)
 
 
-def project_kernel(
+def project_kernel(cuts, programs, *refs):
+    own, refs = refs[:5], refs[5:]
+    weights, outs, other_out = refs[:2], refs[2:4], refs[4]
+    held, scratch = refs[5:8], refs[8:]
+    works = schedule(programs, (weights,), (other_out,), scratch, ("tp",))
+    for place, work in works:
+        if place < 1:
+            work()
+    project_work(cuts, *own, *outs, *held)
+    for place, work in works:
+        if place >= 1:
+            work()
+
+
+def project_work(
     cuts,
     mixed_ref,
     proj_a_ref,
@@ -1763,7 +1777,6 @@
     half, width = middle_ref.shape
     mine, other = half_rows_of(me["tp"], half), half_rows_of(1 - me["tp"], half)
     tile = 512
-    meet_sibling(me)
     copy = remote(sent_ref, got_ref, sems.at[0], sems.at[1], flip(me, "tp"))
 
     def part(rows, target):
@@ -1819,27 +1832,29 @@
     return [(half * lines + shard) * size for shard in range(lines) for half in range(2)]
 
 
-def project(mixed, proj_a, proj_b, stream, vectors, number):
+def project(mixed, proj_a, proj_b, stream, vectors, exchange, weights, number):
     rows, width = stream.shape
     half = rows // 2
     cuts = line_cuts(width, False)
-    middle, normed = pl.pallas_call(
-        functools.partial(project_kernel, cuts),
+    middle, normed, moved = pl.pallas_call(
+        functools.partial(project_kernel, cuts, [placed(exchange, 0.0, 1.0)]),
         out_shape=[
             jax.ShapeDtypeStruct((half, width), F32),
             jax.ShapeDtypeStruct((half, width), BF16),
+            exchange.out,
         ],
-        in_specs=in_vmem(5),
-        out_specs=in_vmem(2),
+        in_specs=in_vmem(5) + [pl.BlockSpec(memory_space=pl.ANY)] * 2,
+        out_specs=in_vmem(2) + [exchange.out_spec],
         scratch_shapes=[
             pltpu.VMEM((half, width), F32),
             pltpu.VMEM((half, width), F32),
             pltpu.SemaphoreType.DMA((2,)),
-        ],
+        ]
+        + exchange.scratch(),
         compiler_params=kernel_params(number),
         cost_estimate=SMALL,
-    )(mixed, proj_a, proj_b, stream, vectors)
-    return middle, normed if cuts else to_line_order(normed)
+    )(mixed, proj_a, proj_b, stream, vectors, *weights)
+    return middle, normed if cuts else to_line_order(normed), moved
 
 
 def middle_back_kernel(
@@ -2209,13 +2224,12 @@
     hops = [0.1 * k for k in range(1, 4)] if lines == 4 else spaced(0.1, 0.3, lines - 1)
     levels = spaced(0.4, 0.98, 2 * lines)
     piece_hops = spaced(0.35, 0.75, lines - 1)
-    _, first_all, other_cut, early_cut, late_cut, mlp_piece, normed_one, cotangent_line, proj_line = run_programs(
+    _, first_all, other_cut, early_cut, mlp_piece, normed_one, cotangent_line, proj_line = run_programs(
         [
             placed(spread_halves(first_pieces, columns, BF16), 0.0, 0.05),
             placed(rows_gather(first_cut), 0.01, *hops, *levels, 1.0),
             placed(spread_halves(other_pieces, columns, BF16), 0.06, 1.0),
             placed(spread_halves(early_pieces, columns, BF16), 0.06, 1.0),
-            placed(spread_halves(late_pieces, columns, BF16), 0.061, 1.0),
             placed(line_gather((quarters, first_rows, hidden_half), BF16), 0.07, *piece_hops, 1.0),
             placed(Work(norm_work, hidden_in.shape, BF16), 0.31, 0.31),
             placed(Work(functools.partial(reorder_work, cuts or [0]), (half_rows, width), BF16), 0.32, 0.32),
@@ -2224,7 +2238,6 @@
         [
             lambda more, outs: more[3:5],
             lambda more, outs: more[5],
-            lambda more, outs: more[3:5],
             lambda more, outs: more[3:5],
             lambda more, outs: more[3:5],
             lambda more, outs: outs[0],
@@ -2285,11 +2298,18 @@
         2,
     )
     proj_a, proj_b = flat(proj_a), flat(proj_b)
-    mixed_low, mlp_early, late_cut = lax.optimization_barrier((mixed_low, mlp_early, late_cut))
+    mixed_low, mlp_early = lax.optimization_barrier((mixed_low, mlp_early))
+    middle, normed_two_line, late_cut = project(
+        mixed_low,
+        proj_a,
+        proj_b,
+        hidden_in,
+        vectors,
+        spread_halves(late_pieces, columns, BF16),
+        (down_weight, up_weight),
+        5,
+    )
     mlp_late = lax.all_gather(late_cut, "line", axis=0, tiled=False)
-    middle, normed_two_line = project(
-        mixed_low, proj_a, proj_b, hidden_in, vectors, 5
-    )
 
     up_shift = lax.dynamic_slice_in_dim(up_bias, quarter * hidden_dev, hidden_dev).astype(F32)
     up_shift = up_shift[None]

time: 552 us -> 557 us (level)
  transfers between devices with their start and end apart: 4 -> 4, of which waited for: 1 -> 1; matrix products, arithmetic and copies ran while one was open for 1% -> 1% of each run, Pallas kernels for 64% -> 62%
where the time goes in v9:
time: 557 us; the launch traced here: 549 us
  Pallas kernels  506 us (91%)
  local copies, waits for them, and re-layouts  18.2 us (3%)
  between operations  14.2 us (3%)
  other arithmetic  7.42 us (1%)
    pallas_call x3, Pallas kernels, run_programs(): pl.pallas_call(kernel, out_shape=[one.out for one in programs], in_specs=...  159 us
    pallas_call x1, Pallas kernels, attend_back(): pl.pallas_call(functools.partial(attend_back_kernel, programs, blocks * h...  85.1 us
    pallas_call x1, Pallas kernels, second_products(): pl.pallas_call(second_kernel, grid=(steps,), out_shape=[jax.ShapeDtypeStr...  59.5 us
    pallas_call x1, Pallas kernels, attend(): pl.pallas_call(functools.partial(attend_kernel, programs, blocks * heads)...  59.1 us
    pallas_call x1, Pallas kernels, forward_products(): pl.pallas_call(forward_kernel, out_shape=[jax.ShapeDtypeStruct(lead + (wi...  57.6 us
    pallas_call x1, Pallas kernels, first_back(): pl.pallas_call(functools.partial(first_back_kernel, cuts, programs), out_...  41.7 us
    pallas_call x1, Pallas kernels, middle_back(): pl.pallas_call(functools.partial(middle_back_kernel, cuts), out_shape=[ja...  18.8 us
    pallas_call x1, Pallas kernels, project(): pl.pallas_call(functools.partial(project_kernel, cuts, [placed(exchange,...  16.8 us
  transfers between devices with their start and end apart: 4, of which 1 were waited for; matrix products, arithmetic and copies ran while one was open for 1% of the time, Pallas kernels for 62%

profile of v9, /device:TPU:0, one launch (start us, length us, event | category | flops | bytes accessed | tf_op | source)
XLA Modules:
  0.0 549.0 jit_solution(18177284980803194855)
XLA Ops:
  9.2 0.7 stack.24
  9.9 0.7 stack.25
  10.6 0.7 stack.26
  11.3 0.7 stack.27
  12.0 0.7 stack.28
  12.7 0.7 stack.29
  14.1 1.7 pad_maximum_fusion.refs_5_
  15.8 67.6 %shard_map.288 = (bf16[4,64,512]{2,1,0:T(8,128)(2,1)}, bf16[2,4,2,128,1152]{4,3,2,1,0:T(8,128)(2,1)}, bf16[4,64,512]{2,1,0:T(8,128)(2,1)}, bf16[4,192,512]{2,1,0...) custom-call(bf16[512,2048]{1,0:T(8,128)(2,1)} %refs_3_.5, ...), custom_call_target="tpu_custom_call" | custom-call | flops 1 | bytes 1 | tf_op jit(solution)/shard_map/pallas_call | solution.py:735
  83.4 38.1 %shard_map.289 = (bf16[512,128]{1,0:T(8,128)(2,1)}, bf16[512,1024]{1,0:T(8,128)(2,1)}, bf16[2,4,2,512,128]{4,3,2,1,0:T(8,128)(2,1)}, bf16[4,4,64,512]{3,2,1,0:T(8,128)(2,1)}, bf16[2,4,2,128,512]{4,3,2,1,0:T(8,128)(2,1)}) custom-call(bf16[512,2048]{1,0:T(8,128)(2,1)} %get-tuple-element.69.refs_0_.refs_7_.refs_4_, bf16[2048,1152]{1,0:T(8,128)(2,1)} %bitcast.52, ...), custom_call_target="tpu_custom_call" | custom-call | flops 1 | bytes 1 | tf_op jit(solution)/shard_map/pallas_call | solution.py:735
  121.5 0.8 slice.42.refs_4_
  124.7 59.1 %shard_map.290 = (bf16[512,1024]{1,0:T(8,128)(2,1)}, f32[2,8,1,256]{3,2,1,0:T(1,128)}, bf16[2,4,2,128,512]{4,3,2,1,0:T(8,128)(2,1)}, bf16[2,2,2,256,2048]{4,3,2,1,0:T(8,128)(2,1)}) custom-call(s32[2]{0:T(128)} %and_select_fusion.2.refs_0_, s32[2,9]{1,0:T(2,128)} %pad_add_fusion.refs_1_.slot_ref, bf16[512,1024]{1,0:T(8,128)(2,1)} %get-tuple-element.73.refs_2_, ...), custom_call_target="tpu_custom_call" | custom-call | flops 1 | bytes 1 | tf_op jit(solution)/shard_map/pallas_call | solution.py:899
  183.9 16.8 %shard_map.291 = (f32[256,2048]{1,0:T(8,128)}, bf16[256,2048]{1,0:T(8,128)(2,1)}, bf16[4,192,512]{2,1,0:T(8,128)(2,1)}) custom-call(bf16[512,1024]{1,0:T(8,128)(2,1)} %get-tuple-element.80.refs_0_.mixed_ref.refs_4_, bf16[2048,512]{1,0:T(8,128)(2,1)} %bitcast.61, bf16[2048,512]{1,0:T(8,128)(2,1)} %bitcast.63, bf16[512,2048]{1,0:T(8,128)(2,1)} %refs_3_.5, ...), custom_call_target="tpu_custom_call" | custom-call | flops 1 | bytes 1 | tf_op jit(solution)/shard_map/pallas_call | solution.py:1839
  200.8 0.7 dynamic-slice_convert_fusion
  202.1 57.6 %shard_map.292 = (bf16[2,2,2,256,2048]{4,3,2,1,0:T(8,128)(2,1)}, bf16[2,2,2,256,512]{4,3,2,1,0:T(8,128)(2,1)}, bf16[2,2,2,256,512]{4,3,2,1,0:T(8,128)(2,1)}, bf1...) custom-call(bf16[256,2048]{1,0:T(8,128)(2,1)} %get-tuple-element.83.x_ref, ...), custom_call_target="tpu_custom_call" | custom-call | flops 1 | bytes 1 | tf_op jit(solution)/shard_map/pallas_call | solution.py:1326
  259.8 2.5 all-gather.7.cloned.1.call-done
  262.2 59.5 %shard_map.293 = (bf16[2048,2048]{1,0:T(8,128)(2,1)}, bf16[16,2,128,512]{3,2,1,0:T(8,128)(2,1)}, f32[8,512]{1,0:T(8,128)}, f32[256,2048]{1,0:T(8,128)}) custom-call(bf16[2048,2048]{1,0:T(8,128)(2,1)} %bitcast.50, bf16[2048,2048]{1,0:T(8,128)(2,1)} %bitcast.48, bf16[2048,2048]{1,0:T(8,128)(2,1)} %bitcast.57, bf16[2048,2048]{1,0:T(8,128)(2,1)} %bitcast.51, ...), custom_call_target="tpu_custom_call" | custom-call | flops 1 | bytes 1 | tf_op jit(solution)/shard_map/pallas_call | solution.py:1582
  321.8 18.8 %shard_map.294 = (f32[256,2048]{1,0:T(8,128)}, bf16[512,1024]{1,0:T(8,128)(2,1)}, bf16[2048,1024]{1,0:T(8,128)(2,1)}, f32[8,2048]{1,0:T(8,128)}) custom-call(f32[256,2048]{1,0:T(8,128)} %get-tuple-element.94.sum_ref, f32[256,2048]{1,0:T(8,128)} %get-tuple-element.95.middle_ref.refs_8_, bf16[512,2048]{1,0:T(8,128)(2,1)} %cotangent_ref.1, ...), custom_call_target="tpu_custom_call" | custom-call | flops 1 | bytes 1 | tf_op jit(solution)/shard_map/pallas_call | solution.py:1941
  340.6 85.1 %shard_map.295 = (bf16[512,1024]{1,0:T(8,128)(2,1)}, f32[2,2304,256]{2,1,0:T(8,128)}, bf16[2048,1024]{1,0:T(8,128)(2,1)}, f32[128,1024]{1,0:T(8,128)}, f32[256,2048]{1,0:T(8,128)}) custom-call(s32[2]{0:T(128)} %and_select_fusion.2.refs_0_, s32[2,9]{1,0:T(2,128)} %pad_add_fusion.refs_1_.slot_ref, bf16[512,1024]{1,0:T(8,128)(2,1)} %get-tuple-element.73.refs_2_, ...), custom_call_target="tpu_custom_call" | custom-call | flops 1 | bytes 1 | tf_op jit(solution)/shard_map/pallas_call | solution.py:1001
  425.7 4.7 shard_map.296
  430.4 53.7 %shard_map.297 = (bf16[1024,128]{1,0:T(8,128)(2,1)}, f32[512,128]{1,0:T(8,128)}, f32[128,1024]{1,0:T(8,128)}, bf16[256,2048]{1,0:T(8,128)(2,1)}) custom-call(bf16[2,4,1024,128]{3,2,1,0:T(8,128)(2,1)} %bitcast.60, bf16[2,4,2,128,1024]{4,3,2,1,0:T(8,128)(2,1)} %bitcast.66, bf16[4,256,512]{2,1,0:T(8,128)(2,1)} %bitcast.69), custom_call_target="tpu_custom_call" | custom-call | flops 1 | bytes 1 | tf_op jit(solution)/shard_map/pallas_call | solution.py:735
  484.2 41.7 %shard_map.298 = (bf16[512,2048]{1,0:T(8,128)(2,1)}, bf16[512,2048]{1,0:T(8,128)(2,1)}, bf16[256,2048]{1,0:T(8,128)(2,1)}, f32[128,256]{1,0:T(8,128)}, f32[8,4096]{1,0:T(8,128)}) custom-call(bf16[512,1024]{1,0:T(8,128)(2,1)} %get-tuple-element.103.refs_0_, f32[512,128]{1,0:T(8,128)} %get-tuple-element.107.refs_1_, bf16[2048,1152]{1,0:T(8,128)(2,1)} %bitcast.53, ...), custom_call_target="tpu_custom_call" | custom-call | flops 1 | bytes 1 | tf_op jit(solution)/shard_map/pallas_call | solution.py:2108
  525.9 1.3 slice_bitcast_fusion.1
  527.3 1.4 slice.47
  528.6 0.8 slice_bitcast_fusion
  529.4 1.7 fusion.1
  531.7 0.9 slice_select_fusion.1
  533.3 3.7 shard_map.299
  537.0 1.3 copy.40
  538.3 1.0 copy-done.3
  539.3 1.3 copy.41
  540.7 0.8 copy.42
  541.5 0.8 copy.43
  (48 shorter events, 7.3 us)
Async XLA Ops:
  7.2 6.9 %copy-start = (bf16[128,256]{1,0:T(8,128)(2,1)S(1)}, bf16[128,256]{1,0:T(8,128)(2,1)}, u32[]{:S(2)}) copy-start(bf16[128,256]{1,0:T(8,128)(2,1)} %param.23) | copy-start | bytes 196612
  7.2 176.7 %all-gather.5.cloned.1.call-start = ((), (), s32[]{:S(2)}) async-start(), calls=%async_computation.4 | async-start | bytes 3932160 | tf_op jit(solution)/shard_map/all_gather | solution.py:2286
  83.4 38.2 %copy-start.2 = (bf16[4,128,1024]{2,1,0:T(8,128)(2,1)S(1)}, bf16[4,128,1024]{2,1,0:T(8,128)(2,1)}, u32[]{:S(2)}) copy-start(bf16[4,128,1024]{2,1,0:T(8,128)(2,1)} %get-tuple-element.72.refs_4_) | copy-start | bytes 3145732
  83.4 39.0 %copy-start.7 = (s32[1,16]{1,0:T(1,128)S(1)}, s32[1,16]{1,0:T(1,128)}, u32[]{:S(2)}) copy-start(s32[1,16]{1,0:T(1,128)} %param.18) | copy-start | bytes 196
  121.5 140.7 %all-gather.7.cloned.1.call-start = ((), (), s32[]{:S(2)}) async-start(), calls=%async_computation.5 | async-start | bytes 3932160 | tf_op jit(solution)/shard_map/all_gather | solution.py:2312
  200.7 139.9 %reduce-scatter.3.cloned.1.call-start = ((), (), s32[]{:S(2)}) async-start(), calls=%async_computation.2 | async-start | bytes 5242880 | tf_op jit(solution)/shard_map/reduce_scatter | solution.py:2321
  259.7 224.5 %reduce-scatter.5.cloned.1.call-start = ((), (), s32[]{:S(2)}) async-start(), calls=%async_computation.3 | async-start | bytes 5242880 | tf_op jit(solution)/shard_map/reduce_scatter | solution.py:2332
  525.9 11.0 %copy-start.4 = (bf16[512,2048]{1,0:T(8,128)(2,1)S(1)}, bf16[512,2048]{1,0:T(8,128)(2,1)}, u32[]{:S(2)}) copy-start(bf16[512,2048]{1,0:T(8,128)(2,1)} %get-tuple-element.150) | copy-start | bytes 6291460
  537.0 2.3 copy-start.3
  539.3 1.4 copy-start.6
  539.3 2.2 copy-start.5
  539.3 3.0 copy-start.1
Sparse Core Ops, SparseCore 0:
  121.6 61.3 all-gather.4
  200.9 61.3 all-gather.6
  264.5 75.4 reduce-scatter.2
  342.2 94.1 reduce-scatter.4

commit v10 on v8

--- a/solution.py
+++ b/solution.py
@@ -1672,7 +1672,7 @@
         work(pl.ds(pl.multiple_of(index * tile, tile), tile))
         return carry
 
-    lax.fori_loop(0, total // tile, one, 0)
+    lax.fori_loop(0, total // tile, one, 0, unroll=2)
 
 
 def each_columns(total, tile, work):

time: 552 us -> 561 us (1.016)
  starting transfers between devices: 0.34 us -> 11 us
    reduce_scatter x1, starting transfers between devices: 0.22 us -> 10.9 us  [body(): lax.psum_scatter(weight_grad_a, 'line', scatter_dimension=0, tiled=True)]
  transfers between devices with their start and end apart: 4 -> 4, of which waited for: 1 -> 1; matrix products, arithmetic and copies ran while one was open for 1% -> 1% of each run, Pallas kernels for 64% -> 63%
where the time goes in v10:
time: 561 us; the launch traced here: 555 us
  Pallas kernels  503 us (90%)
  local copies, waits for them, and re-layouts  18.2 us (3%)
  between operations  14.2 us (3%)
  starting transfers between devices  11 us (2%)
  other arithmetic  7.42 us (1%)
    pallas_call x3, Pallas kernels, run_programs(): pl.pallas_call(kernel, out_shape=[one.out for one in programs], in_specs=...  163 us
    pallas_call x1, Pallas kernels, attend_back(): pl.pallas_call(functools.partial(attend_back_kernel, programs, blocks * h...  83.8 us
    pallas_call x1, Pallas kernels, second_products(): pl.pallas_call(second_kernel, grid=(steps,), out_shape=[jax.ShapeDtypeStr...  59.4 us
    pallas_call x1, Pallas kernels, attend(): pl.pallas_call(functools.partial(attend_kernel, programs, blocks * heads)...  59 us
    pallas_call x1, Pallas kernels, forward_products(): pl.pallas_call(forward_kernel, out_shape=[jax.ShapeDtypeStruct(lead + (wi...  58.6 us
    pallas_call x1, Pallas kernels, first_back(): pl.pallas_call(functools.partial(first_back_kernel, cuts, programs), out_...  41.7 us
    pallas_call x1, Pallas kernels, middle_back(): pl.pallas_call(functools.partial(middle_back_kernel, cuts), out_shape=[ja...  16.6 us
    pallas_call x1, Pallas kernels, project(): pl.pallas_call(functools.partial(project_kernel, cuts), out_shape=[jax.Sh...  11.9 us
  transfers between devices with their start and end apart: 4, of which 1 were waited for; matrix products, arithmetic and copies ran while one was open for 1% of the time, Pallas kernels for 63%

profile of v10, /device:TPU:0, one launch (start us, length us, event | category | flops | bytes accessed | tf_op | source)
XLA Modules:
  0.0 554.7 jit_solution(16950417632647742227)
XLA Ops:
  9.2 0.7 stack.24
  9.9 0.7 stack.25
  10.6 0.7 stack.26
  11.3 0.7 stack.27
  12.0 0.7 stack.28
  12.7 0.7 stack.29
  14.1 1.7 pad_maximum_fusion.refs_5_
  15.8 71.0 %shard_map.288 = (bf16[4,64,512]{2,1,0:T(8,128)(2,1)}, bf16[2,4,2,128,1152]{4,3,2,1,0:T(8,128)(2,1)}, bf16[4,64,512]{2,1,0:T(8,128)(2,1)}, bf16[4,192,512]{2,1,0...) custom-call(bf16[512,2048]{1,0:T(8,128)(2,1)} %refs_3_.3, ...), custom_call_target="tpu_custom_call" | custom-call | flops 1 | bytes 1 | tf_op jit(solution)/shard_map/pallas_call | solution.py:735
  86.8 38.8 %shard_map.289 = (bf16[512,128]{1,0:T(8,128)(2,1)}, bf16[512,1024]{1,0:T(8,128)(2,1)}, bf16[2,4,2,512,128]{4,3,2,1,0:T(8,128)(2,1)}, bf16[4,4,64,512]{3,2,1,0:T(8,128)(2,1)}, bf16[2,4,2,128,512]{4,3,2,1,0:T(8,128)(2,1)}) custom-call(bf16[512,2048]{1,0:T(8,128)(2,1)} %get-tuple-element.70.refs_0_.refs_7_.refs_4_, bf16[2048,1152]{1,0:T(8,128)(2,1)} %bitcast.52, ...), custom_call_target="tpu_custom_call" | custom-call | flops 1 | bytes 1 | tf_op jit(solution)/shard_map/pallas_call | solution.py:735
  125.7 0.8 slice.42.refs_4_
  128.9 59.0 %shard_map.290 = (bf16[512,1024]{1,0:T(8,128)(2,1)}, f32[2,8,1,256]{3,2,1,0:T(1,128)}, bf16[2,4,2,128,512]{4,3,2,1,0:T(8,128)(2,1)}, bf16[2,2,2,256,2048]{4,3,2,1,0:T(8,128)(2,1)}) custom-call(s32[2]{0:T(128)} %and_select_fusion.2.refs_0_, s32[2,9]{1,0:T(2,128)} %pad_add_fusion.refs_1_.slot_ref, bf16[512,1024]{1,0:T(8,128)(2,1)} %get-tuple-element.74.refs_2_, ...), custom_call_target="tpu_custom_call" | custom-call | flops 1 | bytes 1 | tf_op jit(solution)/shard_map/pallas_call | solution.py:899
  187.9 0.7 all-gather.5.cloned.1.call-done
  188.7 10.9 %reduce-scatter.3.cloned.1.call-start = ((), (), s32[]{:S(2)}) async-start(), calls=%async_computation.2 | async-start | bytes 5242880 | tf_op jit(solution)/shard_map/reduce_scatter | solution.py:2301
  200.9 11.9 %shard_map.291 = (f32[256,2048]{1,0:T(8,128)}, bf16[256,2048]{1,0:T(8,128)(2,1)}) custom-call(bf16[512,1024]{1,0:T(8,128)(2,1)} %get-tuple-element.82.mixed_ref.refs_4_, bf16[2048,512]{1,0:T(8,128)(2,1)} %bitcast.61, bf16[2048,512]{1,0:T(8,128)(2,1)} %bitcast.63, bf16[512,2048]{1,0:T(8,128)(2,1)} %refs_3_.3, ...), custom_call_target="tpu_custom_call" | custom-call | flops 1 | bytes 1 | tf_op jit(solution)/shard_map/pallas_call | solution.py:1826
  212.7 58.6 %shard_map.292 = (bf16[2,2,2,256,2048]{4,3,2,1,0:T(8,128)(2,1)}, bf16[2,2,2,256,512]{4,3,2,1,0:T(8,128)(2,1)}, bf16[2,2,2,256,512]{4,3,2,1,0:T(8,128)(2,1)}, bf1...) custom-call(bf16[256,2048]{1,0:T(8,128)(2,1)} %get-tuple-element.85.x_ref, ...), custom_call_target="tpu_custom_call" | custom-call | flops 1 | bytes 1 | tf_op jit(solution)/shard_map/pallas_call | solution.py:1326
  271.4 59.4 %shard_map.293 = (bf16[2048,2048]{1,0:T(8,128)(2,1)}, bf16[16,2,128,512]{3,2,1,0:T(8,128)(2,1)}, f32[8,512]{1,0:T(8,128)}, f32[256,2048]{1,0:T(8,128)}) custom-call(bf16[2048,2048]{1,0:T(8,128)(2,1)} %bitcast.50, bf16[2048,2048]{1,0:T(8,128)(2,1)} %bitcast.48, bf16[2048,2048]{1,0:T(8,128)(2,1)} %bitcast.57, bf16[2048,2048]{1,0:T(8,128)(2,1)} %bitcast.51, ...), custom_call_target="tpu_custom_call" | custom-call | flops 1 | bytes 1 | tf_op jit(solution)/shard_map/pallas_call | solution.py:1582
  330.9 16.6 %shard_map.294 = (f32[256,2048]{1,0:T(8,128)}, bf16[512,1024]{1,0:T(8,128)(2,1)}, bf16[2048,1024]{1,0:T(8,128)(2,1)}, f32[8,2048]{1,0:T(8,128)}) custom-call(f32[256,2048]{1,0:T(8,128)} %get-tuple-element.96.sum_ref, f32[256,2048]{1,0:T(8,128)} %get-tuple-element.97.middle_ref.refs_8_, bf16[512,2048]{1,0:T(8,128)(2,1)} %cotangent_ref.1, ...), custom_call_target="tpu_custom_call" | custom-call | flops 1 | bytes 1 | tf_op jit(solution)/shard_map/pallas_call | solution.py:1926
  347.5 83.8 %shard_map.295 = (bf16[512,1024]{1,0:T(8,128)(2,1)}, f32[2,2304,256]{2,1,0:T(8,128)}, bf16[2048,1024]{1,0:T(8,128)(2,1)}, f32[128,1024]{1,0:T(8,128)}, f32[256,2048]{1,0:T(8,128)}) custom-call(s32[2]{0:T(128)} %and_select_fusion.2.refs_0_, s32[2,9]{1,0:T(2,128)} %pad_add_fusion.refs_1_.slot_ref, bf16[512,1024]{1,0:T(8,128)(2,1)} %get-tuple-element.74.refs_2_, ...), custom_call_target="tpu_custom_call" | custom-call | flops 1 | bytes 1 | tf_op jit(solution)/shard_map/pallas_call | solution.py:1001
  431.3 4.8 shard_map.296
  436.1 53.7 %shard_map.297 = (bf16[1024,128]{1,0:T(8,128)(2,1)}, f32[512,128]{1,0:T(8,128)}, f32[128,1024]{1,0:T(8,128)}, bf16[256,2048]{1,0:T(8,128)(2,1)}) custom-call(bf16[2,4,1024,128]{3,2,1,0:T(8,128)(2,1)} %bitcast.60, bf16[2,4,2,128,1024]{4,3,2,1,0:T(8,128)(2,1)} %bitcast.66, bf16[4,256,512]{2,1,0:T(8,128)(2,1)} %bitcast.69), custom_call_target="tpu_custom_call" | custom-call | flops 1 | bytes 1 | tf_op jit(solution)/shard_map/pallas_call | solution.py:735
  489.8 41.7 %shard_map.298 = (bf16[512,2048]{1,0:T(8,128)(2,1)}, bf16[512,2048]{1,0:T(8,128)(2,1)}, bf16[256,2048]{1,0:T(8,128)(2,1)}, f32[128,256]{1,0:T(8,128)}, f32[8,4096]{1,0:T(8,128)}) custom-call(bf16[512,1024]{1,0:T(8,128)(2,1)} %get-tuple-element.105.refs_0_, f32[512,128]{1,0:T(8,128)} %get-tuple-element.109.refs_1_, bf16[2048,1152]{1,0:T(8,128)(2,1)} %bitcast.53, ...), custom_call_target="tpu_custom_call" | custom-call | flops 1 | bytes 1 | tf_op jit(solution)/shard_map/pallas_call | solution.py:2093
  531.6 1.3 slice_bitcast_fusion.1
  532.9 1.4 slice.47
  534.3 0.8 slice_bitcast_fusion
  535.0 1.7 fusion.1
  537.4 0.9 slice_select_fusion.1
  538.9 3.7 shard_map.299
  542.6 1.3 copy.40
  543.9 1.0 copy-done.3
  544.9 1.3 copy.41
  546.3 0.8 copy.42
  547.1 0.8 copy.43
  (48 shorter events, 7.9 us)
Async XLA Ops:
  7.2 6.9 %copy-start = (bf16[128,256]{1,0:T(8,128)(2,1)S(1)}, bf16[128,256]{1,0:T(8,128)(2,1)}, u32[]{:S(2)}) copy-start(bf16[128,256]{1,0:T(8,128)(2,1)} %param.23) | copy-start | bytes 196612
  7.2 181.5 %all-gather.5.cloned.1.call-start = ((), (), s32[]{:S(2)}) async-start(), calls=%async_computation.4 | async-start | bytes 3932160 | tf_op jit(solution)/shard_map/all_gather | solution.py:2273
  86.8 38.9 %copy-start.2 = (bf16[4,128,1024]{2,1,0:T(8,128)(2,1)S(1)}, bf16[4,128,1024]{2,1,0:T(8,128)(2,1)}, u32[]{:S(2)}) copy-start(bf16[4,128,1024]{2,1,0:T(8,128)(2,1)} %get-tuple-element.73.refs_4_) | copy-start | bytes 3145732
  86.8 39.7 %copy-start.7 = (s32[1,16]{1,0:T(1,128)S(1)}, s32[1,16]{1,0:T(1,128)}, u32[]{:S(2)}) copy-start(s32[1,16]{1,0:T(1,128)} %param.18) | copy-start | bytes 196
  125.7 145.8 %all-gather.7.cloned.1.call-start = ((), (), s32[]{:S(2)}) async-start(), calls=%async_computation.5 | async-start | bytes 3932160 | tf_op jit(solution)/shard_map/all_gather | solution.py:2289
  188.7 158.8 %reduce-scatter.3.cloned.1.call-start = ((), (), s32[]{:S(2)}) async-start(), calls=%async_computation.2 | async-start | bytes 5242880 | tf_op jit(solution)/shard_map/reduce_scatter | solution.py:2301
  271.4 218.5 %reduce-scatter.5.cloned.1.call-start = ((), (), s32[]{:S(2)}) async-start(), calls=%async_computation.3 | async-start | bytes 5242880 | tf_op jit(solution)/shard_map/reduce_scatter | solution.py:2312
  531.5 11.0 %copy-start.4 = (bf16[512,2048]{1,0:T(8,128)(2,1)S(1)}, bf16[512,2048]{1,0:T(8,128)(2,1)}, u32[]{:S(2)}) copy-start(bf16[512,2048]{1,0:T(8,128)(2,1)} %get-tuple-element.152) | copy-start | bytes 6291460
  542.6 2.3 copy-start.3
  544.9 1.4 copy-start.6
  544.9 2.2 copy-start.5
  544.9 3.0 copy-start.1
Sparse Core Ops, SparseCore 0:
  125.8 62.8 all-gather.4
  190.2 62.1 all-gather.6
  271.5 74.9 reduce-scatter.2
  348.7 94.1 reduce-scatter.4
